TPU v7x, 32 devices: a whole 2x2x4 slice. The times are simulated.
32 devices in a mesh: tok: 16 (over z, y, x), hid: 2 (over core).
Axes of the slice: x: 2, y: 2, z: 4, core: 2. Of those that a mesh axis runs over, the one named last changes fastest.
Arguments:
- tokens: bfloat16 [4096, 1536], P('tok', 'hid'), may hold values from -6 to 6
- ffn_gain: float32 [1536], replicated, may hold values from 0.5 to 1.5
- w_in: bfloat16 [1536, 6144], P('tok', 'hid'), may hold values from -0.15625 to 0.15625
- w_out: bfloat16 [6144, 1536], P('hid', 'tok'), may hold values from -0.078125 to 0.078125
- conv_gain: float32 [1536], replicated, may hold values from 0.5 to 1.5
- w_value: bfloat16 [1536, 1536], P(None, 'hid'), may hold values from -0.15625 to 0.15625
- w_gate: bfloat16 [1536, 1536], P(None, 'hid'), may hold values from -0.15625 to 0.15625
- depth_kernel: float32 [32, 1536], P(None, 'hid'), may hold values from -1 to 1
- bn_scale: float32 [1536], P('hid'), may hold values from 0.5 to 2
- bn_shift: float32 [1536], P('hid'), may hold values from -3 to 3
- w_proj: bfloat16 [1536, 1536], P(None, 'hid'), may hold values from -0.15625 to 0.15625
- lengths: int32 [64], replicated, may hold values from 1 to 128, 4096 in all
Outputs:
- layer_out: bfloat16 [4096, 1536], P('tok', 'hid')
Inputs may be any that keep to these rules, and one draw needn't show every extreme that they name: The lengths sum to 4096 and the longest is exactly 128.
All inputs are finite; a program needn't handle non-finite values.
Results may differ from a plain program's by a relative error of at most 0.0095.
Values may be sent and summed in bfloat16 or wider, within the bound.
No kernel may reach another device: no remote copies, remote signals or barrier semaphores. Data moves between devices by JAX's collectives and lax.ppermute only.
A program may use at most 64 MiB of HBM per device.

v0:
```python
import jax
import jax.numpy as jnp
from jax import lax
from jax.sharding import PartitionSpec as P


def padded(cells, sides, width):
    for axis, dim in sides:
        count = lax.axis_size(axis)
        ends = count - 1
        head = lax.slice_in_dim(cells, 0, width, axis=dim)
        tail = lax.slice_in_dim(cells, cells.shape[dim] - width, cells.shape[dim], axis=dim)
        cells = jnp.concatenate(
            [
                lax.ppermute(tail, axis, [(i, (i + 1) % count) for i in range(ends)]),
                cells,
                lax.ppermute(head, axis, [((i + 1) % count, i) for i in range(ends)]),
            ],
            axis=dim,
        )
    return cells


def norm_rows(values, gain):
    mean = jnp.mean(values, axis=-1, keepdims=True)
    centred = values - mean
    var = jnp.mean(centred * centred, axis=-1, keepdims=True)
    return centred * lax.rsqrt(var + 1e-05) * gain


def local(
    tokens,
    ffn_gain,
    w_in,
    w_out,
    conv_gain,
    w_value,
    w_gate,
    depth_kernel,
    bn_scale,
    bn_shift,
    w_proj,
    lengths,
):
    rows = tokens.shape[0]
    width = tokens.shape[1]
    whole = lax.all_gather(tokens, "hid", axis=1, tiled=True)
    normed = norm_rows(whole.astype(jnp.float32), ffn_gain).astype(jnp.bfloat16)
    pre = jnp.dot(
        normed, lax.all_gather(w_in, "tok", axis=0, tiled=True), preferred_element_type=jnp.float32
    )
    hidden = jax.nn.silu(pre).astype(jnp.bfloat16)
    partial_sum = jnp.dot(
        hidden, lax.all_gather(w_out, "tok", axis=1, tiled=True), preferred_element_type=jnp.float32
    )
    share = lax.psum_scatter(
        partial_sum.astype(jnp.bfloat16), "hid", scatter_dimension=1, tiled=True
    ).astype(jnp.float32)
    mid_own = (tokens.astype(jnp.float32) + 0.5 * share).astype(jnp.bfloat16)
    mid_full = lax.all_gather(mid_own, "hid", axis=1, tiled=True)
    mid_normed = norm_rows(mid_full.astype(jnp.float32), conv_gain).astype(jnp.bfloat16)
    value = jnp.dot(mid_normed, w_value, preferred_element_type=jnp.float32)
    gate = jnp.dot(mid_normed, w_gate, preferred_element_type=jnp.float32)
    glu = (value * jax.nn.sigmoid(gate)).astype(jnp.bfloat16)
    extended = padded(glu, (("tok", 0),), 16).astype(jnp.float32)
    ends = jnp.cumsum(lengths)
    first_row = lax.axis_index("tok") * rows - 16
    positions = first_row + jnp.arange(rows + 32, dtype=jnp.int32)
    utter = jnp.sum((ends[None, :] <= positions[:, None]).astype(jnp.int32), axis=1)
    centre = utter[16 : 16 + rows]
    conv = jnp.zeros((rows, width), jnp.float32)
    for tap in range(depth_kernel.shape[0]):
        same = (utter[tap + 1 : tap + 1 + rows] == centre)[:, None]
        conv = conv + jnp.where(
            same, extended[tap + 1 : tap + 1 + rows] * depth_kernel[tap][None, :], 0.0
        )
    act = jax.nn.silu(conv * bn_scale + bn_shift).astype(jnp.bfloat16)
    act_full = lax.all_gather(act, "hid", axis=1, tiled=True)
    projected = jnp.dot(act_full, w_proj, preferred_element_type=jnp.float32)
    return (mid_own.astype(jnp.float32) + projected).astype(jnp.bfloat16)


def solution(mesh):
    placed = (
        P("tok", "hid"),
        P(),
        P("tok", "hid"),
        P("hid", "tok"),
        P(),
        P(None, "hid"),
        P(None, "hid"),
        P(None, "hid"),
        P("hid"),
        P("hid"),
        P(None, "hid"),
        P(),
    )
    return jax.shard_map(
        local, mesh=mesh, in_specs=placed, out_specs=P("tok", "hid"), check_vma=False
    )
```

profile of v0, /device:TPU:5, one launch (start us, length us, event | category | flops | bytes accessed | tf_op | source)
XLA Modules:
  0.0 308.2 jit_solution(11313606012940823467)
XLA Ops:
  6.5 0.0 copy-start
  6.5 0.0 all-gather.3.cloned.1.call-start
  6.5 0.7 all-gather.3.cloned.1.call-update
  7.3 0.0 all-gather.5.cloned.1.call-start
  7.3 0.7 all-gather.5.cloned.1.call-update
  8.0 0.0 reduce-scatter.2.cloned.1.call-start
  8.1 2.9 all_gather.15
  10.9 0.2 convert_reduce_fusion.1
  11.1 0.3 fusion.7
  11.5 0.0 copy-start.4
  11.5 0.0 copy-start.1
  11.5 121.8 %all-gather.3.cloned.1.call-done = bf16[1536,3072]{1,0:T(8,128)(2,1)} async-done(((bf16[96,3072]{1,0:T(8,128)(2,1)}), bf16[1536,3072]{1,0:T(8,128)(2,1)}) %all-gather.3.cloned.1.call-update) | async-done | bytes 9437200 | tf_op jit(solution)/shard_map/all_gather | solution.py:50
  133.4 123.5 %all-gather.5.cloned.1.call-done = bf16[3072,1536]{0,1:T(8,128)(2,1)} async-done(((bf16[3072,96]{0,1:T(8,128)(2,1)}), bf16[3072,1536]{0,1:T(8,128)(2,1)}) %all-gather.5.cloned.1.call-update) | async-done | bytes 9437200 | tf_op jit(solution)/shard_map/all_gather | solution.py:54
  256.8 12.5 %convolution_convert_fusion = bf16[256,1536]{1,0:T(8,128)(2,1)} fusion(bf16[3072,1536]{0,1:T(8,128)(2,1)} %all-gather.5.cloned.1.call-done, bf16[1536,3072]{1,0:T(8,128)(2,1)} %all-gather.3.cloned.1.call-done, bf16[256,1536]{1,0:T(8,128)(2,1)S(1)} %all_gather.15, f32[1536]{0:T(1024)} %param.13, f32[256]{0:T(256)S(1)} %add_rsqrt_fusion.1, ...), kind=kOutput, calls=%fused_computation.1 | convolution fusion | flops 4838129664 | bytes 20455424 | tf_op jit(solution)/shard_map/dot_general | solution.py:53
  269.3 0.0 reduce-scatter.2.cloned.1.call-update
  269.3 0.0 copy-done.4
  269.3 0.1 copy.15
  269.4 0.1 reduce-window.8
  269.5 0.1 reduce
  269.6 0.1 convert_reduce_fusion.2
  269.7 1.4 slice_reduce_fusion.31
  271.2 0.1 slice_compare_fusion.27
  271.3 0.1 slice_compare_fusion.30
  271.3 0.1 slice_compare_fusion.29
  271.4 0.1 slice_compare_fusion.28
  271.5 5.6 %reduce-scatter.2.cloned.1.call-done = bf16[256,768]{1,0:T(8,128)(2,1)} async-done(((bf16[256,1536]{1,0:T(8,128)(2,1)}), bf16[256,768]{1,0:T(8,128)(2,1)}) %reduce-scatter.2.cloned.1.call-update) | async-done | bytes 393232 | tf_op jit(solution)/shard_map/reduce_scatter | solution.py:56
  277.1 0.0 copy-done.1
  277.2 1.1 add_convert_fusion
  278.3 0.0 copy-start.7
  278.3 2.4 all_gather.18
  280.6 0.2 convert_reduce_fusion
  280.8 0.3 fusion.4
  281.2 0.0 copy-done
  281.2 0.0 copy-done.7
  281.2 0.0 copy-start.5
  281.2 0.9 fusion.13
  282.2 0.7 copy-done.5
  282.9 0.9 fusion.14
  283.8 0.0 copy-start.2
  283.8 0.0 copy-start.3
  283.8 3.1 %collective-permute-start = (bf16[16,768]{1,0:T(8,128)(2,1)S(1)}, bf16[16,768]{1,0:T(8,128)(2,1)S(1)}, u32[]{:S(2)}, u32[]{:S(2)}) collective-permute-start(bf16[16,768]{1,0:T(8,128)(2,1)S(1)} %get-tuple-element.37), channel_id=1, source_target_pairs={{0,2},{2,4},{4,6},{6,8},{8,10},{10,12},{12,14},{14,16},{16,18},{18... | collective-permute-start | bytes 73736 | tf_op jit(solution)/shard_map/ppermute | solution.py:15
  286.9 3.1 %collective-permute-start.1 = (bf16[16,768]{1,0:T(8,128)(2,1)S(1)}, bf16[16,768]{1,0:T(8,128)(2,1)S(1)}, u32[]{:S(2)}, u32[]{:S(2)}) collective-permute-start(bf16[16,768]{1,0:T(8,128)(2,1)S(1)} %get-tuple-element.38), channel_id=1, source_target_pairs={{2,0},{4,2},{6,4},{8,6},{10,8},{12,10},{14,12},{16,14},{18,16},{20... | collective-permute-start | bytes 73736 | tf_op jit(solution)/shard_map/ppermute | solution.py:17
  290.0 1.2 slice_reduce_fusion.30
  291.2 0.0 collective-permute-done
  291.2 0.2 collective-permute-done.1
  291.5 0.1 maximum_convert_fusion
  291.5 0.0 copy-done.2
  291.6 0.0 copy-done.3
  291.6 0.0 copy-start.6
  291.6 4.9 %multiply_convert_fusion.2 = bf16[256,768]{1,0:T(8,128)(2,1)S(1)} fusion(f32[288,768]{1,0:T(8,128)S(1)} %maximum_convert_fusion, f32[768]{0:T(1024)S(1)} %copy-done.2, f32[768]{0:T(1024)S(1)} %copy-done.3, f32[768]{0:T(1024)S(1)} %get-tuple-element.35, f32[768]{0:T(1024)S(1)} %get-tuple-element.36, f32[768]{0:T(1024)S(1)} %get-tuple-element.6, ...), kind=kLoop, calls=%fused_computation.122 | loop fusion | flops 19857408 | bytes 25671424 | tf_op jit(solution)/shard_map/convert_element_type | solution.py:77
  296.5 3.6 %all_gather.19 = bf16[256,1536]{1,0:T(8,128)(2,1)S(1)} all-gather(bf16[256,768]{1,0:T(8,128)(2,1)S(1)} %multiply_convert_fusion.2), channel_id=1, replica_groups=mesh['tok'=16,'hid'=2] {'hid'}, dimensions={1}, use_global_device_ids=true | all-gather | bytes 1179648 | tf_op jit(solution)/shard_map/all_gather | solution.py:78
  300.2 0.0 copy-done.6
  300.2 1.5 fusion.15
  (6 shorter events, 0.0 us)
Async XLA Ops:
  6.5 274.7 %copy-start = (bf16[1536,768]{1,0:T(8,128)(2,1)S(1)}, bf16[1536,768]{1,0:T(8,128)(2,1)}, u32[]{:S(2)}) copy-start(bf16[1536,768]{1,0:T(8,128)(2,1)} %param.18) | copy-start | bytes 7077892
  6.5 126.8 %all-gather.3.cloned.1.call-start = ((), (), s32[]{:S(2)}) async-start(), calls=%async_computation.1 | async-start | bytes 10027008 | tf_op jit(solution)/shard_map/all_gather | solution.py:50
  7.3 249.6 %all-gather.5.cloned.1.call-start = ((), (), s32[]{:S(2)}) async-start(), calls=%async_computation.2 | async-start | bytes 10027008 | tf_op jit(solution)/shard_map/all_gather | solution.py:54
  8.0 269.1 %reduce-scatter.2.cloned.1.call-start = ((), (), s32[]{:S(2)}) async-start(), calls=%async_computation.3 | async-start | bytes 1179648 | tf_op jit(solution)/shard_map/reduce_scatter | solution.py:56
  11.5 257.8 %copy-start.4 = (s32[64]{0:T(128)S(1)}, s32[64]{0:T(128)}, u32[]{:S(2)}) copy-start(s32[64]{0:T(128)} %param.23) | copy-start | bytes 772
  11.5 265.6 %copy-start.1 = (bf16[256,768]{1,0:T(8,128)(2,1)S(1)}, bf16[256,768]{1,0:T(8,128)(2,1)}, u32[]{:S(2)}) copy-start(bf16[256,768]{1,0:T(8,128)(2,1)} %param.12) | copy-start | bytes 1179652
  278.3 2.9 copy-start.7
  281.2 1.7 copy-start.5
  283.8 7.8 %copy-start.2 = (f32[768]{0:T(1024)S(1)}, f32[768]{0:T(1024)}, u32[]{:S(2)}) copy-start(f32[768]{0:T(1024)} %param.21) | copy-start | bytes 9220
  283.8 7.8 %copy-start.3 = (f32[768]{0:T(1024)S(1)}, f32[768]{0:T(1024)}, u32[]{:S(2)}) copy-start(f32[768]{0:T(1024)} %param.20) | copy-start | bytes 9220
  283.8 7.4 %collective-permute-start = (bf16[16,768]{1,0:T(8,128)(2,1)S(1)}, bf16[16,768]{1,0:T(8,128)(2,1)S(1)}, u32[]{:S(2)}, u32[]{:S(2)}) collective-permute-start(bf16[16,768]{1,0:T(8,128)(2,1)S(1)} %get-tuple-element.37), channel_id=1, source_target_pairs={{0,2},{2,4},{4,6},{6,8},{8,10},{10,12},{12,14},{14,16},{16,18},{18... | collective-permute-start | bytes 73736 | tf_op jit(solution)/shard_map/ppermute | solution.py:15
  286.9 4.6 %collective-permute-start.1 = (bf16[16,768]{1,0:T(8,128)(2,1)S(1)}, bf16[16,768]{1,0:T(8,128)(2,1)S(1)}, u32[]{:S(2)}, u32[]{:S(2)}) collective-permute-start(bf16[16,768]{1,0:T(8,128)(2,1)S(1)} %get-tuple-element.38), channel_id=1, source_target_pairs={{2,0},{4,2},{6,4},{8,6},{10,8},{12,10},{14,12},{16,14},{18,16},{20... | collective-permute-start | bytes 73736 | tf_op jit(solution)/shard_map/ppermute | solution.py:17
  291.6 8.6 %copy-start.6 = (bf16[1536,768]{1,0:T(8,128)(2,1)S(1)}, bf16[1536,768]{1,0:T(8,128)(2,1)}, u32[]{:S(2)}) copy-start(bf16[1536,768]{1,0:T(8,128)(2,1)} %param.22) | copy-start | bytes 7077892
Sparse Core Ops, SparseCore 0:
  10.2 123.1 all-gather.2
  136.1 120.6 all-gather.4
  269.4 7.6 reduce-scatter.1
where the time goes:
time: 310 us; the launch traced here: 308 us
  waiting for transfers between devices  253 us (82%)
  matrix products  15.8 us (5%)
  between operations  13.3 us (4%)
  blocking collectives  8.88 us (3%)
  other arithmetic  7.83 us (3%)
  starting transfers between devices  6.26 us (2%)
  local copies, waits for them, and re-layouts  3.52 us (1%)
    all_gather x1, waiting for transfers between devices, local(): lax.all_gather(w_out, 'tok', axis=1, tiled=True)  123 us
    all_gather x1, waiting for transfers between devices, local(): lax.all_gather(w_in, 'tok', axis=0, tiled=True)  122 us
    dot_general x1, matrix products, local(): jnp.dot(hidden, lax.all_gather(w_out, 'tok', axis=1, tiled=True), preferr...  12.5 us
  transfers between devices with their start and end apart: 5, of which 4 were waited for; matrix products, arithmetic and copies ran while one was open for 1% of the time, Pallas kernels for 0%

commit v1 on v0

v1 whole, which is shorter than its diff:
```python
import jax
import jax.numpy as jnp
from jax import lax
from jax.sharding import Mesh, PartitionSpec as P

SWAP = [(0, 1), (1, 0)]


def norm_rows(values, gain):
    mean = jnp.mean(values, axis=-1, keepdims=True)
    centred = values - mean
    var = jnp.mean(centred * centred, axis=-1, keepdims=True)
    return centred * lax.rsqrt(var + 1e-05) * gain


def padded(cells, axis, width):
    count = lax.axis_size(axis)
    ends = count - 1
    head = cells[:width]
    tail = cells[cells.shape[0] - width :]
    return jnp.concatenate(
        [
            lax.ppermute(tail, axis, [(i, (i + 1) % count) for i in range(ends)]),
            cells,
            lax.ppermute(head, axis, [((i + 1) % count, i) for i in range(ends)]),
        ],
        axis=0,
    )


def conv_module(mid_own, mid_full, axis, conv_gain, w_value, w_gate, depth_kernel, bn_scale, bn_shift, w_proj, lengths):
    rows, width = mid_own.shape
    mid_normed = norm_rows(mid_full.astype(jnp.float32), conv_gain).astype(jnp.bfloat16)
    value = jnp.dot(mid_normed, w_value, preferred_element_type=jnp.float32)
    gate = jnp.dot(mid_normed, w_gate, preferred_element_type=jnp.float32)
    glu = (value * jax.nn.sigmoid(gate)).astype(jnp.bfloat16)
    extended = padded(glu, axis, 16).astype(jnp.float32)
    ends = jnp.cumsum(lengths)
    first_row = lax.axis_index(axis) * rows - 16
    positions = first_row + jnp.arange(rows + 32, dtype=jnp.int32)
    utter = jnp.sum((ends[None, :] <= positions[:, None]).astype(jnp.int32), axis=1)
    centre = utter[16 : 16 + rows]
    conv = jnp.zeros((rows, width), jnp.float32)
    for tap in range(depth_kernel.shape[0]):
        same = (utter[tap + 1 : tap + 1 + rows] == centre)[:, None]
        conv = conv + jnp.where(
            same, extended[tap + 1 : tap + 1 + rows] * depth_kernel[tap][None, :], 0.0
        )
    act = jax.nn.silu(conv * bn_scale + bn_shift).astype(jnp.bfloat16)
    act_full = lax.all_gather(act, "hid", axis=1, tiled=True)
    projected = jnp.dot(act_full, w_proj, preferred_element_type=jnp.float32)
    return (mid_own.astype(jnp.float32) + projected).astype(jnp.bfloat16)


def gathered_ffn(tokens, ffn_gain, w_in, w_out):
    whole = lax.all_gather(tokens, "hid", axis=1, tiled=True)
    normed = norm_rows(whole.astype(jnp.float32), ffn_gain).astype(jnp.bfloat16)
    pre = jnp.dot(
        normed, lax.all_gather(w_in, "tok", axis=0, tiled=True), preferred_element_type=jnp.float32
    )
    hidden = jax.nn.silu(pre).astype(jnp.bfloat16)
    partial_sum = jnp.dot(
        hidden, lax.all_gather(w_out, "tok", axis=1, tiled=True), preferred_element_type=jnp.float32
    )
    share = lax.psum_scatter(
        partial_sum.astype(jnp.bfloat16), "hid", scatter_dimension=1, tiled=True
    ).astype(jnp.float32)
    mid_own = (tokens.astype(jnp.float32) + 0.5 * share).astype(jnp.bfloat16)
    return mid_own, lax.all_gather(mid_own, "hid", axis=1, tiled=True)


GROUP = ("bh", "bl")


def partner(values, step):
    return lax.ppermute(values, GROUP, [(i, i ^ step) for i in range(4)])


def ordered(first, second, index, axis):
    return jnp.where(
        index == 0, jnp.stack([first, second], axis), jnp.stack([second, first], axis)
    )


def grouped_ffn(tokens, ffn_gain, w_in, w_out):
    rows, width = tokens.shape
    half = rows // 2
    me_c = lax.axis_index("hid")
    me_a = lax.axis_index("ah")
    me_l = lax.axis_index("al")
    whole = lax.all_gather(tokens, "hid", axis=1, tiled=True)
    normed = norm_rows(whole.astype(jnp.float32), ffn_gain).astype(jnp.bfloat16)
    mine = lax.dynamic_slice_in_dim(normed, me_c * half, half, 0)
    x_own = jnp.concatenate([mine] + [partner(mine, k) for k in (1, 2, 3)], axis=0)
    x_oth = lax.ppermute(x_own, "hid", SWAP)
    x = jnp.concatenate([x_own, x_oth], axis=0)

    def recut(w):
        return lax.all_to_all(
            w.reshape(w.shape[0], 4, w.shape[1] // 4).transpose(1, 0, 2), GROUP, 0, 0
        )

    def spread(own):
        far = lax.ppermute(own, "ah", SWAP)
        own_l = lax.ppermute(own, "al", SWAP)
        far_l = lax.ppermute(far, "al", SWAP)
        def place(a, b):
            return ordered(a, b, me_l, 1).reshape(-1, own.shape[-1])
        return place(own, own_l), place(far, far_l)

    in_own, in_far = spread(recut(w_in))
    out_own, out_far = spread(recut(w_out.T))
    w_full = ordered(in_own, in_far, me_a, 0).reshape(-1, in_own.shape[-1])
    pre = jnp.dot(x, w_full, preferred_element_type=jnp.float32)
    hidden = jax.nn.silu(pre).astype(jnp.bfloat16)

    def sums(w):
        part = lax.dot_general(
            hidden, w, (((1,), (1,)), ((), ())), preferred_element_type=jnp.float32
        )
        kept, sent = part[: rows * 2], part[rows * 2 :]
        total = (
            kept + lax.ppermute(sent.astype(jnp.bfloat16), "hid", SWAP).astype(jnp.float32)
        ).astype(jnp.bfloat16)
        ffn = total[:half].astype(jnp.float32)
        for k in (1, 2, 3):
            ffn = ffn + partner(total[k * half : (k + 1) * half], k).astype(jnp.float32)
        return ffn

    ffn = ordered(sums(out_own), sums(out_far), me_a, 1).reshape(half, -1)
    mine_tok = lax.dynamic_slice_in_dim(whole, me_c * half, half, 0).astype(jnp.float32)
    mid_rows = (mine_tok + 0.5 * ffn).astype(jnp.bfloat16)
    mid_full = lax.all_gather(mid_rows, "hid", axis=0, tiled=True)
    mid_own = lax.dynamic_slice_in_dim(mid_full, me_c * width, width, 1)
    return mid_own, mid_full


def solution(mesh):
    n_tok, n_hid = mesh.shape["tok"], mesh.shape["hid"]
    grouped = n_tok == 16 and n_hid == 2
    if grouped:
        tok = ("ah", "bh", "bl", "al")
        inner = Mesh(mesh.devices.reshape(2, 2, 2, 2, n_hid), tok + ("hid",))
    else:
        tok, inner = "tok", mesh

    def local(tokens, ffn_gain, w_in, w_out, conv_gain, *rest):
        ffn = grouped_ffn if grouped else gathered_ffn
        mid_own, mid_full = ffn(tokens, ffn_gain, w_in, w_out)
        return conv_module(mid_own, mid_full, tok, conv_gain, *rest)

    placed = (
        P(tok, "hid"),
        P(),
        P(tok, "hid"),
        P("hid", tok),
        P(),
        P(None, "hid"),
        P(None, "hid"),
        P(None, "hid"),
        P("hid"),
        P("hid"),
        P(None, "hid"),
        P(),
    )
    return jax.shard_map(
        local, mesh=inner, in_specs=placed, out_specs=P(tok, "hid"), check_vma=False
    )
```

time: 310 us -> 187 us (0.60)
  waiting for transfers between devices: 253 us -> 82.5 us
  starting transfers between devices: 6.26 us -> 31.2 us
  local copies, waits for them, and re-layouts: 3.52 us -> 23.9 us
  other arithmetic: 7.83 us -> 27.6 us
  between operations: 13.3 us -> 0.35 us
  matrix products: 15.8 us -> 9.01 us
    all_gather x2 -> x0, waiting for transfers between devices: 245 us -> none  [the longest x1 123 us: local(): lax.all_gather(w_out, 'tok', axis=1, tiled=True)]
    ppermute x0 -> x18, waiting for transfers between devices: none -> 80.8 us  [the longest x2 44.1 us: spread(): far = lax.ppermute(own, 'ah', SWAP)]
    ppermute x0 -> x18, starting transfers between devices: none -> 17.6 us  [the longest x9 6.61 us: partner(): return lax.ppermute(values, GROUP, [(i, i ^ step) for i in range(4)])]
    all_to_all x0 -> x2, starting transfers between devices: none -> 8.29 us  [recut(): lax.all_to_all(w.reshape(w.shape[0], 4, w.shape[1] // 4).transpose(1, 0,...]
    dot_general x4 -> x6, matrix products: 15.8 us -> 9.01 us  [the longest x1 2.87 us: grouped_ffn(): pre = jnp.dot(x, w_full, preferred_element_type=jnp.float32)]
    unnamed x16 -> x23, local copies, waits for them, and re-layouts: 0.76 us -> 7.26 us
    reduce_scatter x1 -> x0, waiting for transfers between devices: 5.63 us -> none  [local(): lax.psum_scatter(partial_sum.astype(jnp.bfloat16), 'hid', scatter_dimensi...]
    select_n x0 -> x5, other arithmetic: none -> 5.31 us  [ordered(): jnp.where(index == 0, jnp.stack([first, second], axis), jnp.stack([second...]
  transfers between devices with their start and end apart: 5 -> 22, of which waited for: 4 -> 11; matrix products, arithmetic and copies ran while one was open for 1% -> 21% of each run, Pallas kernels for 0% -> 0%
where the time goes in v1:
time: 187 us; the launch traced here: 184 us
  waiting for transfers between devices  82.5 us (44%)
  starting transfers between devices  31.2 us (17%)
  other arithmetic  27.6 us (15%)
  local copies, waits for them, and re-layouts  23.9 us (13%)
  blocking collectives  9.24 us (5%)
  matrix products  9.01 us (5%)
    ppermute x2, waiting for transfers between devices, spread(): far = lax.ppermute(own, 'ah', SWAP)  44.1 us
    ppermute x9, waiting for transfers between devices, partner(): return lax.ppermute(values, GROUP, [(i, i ^ step) for i in range(4)])  21.6 us
    ppermute x2, waiting for transfers between devices, spread(): far_l = lax.ppermute(far, 'al', SWAP)  15.1 us
    all_to_all x2, starting transfers between devices, recut(): lax.all_to_all(w.reshape(w.shape[0], 4, w.shape[1] // 4).transpose(1, 0,...  8.29 us
    unnamed x23, local copies, waits for them, and re-layouts  7.26 us
    convert_element_type x1, other arithmetic, conv_module(): act = jax.nn.silu(conv * bn_scale + bn_shift).astype(jnp.bfloat16)  6.72 us
    ppermute x9, starting transfers between devices, partner(): return lax.ppermute(values, GROUP, [(i, i ^ step) for i in range(4)])  6.61 us
    select_n x5, other arithmetic, ordered(): jnp.where(index == 0, jnp.stack([first, second], axis), jnp.stack([second...  5.31 us
  transfers between devices with their start and end apart: 22, of which 11 were waited for; matrix products, arithmetic and copies ran while one was open for 21% of the time, Pallas kernels for 0%

profile of v1, /device:TPU:5, one launch (start us, length us, event | category | flops | bytes accessed | tf_op | source)
XLA Modules:
  0.0 183.8 jit_solution(15587997986907925849)
XLA Ops:
  0.0 1.9 %reshape.153 = bf16[96,4,768]{2,1,0:T(4,128)(2,1)S(1)} reshape(bf16[96,3072]{1,0:T(8,128)(2,1)} %param.14) | data formatting | bytes 1179648 | tf_op jit(solution)/shard_map/reshape | solution.py:100
  1.9 0.9 copy.31
  2.8 4.2 %all-to-all-start = ((bf16[4,96,768]{2,1,0:T(8,128)(2,1)}), bf16[4,96,768]{2,1,0:T(8,128)(2,1)}, u32[]{:S(2)}, u32[]{:S(2)}) async-start(bf16[4,96,768]{2,1,0:T(8,128)(2,1)} %copy.31), calls=%async_computation | async-start | bytes 1179648 | tf_op jit(solution)/shard_map/all_to_all | solution.py:99
  7.0 2.8 %all_gather.9 = bf16[256,1536]{1,0:T(8,128)(2,1)S(1)} all-gather(bf16[256,768]{1,0:T(8,128)(2,1)S(1)} %copy-done.1), channel_id=1, replica_groups=mesh['ah'=2,'bh'=2,'bl'=2,'al'=2,'hid'=2] {'hid'}, dimensions={1}, use_global_device_ids=true | all-gather | bytes 1179648 | tf_op jit(solution)/shard_map/all_gather | solution.py:91
  10.0 1.4 convert_subtract_fusion.1
  11.5 2.1 %constant_dynamic-update-slice_fusion.4 = (bf16[1024,1536]{1,0:T(8,128)(2,1)}, bf16[128,1536]{1,0:T(8,128)(2,1)}) fusion(f32[1536]{0:T(1024)S(1)} %copy-done.5, f32[128]{0:T(128)S(1)} %dynamic-slice, f32[256,1536]{1,0:T(8,128)} %get-tuple-element.39, s32[]{:T(128)S(6)} %select_n.172), kind=kLoop, calls=%fused_computation.142 | loop fusion | flops 589823 | bytes 1579524
  13.6 1.5 collective-permute-start.1
  15.1 1.2 collective-permute-start.2
  16.3 2.5 %reshape.154 = bf16[96,4,768]{2,1,0:T(4,128)(2,1)} reshape(bf16[96,3072]{1,0:T(8,128)(2,1)} %bitcast.44) | data formatting | bytes 1179648 | tf_op jit(solution)/shard_map/reshape | solution.py:100
  18.8 1.9 %copy.32 = bf16[4,96,768]{2,1,0:T(8,128)(2,1)} copy(bf16[4,96,768]{2,0,1:T(4,128)(2,1)} %bitcast.37) | data formatting | bytes 1179648 | tf_op jit(solution)/shard_map/transpose | solution.py:100
  20.7 0.7 copy.34
  21.4 1.4 reduce-window.8
  22.8 0.9 reduce
  23.7 4.1 %all-to-all-start.1 = ((bf16[4,96,768]{2,1,0:T(8,128)(2,1)}), bf16[4,96,768]{2,1,0:T(8,128)(2,1)}, u32[]{:S(2)}, u32[]{:S(2)}) async-start(bf16[4,96,768]{2,1,0:T(8,128)(2,1)} %copy.32), calls=%async_computation.1 | async-start | bytes 1179648 | tf_op jit(solution)/shard_map/all_to_all | solution.py:99
  27.9 5.6 %collective-permute-done.2 = bf16[128,1536]{1,0:T(8,128)(2,1)S(1)} collective-permute-done((bf16[128,1536]{1,0:T(8,128)(2,1)}, bf16[128,1536]{1,0:T(8,128)(2,1)S(1)}, u32[]{:S(2)}, u32[]{:S(2)}) %collective-permute-start.2) | collective-permute-done | bytes 393248 | tf_op jit(solution)/shard_map/ppermute | solution.py:76
  33.5 2.5 %pad_maximum_fusion = bf16[512,1536]{1,0:T(8,128)(2,1)} fusion(bf16[128,1536]{1,0:T(8,128)(2,1)S(1)} %collective-permute-done.2, bf16[128,1536]{1,0:T(8,128)(2,1)} %collective-permute-done.1, bf16[128,1536]{1,0:T(8,128)(2,1)} %collective-permute-done, bf16[128,1536]{1,0:T(8,128)(2,1)} %get-tuple-element.38), kind=kLoop, calls=%fused_computation.17 | loop fusion | flops 6291456 | bytes 3145728 | tf_op jit(solution)/shard_map/concatenate | solution.py:94
  36.0 2.7 %collective-permute-start.3 = (bf16[512,1536]{1,0:T(8,128)(2,1)}, bf16[512,1536]{1,0:T(8,128)(2,1)}, u32[]{:S(2)}, u32[]{:S(2)}) collective-permute-start(bf16[512,1536]{1,0:T(8,128)(2,1)} %pad_maximum_fusion), channel_id=1, source_target_pairs={{0,1},{1,0},{2,3},{3,2},{4,5},{5,4},{6,7},{7,6},{8,9},{9,8},{10,11... | collective-permute-start | bytes 4718600 | tf_op jit(solution)/shard_map/ppermute | solution.py:95
  39.5 0.7 slice_compare_fusion.29
  40.2 2.6 %collective-permute-start.5 = (bf16[4,96,768]{2,1,0:T(8,128)(2,1)}, bf16[4,96,768]{2,1,0:T(8,128)(2,1)}, u32[]{:S(2)}, u32[]{:S(2)}) collective-permute-start(bf16[4,96,768]{2,1,0:T(8,128)(2,1)} %all-to-all-done), channel_id=1, source_target_pairs={{0,16},{16,0},{1,17},{17,1},{2,18},{18,2},{3,19},{19,3},{4,20},{20... | collective-permute-start | bytes 1769480 | tf_op jit(solution)/shard_map/ppermute | solution.py:104
  42.8 0.7 slice_compare_fusion.27
  43.5 1.2 collective-permute-start.4
  44.7 1.8 constant_dynamic-update-slice_fusion.3
  46.5 1.8 constant_dynamic-update-slice_fusion.2
  48.3 33.8 %collective-permute-done.5 = bf16[4,96,768]{2,1,0:T(8,128)(2,1)} collective-permute-done((bf16[4,96,768]{2,1,0:T(8,128)(2,1)}, bf16[4,96,768]{2,1,0:T(8,128)(2,1)}, u32[]{:S(2)}, u32[]{:S(2)}) %collective-permute-start.5) | collective-permute-done | bytes 589856 | tf_op jit(solution)/shard_map/ppermute | solution.py:104
  82.1 1.1 collective-permute-start.6
  83.2 0.8 constant_dynamic-update-slice_fusion.1
  84.3 10.3 %collective-permute-done.12 = bf16[4,96,768]{2,1,0:T(8,128)(2,1)S(1)} collective-permute-done((bf16[4,96,768]{2,1,0:T(8,128)(2,1)}, bf16[4,96,768]{2,1,0:T(8,128)(2,1)S(1)}, u32[]{:S(2)}, u32[]{:S(2)}) %collective-permute-start.12) | collective-permute-done | bytes 589856 | tf_op jit(solution)/shard_map/ppermute | solution.py:104
  94.6 1.1 collective-permute-start.13
  95.7 1.8 maximum_select_fusion.1
  97.5 2.7 %constant_dynamic-update-slice_fusion = bf16[1024,1536]{1,0:T(8,128)(2,1)} fusion(bf16[1024,1536]{1,0:T(8,128)(2,1)} %constant_dynamic-update-slice_fusion.1, bf16[512,1536]{1,0:T(8,128)(2,1)} %collective-permute-done.3), kind=kLoop, calls=%fused_computation.138 | loop fusion | bytes 3145728 | tf_op jit(solution)/shard_map/concatenate | solution.py:96
  100.2 1.5 maximum_select_fusion.2
  102.1 1.5 copy-done.3
  103.6 2.9 %multiply_convert_fusion = bf16[1024,768]{1,0:T(8,128)(2,1)S(1)} fusion(bf16[1024,1536]{1,0:T(8,128)(2,1)S(1)} %copy-done.3, bf16[1536,768]{1,0:T(8,128)(2,1)S(1)} %bitcast.35), kind=kOutput, calls=%fused_computation | convolution fusion | flops 2419851264 | bytes 7077888 | tf_op jit(solution)/shard_map/dot_general | solution.py:114
  106.5 15.1 %collective-permute-done.13 = bf16[4,96,768]{2,1,0:T(8,128)(2,1)S(1)} collective-permute-done((bf16[4,96,768]{2,1,0:T(8,128)(2,1)S(1)}, bf16[4,96,768]{2,1,0:T(8,128)(2,1)S(1)}, u32[]{:S(2)}, u32[]{:S(2)}) %collective-permute-start.13) | collective-permute-done | bytes 589856 | tf_op jit(solution)/shard_map/ppermute | solution.py:106
  121.7 1.4 fusion.86
  123.3 1.8 collective-permute-start.14
  125.0 1.5 maximum_select_fusion.3
  126.5 1.4 fusion.85
  128.8 0.7 slice_reduce_fusion.31
  129.6 0.7 slice_compare_fusion.28
  130.8 0.9 collective-permute-start.16
  131.7 1.7 collective-permute-start.15
  134.1 0.9 collective-permute-start.10
  135.0 3.2 %collective-permute-done.17 = bf16[128,768]{0,1:T(8,128)(2,1)S(1)} collective-permute-done((bf16[128,768]{0,1:T(8,128)(2,1)S(1)}, bf16[128,768]{0,1:T(8,128)(2,1)S(1)}, u32[]{:S(2)}, u32[]{:S(2)}) %collective-permute-start.17) | collective-permute-done | bytes 196640 | tf_op jit(solution)/shard_map/ppermute | solution.py:76
  138.2 2.8 %collective-permute-done.16 = bf16[128,768]{0,1:T(8,128)(2,1)S(1)} collective-permute-done((bf16[128,768]{0,1:T(8,128)(2,1)S(1)}, bf16[128,768]{0,1:T(8,128)(2,1)S(1)}, u32[]{:S(2)}, u32[]{:S(2)}) %collective-permute-start.16) | collective-permute-done | bytes 196640 | tf_op jit(solution)/shard_map/ppermute | solution.py:76
  141.0 2.0 %collective-permute-done.15 = bf16[128,768]{0,1:T(8,128)(2,1)S(1)} collective-permute-done((bf16[128,768]{0,1:T(8,128)(2,1)S(1)}, bf16[128,768]{0,1:T(8,128)(2,1)S(1)}, u32[]{:S(2)}, u32[]{:S(2)}) %collective-permute-start.15) | collective-permute-done | bytes 196640 | tf_op jit(solution)/shard_map/ppermute | solution.py:76
  143.0 3.6 %collective-permute-done.11 = bf16[128,768]{0,1:T(8,128)(2,1)S(1)} collective-permute-done((bf16[128,768]{0,1:T(8,128)(2,1)S(1)}, bf16[128,768]{0,1:T(8,128)(2,1)S(1)}, u32[]{:S(2)}, u32[]{:S(2)}) %collective-permute-start.11) | collective-permute-done | bytes 196640 | tf_op jit(solution)/shard_map/ppermute | solution.py:76
  146.6 2.8 %collective-permute-done.10 = bf16[128,768]{0,1:T(8,128)(2,1)S(1)} collective-permute-done((bf16[128,768]{0,1:T(8,128)(2,1)S(1)}, bf16[128,768]{0,1:T(8,128)(2,1)S(1)}, u32[]{:S(2)}, u32[]{:S(2)}) %collective-permute-start.10) | collective-permute-done | bytes 196640 | tf_op jit(solution)/shard_map/ppermute | solution.py:76
  149.4 1.7 collective-permute-done.9
  151.2 0.9 fusion.78
  152.1 2.3 %copy.33 = f32[128,1536]{1,0:T(8,128)} copy(f32[128,1536]{0,1:T(8,128)} %bitcast.34) | data formatting | bytes 1572864 | tf_op jit(solution)/shard_map/mul | solution.py:132
  154.4 1.2 add_convert_fusion
  155.6 2.6 %all_gather.10 = bf16[256,1536]{1,0:T(8,128)(2,1)S(1)} all-gather(bf16[128,1536]{1,0:T(8,128)(2,1)S(1)} %add_convert_fusion), channel_id=1, replica_groups=mesh['ah'=2,'bh'=2,'bl'=2,'al'=2,'hid'=2] {'hid'}, dimensions={0}, use_global_device_ids=true | all-gather | bytes 1179648 | tf_op jit(solution)/shard_map/all_gather | solution.py:133
  158.9 0.9 fusion.9
  159.8 0.7 copy-done.7
  160.5 0.9 fusion.10
  162.0 3.1 %collective-permute-start.19 = (bf16[16,768]{1,0:T(8,128)(2,1)}, bf16[16,768]{1,0:T(8,128)(2,1)}, u32[]{:S(2)}, u32[]{:S(2)}) collective-permute-start(bf16[16,768]{1,0:T(8,128)(2,1)} %get-tuple-element.48), channel_id=1, source_target_pairs={{2,0},{4,2},{6,4},{8,6},{10,8},{12,10},{14,12},{16,14},{18,16},{20... | collective-permute-start | bytes 73736 | tf_op jit(solution)/shard_map/ppermute | solution.py:25
  165.1 2.2 %collective-permute-start.18 = (bf16[16,768]{1,0:T(8,128)(2,1)}, bf16[16,768]{1,0:T(8,128)(2,1)}, u32[]{:S(2)}, u32[]{:S(2)}) collective-permute-start(bf16[16,768]{1,0:T(8,128)(2,1)} %get-tuple-element.47), channel_id=1, source_target_pairs={{0,2},{2,4},{4,6},{6,8},{8,10},{10,12},{12,14},{14,16},{16,18},{18... | collective-permute-start | bytes 73736 | tf_op jit(solution)/shard_map/ppermute | solution.py:23
  167.3 1.9 %slice_reduce_fusion.30 = (f32[768]{0:T(1024)}, f32[768]{0:T(1024)}, f32[768]{0:T(1024)}, f32[768]{0:T(1024)}, f32[768]{0:T(1024)}, /*index=5*/f32[768]{0:T(1024...) fusion(f32[32,768]{1,0:T(8,128)} %param.19), kind=kLoop, calls=%fused_computation.173 | loop fusion | bytes 79872 | tf_op jit(solution)/shard_map/slice | solution.py:47
  169.2 1.7 collective-permute-done.18
  170.9 0.8 maximum_convert_fusion
  171.7 6.7 %multiply_convert_fusion.1 = bf16[256,768]{1,0:T(8,128)(2,1)S(1)} fusion(f32[288,768]{1,0:T(8,128)S(1)} %maximum_convert_fusion, f32[768]{0:T(1024)} %param.21, f32[768]{0:T(1024)} %param.20, f32[768]{0:T(1024)} %get-tuple-element.35, f32[768]{0:T(1024)} %get-tuple-element.36, f32[768]{0:T(1024)S(1)} %get-tuple-element.6, f32[768]{0:T(1024)S(1)} %get-tuple-element.7, ...), kind=kLoop, calls=%fused_computation.132 | loop fusion | flops 19857408 | bytes 25671424 | tf_op jit(solution)/shard_map/convert_element_type | solution.py:49
  178.5 3.8 %all_gather.11 = bf16[256,1536]{1,0:T(8,128)(2,1)S(1)} all-gather(bf16[256,768]{1,0:T(8,128)(2,1)S(1)} %multiply_convert_fusion.1), channel_id=1, replica_groups=mesh['ah'=2,'bh'=2,'bl'=2,'al'=2,'hid'=2] {'hid'}, dimensions={1}, use_global_device_ids=true | all-gather | bytes 1179648 | tf_op jit(solution)/shard_map/all_gather | solution.py:50
  182.3 1.5 fusion.11
  (58 shorter events, 5.7 us)
Async XLA Ops:
  0.0 158.8 %copy-start = (bf16[1536,768]{1,0:T(8,128)(2,1)S(1)}, bf16[1536,768]{1,0:T(8,128)(2,1)}, u32[]{:S(2)}) copy-start(bf16[1536,768]{1,0:T(8,128)(2,1)} %param.18) | copy-start | bytes 7077892
  0.0 7.0 %copy-start.1 = (bf16[256,768]{1,0:T(8,128)(2,1)S(1)}, bf16[256,768]{1,0:T(8,128)(2,1)}, u32[]{:S(2)}) copy-start(bf16[256,768]{1,0:T(8,128)(2,1)} %param.12) | copy-start | bytes 1179652
  2.8 20.9 %all-to-all-start = ((bf16[4,96,768]{2,1,0:T(8,128)(2,1)}), bf16[4,96,768]{2,1,0:T(8,128)(2,1)}, u32[]{:S(2)}, u32[]{:S(2)}) async-start(bf16[4,96,768]{2,1,0:T(8,128)(2,1)} %copy.31), calls=%async_computation | async-start | bytes 1179648 | tf_op jit(solution)/shard_map/all_to_all | solution.py:99
  9.8 1.7 copy-start.5
  13.6 7.1 %copy-start.6 = (s32[64]{0:T(128)S(1)}, s32[64]{0:T(128)}, u32[]{:S(2)}) copy-start(s32[64]{0:T(128)} %param.23) | copy-start | bytes 772
  13.6 14.2 %collective-permute-start = (bf16[128,1536]{1,0:T(8,128)(2,1)}, bf16[128,1536]{1,0:T(8,128)(2,1)}, u32[]{:S(2)}, u32[]{:S(2)}) collective-permute-start(bf16[128,1536]{1,0:T(8,128)(2,1)} %get-tuple-element.38), channel_id=1, source_target_pairs={{0,4},{4,0},{8,12},{12,8},{1,5},{5,1},{9,13},{13,9},{2,6},{6,2},{1... | collective-permute-start | bytes 1179656 | tf_op jit(solution)/shard_map/ppermute | solution.py:76
  13.6 14.2 %collective-permute-start.1 = (bf16[128,1536]{1,0:T(8,128)(2,1)}, bf16[128,1536]{1,0:T(8,128)(2,1)}, u32[]{:S(2)}, u32[]{:S(2)}) collective-permute-start(bf16[128,1536]{1,0:T(8,128)(2,1)} %get-tuple-element.38), channel_id=1, source_target_pairs={{0,8},{4,12},{8,0},{12,4},{1,9},{5,13},{9,1},{13,5},{2,10},{6,14},... | collective-permute-start | bytes 1179656 | tf_op jit(solution)/shard_map/ppermute | solution.py:76
  15.1 18.4 %collective-permute-start.2 = (bf16[128,1536]{1,0:T(8,128)(2,1)}, bf16[128,1536]{1,0:T(8,128)(2,1)S(1)}, u32[]{:S(2)}, u32[]{:S(2)}) collective-permute-start(bf16[128,1536]{1,0:T(8,128)(2,1)} %get-tuple-element.38), channel_id=1, source_target_pairs={{0,12},{4,8},{8,4},{12,0},{1,13},{5,9},{9,5},{13,1},{2,14},{6,10},... | collective-permute-start | bytes 1179656 | tf_op jit(solution)/shard_map/ppermute | solution.py:76
  23.7 21.0 %all-to-all-start.1 = ((bf16[4,96,768]{2,1,0:T(8,128)(2,1)}), bf16[4,96,768]{2,1,0:T(8,128)(2,1)}, u32[]{:S(2)}, u32[]{:S(2)}) async-start(bf16[4,96,768]{2,1,0:T(8,128)(2,1)} %copy.32), calls=%async_computation.1 | async-start | bytes 1179648 | tf_op jit(solution)/shard_map/all_to_all | solution.py:99
  36.0 61.5 %collective-permute-start.3 = (bf16[512,1536]{1,0:T(8,128)(2,1)}, bf16[512,1536]{1,0:T(8,128)(2,1)}, u32[]{:S(2)}, u32[]{:S(2)}) collective-permute-start(bf16[512,1536]{1,0:T(8,128)(2,1)} %pad_maximum_fusion), channel_id=1, source_target_pairs={{0,1},{1,0},{2,3},{3,2},{4,5},{5,4},{6,7},{7,6},{8,9},{9,8},{10,11... | collective-permute-start | bytes 4718600 | tf_op jit(solution)/shard_map/ppermute | solution.py:95
  40.2 41.9 %collective-permute-start.5 = (bf16[4,96,768]{2,1,0:T(8,128)(2,1)}, bf16[4,96,768]{2,1,0:T(8,128)(2,1)}, u32[]{:S(2)}, u32[]{:S(2)}) collective-permute-start(bf16[4,96,768]{2,1,0:T(8,128)(2,1)} %all-to-all-done), channel_id=1, source_target_pairs={{0,16},{16,0},{1,17},{17,1},{2,18},{18,2},{3,19},{19,3},{4,20},{20... | collective-permute-start | bytes 1769480 | tf_op jit(solution)/shard_map/ppermute | solution.py:104
  43.5 52.2 %collective-permute-start.4 = (bf16[4,96,768]{2,1,0:T(8,128)(2,1)}, bf16[4,96,768]{2,1,0:T(8,128)(2,1)}, u32[]{:S(2)}, u32[]{:S(2)}) collective-permute-start(bf16[4,96,768]{2,1,0:T(8,128)(2,1)} %all-to-all-done), channel_id=1, source_target_pairs={{0,2},{2,0},{1,3},{3,1},{4,6},{6,4},{5,7},{7,5},{8,10},{10,8},{9,1... | collective-permute-start | bytes 1769480 | tf_op jit(solution)/shard_map/ppermute | solution.py:105
  44.7 49.9 %collective-permute-start.12 = (bf16[4,96,768]{2,1,0:T(8,128)(2,1)}, bf16[4,96,768]{2,1,0:T(8,128)(2,1)S(1)}, u32[]{:S(2)}, u32[]{:S(2)}) collective-permute-start(bf16[4,96,768]{2,1,0:T(8,128)(2,1)} %all-to-all-done.1), channel_id=1, source_target_pairs={{0,16},{16,0},{1,17},{17,1},{2,18},{18,2},{3,19},{19,3},{4,20},{20... | collective-permute-start | bytes 1769480 | tf_op jit(solution)/shard_map/ppermute | solution.py:104
  82.1 18.1 %collective-permute-start.6 = (bf16[4,96,768]{2,1,0:T(8,128)(2,1)}, bf16[4,96,768]{2,1,0:T(8,128)(2,1)S(1)}, u32[]{:S(2)}, u32[]{:S(2)}) collective-permute-start(bf16[4,96,768]{2,1,0:T(8,128)(2,1)} %collective-permute-done.5), channel_id=1, source_target_pairs={{0,2},{2,0},{1,3},{3,1},{4,6},{6,4},{5,7},{7,5},{8,10},{10,8},{9,1... | collective-permute-start | bytes 1769480 | tf_op jit(solution)/shard_map/ppermute | solution.py:106
  84.0 41.1 %collective-permute-start.7 = (bf16[4,96,768]{2,1,0:T(8,128)(2,1)}, bf16[4,96,768]{2,1,0:T(8,128)(2,1)S(1)}, u32[]{:S(2)}, u32[]{:S(2)}) collective-permute-start(bf16[4,96,768]{2,1,0:T(8,128)(2,1)} %all-to-all-done.1), channel_id=1, source_target_pairs={{0,2},{2,0},{1,3},{3,1},{4,6},{6,4},{5,7},{7,5},{8,10},{10,8},{9,1... | collective-permute-start | bytes 1769480 | tf_op jit(solution)/shard_map/ppermute | solution.py:105
  94.6 27.0 %collective-permute-start.13 = (bf16[4,96,768]{2,1,0:T(8,128)(2,1)S(1)}, bf16[4,96,768]{2,1,0:T(8,128)(2,1)S(1)}, u32[]{:S(2)}, u32[]{:S(2)}) collective-permute-start(bf16[4,96,768]{2,1,0:T(8,128)(2,1)S(1)} %collective-permute-done.12), channel_id=1, source_target_pairs={{0,2},{2,0},{1,3},{3,1},{4,6},{6,4},{5,7},{7,5},{8,10},{10,8},{9,1... | collective-permute-start | bytes 1769480 | tf_op jit(solution)/shard_map/ppermute | solution.py:106
  101.7 1.9 %copy-start.3 = (bf16[1024,1536]{1,0:T(8,128)(2,1)S(1)}, bf16[1024,1536]{1,0:T(8,128)(2,1)}, u32[]{:S(2)}) copy-start(bf16[1024,1536]{1,0:T(8,128)(2,1)} %constant_dynamic-update-slice_fusion) | copy-start | bytes 9437188
  123.3 7.0 %collective-permute-start.14 = (bf16[512,768]{0,1:T(8,128)(2,1)S(1)}, bf16[512,768]{0,1:T(8,128)(2,1)S(1)}, u32[]{:S(2)}, u32[]{:S(2)}) collective-permute-start(bf16[512,768]{0,1:T(8,128)(2,1)S(1)} %slice.879), channel_id=1, source_target_pairs={{0,1},{1,0},{2,3},{3,2},{4,5},{5,4},{6,7},{7,6},{8,9},{9,8},{10,11... | collective-permute-start | bytes 2359304 | tf_op jit(solution)/shard_map/ppermute | solution.py:123
  127.9 0.9 copy-start.2
  128.0 5.3 %collective-permute-start.8 = (bf16[512,768]{0,1:T(8,128)(2,1)S(1)}, bf16[512,768]{0,1:T(8,128)(2,1)S(1)}, u32[]{:S(2)}, u32[]{:S(2)}) collective-permute-start(bf16[512,768]{0,1:T(8,128)(2,1)S(1)} %slice.880), channel_id=1, source_target_pairs={{0,1},{1,0},{2,3},{3,2},{4,5},{5,4},{6,7},{7,6},{8,9},{9,8},{10,11... | collective-permute-start | bytes 2359304 | tf_op jit(solution)/shard_map/ppermute | solution.py:123
  130.6 7.5 %collective-permute-start.17 = (bf16[128,768]{0,1:T(8,128)(2,1)S(1)}, bf16[128,768]{0,1:T(8,128)(2,1)S(1)}, u32[]{:S(2)}, u32[]{:S(2)}) collective-permute-start(bf16[128,768]{0,1:T(8,128)(2,1)S(1)} %get-tuple-element.45), channel_id=1, source_target_pairs={{0,12},{4,8},{8,4},{12,0},{1,13},{5,9},{9,5},{13,1},{2,14},{6,10},... | collective-permute-start | bytes 589832 | tf_op jit(solution)/shard_map/ppermute | solution.py:76
  130.8 10.2 %collective-permute-start.16 = (bf16[128,768]{0,1:T(8,128)(2,1)S(1)}, bf16[128,768]{0,1:T(8,128)(2,1)S(1)}, u32[]{:S(2)}, u32[]{:S(2)}) collective-permute-start(bf16[128,768]{0,1:T(8,128)(2,1)S(1)} %get-tuple-element.46), channel_id=1, source_target_pairs={{0,8},{4,12},{8,0},{12,4},{1,9},{5,13},{9,1},{13,5},{2,10},{6,14},... | collective-permute-start | bytes 589832 | tf_op jit(solution)/shard_map/ppermute | solution.py:76
  131.7 11.3 %collective-permute-start.15 = (bf16[128,768]{0,1:T(8,128)(2,1)S(1)}, bf16[128,768]{0,1:T(8,128)(2,1)S(1)}, u32[]{:S(2)}, u32[]{:S(2)}) collective-permute-start(bf16[128,768]{0,1:T(8,128)(2,1)S(1)} %get-tuple-element.44), channel_id=1, source_target_pairs={{0,4},{4,0},{8,12},{12,8},{1,5},{5,1},{9,13},{13,9},{2,6},{6,2},{1... | collective-permute-start | bytes 589832 | tf_op jit(solution)/shard_map/ppermute | solution.py:76
  133.7 12.9 %collective-permute-start.11 = (bf16[128,768]{0,1:T(8,128)(2,1)S(1)}, bf16[128,768]{0,1:T(8,128)(2,1)S(1)}, u32[]{:S(2)}, u32[]{:S(2)}) collective-permute-start(bf16[128,768]{0,1:T(8,128)(2,1)S(1)} %get-tuple-element.42), channel_id=1, source_target_pairs={{0,12},{4,8},{8,4},{12,0},{1,13},{5,9},{9,5},{13,1},{2,14},{6,10},... | collective-permute-start | bytes 589832 | tf_op jit(solution)/shard_map/ppermute | solution.py:76
  134.1 15.3 %collective-permute-start.10 = (bf16[128,768]{0,1:T(8,128)(2,1)S(1)}, bf16[128,768]{0,1:T(8,128)(2,1)S(1)}, u32[]{:S(2)}, u32[]{:S(2)}) collective-permute-start(bf16[128,768]{0,1:T(8,128)(2,1)S(1)} %get-tuple-element.43), channel_id=1, source_target_pairs={{0,8},{4,12},{8,0},{12,4},{1,9},{5,13},{9,1},{13,5},{2,10},{6,14},... | collective-permute-start | bytes 589832 | tf_op jit(solution)/shard_map/ppermute | solution.py:76
  138.2 12.9 %collective-permute-start.9 = (bf16[128,768]{0,1:T(8,128)(2,1)S(1)}, bf16[128,768]{0,1:T(8,128)(2,1)S(1)}, u32[]{:S(2)}, u32[]{:S(2)}) collective-permute-start(bf16[128,768]{0,1:T(8,128)(2,1)S(1)} %get-tuple-element.41), channel_id=1, source_target_pairs={{0,4},{4,0},{8,12},{12,8},{1,5},{5,1},{9,13},{13,9},{2,6},{6,2},{1... | collective-permute-start | bytes 589832 | tf_op jit(solution)/shard_map/ppermute | solution.py:76
  155.6 3.2 %copy-start.9 = (f32[1536]{0:T(1024)S(1)}, f32[1536]{0:T(1024)}, u32[]{:S(2)}) copy-start(f32[1536]{0:T(1024)} %param.16) | copy-start | bytes 18436
  158.9 1.7 copy-start.7
  161.4 10.3 %copy-start.4 = (f32[768]{0:T(1024)S(1)}, f32[768]{0:T(1024)}, u32[]{:S(2)}) copy-start(f32[768]{0:T(1024)} %get-tuple-element.8) | copy-start | bytes 9220
  162.0 7.2 %collective-permute-start.19 = (bf16[16,768]{1,0:T(8,128)(2,1)}, bf16[16,768]{1,0:T(8,128)(2,1)}, u32[]{:S(2)}, u32[]{:S(2)}) collective-permute-start(bf16[16,768]{1,0:T(8,128)(2,1)} %get-tuple-element.48), channel_id=1, source_target_pairs={{2,0},{4,2},{6,4},{8,6},{10,8},{12,10},{14,12},{16,14},{18,16},{20... | collective-permute-start | bytes 73736 | tf_op jit(solution)/shard_map/ppermute | solution.py:25
  165.1 5.8 %collective-permute-start.18 = (bf16[16,768]{1,0:T(8,128)(2,1)}, bf16[16,768]{1,0:T(8,128)(2,1)}, u32[]{:S(2)}, u32[]{:S(2)}) collective-permute-start(bf16[16,768]{1,0:T(8,128)(2,1)} %get-tuple-element.47), channel_id=1, source_target_pairs={{0,2},{2,4},{4,6},{6,8},{8,10},{10,12},{12,14},{14,16},{16,18},{18... | collective-permute-start | bytes 73736 | tf_op jit(solution)/shard_map/ppermute | solution.py:23
  171.7 10.5 %copy-start.8 = (bf16[1536,768]{1,0:T(8,128)(2,1)S(1)}, bf16[1536,768]{1,0:T(8,128)(2,1)}, u32[]{:S(2)}) copy-start(bf16[1536,768]{1,0:T(8,128)(2,1)} %param.22) | copy-start | bytes 7077892

commit v2 on v1

--- a/solution.py
+++ b/solution.py
@@ -1,6 +1,8 @@
 import jax
 import jax.numpy as jnp
 from jax import lax
+from jax.experimental import pallas as pl
+from jax.experimental.pallas import tpu as pltpu
 from jax.sharding import Mesh, PartitionSpec as P
 
 SWAP = [(0, 1), (1, 0)]
@@ -70,69 +72,315 @@
 
 
 GROUP = ("bh", "bl")
+VMEM_LIMIT = 40 * 2**20
+VMEM = pl.BlockSpec(memory_space=pltpu.VMEM)
+SMEM = pl.BlockSpec(memory_space=pltpu.SMEM)
+
+
+def kernel_call(body, outs, ins, scratch=(), scalars=0):
+    return pl.pallas_call(
+        body,
+        out_shape=[jax.ShapeDtypeStruct(shape, dtype) for shape, dtype in outs],
+        in_specs=[SMEM] * scalars + [VMEM] * (len(ins) - scalars),
+        out_specs=[VMEM] * len(outs),
+        scratch_shapes=list(scratch),
+        compiler_params=pltpu.CompilerParams(vmem_limit_bytes=VMEM_LIMIT),
+        cost_estimate=pl.CostEstimate(flops=0, bytes_accessed=0, transcendentals=0),
+    )(*ins)
+
+
+def f32(values):
+    return values.astype(jnp.float32)
+
+
+def silu(values):
+    return values / (1.0 + jnp.exp(-values))
+
+
+def cut_kernel(in_ref, out_ref, in_cut_ref, out_cut_ref):
+    parts, _, width = in_cut_ref.shape
+    for part in range(parts):
+        at = slice(part * width, (part + 1) * width)
+        in_cut_ref[part] = in_ref[:, at]
+        out_cut_ref[part] = out_ref[:, at]
+
+
+def part_kernel(both_ref, first_ref, second_ref):
+    half = first_ref.shape[0]
+    first_ref[...] = both_ref[:half]
+    second_ref[...] = both_ref[half:]
+
+
+def norm_kernel(start_ref, whole_ref, gain_ref, mine_ref, out_ref):
+    rows = mine_ref.shape[0]
+    mine = whole_ref[pl.ds(pl.multiple_of(start_ref[0], rows), rows), :]
+    mine_ref[...] = mine
+    out_ref[...] = norm_rows(f32(mine), gain_ref[...]).astype(jnp.bfloat16)
+
+
+def join_kernel(*refs):
+    *pieces, out_ref = refs
+    rows = pieces[0].shape[0]
+    for i, piece in enumerate(pieces):
+        out_ref[i * rows : (i + 1) * rows] = piece[...]
+
+
+def interleave(full_ref, base, own_refs, other_refs, me_l):
+    block = own_refs[0].shape[1]
+    for refs, turn in ((own_refs, me_l), (other_refs, 1 - me_l)):
+        blocks = [(ref, j) for ref in refs for j in range(ref.shape[0])]
+        for i, (ref, j) in enumerate(blocks):
+            at = pl.multiple_of(base + (2 * i + turn) * block, block)
+            full_ref[pl.ds(at, block), :] = ref[j]
+
+
+def hidden_kernel(me_ref, x_ref, o_ref, ox_ref, z_ref, zx_ref, h_ref, w_ref):
+    me_l, me_a = me_ref[0], me_ref[2]
+    part = w_ref.shape[0] // 2
+    interleave(w_ref, me_a * part, [o_ref], [ox_ref], me_l)
+    interleave(w_ref, (1 - me_a) * part, [z_ref], [zx_ref], me_l)
+    step = 256
+    for at in range(0, x_ref.shape[0], step):
+        pre = jnp.dot(x_ref[at : at + step, :], w_ref[...], preferred_element_type=jnp.float32)
+        h_ref[at : at + step, :] = silu(pre).astype(jnp.bfloat16)
+
+
+def sums_kernel(me_ref, own_ref, oth_ref, first_ref, second_ref, *refs):
+    *others, kept_ref, sent_ref, w_ref = refs
+    interleave(w_ref, 0, [first_ref, second_ref], others, me_ref[0])
+    step = 256
+    for h_ref, out_ref in ((oth_ref, sent_ref), (own_ref, kept_ref)):
+        for at in range(0, h_ref.shape[0], step):
+            out_ref[at : at + step, :] = lax.dot_general(
+                h_ref[at : at + step, :],
+                w_ref[...],
+                (((1,), (1,)), ((), ())),
+                preferred_element_type=jnp.float32,
+            ).astype(out_ref.dtype)
+
+
+def add_kernel(kept_ref, came_ref, *out_refs):
+    rows = out_refs[0].shape[0]
+    for k, out_ref in enumerate(out_refs):
+        at = slice(k * rows, (k + 1) * rows)
+        out_ref[...] = (kept_ref[at, :] + f32(came_ref[at, :])).astype(out_ref.dtype)
+
+
+def mid_kernel(me_ref, mine_ref, *refs):
+    *sums, out_ref = refs
+    for place, part in ((me_ref[2], sums[:4]), (1 - me_ref[2], sums[4:])):
+        total = part[0][...]
+        for other in part[1:]:
+            total = total + f32(other[...])
+        width = part[0].shape[1]
+        at = pl.ds(pl.multiple_of(place * width, width), width)
+        out_ref[:, at] = (f32(mine_ref[:, at]) + 0.5 * total).astype(jnp.bfloat16)
+
+
+HALO = 16
+
+
+def utter_kernel(first_ref, lengths_ref, out_ref):
+    position = first_ref[0] + lax.broadcasted_iota(jnp.int32, out_ref.shape, 0)
+
+    def step(u, carry):
+        end, utter = carry
+        end = end + lengths_ref[u]
+        return end, utter + jnp.where(position >= end, 1, 0)
+
+    zero = jnp.zeros(out_ref.shape, jnp.int32)
+    out_ref[...] = lax.fori_loop(0, lengths_ref.shape[0], step, (jnp.int32(0), zero))[1]
+
+
+def glu_kernel(mid_ref, gain_ref, value_ref, gate_ref, glu_ref, head_ref, tail_ref):
+    normed = norm_rows(f32(mid_ref[...]), gain_ref[...]).astype(jnp.bfloat16)
+    value = jnp.dot(normed, value_ref[...], preferred_element_type=jnp.float32)
+    gate = jnp.dot(normed, gate_ref[...], preferred_element_type=jnp.float32)
+    glu = (value / (1.0 + jnp.exp(-gate))).astype(jnp.bfloat16)
+    glu_ref[...] = glu
+    head_ref[...] = glu[:HALO]
+    tail_ref[...] = glu[glu.shape[0] - HALO :]
+
+
+def conv_rows(ext_ref, utter_ref, taps_ref, scale_ref, shift_ref, out_ref, ext_at, utter_at, out_at, rows):
+    lanes = 128
+    taps = taps_ref.shape[0]
+    span = rows + taps - 8
+
+    def column(j, _):
+        at = pl.ds(pl.multiple_of(j * lanes, lanes), lanes)
+        centre = utter_ref[utter_at + HALO : utter_at + HALO + rows, :]
+        total = jnp.zeros((rows, lanes), jnp.float32)
+        for r in range(8):
+            cells = ext_ref[ext_at + 1 + r : ext_at + 1 + r + span, at]
+            utter = utter_ref[utter_at + 1 + r : utter_at + 1 + r + span, :]
+            for q in range(0, taps, 8):
+                term = cells[q : q + rows] * taps_ref[q + r : q + r + 1, at]
+                total = total + jnp.where(utter[q : q + rows] == centre, term, 0.0)
+        act = silu(total * scale_ref[:, at] + shift_ref[:, at])
+        out_ref[out_at : out_at + rows, at] = act.astype(out_ref.dtype)
+        return 0
+
+    lax.fori_loop(0, out_ref.shape[1] // lanes, column, 0)
+
+
+def inner_conv_kernel(glu_ref, utter_ref, taps_ref, scale_ref, shift_ref, out_ref, ext_ref):
+    ext_ref[...] = f32(glu_ref[...])
+    step = 32
+    for at in range(HALO, out_ref.shape[0] - HALO, step):
+        conv_rows(
+            ext_ref, utter_ref, taps_ref, scale_ref, shift_ref, out_ref, at - HALO, at, at, step
+        )
+
+
+def edge_conv_kernel(
+    act_ref, top_ref, glu_ref, bottom_ref, utter_ref, taps_ref, scale_ref, shift_ref, out_ref, ext_ref
+):
+    rows = out_ref.shape[0]
+    last = rows - HALO
+    out_ref[HALO:last, :] = act_ref[HALO:last, :]
+    ext_ref[:HALO, :] = f32(top_ref[...])
+    ext_ref[HALO : 3 * HALO, :] = f32(glu_ref[: 2 * HALO, :])
+    ext_ref[3 * HALO : 5 * HALO, :] = f32(glu_ref[rows - 2 * HALO :, :])
+    ext_ref[5 * HALO :, :] = f32(bottom_ref[...])
+    rest = (utter_ref, taps_ref, scale_ref, shift_ref, out_ref)
+    conv_rows(ext_ref, *rest, 0, 0, 0, HALO)
+    conv_rows(ext_ref, *rest, 3 * HALO, last, last, HALO)
+
+
+def utterances(rows, axis, lengths):
+    return kernel_call(
+        utter_kernel,
+        [((rows + 2 * HALO, 128), jnp.int32)],
+        [(lax.axis_index(axis) * rows - HALO)[None], lengths],
+        scalars=2,
+    )[0]
+
+
+def grouped_conv_module(
+    mid_own, mid_full, axis, utter, conv_gain, w_value, w_gate, depth_kernel, bn_scale, bn_shift, w_proj
+):
+    rows, width = mid_own.shape
+    bf16 = jnp.bfloat16
+    glu, head, tail = kernel_call(
+        glu_kernel,
+        [((rows, width), bf16)] + [((HALO, width), bf16)] * 2,
+        [mid_full, conv_gain[None, :], w_value, w_gate],
+    )
+    count = lax.axis_size(axis)
+    top = lax.ppermute(tail, axis, [(i, i + 1) for i in range(count - 1)])
+    bottom = lax.ppermute(head, axis, [(i + 1, i) for i in range(count - 1)])
+    rest = [utter, depth_kernel, bn_scale[None, :], bn_shift[None, :]]
+    (act,) = kernel_call(
+        inner_conv_kernel,
+        [((rows, width), bf16)],
+        [glu, *rest],
+        scratch=[pltpu.VMEM((rows, width), jnp.float32)],
+    )
+    (act,) = kernel_call(
+        edge_conv_kernel,
+        [((rows, width), bf16)],
+        [act, top, glu, bottom, *rest],
+        scratch=[pltpu.VMEM((6 * HALO, width), jnp.float32)],
+    )
+    act_full = lax.all_gather(act, "hid", axis=1, tiled=True)
+    projected = jnp.dot(act_full, w_proj, preferred_element_type=jnp.float32)
+    return (mid_own.astype(jnp.float32) + projected).astype(jnp.bfloat16)
 
 
 def partner(values, step):
     return lax.ppermute(values, GROUP, [(i, i ^ step) for i in range(4)])
 
 
-def ordered(first, second, index, axis):
-    return jnp.where(
-        index == 0, jnp.stack([first, second], axis), jnp.stack([second, first], axis)
-    )
-
-
-def grouped_ffn(tokens, ffn_gain, w_in, w_out):
+def swap(values, axis):
+    return lax.ppermute(values, axis, SWAP)
+
+
+def recut(parts):
+    return lax.all_to_all(parts, GROUP, 0, 0)
+
+
+def grouped_ffn(tokens, ffn_gain, w_in, w_out, early):
     rows, width = tokens.shape
     half = rows // 2
+    shard, hid = w_in.shape
+    wide = 2 * width
+    units = hid // 4
+    bf16 = jnp.bfloat16
     me_c = lax.axis_index("hid")
-    me_a = lax.axis_index("ah")
-    me_l = lax.axis_index("al")
+    me = jnp.stack([lax.axis_index("al"), me_c, lax.axis_index("ah")])
+    tie = lax.optimization_barrier
+
+    in_cut, out_cut = kernel_call(cut_kernel, [((4, shard, units), bf16)] * 2, [w_in, w_out.T])
+    in_far = swap(in_cut, "ah")
+    out_o = recut(out_cut)
+    in_o = recut(in_cut)
+    out_1, out_2 = kernel_call(part_kernel, [((2, shard, units), bf16)] * 2, [out_o])
+    out_x1 = swap(out_1, "al")
+    out_x2 = swap(out_2, "al")
     whole = lax.all_gather(tokens, "hid", axis=1, tiled=True)
-    normed = norm_rows(whole.astype(jnp.float32), ffn_gain).astype(jnp.bfloat16)
-    mine = lax.dynamic_slice_in_dim(normed, me_c * half, half, 0)
-    x_own = jnp.concatenate([mine] + [partner(mine, k) for k in (1, 2, 3)], axis=0)
-    x_oth = lax.ppermute(x_own, "hid", SWAP)
-    x = jnp.concatenate([x_own, x_oth], axis=0)
-
-    def recut(w):
-        return lax.all_to_all(
-            w.reshape(w.shape[0], 4, w.shape[1] // 4).transpose(1, 0, 2), GROUP, 0, 0
+    mine, normed = kernel_call(
+        norm_kernel,
+        [((half, wide), bf16)] * 2,
+        [(me_c * half)[None], whole, ffn_gain[None, :]],
+        scalars=1,
+    )
+    frames1 = partner(normed, 1)
+    in_far, out_1, out_2, out_x1, out_x2, normed, frames1, early = tie(
+        (in_far, out_1, out_2, out_x1, out_x2, normed, frames1, early)
+    )
+    out_z1 = swap(out_1, "ah")
+    in_ox = swap(in_o, "al")
+    in_z = recut(in_far)
+    frames3 = partner(normed, 3)
+    out_z1, in_ox, in_z, out_2, normed, frames3 = tie((out_z1, in_ox, in_z, out_2, normed, frames3))
+    out_z2 = swap(out_2, "ah")
+    in_zx = swap(in_z, "al")
+    frames2 = partner(normed, 2)
+    (x_own,) = kernel_call(
+        join_kernel, [((4 * half, wide), bf16)], [normed, frames1, frames2, frames3]
+    )
+    out_z1, out_z2, in_zx, x_own = tie((out_z1, out_z2, in_zx, x_own))
+    out_zx1 = swap(out_z1, "al")
+    out_zx2 = swap(out_z2, "al")
+    x_oth = swap(x_own, "hid")
+
+    def units_of(x):
+        return kernel_call(
+            hidden_kernel,
+            [((4 * half, units), bf16)],
+            [me, x, in_o, in_ox, in_z, in_zx],
+            scratch=[pltpu.VMEM((wide, units), bf16)],
+            scalars=1,
+        )[0]
+
+    hidden = [units_of(x_own), units_of(x_oth)]
+
+    def products(*blocks):
+        return kernel_call(
+            sums_kernel,
+            [((4 * half, width), jnp.float32), ((4 * half, width), bf16)],
+            [me, *hidden, *blocks],
+            scratch=[pltpu.VMEM((width, units), bf16)],
+            scalars=1,
         )
 
-    def spread(own):
-        far = lax.ppermute(own, "ah", SWAP)
-        own_l = lax.ppermute(own, "al", SWAP)
-        far_l = lax.ppermute(far, "al", SWAP)
-        def place(a, b):
-            return ordered(a, b, me_l, 1).reshape(-1, own.shape[-1])
-        return place(own, own_l), place(far, far_l)
-
-    in_own, in_far = spread(recut(w_in))
-    out_own, out_far = spread(recut(w_out.T))
-    w_full = ordered(in_own, in_far, me_a, 0).reshape(-1, in_own.shape[-1])
-    pre = jnp.dot(x, w_full, preferred_element_type=jnp.float32)
-    hidden = jax.nn.silu(pre).astype(jnp.bfloat16)
-
-    def sums(w):
-        part = lax.dot_general(
-            hidden, w, (((1,), (1,)), ((), ())), preferred_element_type=jnp.float32
+    def scatter(kept, sent):
+        total = kernel_call(
+            add_kernel,
+            [((half, width), jnp.float32)] + [((half, width), bf16)] * 3,
+            [kept, swap(sent, "hid")],
         )
-        kept, sent = part[: rows * 2], part[rows * 2 :]
-        total = (
-            kept + lax.ppermute(sent.astype(jnp.bfloat16), "hid", SWAP).astype(jnp.float32)
-        ).astype(jnp.bfloat16)
-        ffn = total[:half].astype(jnp.float32)
-        for k in (1, 2, 3):
-            ffn = ffn + partner(total[k * half : (k + 1) * half], k).astype(jnp.float32)
-        return ffn
-
-    ffn = ordered(sums(out_own), sums(out_far), me_a, 1).reshape(half, -1)
-    mine_tok = lax.dynamic_slice_in_dim(whole, me_c * half, half, 0).astype(jnp.float32)
-    mid_rows = (mine_tok + 0.5 * ffn).astype(jnp.bfloat16)
+        return [total[0]] + [partner(v, k + 1) for k, v in enumerate(total[1:])]
+
+    near, out_zx1, out_zx2 = tie((products(out_1, out_2, out_x1, out_x2), out_zx1, out_zx2))
+    far = products(out_z1, out_z2, out_zx1, out_zx2)
+    (mid_rows,) = kernel_call(
+        mid_kernel, [((half, wide), bf16)], [me, mine, *scatter(*near), *scatter(*far)], scalars=1
+    )
     mid_full = lax.all_gather(mid_rows, "hid", axis=0, tiled=True)
     mid_own = lax.dynamic_slice_in_dim(mid_full, me_c * width, width, 1)
-    return mid_own, mid_full
+    return mid_own, mid_full, early
 
 
 def solution(mesh):
@@ -145,8 +393,12 @@
         tok, inner = "tok", mesh
 
     def local(tokens, ffn_gain, w_in, w_out, conv_gain, *rest):
-        ffn = grouped_ffn if grouped else gathered_ffn
-        mid_own, mid_full = ffn(tokens, ffn_gain, w_in, w_out)
+        if grouped:
+            *rest, lengths = rest
+            utter = utterances(tokens.shape[0], tok, lengths)
+            mid_own, mid_full, utter = grouped_ffn(tokens, ffn_gain, w_in, w_out, utter)
+            return grouped_conv_module(mid_own, mid_full, tok, utter, conv_gain, *rest)
+        mid_own, mid_full = gathered_ffn(tokens, ffn_gain, w_in, w_out)
         return conv_module(mid_own, mid_full, tok, conv_gain, *rest)
 
     placed = (

time: 187 us -> 163 us (0.87); the launches traced: 184 us -> 162 us
  other arithmetic: 27.6 us -> 0.08 us
  Pallas kernels: 0 us -> 26.3 us
  waiting for transfers between devices: 82.5 us -> 61.7 us
  blocking collectives: 9.24 us -> 22.4 us
  local copies, waits for them, and re-layouts: 23.9 us -> 11.1 us
  starting transfers between devices: 31.2 us -> 39 us
  matrix products: 9.01 us -> 1.53 us
    ppermute x11 -> x14, waiting for transfers between devices: 60.9 us -> 27.5 us  [the longest x12 27.5 us: swap(): return lax.ppermute(values, axis, SWAP)]
    pallas_call x0 -> x15, Pallas kernels: none -> 26.3 us  [kernel_call(): pl.pallas_call(body, out_shape=[jax.ShapeDtypeStruct(shape, dtype) for sh...]
    ppermute x9, waiting for transfers between devices: 21.6 us -> 34.3 us  [partner(): return lax.ppermute(values, GROUP, [(i, i ^ step) for i in range(4)])]
    all_to_all x0 -> x1, blocking collectives: none -> 11.2 us  [recut(): return lax.all_to_all(parts, GROUP, 0, 0)]
    convert_element_type x5 -> x0, other arithmetic: 9.28 us -> none  [the longest x1 6.72 us: conv_module(): act = jax.nn.silu(conv * bn_scale + bn_shift).astype(jnp.bfloat16)]
    dot_general x6 -> x1, matrix products: 9.01 us -> 1.53 us  [grouped_conv_module(): projected = jnp.dot(act_full, w_proj, preferred_element_type=jnp.float32)]
    ppermute x11 -> x14, starting transfers between devices: 16.3 us -> 22.5 us  [the longest x12 16.3 us: swap(): return lax.ppermute(values, axis, SWAP)]
    select_n x5 -> x0, other arithmetic: 5.31 us -> none  [ordered(): jnp.where(index == 0, jnp.stack([first, second], axis), jnp.stack([second...]
  transfers between devices with their start and end apart: 22 -> 25, of which waited for: 11 -> 11; matrix products, arithmetic and copies ran while one was open for 21% -> 0% of each run, Pallas kernels for 0% -> 12%
where the time goes in v2:
time: 163 us; the launch traced here: 162 us
  waiting for transfers between devices  61.7 us (38%)
  starting transfers between devices  39 us (24%)
  Pallas kernels  26.3 us (16%)
  blocking collectives  22.4 us (14%)
  local copies, waits for them, and re-layouts  11.1 us (7%)
    ppermute x9, waiting for transfers between devices, partner(): return lax.ppermute(values, GROUP, [(i, i ^ step) for i in range(4)])  34.3 us
    ppermute x12, waiting for transfers between devices, swap(): return lax.ppermute(values, axis, SWAP)  27.5 us
    pallas_call x15, Pallas kernels, kernel_call(): pl.pallas_call(body, out_shape=[jax.ShapeDtypeStruct(shape, dtype) for sh...  26.3 us
    ppermute x12, starting transfers between devices, swap(): return lax.ppermute(values, axis, SWAP)  16.3 us
    all_to_all x1, blocking collectives, recut(): return lax.all_to_all(parts, GROUP, 0, 0)  11.2 us
    unnamed x52, local copies, waits for them, and re-layouts  10.4 us
    ppermute x9, starting transfers between devices, partner(): return lax.ppermute(values, GROUP, [(i, i ^ step) for i in range(4)])  8.45 us
    all_to_all x2, starting transfers between devices, recut(): return lax.all_to_all(parts, GROUP, 0, 0)  8.07 us
  transfers between devices with their start and end apart: 25, of which 11 were waited for; matrix products, arithmetic and copies ran while one was open for 0% of the time, Pallas kernels for 12%

profile of v2, /device:TPU:5, one launch (start us, length us, event | category | flops | bytes accessed | tf_op | source)
XLA Modules:
  0.0 162.5 jit_solution(6975195043432369721)
XLA Ops:
  0.0 1.2 copy-done.7
  1.2 1.1 copy-done.8
  2.3 0.1 shard_map.119
  2.4 11.2 %all_to_all.15.both_ref = bf16[4,96,768]{2,1,0:T(8,128)(2,1)S(1)} all-to-all(bf16[4,96,768]{2,1,0:T(8,128)(2,1)S(1)} %get-tuple-element.50), channel_id=1, replica_groups=mesh['ah'=2,'bh'=2,'bl'=2,'al'=2,'hid'=2] {'bh','bl'}, dimensions={0} | all-to-all | bytes 1179648 | tf_op jit(solution)/shard_map/all_to_all | solution.py:300
  13.6 4.3 %all-to-all-start.1 = ((bf16[4,96,768]{2,1,0:T(8,128)(2,1)}), bf16[4,96,768]{2,1,0:T(8,128)(2,1)S(1)}, u32[]{:S(2)}, u32[]{:S(2)}) async-start(bf16[4,96,768]{2,1,0:T(8,128)(2,1)} %copy-done.9), calls=%async_computation.1 | async-start | bytes 1179648 | tf_op jit(solution)/shard_map/all_to_all | solution.py:300
  17.8 2.3 %collective-permute-start = (bf16[4,96,768]{2,1,0:T(8,128)(2,1)}, bf16[4,96,768]{2,1,0:T(8,128)(2,1)}, u32[]{:S(2)}, u32[]{:S(2)}) collective-permute-start(bf16[4,96,768]{2,1,0:T(8,128)(2,1)} %copy-done.9), channel_id=1, source_target_pairs={{0,16},{16,0},{1,17},{17,1},{2,18},{18,2},{3,19},{19,3},{4,20},{20... | collective-permute-start | bytes 1769480 | tf_op jit(solution)/shard_map/ppermute | solution.py:296
  20.1 0.7 broadcast_in_dim.19.gain_ref
  20.8 4.8 %all_gather.9.whole_ref = bf16[256,1536]{1,0:T(8,128)(2,1)S(1)} all-gather(bf16[256,768]{1,0:T(8,128)(2,1)} %param.12), channel_id=1, replica_groups=mesh['ah'=2,'bh'=2,'bl'=2,'al'=2,'hid'=2] {'hid'}, dimensions={1}, use_global_device_ids=true | all-gather | bytes 1179648 | tf_op jit(solution)/shard_map/all_gather | solution.py:321
  25.6 1.1 shard_map.118
  26.7 0.9 shard_map.120
  27.6 1.2 collective-permute-start.1
  28.9 0.3 collective-permute-start.2
  29.1 2.3 %shard_map.121.utter_ref = s32[288,128]{1,0:T(8,128)S(1)} custom-call(s32[1]{0:T(128)} %bitcast.5.first_ref, s32[64]{0:T(128)S(1)} %copy-done.22), custom_call_target="tpu_custom_call" | custom-call | tf_op jit(solution)/shard_map/pallas_call | solution.py:81
  31.4 0.6 copy-done.5
  32.1 6.3 %collective-permute-done.3.refs_1_ = bf16[128,1536]{1,0:T(8,128)(2,1)} collective-permute-done((bf16[128,1536]{1,0:T(8,128)(2,1)}, bf16[128,1536]{1,0:T(8,128)(2,1)}, u32[]{:S(2)}, u32[]{:S(2)}) %collective-permute-start.3) | collective-permute-done | bytes 393248 | tf_op jit(solution)/shard_map/ppermute | solution.py:292
  38.4 5.9 %collective-permute-done = bf16[4,96,768]{2,1,0:T(8,128)(2,1)} collective-permute-done((bf16[4,96,768]{2,1,0:T(8,128)(2,1)}, bf16[4,96,768]{2,1,0:T(8,128)(2,1)}, u32[]{:S(2)}, u32[]{:S(2)}) %collective-permute-start) | collective-permute-done | bytes 589856 | tf_op jit(solution)/shard_map/ppermute | solution.py:296
  44.3 0.7 copy-done.16
  45.0 0.7 copy-done.18
  45.7 3.8 %all-to-all-start.2 = ((bf16[4,96,768]{2,1,0:T(8,128)(2,1)}), bf16[4,96,768]{2,1,0:T(8,128)(2,1)S(1)}, u32[]{:S(2)}, u32[]{:S(2)}) async-start(bf16[4,96,768]{2,1,0:T(8,128)(2,1)} %collective-permute-done), calls=%async_computation.2 | async-start | bytes 1179648 | tf_op jit(solution)/shard_map/all_to_all | solution.py:300
  49.5 1.2 collective-permute-start.5
  50.7 1.2 collective-permute-start.6
  51.9 2.8 %collective-permute-start.4 = (bf16[2,96,768]{2,1,0:T(8,128)(2,1)}, bf16[2,96,768]{2,1,0:T(8,128)(2,1)S(1)}, u32[]{:S(2)}, u32[]{:S(2)}) collective-permute-start(bf16[2,96,768]{2,1,0:T(8,128)(2,1)} %get-tuple-element.54.first_ref), channel_id=1, source_target_pairs={{0,16},{16,0},{1,17},{17,1},{2,18},{18,2},{3,19},{19,3},{4,20},{20... | collective-permute-start | bytes 884744 | tf_op jit(solution)/shard_map/ppermute | solution.py:296
  54.7 13.3 %collective-permute-done.4.first_ref = bf16[2,96,768]{2,1,0:T(8,128)(2,1)S(1)} collective-permute-done((bf16[2,96,768]{2,1,0:T(8,128)(2,1)}, bf16[2,96,768]{2,1,0:T(8,128)(2,1)S(1)}, u32[]{:S(2)}, u32[]{:S(2)}) %collective-permute-start.4) | collective-permute-done | bytes 294944 | tf_op jit(solution)/shard_map/ppermute | solution.py:296
  68.1 0.7 copy-done.20
  68.8 0.8 copy-done.1
  69.6 0.3 collective-permute-done.6.refs_3_
  69.9 0.8 copy-done.10
  70.7 1.2 collective-permute-start.8
  71.9 4.2 %collective-permute-start.9 = (bf16[128,1536]{1,0:T(8,128)(2,1)}, bf16[128,1536]{1,0:T(8,128)(2,1)S(1)}, u32[]{:S(2)}, u32[]{:S(2)}) collective-permute-start(bf16[128,1536]{1,0:T(8,128)(2,1)} %get-tuple-element.61.refs_0_), channel_id=1, source_target_pairs={{0,8},{4,12},{8,0},{12,4},{1,9},{5,13},{9,1},{13,5},{2,10},{6,14},... | collective-permute-start | bytes 1179656 | tf_op jit(solution)/shard_map/ppermute | solution.py:292
  76.0 11.2 %collective-permute-done.9.refs_2_ = bf16[128,1536]{1,0:T(8,128)(2,1)S(1)} collective-permute-done((bf16[128,1536]{1,0:T(8,128)(2,1)}, bf16[128,1536]{1,0:T(8,128)(2,1)S(1)}, u32[]{:S(2)}, u32[]{:S(2)}) %collective-permute-start.9) | collective-permute-done | bytes 393248 | tf_op jit(solution)/shard_map/ppermute | solution.py:292
  87.2 1.0 copy-done.11
  88.2 1.3 shard_map.122.x_ref
  89.5 4.9 %collective-permute-start.10 = (bf16[512,1536]{1,0:T(8,128)(2,1)S(1)}, bf16[512,1536]{1,0:T(8,128)(2,1)S(1)}, u32[]{:S(2)}, u32[]{:S(2)}) collective-permute-start(bf16[512,1536]{1,0:T(8,128)(2,1)S(1)} %shard_map.122.x_ref), channel_id=1, source_target_pairs={{0,1},{1,0},{2,3},{3,2},{4,5},{5,4},{6,7},{7,6},{8,9},{9,8},{10,11... | collective-permute-start | bytes 4718600 | tf_op jit(solution)/shard_map/ppermute | solution.py:296
  94.5 0.3 collective-permute-start.11
  94.7 1.2 collective-permute-start.12
  96.0 2.2 %shard_map.123.own_ref = bf16[512,768]{1,0:T(8,128)(2,1)S(1)} custom-call(s32[3]{0:T(128)S(1)} %pad_add_fusion.me_ref, bf16[512,1536]{1,0:T(8,128)(2,1)S(1)} %shard_map.122.x_ref, bf16[4,96,768]{2,1,0:T(8,128)(2,1)S(1)} %all-to-all-done.1.o_ref, bf16[4,96,768]{2,1,0:T(8,128)(2,1)S(1)} %copy-done.2, bf16[4,96,768]{2,1,0:T(8,128)(2,1)S(1)} %all-to-all-done.2.z_ref, ...), custom_call_target="tpu_custom_call" | custom-call | tf_op jit(solution)/shard_map/pallas_call | solution.py:81
  98.2 2.2 %shard_map.124.oth_ref = bf16[512,768]{1,0:T(8,128)(2,1)S(1)} custom-call(s32[3]{0:T(128)S(1)} %pad_add_fusion.me_ref, bf16[512,1536]{1,0:T(8,128)(2,1)S(1)} %collective-permute-done.10.x_ref, bf16[4,96,768]{2,1,0:T(8,128)(2,1)S(1)} %all-to-all-done.1.o_ref, bf16[4,96,768]{2,1,0:T(8,128)(2,1)S(1)} %copy-done.2, ...), custom_call_target="tpu_custom_call" | custom-call | tf_op jit(solution)/shard_map/pallas_call | solution.py:81
  100.4 2.6 %shard_map.125 = (f32[512,768]{1,0:T(8,128)S(1)}, bf16[512,768]{1,0:T(8,128)(2,1)S(1)}) custom-call(s32[3]{0:T(128)S(1)} %pad_add_fusion.me_ref, bf16[512,768]{1,0:T(8,128)(2,1)S(1)} %shard_map.123.own_ref, bf16[512,768]{1,0:T(8,128)(2,1)S(1)} %shard_map.124.oth_ref, bf16[2,96,768]{2,1,0:T(8,128)(2,1)} %get-tuple-element.54.first_ref, ...), custom_call_target="tpu_custom_call" | custom-call | tf_op jit(solution)/shard_map/pallas_call | solution.py:81
  103.0 6.3 %collective-permute-done.12.refs_1_ = bf16[2,96,768]{2,1,0:T(8,128)(2,1)S(1)} collective-permute-done((bf16[2,96,768]{2,1,0:T(8,128)(2,1)S(1)}, bf16[2,96,768]{2,1,0:T(8,128)(2,1)S(1)}, u32[]{:S(2)}, u32[]{:S(2)}) %collective-permute-start.12) | collective-permute-done | bytes 294944 | tf_op jit(solution)/shard_map/ppermute | solution.py:296
  109.4 2.1 %shard_map.127 = (f32[512,768]{1,0:T(8,128)S(1)}, bf16[512,768]{1,0:T(8,128)(2,1)S(1)}) custom-call(s32[3]{0:T(128)S(1)} %pad_add_fusion.me_ref, bf16[512,768]{1,0:T(8,128)(2,1)S(1)} %shard_map.123.own_ref, bf16[512,768]{1,0:T(8,128)(2,1)S(1)} %shard_map.124.oth_ref, bf16[2,96,768]{2,1,0:T(8,128)(2,1)S(1)} %copy-done.21, ...), custom_call_target="tpu_custom_call" | custom-call | tf_op jit(solution)/shard_map/pallas_call | solution.py:81
  111.4 0.9 collective-permute-start.17
  112.3 0.1 collective-permute-start.13
  112.4 1.8 %collective-permute-done.17.came_ref = bf16[512,768]{1,0:T(8,128)(2,1)S(1)} collective-permute-done((bf16[512,768]{1,0:T(8,128)(2,1)S(1)}, bf16[512,768]{1,0:T(8,128)(2,1)S(1)}, u32[]{:S(2)}, u32[]{:S(2)}) %collective-permute-start.17) | collective-permute-done | bytes 786464 | tf_op jit(solution)/shard_map/ppermute | solution.py:296
  114.3 0.1 shard_map.128
  114.4 0.4 collective-permute-start.18
  114.8 2.3 %collective-permute-start.20 = (bf16[128,768]{1,0:T(8,128)(2,1)S(1)}, bf16[128,768]{1,0:T(8,128)(2,1)S(1)}, u32[]{:S(2)}, u32[]{:S(2)}) collective-permute-start(bf16[128,768]{1,0:T(8,128)(2,1)S(1)} %get-tuple-element.86), channel_id=1, source_target_pairs={{0,12},{4,8},{8,4},{12,0},{1,13},{5,9},{9,5},{13,1},{2,14},{6,10},... | collective-permute-start | bytes 589832 | tf_op jit(solution)/shard_map/ppermute | solution.py:292
  117.1 0.1 shard_map.126
  117.3 0.4 collective-permute-start.14
  117.6 2.9 %collective-permute-done.18.refs_5_ = bf16[128,768]{1,0:T(8,128)(2,1)S(1)} collective-permute-done((bf16[128,768]{1,0:T(8,128)(2,1)S(1)}, bf16[128,768]{1,0:T(8,128)(2,1)S(1)}, u32[]{:S(2)}, u32[]{:S(2)}) %collective-permute-start.18) | collective-permute-done | bytes 196640 | tf_op jit(solution)/shard_map/ppermute | solution.py:292
  120.6 5.1 %collective-permute-done.20.refs_7_ = bf16[128,768]{1,0:T(8,128)(2,1)S(1)} collective-permute-done((bf16[128,768]{1,0:T(8,128)(2,1)S(1)}, bf16[128,768]{1,0:T(8,128)(2,1)S(1)}, u32[]{:S(2)}, u32[]{:S(2)}) %collective-permute-start.20) | collective-permute-done | bytes 196640 | tf_op jit(solution)/shard_map/ppermute | solution.py:292
  125.7 3.3 %collective-permute-done.14.refs_1_ = bf16[128,768]{1,0:T(8,128)(2,1)S(1)} collective-permute-done((bf16[128,768]{1,0:T(8,128)(2,1)S(1)}, bf16[128,768]{1,0:T(8,128)(2,1)S(1)}, u32[]{:S(2)}, u32[]{:S(2)}) %collective-permute-start.14) | collective-permute-done | bytes 196640 | tf_op jit(solution)/shard_map/ppermute | solution.py:292
  129.0 5.1 %collective-permute-done.16.refs_3_ = bf16[128,768]{1,0:T(8,128)(2,1)S(1)} collective-permute-done((bf16[128,768]{1,0:T(8,128)(2,1)S(1)}, bf16[128,768]{1,0:T(8,128)(2,1)S(1)}, u32[]{:S(2)}, u32[]{:S(2)}) %collective-permute-start.16) | collective-permute-done | bytes 196640 | tf_op jit(solution)/shard_map/ppermute | solution.py:292
  134.1 0.8 shard_map.129
  134.9 3.5 %all_gather.10.mid_ref = bf16[256,1536]{1,0:T(8,128)(2,1)S(1)} all-gather(bf16[128,1536]{1,0:T(8,128)(2,1)S(1)} %shard_map.129), channel_id=1, replica_groups=mesh['ah'=2,'bh'=2,'bl'=2,'al'=2,'hid'=2] {'hid'}, dimensions={0}, use_global_device_ids=true | all-gather | bytes 1179648 | tf_op jit(solution)/shard_map/all_gather | solution.py:381
  138.4 2.5 %shard_map.130 = (bf16[256,768]{1,0:T(8,128)(2,1)S(1)}, bf16[16,768]{1,0:T(8,128)(2,1)}, bf16[16,768]{1,0:T(8,128)(2,1)}) custom-call(bf16[256,1536]{1,0:T(8,128)(2,1)S(1)} %all_gather.10.mid_ref, f32[1,1536]{1,0:T(1,128)S(1)} %broadcast_in_dim.21.gain_ref, bf16[1536,768]{1,0:T(8,128)(2,1)S(1)} %copy-done.3, bf16[1536,768]{1,0:T(8,128)(2,1)S(1)} %copy-done.4), custom_call_target="tpu_custom_call" | custom-call | tf_op jit(solution)/shard_map/pallas_call | solution.py:81
  141.0 2.2 %collective-permute-start.21 = (bf16[16,768]{1,0:T(8,128)(2,1)}, bf16[16,768]{1,0:T(8,128)(2,1)}, u32[]{:S(2)}, u32[]{:S(2)}) collective-permute-start(bf16[16,768]{1,0:T(8,128)(2,1)} %get-tuple-element.89), channel_id=1, source_target_pairs={{0,2},{2,4},{4,6},{6,8},{8,10},{10,12},{12,14},{14,16},{16,18},{18... | collective-permute-start | bytes 73736 | tf_op jit(solution)/shard_map/ppermute | solution.py:271
  143.1 4.0 %collective-permute-start.22 = (bf16[16,768]{1,0:T(8,128)(2,1)}, bf16[16,768]{1,0:T(8,128)(2,1)}, u32[]{:S(2)}, u32[]{:S(2)}) collective-permute-start(bf16[16,768]{1,0:T(8,128)(2,1)} %get-tuple-element.90), channel_id=1, source_target_pairs={{2,0},{4,2},{6,4},{8,6},{10,8},{12,10},{14,12},{16,14},{18,16},{20... | collective-permute-start | bytes 73736 | tf_op jit(solution)/shard_map/ppermute | solution.py:272
  147.2 0.9 copy-done.6
  148.1 0.9 copy-done.14
  149.0 6.2 %shard_map.131.act_ref = bf16[256,768]{1,0:T(8,128)(2,1)S(1)} custom-call(bf16[256,768]{1,0:T(8,128)(2,1)S(1)} %get-tuple-element.87.glu_ref, s32[288,128]{1,0:T(8,128)S(1)} %copy-done.6, f32[32,768]{1,0:T(8,128)S(1)} %copy-done.14, f32[1,768]{1,0:T(1,128)S(1)} %broadcast_in_dim.22.scale_ref, f32[1,768]{1,0:T(1,128)S(1)} %broadcast_in_dim.23.shift_ref), custom_call_target="tpu_custom_call" | custom-call | tf_op jit(solution)/shard_map/pallas_call | solution.py:81
  155.3 0.9 copy-done.15
  156.2 1.9 %shard_map.132 = bf16[256,768]{1,0:T(8,128)(2,1)S(1)} custom-call(bf16[256,768]{1,0:T(8,128)(2,1)S(1)} %shard_map.131.act_ref, bf16[16,768]{1,0:T(8,128)(2,1)} %collective-permute-done.21.top_ref, bf16[256,768]{1,0:T(8,128)(2,1)S(1)} %get-tuple-element.87.glu_ref, bf16[16,768]{1,0:T(8,128)(2,1)} %collective-permute-done.22.bottom_ref, ...), custom_call_target="tpu_custom_call" | custom-call | tf_op jit(solution)/shard_map/pallas_call | solution.py:81
  158.0 2.9 %all_gather.11 = bf16[256,1536]{1,0:T(8,128)(2,1)S(1)} all-gather(bf16[256,768]{1,0:T(8,128)(2,1)S(1)} %shard_map.132), channel_id=1, replica_groups=mesh['ah'=2,'bh'=2,'bl'=2,'al'=2,'hid'=2] {'hid'}, dimensions={1}, use_global_device_ids=true | all-gather | bytes 1179648 | tf_op jit(solution)/shard_map/all_gather | solution.py:286
  161.0 1.5 add_convert_fusion
  (63 shorter events, 0.3 us)
Async XLA Ops:
  0.0 161.0 %copy-start = (bf16[1536,768]{1,0:T(8,128)(2,1)S(1)}, bf16[1536,768]{1,0:T(8,128)(2,1)}, u32[]{:S(2)}) copy-start(bf16[1536,768]{1,0:T(8,128)(2,1)} %param.22) | copy-start | bytes 7077892
  0.0 1.2 copy-start.7
  1.2 1.1 copy-start.8
  2.4 11.2 %copy-start.9 = (bf16[4,96,768]{2,1,0:T(8,128)(2,1)}, bf16[4,96,768]{2,1,0:T(8,128)(2,1)S(1)}, u32[]{:S(2)}) copy-start(bf16[4,96,768]{2,1,0:T(8,128)(2,1)S(1)} %get-tuple-element.49) | copy-start | bytes 1769476
  2.4 26.7 %copy-start.22 = (s32[64]{0:T(128)S(1)}, s32[64]{0:T(128)}, u32[]{:S(2)}) copy-start(s32[64]{0:T(128)} %lengths_ref.1) | copy-start | bytes 772
  13.6 32.2 %all-to-all-start.1 = ((bf16[4,96,768]{2,1,0:T(8,128)(2,1)}), bf16[4,96,768]{2,1,0:T(8,128)(2,1)S(1)}, u32[]{:S(2)}, u32[]{:S(2)}) async-start(bf16[4,96,768]{2,1,0:T(8,128)(2,1)} %copy-done.9), calls=%async_computation.1 | async-start | bytes 1179648 | tf_op jit(solution)/shard_map/all_to_all | solution.py:300
  17.8 26.5 %collective-permute-start = (bf16[4,96,768]{2,1,0:T(8,128)(2,1)}, bf16[4,96,768]{2,1,0:T(8,128)(2,1)}, u32[]{:S(2)}, u32[]{:S(2)}) collective-permute-start(bf16[4,96,768]{2,1,0:T(8,128)(2,1)} %copy-done.9), channel_id=1, source_target_pairs={{0,16},{16,0},{1,17},{17,1},{2,18},{18,2},{3,19},{19,3},{4,20},{20... | collective-permute-start | bytes 1769480 | tf_op jit(solution)/shard_map/ppermute | solution.py:296
  26.7 0.9 copy-start.12
  26.7 11.7 %collective-permute-start.3 = (bf16[128,1536]{1,0:T(8,128)(2,1)}, bf16[128,1536]{1,0:T(8,128)(2,1)}, u32[]{:S(2)}, u32[]{:S(2)}) collective-permute-start(bf16[128,1536]{1,0:T(8,128)(2,1)} %get-tuple-element.61.refs_0_), channel_id=1, source_target_pairs={{0,4},{4,0},{8,12},{12,8},{1,5},{5,1},{9,13},{13,9},{2,6},{6,2},{1... | collective-permute-start | bytes 1179656 | tf_op jit(solution)/shard_map/ppermute | solution.py:292
  27.6 16.7 %collective-permute-start.1 = (bf16[2,96,768]{2,1,0:T(8,128)(2,1)}, bf16[2,96,768]{2,1,0:T(8,128)(2,1)S(1)}, u32[]{:S(2)}, u32[]{:S(2)}) collective-permute-start(bf16[2,96,768]{2,1,0:T(8,128)(2,1)} %get-tuple-element.54.first_ref), channel_id=1, source_target_pairs={{0,2},{2,0},{1,3},{3,1},{4,6},{6,4},{5,7},{7,5},{8,10},{10,8},{9,1... | collective-permute-start | bytes 884744 | tf_op jit(solution)/shard_map/ppermute | solution.py:296
  28.9 16.2 %collective-permute-start.2 = (bf16[2,96,768]{2,1,0:T(8,128)(2,1)}, bf16[2,96,768]{2,1,0:T(8,128)(2,1)S(1)}, u32[]{:S(2)}, u32[]{:S(2)}) collective-permute-start(bf16[2,96,768]{2,1,0:T(8,128)(2,1)} %get-tuple-element.59.second_ref), channel_id=1, source_target_pairs={{0,2},{2,0},{1,3},{3,1},{4,6},{6,4},{5,7},{7,5},{8,10},{10,8},{9,1... | collective-permute-start | bytes 884744 | tf_op jit(solution)/shard_map/ppermute | solution.py:296
  31.4 0.7 copy-start.5
  44.3 0.7 copy-start.16
  45.0 0.7 copy-start.18
  45.7 25.0 %all-to-all-start.2 = ((bf16[4,96,768]{2,1,0:T(8,128)(2,1)}), bf16[4,96,768]{2,1,0:T(8,128)(2,1)S(1)}, u32[]{:S(2)}, u32[]{:S(2)}) async-start(bf16[4,96,768]{2,1,0:T(8,128)(2,1)} %collective-permute-done), calls=%async_computation.2 | async-start | bytes 1179648 | tf_op jit(solution)/shard_map/all_to_all | solution.py:300
  49.5 18.5 %collective-permute-start.5 = (bf16[4,96,768]{2,1,0:T(8,128)(2,1)S(1)}, bf16[4,96,768]{2,1,0:T(8,128)(2,1)S(1)}, u32[]{:S(2)}, u32[]{:S(2)}) collective-permute-start(bf16[4,96,768]{2,1,0:T(8,128)(2,1)S(1)} %all-to-all-done.1.o_ref), channel_id=1, source_target_pairs={{0,2},{2,0},{1,3},{3,1},{4,6},{6,4},{5,7},{7,5},{8,10},{10,8},{9,1... | collective-permute-start | bytes 1769480 | tf_op jit(solution)/shard_map/ppermute | solution.py:296
  50.7 19.2 %collective-permute-start.6 = (bf16[128,1536]{1,0:T(8,128)(2,1)}, bf16[128,1536]{1,0:T(8,128)(2,1)S(1)}, u32[]{:S(2)}, u32[]{:S(2)}) collective-permute-start(bf16[128,1536]{1,0:T(8,128)(2,1)} %get-tuple-element.61.refs_0_), channel_id=1, source_target_pairs={{0,12},{4,8},{8,4},{12,0},{1,13},{5,9},{9,5},{13,1},{2,14},{6,10},... | collective-permute-start | bytes 1179656 | tf_op jit(solution)/shard_map/ppermute | solution.py:292
  51.9 16.1 %collective-permute-start.4 = (bf16[2,96,768]{2,1,0:T(8,128)(2,1)}, bf16[2,96,768]{2,1,0:T(8,128)(2,1)S(1)}, u32[]{:S(2)}, u32[]{:S(2)}) collective-permute-start(bf16[2,96,768]{2,1,0:T(8,128)(2,1)} %get-tuple-element.54.first_ref), channel_id=1, source_target_pairs={{0,16},{16,0},{1,17},{17,1},{2,18},{18,2},{3,19},{19,3},{4,20},{20... | collective-permute-start | bytes 884744 | tf_op jit(solution)/shard_map/ppermute | solution.py:296
  68.0 0.7 copy-start.20
  68.8 0.8 copy-start.1
  69.9 0.8 copy-start.10
  70.7 25.3 %copy-start.2 = (bf16[4,96,768]{2,1,0:T(8,128)(2,1)S(1)}, bf16[4,96,768]{2,1,0:T(8,128)(2,1)}, u32[]{:S(2)}) copy-start(bf16[4,96,768]{2,1,0:T(8,128)(2,1)} %copy-done.1) | copy-start | bytes 1769476
  70.7 18.8 %collective-permute-start.8 = (bf16[4,96,768]{2,1,0:T(8,128)(2,1)S(1)}, bf16[4,96,768]{2,1,0:T(8,128)(2,1)S(1)}, u32[]{:S(2)}, u32[]{:S(2)}) collective-permute-start(bf16[4,96,768]{2,1,0:T(8,128)(2,1)S(1)} %all-to-all-done.2.z_ref), channel_id=1, source_target_pairs={{0,2},{2,0},{1,3},{3,1},{4,6},{6,4},{5,7},{7,5},{8,10},{10,8},{9,1... | collective-permute-start | bytes 1769480 | tf_op jit(solution)/shard_map/ppermute | solution.py:296
  71.9 15.4 %collective-permute-start.9 = (bf16[128,1536]{1,0:T(8,128)(2,1)}, bf16[128,1536]{1,0:T(8,128)(2,1)S(1)}, u32[]{:S(2)}, u32[]{:S(2)}) collective-permute-start(bf16[128,1536]{1,0:T(8,128)(2,1)} %get-tuple-element.61.refs_0_), channel_id=1, source_target_pairs={{0,8},{4,12},{8,0},{12,4},{1,9},{5,13},{9,1},{13,5},{2,10},{6,14},... | collective-permute-start | bytes 1179656 | tf_op jit(solution)/shard_map/ppermute | solution.py:292
  76.0 13.5 %collective-permute-start.7 = (bf16[2,96,768]{2,1,0:T(8,128)(2,1)}, bf16[2,96,768]{2,1,0:T(8,128)(2,1)S(1)}, u32[]{:S(2)}, u32[]{:S(2)}) collective-permute-start(bf16[2,96,768]{2,1,0:T(8,128)(2,1)} %get-tuple-element.59.second_ref), channel_id=1, source_target_pairs={{0,16},{16,0},{1,17},{17,1},{2,18},{18,2},{3,19},{19,3},{4,20},{20... | collective-permute-start | bytes 884744 | tf_op jit(solution)/shard_map/ppermute | solution.py:296
  87.2 1.0 copy-start.11
  88.2 6.2 %copy-start.21 = (bf16[2,96,768]{2,1,0:T(8,128)(2,1)S(1)}, bf16[2,96,768]{2,1,0:T(8,128)(2,1)}, u32[]{:S(2)}) copy-start(bf16[2,96,768]{2,1,0:T(8,128)(2,1)} %copy-done.20) | copy-start | bytes 884740
  89.5 8.7 %collective-permute-start.10 = (bf16[512,1536]{1,0:T(8,128)(2,1)S(1)}, bf16[512,1536]{1,0:T(8,128)(2,1)S(1)}, u32[]{:S(2)}, u32[]{:S(2)}) collective-permute-start(bf16[512,1536]{1,0:T(8,128)(2,1)S(1)} %shard_map.122.x_ref), channel_id=1, source_target_pairs={{0,1},{1,0},{2,3},{3,2},{4,5},{5,4},{6,7},{7,6},{8,9},{9,8},{10,11... | collective-permute-start | bytes 4718600 | tf_op jit(solution)/shard_map/ppermute | solution.py:296
  94.5 8.6 %collective-permute-start.11 = (bf16[2,96,768]{2,1,0:T(8,128)(2,1)S(1)}, bf16[2,96,768]{2,1,0:T(8,128)(2,1)S(1)}, u32[]{:S(2)}, u32[]{:S(2)}) collective-permute-start(bf16[2,96,768]{2,1,0:T(8,128)(2,1)S(1)} %copy-done.21), channel_id=1, source_target_pairs={{0,2},{2,0},{1,3},{3,1},{4,6},{6,4},{5,7},{7,5},{8,10},{10,8},{9,1... | collective-permute-start | bytes 884744 | tf_op jit(solution)/shard_map/ppermute | solution.py:296
  94.7 14.6 %collective-permute-start.12 = (bf16[2,96,768]{2,1,0:T(8,128)(2,1)S(1)}, bf16[2,96,768]{2,1,0:T(8,128)(2,1)S(1)}, u32[]{:S(2)}, u32[]{:S(2)}) collective-permute-start(bf16[2,96,768]{2,1,0:T(8,128)(2,1)S(1)} %collective-permute-done.7.second_ref), channel_id=1, source_target_pairs={{0,2},{2,0},{1,3},{3,1},{4,6},{6,4},{5,7},{7,5},{8,10},{10,8},{9,1... | collective-permute-start | bytes 884744 | tf_op jit(solution)/shard_map/ppermute | solution.py:296
  98.2 2.2 %copy-start.17 = (bf16[2,96,768]{2,1,0:T(8,128)(2,1)S(1)}, bf16[2,96,768]{2,1,0:T(8,128)(2,1)}, u32[]{:S(2)}) copy-start(bf16[2,96,768]{2,1,0:T(8,128)(2,1)} %copy-done.16) | copy-start | bytes 884740
  98.2 2.2 %copy-start.19 = (bf16[2,96,768]{2,1,0:T(8,128)(2,1)S(1)}, bf16[2,96,768]{2,1,0:T(8,128)(2,1)}, u32[]{:S(2)}) copy-start(bf16[2,96,768]{2,1,0:T(8,128)(2,1)} %copy-done.18) | copy-start | bytes 884740
  111.4 2.8 %collective-permute-start.17 = (bf16[512,768]{1,0:T(8,128)(2,1)S(1)}, bf16[512,768]{1,0:T(8,128)(2,1)S(1)}, u32[]{:S(2)}, u32[]{:S(2)}) collective-permute-start(bf16[512,768]{1,0:T(8,128)(2,1)S(1)} %get-tuple-element.82), channel_id=1, source_target_pairs={{0,1},{1,0},{2,3},{3,2},{4,5},{5,4},{6,7},{7,6},{8,9},{9,8},{10,11... | collective-permute-start | bytes 2359304 | tf_op jit(solution)/shard_map/ppermute | solution.py:296
  112.3 4.8 %collective-permute-start.13 = (bf16[512,768]{1,0:T(8,128)(2,1)S(1)}, bf16[512,768]{1,0:T(8,128)(2,1)S(1)}, u32[]{:S(2)}, u32[]{:S(2)}) collective-permute-start(bf16[512,768]{1,0:T(8,128)(2,1)S(1)} %get-tuple-element.74), channel_id=1, source_target_pairs={{0,1},{1,0},{2,3},{3,2},{4,5},{5,4},{6,7},{7,6},{8,9},{9,8},{10,11... | collective-permute-start | bytes 2359304 | tf_op jit(solution)/shard_map/ppermute | solution.py:296
  114.3 6.3 %copy-start.23 = (f32[1536]{0:T(1024)S(1)}, f32[1536]{0:T(1024)}, u32[]{:S(2)}) copy-start(f32[1536]{0:T(1024)} %param.16) | copy-start | bytes 18436
  114.3 19.9 %copy-start.13 = (bf16[128,1536]{1,0:T(8,128)(2,1)S(1)}, bf16[128,1536]{1,0:T(8,128)(2,1)}, u32[]{:S(2)}) copy-start(bf16[128,1536]{1,0:T(8,128)(2,1)} %copy-done.12) | copy-start | bytes 1179652
  114.4 6.2 %collective-permute-start.18 = (bf16[128,768]{1,0:T(8,128)(2,1)S(1)}, bf16[128,768]{1,0:T(8,128)(2,1)S(1)}, u32[]{:S(2)}, u32[]{:S(2)}) collective-permute-start(bf16[128,768]{1,0:T(8,128)(2,1)S(1)} %get-tuple-element.84), channel_id=1, source_target_pairs={{0,4},{4,0},{8,12},{12,8},{1,5},{5,1},{9,13},{13,9},{2,6},{6,2},{1... | collective-permute-start | bytes 589832 | tf_op jit(solution)/shard_map/ppermute | solution.py:292
  114.8 5.8 %collective-permute-start.19 = (bf16[128,768]{1,0:T(8,128)(2,1)S(1)}, bf16[128,768]{1,0:T(8,128)(2,1)S(1)}, u32[]{:S(2)}, u32[]{:S(2)}) collective-permute-start(bf16[128,768]{1,0:T(8,128)(2,1)S(1)} %get-tuple-element.85), channel_id=1, source_target_pairs={{0,8},{4,12},{8,0},{12,4},{1,9},{5,13},{9,1},{13,5},{2,10},{6,14},... | collective-permute-start | bytes 589832 | tf_op jit(solution)/shard_map/ppermute | solution.py:292
  114.8 10.9 %collective-permute-start.20 = (bf16[128,768]{1,0:T(8,128)(2,1)S(1)}, bf16[128,768]{1,0:T(8,128)(2,1)S(1)}, u32[]{:S(2)}, u32[]{:S(2)}) collective-permute-start(bf16[128,768]{1,0:T(8,128)(2,1)S(1)} %get-tuple-element.86), channel_id=1, source_target_pairs={{0,12},{4,8},{8,4},{12,0},{1,13},{5,9},{9,5},{13,1},{2,14},{6,10},... | collective-permute-start | bytes 589832 | tf_op jit(solution)/shard_map/ppermute | solution.py:292
  117.1 21.3 %copy-start.4 = (bf16[1536,768]{1,0:T(8,128)(2,1)S(1)}, bf16[1536,768]{1,0:T(8,128)(2,1)}, u32[]{:S(2)}) copy-start(bf16[1536,768]{1,0:T(8,128)(2,1)} %gate_ref.1) | copy-start | bytes 7077892
  117.2 21.2 %copy-start.3 = (bf16[1536,768]{1,0:T(8,128)(2,1)S(1)}, bf16[1536,768]{1,0:T(8,128)(2,1)}, u32[]{:S(2)}) copy-start(bf16[1536,768]{1,0:T(8,128)(2,1)} %value_ref.1) | copy-start | bytes 7077892
  117.3 11.7 %collective-permute-start.14 = (bf16[128,768]{1,0:T(8,128)(2,1)S(1)}, bf16[128,768]{1,0:T(8,128)(2,1)S(1)}, u32[]{:S(2)}, u32[]{:S(2)}) collective-permute-start(bf16[128,768]{1,0:T(8,128)(2,1)S(1)} %get-tuple-element.76), channel_id=1, source_target_pairs={{0,4},{4,0},{8,12},{12,8},{1,5},{5,1},{9,13},{13,9},{2,6},{6,2},{1... | collective-permute-start | bytes 589832 | tf_op jit(solution)/shard_map/ppermute | solution.py:292
  117.6 11.4 %collective-permute-start.15 = (bf16[128,768]{1,0:T(8,128)(2,1)S(1)}, bf16[128,768]{1,0:T(8,128)(2,1)S(1)}, u32[]{:S(2)}, u32[]{:S(2)}) collective-permute-start(bf16[128,768]{1,0:T(8,128)(2,1)S(1)} %get-tuple-element.77), channel_id=1, source_target_pairs={{0,8},{4,12},{8,0},{12,4},{1,9},{5,13},{9,1},{13,5},{2,10},{6,14},... | collective-permute-start | bytes 589832 | tf_op jit(solution)/shard_map/ppermute | solution.py:292
  120.6 13.5 %collective-permute-start.16 = (bf16[128,768]{1,0:T(8,128)(2,1)S(1)}, bf16[128,768]{1,0:T(8,128)(2,1)S(1)}, u32[]{:S(2)}, u32[]{:S(2)}) collective-permute-start(bf16[128,768]{1,0:T(8,128)(2,1)S(1)} %get-tuple-element.78), channel_id=1, source_target_pairs={{0,12},{4,8},{8,4},{12,0},{1,13},{5,9},{9,5},{13,1},{2,14},{6,10},... | collective-permute-start | bytes 589832 | tf_op jit(solution)/shard_map/ppermute | solution.py:292
  138.4 8.7 %copy-start.24 = (f32[768]{0:T(1024)S(1)}, f32[768]{0:T(1024)}, u32[]{:S(2)}) copy-start(f32[768]{0:T(1024)} %param.20) | copy-start | bytes 9220
  138.4 8.7 %copy-start.25 = (f32[768]{0:T(1024)S(1)}, f32[768]{0:T(1024)}, u32[]{:S(2)}) copy-start(f32[768]{0:T(1024)} %param.21) | copy-start | bytes 9220
  141.0 14.3 %collective-permute-start.21 = (bf16[16,768]{1,0:T(8,128)(2,1)}, bf16[16,768]{1,0:T(8,128)(2,1)}, u32[]{:S(2)}, u32[]{:S(2)}) collective-permute-start(bf16[16,768]{1,0:T(8,128)(2,1)} %get-tuple-element.89), channel_id=1, source_target_pairs={{0,2},{2,4},{4,6},{6,8},{8,10},{10,12},{12,14},{14,16},{16,18},{18... | collective-permute-start | bytes 73736 | tf_op jit(solution)/shard_map/ppermute | solution.py:271
  143.1 12.1 %collective-permute-start.22 = (bf16[16,768]{1,0:T(8,128)(2,1)}, bf16[16,768]{1,0:T(8,128)(2,1)}, u32[]{:S(2)}, u32[]{:S(2)}) collective-permute-start(bf16[16,768]{1,0:T(8,128)(2,1)} %get-tuple-element.90), channel_id=1, source_target_pairs={{2,0},{4,2},{6,4},{8,6},{10,8},{12,10},{14,12},{16,14},{18,16},{20... | collective-permute-start | bytes 73736 | tf_op jit(solution)/shard_map/ppermute | solution.py:272
  147.2 0.9 copy-start.6
  148.1 0.9 copy-start.14
  155.3 0.9 copy-start.15

commit v3 on v2

--- a/solution.py
+++ b/solution.py
@@ -1,3 +1,5 @@
+import functools
+
 import jax
 import jax.numpy as jnp
 from jax import lax
@@ -77,7 +79,7 @@
 SMEM = pl.BlockSpec(memory_space=pltpu.SMEM)
 
 
-def kernel_call(body, outs, ins, scratch=(), scalars=0):
+def kernel_call(body, outs, ins, scratch=(), scalars=0, flops=0, moved=0):
     return pl.pallas_call(
         body,
         out_shape=[jax.ShapeDtypeStruct(shape, dtype) for shape, dtype in outs],
@@ -85,7 +87,7 @@
         out_specs=[VMEM] * len(outs),
         scratch_shapes=list(scratch),
         compiler_params=pltpu.CompilerParams(vmem_limit_bytes=VMEM_LIMIT),
-        cost_estimate=pl.CostEstimate(flops=0, bytes_accessed=0, transcendentals=0),
+        cost_estimate=pl.CostEstimate(flops=flops, bytes_accessed=moved, transcendentals=0),
     )(*ins)
 
 
@@ -97,12 +99,15 @@
     return values / (1.0 + jnp.exp(-values))
 
 
-def cut_kernel(in_ref, out_ref, in_cut_ref, out_cut_ref):
-    parts, _, width = in_cut_ref.shape
+def cut_kernel(*refs):
+    *arrays, out_ref = refs
+    parts, _, width = out_ref.shape
     for part in range(parts):
-        at = slice(part * width, (part + 1) * width)
-        in_cut_ref[part] = in_ref[:, at]
-        out_cut_ref[part] = out_ref[:, at]
+        at = 0
+        for ref in arrays:
+            rows = ref.shape[0]
+            out_ref[part, at : at + rows, :] = ref[:, part * width : (part + 1) * width]
+            at += rows
 
 
 def part_kernel(both_ref, first_ref, second_ref):
@@ -125,29 +130,28 @@
         out_ref[i * rows : (i + 1) * rows] = piece[...]
 
 
-def interleave(full_ref, base, own_refs, other_refs, me_l):
-    block = own_refs[0].shape[1]
+def interleave(full_ref, base, block, own_refs, other_refs, me_l, skip=0):
     for refs, turn in ((own_refs, me_l), (other_refs, 1 - me_l)):
         blocks = [(ref, j) for ref in refs for j in range(ref.shape[0])]
         for i, (ref, j) in enumerate(blocks):
             at = pl.multiple_of(base + (2 * i + turn) * block, block)
-            full_ref[pl.ds(at, block), :] = ref[j]
-
-
-def hidden_kernel(me_ref, x_ref, o_ref, ox_ref, z_ref, zx_ref, h_ref, w_ref):
+            full_ref[pl.ds(at, block), :] = ref[j, skip : skip + block, :]
+
+
+def hidden_kernel(me_ref, x_ref, b_ref, bx_ref, h_ref, w_ref):
     me_l, me_a = me_ref[0], me_ref[2]
-    part = w_ref.shape[0] // 2
-    interleave(w_ref, me_a * part, [o_ref], [ox_ref], me_l)
-    interleave(w_ref, (1 - me_a) * part, [z_ref], [zx_ref], me_l)
+    part, block = w_ref.shape[0] // 2, b_ref.shape[1] // 2
+    interleave(w_ref, me_a * part, block, [b_ref], [bx_ref], me_l)
+    interleave(w_ref, (1 - me_a) * part, block, [b_ref], [bx_ref], me_l, block)
     step = 256
     for at in range(0, x_ref.shape[0], step):
         pre = jnp.dot(x_ref[at : at + step, :], w_ref[...], preferred_element_type=jnp.float32)
         h_ref[at : at + step, :] = silu(pre).astype(jnp.bfloat16)
 
 
-def sums_kernel(me_ref, own_ref, oth_ref, first_ref, second_ref, *refs):
-    *others, kept_ref, sent_ref, w_ref = refs
-    interleave(w_ref, 0, [first_ref, second_ref], others, me_ref[0])
+def sums_kernel(n_own, me_ref, own_ref, oth_ref, *refs):
+    *blocks, kept_ref, sent_ref, w_ref = refs
+    interleave(w_ref, 0, blocks[0].shape[1], blocks[:n_own], blocks[n_own:], me_ref[0])
     step = 256
     for h_ref, out_ref in ((oth_ref, sent_ref), (own_ref, kept_ref)):
         for at in range(0, h_ref.shape[0], step):
@@ -180,16 +184,18 @@
 HALO = 16
 
 
-def utter_kernel(first_ref, lengths_ref, out_ref):
-    position = first_ref[0] + lax.broadcasted_iota(jnp.int32, out_ref.shape, 0)
+def utter_kernel(first_ref, lengths_ref, out_ref, base_ref):
+    position = first_ref[0] + lax.broadcasted_iota(jnp.int32, base_ref.shape, 0)
 
     def step(u, carry):
         end, utter = carry
         end = end + lengths_ref[u]
         return end, utter + jnp.where(position >= end, 1, 0)
 
-    zero = jnp.zeros(out_ref.shape, jnp.int32)
-    out_ref[...] = lax.fori_loop(0, lengths_ref.shape[0], step, (jnp.int32(0), zero))[1]
+    zero = jnp.zeros(base_ref.shape, jnp.int32)
+    base_ref[...] = lax.fori_loop(0, lengths_ref.shape[0], step, (jnp.int32(0), zero))[1]
+    for r in range(8):
+        out_ref[r] = base_ref[1 + r : 1 + r + out_ref.shape[1], :]
 
 
 def glu_kernel(mid_ref, gain_ref, value_ref, gate_ref, glu_ref, head_ref, tail_ref):
@@ -202,35 +208,38 @@
     tail_ref[...] = glu[glu.shape[0] - HALO :]
 
 
-def conv_rows(ext_ref, utter_ref, taps_ref, scale_ref, shift_ref, out_ref, ext_at, utter_at, out_at, rows):
+def conv_rows(ext_ref, utter_ref, taps_ref, scale_ref, shift_ref, out_ref, tiles, step):
+    width = out_ref.shape[1]
+    taps = taps_ref.shape[0]
     lanes = 128
-    taps = taps_ref.shape[0]
-    span = rows + taps - 8
-
-    def column(j, _):
-        at = pl.ds(pl.multiple_of(j * lanes, lanes), lanes)
-        centre = utter_ref[utter_at + HALO : utter_at + HALO + rows, :]
-        total = jnp.zeros((rows, lanes), jnp.float32)
-        for r in range(8):
-            cells = ext_ref[ext_at + 1 + r : ext_at + 1 + r + span, at]
-            utter = utter_ref[utter_at + 1 + r : utter_at + 1 + r + span, :]
-            for q in range(0, taps, 8):
-                term = cells[q : q + rows] * taps_ref[q + r : q + r + 1, at]
-                total = total + jnp.where(utter[q : q + rows] == centre, term, 0.0)
-        act = silu(total * scale_ref[:, at] + shift_ref[:, at])
-        out_ref[out_at : out_at + rows, at] = act.astype(out_ref.dtype)
+    group = 3 if width % (3 * lanes) == 0 else 1
+    span = step + taps - 8
+
+    def columns(i, _):
+        at_lane = [pl.ds(pl.multiple_of((i * group + g) * lanes, lanes), lanes) for g in range(group)]
+        for ext_at, at, out_at in tiles:
+            centre = utter_ref[7, at + HALO - 8 : at + HALO - 8 + step, :]
+            totals = [jnp.zeros((step, lanes), jnp.float32)] * group
+            for r in range(8):
+                cells = [ext_ref[ext_at + 1 + r : ext_at + 1 + r + span, c] for c in at_lane]
+                for q in range(0, taps, 8):
+                    same = utter_ref[r, at + q : at + q + step, :] == centre
+                    for g, c in enumerate(at_lane):
+                        term = cells[g][q : q + step] * taps_ref[q + r : q + r + 1, c]
+                        totals[g] = totals[g] + jnp.where(same, term, 0.0)
+            for total, c in zip(totals, at_lane):
+                act = silu(total * scale_ref[:, c] + shift_ref[:, c])
+                out_ref[out_at : out_at + step, c] = act.astype(out_ref.dtype)
         return 0
 
-    lax.fori_loop(0, out_ref.shape[1] // lanes, column, 0)
+    lax.fori_loop(0, width // (group * lanes), columns, 0)
 
 
 def inner_conv_kernel(glu_ref, utter_ref, taps_ref, scale_ref, shift_ref, out_ref, ext_ref):
     ext_ref[...] = f32(glu_ref[...])
-    step = 32
-    for at in range(HALO, out_ref.shape[0] - HALO, step):
-        conv_rows(
-            ext_ref, utter_ref, taps_ref, scale_ref, shift_ref, out_ref, at - HALO, at, at, step
-        )
+    step = 2 * HALO
+    tiles = [(at - HALO, at, at) for at in range(HALO, out_ref.shape[0] - HALO, step)]
+    conv_rows(ext_ref, utter_ref, taps_ref, scale_ref, shift_ref, out_ref, tiles, step)
 
 
 def edge_conv_kernel(
@@ -243,45 +252,50 @@
     ext_ref[HALO : 3 * HALO, :] = f32(glu_ref[: 2 * HALO, :])
     ext_ref[3 * HALO : 5 * HALO, :] = f32(glu_ref[rows - 2 * HALO :, :])
     ext_ref[5 * HALO :, :] = f32(bottom_ref[...])
-    rest = (utter_ref, taps_ref, scale_ref, shift_ref, out_ref)
-    conv_rows(ext_ref, *rest, 0, 0, 0, HALO)
-    conv_rows(ext_ref, *rest, 3 * HALO, last, last, HALO)
-
-
-def utterances(rows, axis, lengths):
+    tiles = [(0, 0, 0), (3 * HALO, last, last)]
+    conv_rows(ext_ref, utter_ref, taps_ref, scale_ref, shift_ref, out_ref, tiles, HALO)
+
+
+def utterances(rows, axis, lengths, taps):
     return kernel_call(
         utter_kernel,
-        [((rows + 2 * HALO, 128), jnp.int32)],
+        [((8, rows + taps - 8, 128), jnp.int32)],
         [(lax.axis_index(axis) * rows - HALO)[None], lengths],
+        scratch=[pltpu.VMEM((rows + 2 * HALO, 128), jnp.int32)],
         scalars=2,
     )[0]
 
 
-def grouped_conv_module(
-    mid_own, mid_full, axis, utter, conv_gain, w_value, w_gate, depth_kernel, bn_scale, bn_shift, w_proj
-):
+def grouped_conv_module(mid_own, mid_full, axis, early, w_value, w_gate, depth_kernel, w_proj):
     rows, width = mid_own.shape
+    utter, conv_gain, bn_scale, bn_shift = early
     bf16 = jnp.bfloat16
     glu, head, tail = kernel_call(
         glu_kernel,
         [((rows, width), bf16)] + [((HALO, width), bf16)] * 2,
-        [mid_full, conv_gain[None, :], w_value, w_gate],
+        [mid_full, conv_gain, w_value, w_gate],
+        flops=4 * rows * w_value.size,
+        moved=4 * w_value.size,
     )
     count = lax.axis_size(axis)
     top = lax.ppermute(tail, axis, [(i, i + 1) for i in range(count - 1)])
     bottom = lax.ppermute(head, axis, [(i + 1, i) for i in range(count - 1)])
-    rest = [utter, depth_kernel, bn_scale[None, :], bn_shift[None, :]]
+    rest = [utter, depth_kernel, bn_scale, bn_shift]
     (act,) = kernel_call(
         inner_conv_kernel,
         [((rows, width), bf16)],
         [glu, *rest],
         scratch=[pltpu.VMEM((rows, width), jnp.float32)],
+        flops=rows * depth_kernel.size,
+        moved=16 * rows * width,
     )
     (act,) = kernel_call(
         edge_conv_kernel,
         [((rows, width), bf16)],
         [act, top, glu, bottom, *rest],
         scratch=[pltpu.VMEM((6 * HALO, width), jnp.float32)],
+        flops=HALO * depth_kernel.size,
+        moved=4 * rows * width,
     )
     act_full = lax.all_gather(act, "hid", axis=1, tiled=True)
     projected = jnp.dot(act_full, w_proj, preferred_element_type=jnp.float32)
@@ -311,13 +325,10 @@
     me = jnp.stack([lax.axis_index("al"), me_c, lax.axis_index("ah")])
     tie = lax.optimization_barrier
 
-    in_cut, out_cut = kernel_call(cut_kernel, [((4, shard, units), bf16)] * 2, [w_in, w_out.T])
-    in_far = swap(in_cut, "ah")
+    block, pair = (4, shard, units), (2, shard, units)
+    in_far = swap(w_in, "ah")
+    (out_cut,) = kernel_call(cut_kernel, [(block, bf16)], [w_out.T])
     out_o = recut(out_cut)
-    in_o = recut(in_cut)
-    out_1, out_2 = kernel_call(part_kernel, [((2, shard, units), bf16)] * 2, [out_o])
-    out_x1 = swap(out_1, "al")
-    out_x2 = swap(out_2, "al")
     whole = lax.all_gather(tokens, "hid", axis=1, tiled=True)
     mine, normed = kernel_call(
         norm_kernel,
@@ -326,41 +337,41 @@
         scalars=1,
     )
     frames1 = partner(normed, 1)
-    in_far, out_1, out_2, out_x1, out_x2, normed, frames1, early = tie(
-        (in_far, out_1, out_2, out_x1, out_x2, normed, frames1, early)
-    )
+    in_far, out_o, normed, frames1, early = tie((in_far, out_o, normed, frames1, early))
+    (in_both,) = kernel_call(cut_kernel, [((4, 2 * shard, units), bf16)], [w_in, in_far])
+    in_b = recut(in_both)
+    out_1, out_2 = kernel_call(part_kernel, [(pair, bf16)] * 2, [out_o])
     out_z1 = swap(out_1, "ah")
-    in_ox = swap(in_o, "al")
-    in_z = recut(in_far)
+    out_x = swap(out_o, "al")
+    in_b, out_z1, out_2, out_o, out_x, normed = tie((in_b, out_z1, out_2, out_o, out_x, normed))
+    in_bx = swap(in_b, "al")
+    out_z2 = swap(out_2, "ah")
+    frames2 = partner(normed, 2)
     frames3 = partner(normed, 3)
-    out_z1, in_ox, in_z, out_2, normed, frames3 = tie((out_z1, in_ox, in_z, out_2, normed, frames3))
-    out_z2 = swap(out_2, "ah")
-    in_zx = swap(in_z, "al")
-    frames2 = partner(normed, 2)
+    out_z1, out_z2, in_bx, frames2, frames3 = tie((out_z1, out_z2, in_bx, frames2, frames3))
+    out_zx1 = swap(out_z1, "al")
+    out_zx2 = swap(out_z2, "al")
     (x_own,) = kernel_call(
         join_kernel, [((4 * half, wide), bf16)], [normed, frames1, frames2, frames3]
     )
-    out_z1, out_z2, in_zx, x_own = tie((out_z1, out_z2, in_zx, x_own))
-    out_zx1 = swap(out_z1, "al")
-    out_zx2 = swap(out_z2, "al")
     x_oth = swap(x_own, "hid")
 
     def units_of(x):
         return kernel_call(
             hidden_kernel,
             [((4 * half, units), bf16)],
-            [me, x, in_o, in_ox, in_z, in_zx],
+            [me, x, in_b, in_bx],
             scratch=[pltpu.VMEM((wide, units), bf16)],
             scalars=1,
         )[0]
 
     hidden = [units_of(x_own), units_of(x_oth)]
 
-    def products(*blocks):
+    def products(own, other):
         return kernel_call(
-            sums_kernel,
+            functools.partial(sums_kernel, len(own)),
             [((4 * half, width), jnp.float32), ((4 * half, width), bf16)],
-            [me, *hidden, *blocks],
+            [me, *hidden, *own, *other],
             scratch=[pltpu.VMEM((width, units), bf16)],
             scalars=1,
         )
@@ -373,8 +384,8 @@
         )
         return [total[0]] + [partner(v, k + 1) for k, v in enumerate(total[1:])]
 
-    near, out_zx1, out_zx2 = tie((products(out_1, out_2, out_x1, out_x2), out_zx1, out_zx2))
-    far = products(out_z1, out_z2, out_zx1, out_zx2)
+    near, out_zx1, out_zx2 = tie((products([out_o], [out_x]), out_zx1, out_zx2))
+    far = products([out_z1, out_z2], [out_zx1, out_zx2])
     (mid_rows,) = kernel_call(
         mid_kernel, [((half, wide), bf16)], [me, mine, *scatter(*near), *scatter(*far)], scalars=1
     )
@@ -394,10 +405,13 @@
 
     def local(tokens, ffn_gain, w_in, w_out, conv_gain, *rest):
         if grouped:
-            *rest, lengths = rest
-            utter = utterances(tokens.shape[0], tok, lengths)
-            mid_own, mid_full, utter = grouped_ffn(tokens, ffn_gain, w_in, w_out, utter)
-            return grouped_conv_module(mid_own, mid_full, tok, utter, conv_gain, *rest)
+            w_value, w_gate, depth_kernel, bn_scale, bn_shift, w_proj, lengths = rest
+            utter = utterances(tokens.shape[0], tok, lengths, depth_kernel.shape[0])
+            early = utter, conv_gain[None, :], bn_scale[None, :], bn_shift[None, :]
+            mid_own, mid_full, early = grouped_ffn(tokens, ffn_gain, w_in, w_out, early)
+            return grouped_conv_module(
+                mid_own, mid_full, tok, early, w_value, w_gate, depth_kernel, w_proj
+            )
         mid_own, mid_full = gathered_ffn(tokens, ffn_gain, w_in, w_out)
         return conv_module(mid_own, mid_full, tok, conv_gain, *rest)
 

time: 163 us -> 158 us (0.969)
  blocking collectives: 22.4 us -> 9.85 us
  waiting for transfers between devices: 61.7 us -> 67.8 us
  local copies, waits for them, and re-layouts: 11.1 us -> 12.8 us
    ppermute x12 -> x10, waiting for transfers between devices: 27.5 us -> 46.2 us  [swap(): return lax.ppermute(values, axis, SWAP)]
    ppermute x9, waiting for transfers between devices: 34.3 us -> 21.2 us  [partner(): return lax.ppermute(values, GROUP, [(i, i ^ step) for i in range(4)])]
    all_to_all x1 -> x0, blocking collectives: 11.2 us -> none  [recut(): return lax.all_to_all(parts, GROUP, 0, 0)]
    broadcast_in_dim x3, local copies, waits for them, and re-layouts: 0.01 us -> 2.08 us  [local(): early = (utter, conv_gain[None, :], bn_scale[None, :], bn_shift[None, :])]
    ppermute x9, starting transfers between devices: 8.45 us -> 10.4 us  [partner(): return lax.ppermute(values, GROUP, [(i, i ^ step) for i in range(4)])]
    ppermute x12 -> x10, starting transfers between devices: 16.3 us -> 14.5 us  [swap(): return lax.ppermute(values, axis, SWAP)]
    pallas_call x15 -> x16, Pallas kernels: 26.3 us -> 24.9 us  [kernel_call(): pl.pallas_call(body, out_shape=[jax.ShapeDtypeStruct(shape, dtype) for sh...]
  transfers between devices with their start and end apart: 25 -> 23, of which waited for: 11 -> 14; matrix products, arithmetic and copies ran while one was open for 0% -> 1% of each run, Pallas kernels for 12% -> 9%
where the time goes in v3:
time: 158 us; the launch traced here: 156 us
  waiting for transfers between devices  67.8 us (43%)
  starting transfers between devices  38.8 us (25%)
  Pallas kernels  24.9 us (16%)
  local copies, waits for them, and re-layouts  12.8 us (8%)
  blocking collectives  9.85 us (6%)
    ppermute x10, waiting for transfers between devices, swap(): return lax.ppermute(values, axis, SWAP)  46.2 us
    pallas_call x16, Pallas kernels, kernel_call(): pl.pallas_call(body, out_shape=[jax.ShapeDtypeStruct(shape, dtype) for sh...  24.9 us
    ppermute x9, waiting for transfers between devices, partner(): return lax.ppermute(values, GROUP, [(i, i ^ step) for i in range(4)])  21.2 us
    ppermute x10, starting transfers between devices, swap(): return lax.ppermute(values, axis, SWAP)  14.5 us
    unnamed x52, local copies, waits for them, and re-layouts  10.8 us
    ppermute x9, starting transfers between devices, partner(): return lax.ppermute(values, GROUP, [(i, i ^ step) for i in range(4)])  10.4 us
    all_to_all x2, starting transfers between devices, recut(): return lax.all_to_all(parts, GROUP, 0, 0)  7.54 us
    all_gather x1, blocking collectives, grouped_ffn(): whole = lax.all_gather(tokens, 'hid', axis=1, tiled=True)  3.72 us
  transfers between devices with their start and end apart: 23, of which 14 were waited for; matrix products, arithmetic and copies ran while one was open for 1% of the time, Pallas kernels for 9%

profile of v3, /device:TPU:5, one launch (start us, length us, event | category | flops | bytes accessed | tf_op | source)
XLA Modules:
  0.0 156.1 jit_solution(14037648744597627270)
XLA Ops:
  0.0 1.2 copy-done.13
  1.2 0.9 shard_map.119
  2.1 3.7 %all-to-all-start = ((bf16[4,96,768]{2,1,0:T(8,128)(2,1)}), bf16[4,96,768]{2,1,0:T(8,128)(2,1)S(1)}, u32[]{:S(2)}, u32[]{:S(2)}) async-start(bf16[4,96,768]{2,1,0:T(8,128)(2,1)} %shard_map.119), calls=%async_computation | async-start | bytes 1179648 | tf_op jit(solution)/shard_map/all_to_all | solution.py:314
  5.8 2.3 %collective-permute-start = (bf16[96,3072]{1,0:T(8,128)(2,1)S(1)}, bf16[96,3072]{1,0:T(8,128)(2,1)}, u32[]{:S(2)}, u32[]{:S(2)}) collective-permute-start(bf16[96,3072]{1,0:T(8,128)(2,1)S(1)} %copy-done.14), channel_id=1, source_target_pairs={{0,16},{16,0},{1,17},{17,1},{2,18},{18,2},{3,19},{19,3},{4,20},{20... | collective-permute-start | bytes 1769480 | tf_op jit(solution)/shard_map/ppermute | solution.py:310
  8.2 3.7 %all_gather.9.whole_ref = bf16[256,1536]{1,0:T(8,128)(2,1)S(1)} all-gather(bf16[256,768]{1,0:T(8,128)(2,1)} %param.12), channel_id=1, replica_groups=mesh['ah'=2,'bh'=2,'bl'=2,'al'=2,'hid'=2] {'hid'}, dimensions={1}, use_global_device_ids=true | all-gather | bytes 1179648 | tf_op jit(solution)/shard_map/all_gather | solution.py:332
  11.9 1.1 shard_map.118
  12.9 0.8 copy-done.19
  13.7 0.7 broadcast_in_dim.21.gain_ref
  14.4 0.7 broadcast_in_dim.22.scale_ref
  15.1 0.7 broadcast_in_dim.23.shift_ref
  15.8 0.7 copy-done.23
  16.4 2.4 %shard_map.120.utter_ref = s32[8,280,128]{2,1,0:T(8,128)S(1)} custom-call(s32[1]{0:T(128)} %bitcast.5.first_ref, s32[64]{0:T(128)S(1)} %copy-done.23), custom_call_target="tpu_custom_call" | custom-call | tf_op jit(solution)/shard_map/pallas_call | solution.py:83
  18.8 1.0 copy-done.1
  19.9 6.7 %collective-permute-done.1.refs_1_ = bf16[128,1536]{1,0:T(8,128)(2,1)} collective-permute-done((bf16[128,1536]{1,0:T(8,128)(2,1)}, bf16[128,1536]{1,0:T(8,128)(2,1)}, u32[]{:S(2)}, u32[]{:S(2)}) %collective-permute-start.1) | collective-permute-done | bytes 393248 | tf_op jit(solution)/shard_map/ppermute | solution.py:306
  26.6 6.6 %collective-permute-done.refs_1_ = bf16[96,3072]{1,0:T(8,128)(2,1)} collective-permute-done((bf16[96,3072]{1,0:T(8,128)(2,1)S(1)}, bf16[96,3072]{1,0:T(8,128)(2,1)}, u32[]{:S(2)}, u32[]{:S(2)}) %collective-permute-start) | collective-permute-done | bytes 589856 | tf_op jit(solution)/shard_map/ppermute | solution.py:310
  33.1 1.4 shard_map.121
  34.5 1.1 copy-done.6
  35.6 3.8 %all-to-all-start.1 = ((bf16[4,192,768]{2,1,0:T(8,128)(2,1)}), bf16[4,192,768]{2,1,0:T(8,128)(2,1)S(1)}, u32[]{:S(2)}, u32[]{:S(2)}) async-start(bf16[4,192,768]{2,1,0:T(8,128)(2,1)} %copy-done.6), calls=%async_computation.1 | async-start | bytes 2359296 | tf_op jit(solution)/shard_map/all_to_all | solution.py:314
  39.4 1.3 collective-permute-start.3
  40.7 1.1 copy-done.4
  41.8 0.7 copy-done.24
  42.5 2.1 %collective-permute-start.2 = (bf16[2,96,768]{2,1,0:T(8,128)(2,1)S(1)}, bf16[2,96,768]{2,1,0:T(8,128)(2,1)S(1)}, u32[]{:S(2)}, u32[]{:S(2)}) collective-permute-start(bf16[2,96,768]{2,1,0:T(8,128)(2,1)S(1)} %get-tuple-element.51), channel_id=1, source_target_pairs={{0,16},{16,0},{1,17},{17,1},{2,18},{18,2},{3,19},{19,3},{4,20},{20... | collective-permute-start | bytes 884744 | tf_op jit(solution)/shard_map/ppermute | solution.py:310
  44.6 12.2 %collective-permute-done.2.refs_0_ = bf16[2,96,768]{2,1,0:T(8,128)(2,1)S(1)} collective-permute-done((bf16[2,96,768]{2,1,0:T(8,128)(2,1)S(1)}, bf16[2,96,768]{2,1,0:T(8,128)(2,1)S(1)}, u32[]{:S(2)}, u32[]{:S(2)}) %collective-permute-start.2) | collective-permute-done | bytes 294944 | tf_op jit(solution)/shard_map/ppermute | solution.py:310
  56.8 0.7 copy-done.21
  57.5 0.8 copy-done.15
  58.7 1.3 collective-permute-start.5
  60.0 3.0 %collective-permute-start.6 = (bf16[128,1536]{1,0:T(8,128)(2,1)}, bf16[128,1536]{1,0:T(8,128)(2,1)S(1)}, u32[]{:S(2)}, u32[]{:S(2)}) collective-permute-start(bf16[128,1536]{1,0:T(8,128)(2,1)} %get-tuple-element.54.refs_0_), channel_id=1, source_target_pairs={{0,8},{4,12},{8,0},{12,4},{1,9},{5,13},{9,1},{13,5},{2,10},{6,14},... | collective-permute-start | bytes 1179656 | tf_op jit(solution)/shard_map/ppermute | solution.py:306
  63.1 1.2 collective-permute-start.4
  64.2 18.7 %collective-permute-done.4.refs_1_ = bf16[2,96,768]{2,1,0:T(8,128)(2,1)S(1)} collective-permute-done((bf16[2,96,768]{2,1,0:T(8,128)(2,1)}, bf16[2,96,768]{2,1,0:T(8,128)(2,1)S(1)}, u32[]{:S(2)}, u32[]{:S(2)}) %collective-permute-start.4) | collective-permute-done | bytes 294944 | tf_op jit(solution)/shard_map/ppermute | solution.py:310
  83.0 1.3 collective-permute-done.7.refs_3_
  84.3 1.2 shard_map.123.x_ref
  85.5 3.9 %collective-permute-start.8 = (bf16[512,1536]{1,0:T(8,128)(2,1)S(1)}, bf16[512,1536]{1,0:T(8,128)(2,1)S(1)}, u32[]{:S(2)}, u32[]{:S(2)}) collective-permute-start(bf16[512,1536]{1,0:T(8,128)(2,1)S(1)} %shard_map.123.x_ref), channel_id=1, source_target_pairs={{0,1},{1,0},{2,3},{3,2},{4,5},{5,4},{6,7},{7,6},{8,9},{9,8},{10,11... | collective-permute-start | bytes 4718600 | tf_op jit(solution)/shard_map/ppermute | solution.py:310
  89.7 1.1 collective-permute-start.9
  90.9 2.2 %shard_map.124.own_ref = bf16[512,768]{1,0:T(8,128)(2,1)S(1)} custom-call(s32[3]{0:T(128)S(1)} %pad_add_fusion.me_ref, bf16[512,1536]{1,0:T(8,128)(2,1)S(1)} %shard_map.123.x_ref, bf16[4,192,768]{2,1,0:T(8,128)(2,1)S(1)} %all-to-all-done.1.b_ref, bf16[4,192,768]{2,1,0:T(8,128)(2,1)S(1)} %collective-permute-done.5.bx_ref), custom_call_target="tpu_custom_call" | custom-call | tf_op jit(solution)/shard_map/pallas_call | solution.py:83
  93.1 2.2 %shard_map.125.oth_ref = bf16[512,768]{1,0:T(8,128)(2,1)S(1)} custom-call(s32[3]{0:T(128)S(1)} %pad_add_fusion.me_ref, bf16[512,1536]{1,0:T(8,128)(2,1)S(1)} %collective-permute-done.8.x_ref, bf16[4,192,768]{2,1,0:T(8,128)(2,1)S(1)} %all-to-all-done.1.b_ref, bf16[4,192,768]{2,1,0:T(8,128)(2,1)S(1)} %collective-permute-done.5.bx_ref), custom_call_target="tpu_custom_call" | custom-call | tf_op jit(solution)/shard_map/pallas_call | solution.py:83
  95.3 2.1 %shard_map.126 = (f32[512,768]{1,0:T(8,128)S(1)}, bf16[512,768]{1,0:T(8,128)(2,1)S(1)}) custom-call(s32[3]{0:T(128)S(1)} %pad_add_fusion.me_ref, bf16[512,768]{1,0:T(8,128)(2,1)S(1)} %shard_map.124.own_ref, bf16[512,768]{1,0:T(8,128)(2,1)S(1)} %shard_map.125.oth_ref, bf16[4,96,768]{2,1,0:T(8,128)(2,1)S(1)} %copy-done.5, bf16[4,96,768]{2,1,0:T(8,128)(2,1)S(1)} %copy-done.16), custom_call_target="tpu_custom_call" | custom-call | tf_op jit(solution)/shard_map/pallas_call | solution.py:83
  97.4 0.6 collective-permute-done.10.refs_3_
  98.0 6.3 %collective-permute-done.9.refs_2_ = bf16[2,96,768]{2,1,0:T(8,128)(2,1)S(1)} collective-permute-done((bf16[2,96,768]{2,1,0:T(8,128)(2,1)S(1)}, bf16[2,96,768]{2,1,0:T(8,128)(2,1)S(1)}, u32[]{:S(2)}, u32[]{:S(2)}) %collective-permute-start.9) | collective-permute-done | bytes 294944 | tf_op jit(solution)/shard_map/ppermute | solution.py:310
  104.3 2.1 %shard_map.128 = (f32[512,768]{1,0:T(8,128)S(1)}, bf16[512,768]{1,0:T(8,128)(2,1)S(1)}) custom-call(s32[3]{0:T(128)S(1)} %pad_add_fusion.me_ref, bf16[512,768]{1,0:T(8,128)(2,1)S(1)} %shard_map.124.own_ref, bf16[512,768]{1,0:T(8,128)(2,1)S(1)} %shard_map.125.oth_ref, bf16[2,96,768]{2,1,0:T(8,128)(2,1)S(1)} %copy-done.22, ...), custom_call_target="tpu_custom_call" | custom-call | tf_op jit(solution)/shard_map/pallas_call | solution.py:83
  106.3 0.9 collective-permute-start.15
  107.3 1.8 %collective-permute-done.15.came_ref = bf16[512,768]{1,0:T(8,128)(2,1)S(1)} collective-permute-done((bf16[512,768]{1,0:T(8,128)(2,1)S(1)}, bf16[512,768]{1,0:T(8,128)(2,1)S(1)}, u32[]{:S(2)}, u32[]{:S(2)}) %collective-permute-start.15) | collective-permute-done | bytes 786464 | tf_op jit(solution)/shard_map/ppermute | solution.py:310
  109.3 1.2 collective-permute-start.16
  110.6 1.2 collective-permute-start.17
  111.8 0.9 collective-permute-start.18
  112.8 0.6 collective-permute-start.12
  113.4 1.2 collective-permute-start.13
  114.7 0.8 collective-permute-done.16.refs_5_
  115.5 2.1 %collective-permute-start.14 = (bf16[128,768]{1,0:T(8,128)(2,1)S(1)}, bf16[128,768]{1,0:T(8,128)(2,1)S(1)}, u32[]{:S(2)}, u32[]{:S(2)}) collective-permute-start(bf16[128,768]{1,0:T(8,128)(2,1)S(1)} %get-tuple-element.73), channel_id=1, source_target_pairs={{0,12},{4,8},{8,4},{12,0},{1,13},{5,9},{9,5},{13,1},{2,14},{6,10},... | collective-permute-start | bytes 589832 | tf_op jit(solution)/shard_map/ppermute | solution.py:306
  117.6 4.0 %collective-permute-done.18.refs_7_ = bf16[128,768]{1,0:T(8,128)(2,1)S(1)} collective-permute-done((bf16[128,768]{1,0:T(8,128)(2,1)S(1)}, bf16[128,768]{1,0:T(8,128)(2,1)S(1)}, u32[]{:S(2)}, u32[]{:S(2)}) %collective-permute-start.18) | collective-permute-done | bytes 196640 | tf_op jit(solution)/shard_map/ppermute | solution.py:306
  121.6 2.3 %collective-permute-done.12.refs_1_ = bf16[128,768]{1,0:T(8,128)(2,1)S(1)} collective-permute-done((bf16[128,768]{1,0:T(8,128)(2,1)S(1)}, bf16[128,768]{1,0:T(8,128)(2,1)S(1)}, u32[]{:S(2)}, u32[]{:S(2)}) %collective-permute-start.12) | collective-permute-done | bytes 196640 | tf_op jit(solution)/shard_map/ppermute | solution.py:306
  124.0 0.9 collective-permute-done.13.refs_2_
  124.8 5.2 %collective-permute-done.14.refs_3_ = bf16[128,768]{1,0:T(8,128)(2,1)S(1)} collective-permute-done((bf16[128,768]{1,0:T(8,128)(2,1)S(1)}, bf16[128,768]{1,0:T(8,128)(2,1)S(1)}, u32[]{:S(2)}, u32[]{:S(2)}) %collective-permute-start.14) | collective-permute-done | bytes 196640 | tf_op jit(solution)/shard_map/ppermute | solution.py:306
  130.0 0.8 shard_map.130
  130.8 3.2 %all_gather.10.mid_ref = bf16[256,1536]{1,0:T(8,128)(2,1)S(1)} all-gather(bf16[128,1536]{1,0:T(8,128)(2,1)S(1)} %shard_map.130), channel_id=1, replica_groups=mesh['ah'=2,'bh'=2,'bl'=2,'al'=2,'hid'=2] {'hid'}, dimensions={0}, use_global_device_ids=true | all-gather | bytes 1179648 | tf_op jit(solution)/shard_map/all_gather | solution.py:392
  134.0 2.5 %shard_map.131 = (bf16[256,768]{1,0:T(8,128)(2,1)S(1)}, bf16[16,768]{1,0:T(8,128)(2,1)}, bf16[16,768]{1,0:T(8,128)(2,1)}) custom-call(bf16[256,1536]{1,0:T(8,128)(2,1)S(1)} %all_gather.10.mid_ref, f32[1,1536]{1,0:T(1,128)S(1)} %broadcast_in_dim.21.gain_ref, bf16[1536,768]{1,0:T(8,128)(2,1)S(1)} %copy-done.9, bf16[1536,768]{1,0:T(8,128)(2,1)S(1)} %copy-done.10), custom_call_target="tpu_custom_call" | custom-call | flops 1207959552 | bytes 4718592 | tf_op jit(solution)/shard_map/pallas_call | solution.py:83
  136.5 0.7 copy-done.11
  137.3 3.1 %collective-permute-start.19 = (bf16[16,768]{1,0:T(8,128)(2,1)}, bf16[16,768]{1,0:T(8,128)(2,1)S(1)}, u32[]{:S(2)}, u32[]{:S(2)}) collective-permute-start(bf16[16,768]{1,0:T(8,128)(2,1)} %get-tuple-element.87), channel_id=1, source_target_pairs={{0,2},{2,4},{4,6},{6,8},{8,10},{10,12},{12,14},{14,16},{16,18},{18... | collective-permute-start | bytes 73736 | tf_op jit(solution)/shard_map/ppermute | solution.py:281
  140.4 3.2 %collective-permute-start.20 = (bf16[16,768]{1,0:T(8,128)(2,1)}, bf16[16,768]{1,0:T(8,128)(2,1)}, u32[]{:S(2)}, u32[]{:S(2)}) collective-permute-start(bf16[16,768]{1,0:T(8,128)(2,1)} %get-tuple-element.88), channel_id=1, source_target_pairs={{2,0},{4,2},{6,4},{8,6},{10,8},{12,10},{14,12},{16,14},{18,16},{20... | collective-permute-start | bytes 73736 | tf_op jit(solution)/shard_map/ppermute | solution.py:282
  143.7 1.0 copy-done.12
  144.7 0.9 copy-done.17
  145.6 4.4 %shard_map.132.act_ref = bf16[256,768]{1,0:T(8,128)(2,1)S(1)} custom-call(bf16[256,768]{1,0:T(8,128)(2,1)S(1)} %copy-done.12, s32[8,280,128]{2,1,0:T(8,128)S(1)} %copy-done.2, f32[32,768]{1,0:T(8,128)S(1)} %copy-done.17, f32[1,768]{1,0:T(1,128)S(1)} %broadcast_in_dim.22.scale_ref, f32[1,768]{1,0:T(1,128)S(1)} %broadcast_in_dim.23.shift_ref), custom_call_target="tpu_custom_call" | custom-call | flops 6291456 | bytes 3145728 | tf_op jit(solution)/shard_map/pallas_call | solution.py:83
  150.0 1.6 %shard_map.133 = bf16[256,768]{1,0:T(8,128)(2,1)S(1)} custom-call(bf16[256,768]{1,0:T(8,128)(2,1)S(1)} %shard_map.132.act_ref, bf16[16,768]{1,0:T(8,128)(2,1)S(1)} %collective-permute-done.19.top_ref, bf16[256,768]{1,0:T(8,128)(2,1)S(1)} %copy-done.12, bf16[16,768]{1,0:T(8,128)(2,1)} %collective-permute-done.20.bottom_ref, s32[8,280,128]{2,1,0:T(8,128)S(1)} %copy-done.2, ...), custom_call_target="tpu_custom_call" | custom-call | flops 393216 | bytes 786432 | tf_op jit(solution)/shard_map/pallas_call | solution.py:83
  151.6 2.9 %all_gather.11 = bf16[256,1536]{1,0:T(8,128)(2,1)S(1)} all-gather(bf16[256,768]{1,0:T(8,128)(2,1)S(1)} %shard_map.133), channel_id=1, replica_groups=mesh['ah'=2,'bh'=2,'bl'=2,'al'=2,'hid'=2] {'hid'}, dimensions={1}, use_global_device_ids=true | all-gather | bytes 1179648 | tf_op jit(solution)/shard_map/all_gather | solution.py:300
  154.5 1.5 add_convert_fusion
  (59 shorter events, 1.3 us)
Async XLA Ops:
  0.0 154.5 %copy-start = (bf16[1536,768]{1,0:T(8,128)(2,1)S(1)}, bf16[1536,768]{1,0:T(8,128)(2,1)}, u32[]{:S(2)}) copy-start(bf16[1536,768]{1,0:T(8,128)(2,1)} %param.22) | copy-start | bytes 7077892
  0.0 1.2 copy-start.13
  1.2 4.6 %copy-start.14 = (bf16[96,3072]{1,0:T(8,128)(2,1)S(1)}, bf16[96,3072]{1,0:T(8,128)(2,1)}, u32[]{:S(2)}) copy-start(bf16[96,3072]{1,0:T(8,128)(2,1)} %refs_0_.1) | copy-start | bytes 1769476
  1.2 6.9 %copy-start.25 = (f32[1536]{0:T(1024)S(1)}, f32[1536]{0:T(1024)}, u32[]{:S(2)}) copy-start(f32[1536]{0:T(1024)} %param.13) | copy-start | bytes 18436
  2.1 31.1 %all-to-all-start = ((bf16[4,96,768]{2,1,0:T(8,128)(2,1)}), bf16[4,96,768]{2,1,0:T(8,128)(2,1)S(1)}, u32[]{:S(2)}, u32[]{:S(2)}) async-start(bf16[4,96,768]{2,1,0:T(8,128)(2,1)} %shard_map.119), calls=%async_computation | async-start | bytes 1179648 | tf_op jit(solution)/shard_map/all_to_all | solution.py:314
  5.8 27.3 %collective-permute-start = (bf16[96,3072]{1,0:T(8,128)(2,1)S(1)}, bf16[96,3072]{1,0:T(8,128)(2,1)}, u32[]{:S(2)}, u32[]{:S(2)}) collective-permute-start(bf16[96,3072]{1,0:T(8,128)(2,1)S(1)} %copy-done.14), channel_id=1, source_target_pairs={{0,16},{16,0},{1,17},{17,1},{2,18},{18,2},{3,19},{19,3},{4,20},{20... | collective-permute-start | bytes 1769480 | tf_op jit(solution)/shard_map/ppermute | solution.py:310
  12.9 0.8 copy-start.19
  13.7 12.9 %collective-permute-start.1 = (bf16[128,1536]{1,0:T(8,128)(2,1)}, bf16[128,1536]{1,0:T(8,128)(2,1)}, u32[]{:S(2)}, u32[]{:S(2)}) collective-permute-start(bf16[128,1536]{1,0:T(8,128)(2,1)} %get-tuple-element.54.refs_0_), channel_id=1, source_target_pairs={{0,4},{4,0},{8,12},{12,8},{1,5},{5,1},{9,13},{13,9},{2,6},{6,2},{1... | collective-permute-start | bytes 1179656 | tf_op jit(solution)/shard_map/ppermute | solution.py:306
  15.8 0.7 copy-start.23
  18.8 1.0 copy-start.1
  33.1 2.4 %copy-start.3 = (bf16[4,96,768]{2,1,0:T(8,128)(2,1)}, bf16[4,96,768]{2,1,0:T(8,128)(2,1)S(1)}, u32[]{:S(2)}) copy-start(bf16[4,96,768]{2,1,0:T(8,128)(2,1)S(1)} %all-to-all-done.both_ref.refs_0_) | copy-start | bytes 1769476
  34.5 1.1 copy-start.6
  35.6 23.1 %all-to-all-start.1 = ((bf16[4,192,768]{2,1,0:T(8,128)(2,1)}), bf16[4,192,768]{2,1,0:T(8,128)(2,1)S(1)}, u32[]{:S(2)}, u32[]{:S(2)}) async-start(bf16[4,192,768]{2,1,0:T(8,128)(2,1)} %copy-done.6), calls=%async_computation.1 | async-start | bytes 2359296 | tf_op jit(solution)/shard_map/all_to_all | solution.py:314
  39.4 18.1 %collective-permute-start.3 = (bf16[4,96,768]{2,1,0:T(8,128)(2,1)}, bf16[4,96,768]{2,1,0:T(8,128)(2,1)S(1)}, u32[]{:S(2)}, u32[]{:S(2)}) collective-permute-start(bf16[4,96,768]{2,1,0:T(8,128)(2,1)} %copy-done.3), channel_id=1, source_target_pairs={{0,2},{2,0},{1,3},{3,1},{4,6},{6,4},{5,7},{7,5},{8,10},{10,8},{9,1... | collective-permute-start | bytes 1769480 | tf_op jit(solution)/shard_map/ppermute | solution.py:310
  40.7 1.1 copy-start.4
  41.8 0.7 copy-start.24
  42.5 14.2 %collective-permute-start.2 = (bf16[2,96,768]{2,1,0:T(8,128)(2,1)S(1)}, bf16[2,96,768]{2,1,0:T(8,128)(2,1)S(1)}, u32[]{:S(2)}, u32[]{:S(2)}) collective-permute-start(bf16[2,96,768]{2,1,0:T(8,128)(2,1)S(1)} %get-tuple-element.51), channel_id=1, source_target_pairs={{0,16},{16,0},{1,17},{17,1},{2,18},{18,2},{3,19},{19,3},{4,20},{20... | collective-permute-start | bytes 884744 | tf_op jit(solution)/shard_map/ppermute | solution.py:310
  56.8 0.7 copy-start.21
  57.5 0.8 copy-start.15
  58.7 31.0 %copy-start.22 = (bf16[2,96,768]{2,1,0:T(8,128)(2,1)S(1)}, bf16[2,96,768]{2,1,0:T(8,128)(2,1)}, u32[]{:S(2)}) copy-start(bf16[2,96,768]{2,1,0:T(8,128)(2,1)} %copy-done.21) | copy-start | bytes 884740
  58.7 25.5 %collective-permute-start.5 = (bf16[4,192,768]{2,1,0:T(8,128)(2,1)S(1)}, bf16[4,192,768]{2,1,0:T(8,128)(2,1)S(1)}, u32[]{:S(2)}, u32[]{:S(2)}) collective-permute-start(bf16[4,192,768]{2,1,0:T(8,128)(2,1)S(1)} %all-to-all-done.1.b_ref), channel_id=1, source_target_pairs={{0,2},{2,0},{1,3},{3,1},{4,6},{6,4},{5,7},{7,5},{8,10},{10,8},{9,1... | collective-permute-start | bytes 3538952 | tf_op jit(solution)/shard_map/ppermute | solution.py:310
  60.0 22.9 %collective-permute-start.6 = (bf16[128,1536]{1,0:T(8,128)(2,1)}, bf16[128,1536]{1,0:T(8,128)(2,1)S(1)}, u32[]{:S(2)}, u32[]{:S(2)}) collective-permute-start(bf16[128,1536]{1,0:T(8,128)(2,1)} %get-tuple-element.54.refs_0_), channel_id=1, source_target_pairs={{0,8},{4,12},{8,0},{12,4},{1,9},{5,13},{9,1},{13,5},{2,10},{6,14},... | collective-permute-start | bytes 1179656 | tf_op jit(solution)/shard_map/ppermute | solution.py:306
  63.1 21.2 %collective-permute-start.7 = (bf16[128,1536]{1,0:T(8,128)(2,1)}, bf16[128,1536]{1,0:T(8,128)(2,1)S(1)}, u32[]{:S(2)}, u32[]{:S(2)}) collective-permute-start(bf16[128,1536]{1,0:T(8,128)(2,1)} %get-tuple-element.54.refs_0_), channel_id=1, source_target_pairs={{0,12},{4,8},{8,4},{12,0},{1,13},{5,9},{9,5},{13,1},{2,14},{6,10},... | collective-permute-start | bytes 1179656 | tf_op jit(solution)/shard_map/ppermute | solution.py:306
  63.1 19.9 %collective-permute-start.4 = (bf16[2,96,768]{2,1,0:T(8,128)(2,1)}, bf16[2,96,768]{2,1,0:T(8,128)(2,1)S(1)}, u32[]{:S(2)}, u32[]{:S(2)}) collective-permute-start(bf16[2,96,768]{2,1,0:T(8,128)(2,1)} %copy-done.24), channel_id=1, source_target_pairs={{0,16},{16,0},{1,17},{17,1},{2,18},{18,2},{3,19},{19,3},{4,20},{20... | collective-permute-start | bytes 884744 | tf_op jit(solution)/shard_map/ppermute | solution.py:310
  85.5 7.7 %collective-permute-start.8 = (bf16[512,1536]{1,0:T(8,128)(2,1)S(1)}, bf16[512,1536]{1,0:T(8,128)(2,1)S(1)}, u32[]{:S(2)}, u32[]{:S(2)}) collective-permute-start(bf16[512,1536]{1,0:T(8,128)(2,1)S(1)} %shard_map.123.x_ref), channel_id=1, source_target_pairs={{0,1},{1,0},{2,3},{3,2},{4,5},{5,4},{6,7},{7,6},{8,9},{9,8},{10,11... | collective-permute-start | bytes 4718600 | tf_op jit(solution)/shard_map/ppermute | solution.py:310
  89.4 8.6 %collective-permute-start.10 = (bf16[2,96,768]{2,1,0:T(8,128)(2,1)S(1)}, bf16[2,96,768]{2,1,0:T(8,128)(2,1)S(1)}, u32[]{:S(2)}, u32[]{:S(2)}) collective-permute-start(bf16[2,96,768]{2,1,0:T(8,128)(2,1)S(1)} %collective-permute-done.4.refs_1_), channel_id=1, source_target_pairs={{0,2},{2,0},{1,3},{3,1},{4,6},{6,4},{5,7},{7,5},{8,10},{10,8},{9,1... | collective-permute-start | bytes 884744 | tf_op jit(solution)/shard_map/ppermute | solution.py:310
  89.7 14.6 %collective-permute-start.9 = (bf16[2,96,768]{2,1,0:T(8,128)(2,1)S(1)}, bf16[2,96,768]{2,1,0:T(8,128)(2,1)S(1)}, u32[]{:S(2)}, u32[]{:S(2)}) collective-permute-start(bf16[2,96,768]{2,1,0:T(8,128)(2,1)S(1)} %copy-done.22), channel_id=1, source_target_pairs={{0,2},{2,0},{1,3},{3,1},{4,6},{6,4},{5,7},{7,5},{8,10},{10,8},{9,1... | collective-permute-start | bytes 884744 | tf_op jit(solution)/shard_map/ppermute | solution.py:310
  93.1 2.2 %copy-start.5 = (bf16[4,96,768]{2,1,0:T(8,128)(2,1)S(1)}, bf16[4,96,768]{2,1,0:T(8,128)(2,1)}, u32[]{:S(2)}) copy-start(bf16[4,96,768]{2,1,0:T(8,128)(2,1)} %copy-done.3) | copy-start | bytes 1769476
  93.1 2.2 %copy-start.16 = (bf16[4,96,768]{2,1,0:T(8,128)(2,1)S(1)}, bf16[4,96,768]{2,1,0:T(8,128)(2,1)}, u32[]{:S(2)}) copy-start(bf16[4,96,768]{2,1,0:T(8,128)(2,1)} %copy-done.15) | copy-start | bytes 1769476
  106.3 2.8 %collective-permute-start.15 = (bf16[512,768]{1,0:T(8,128)(2,1)S(1)}, bf16[512,768]{1,0:T(8,128)(2,1)S(1)}, u32[]{:S(2)}, u32[]{:S(2)}) collective-permute-start(bf16[512,768]{1,0:T(8,128)(2,1)S(1)} %get-tuple-element.77), channel_id=1, source_target_pairs={{0,1},{1,0},{2,3},{3,2},{4,5},{5,4},{6,7},{7,6},{8,9},{9,8},{10,11... | collective-permute-start | bytes 2359304 | tf_op jit(solution)/shard_map/ppermute | solution.py:310
  107.3 5.5 %collective-permute-start.11 = (bf16[512,768]{1,0:T(8,128)(2,1)S(1)}, bf16[512,768]{1,0:T(8,128)(2,1)S(1)}, u32[]{:S(2)}, u32[]{:S(2)}) collective-permute-start(bf16[512,768]{1,0:T(8,128)(2,1)S(1)} %get-tuple-element.69), channel_id=1, source_target_pairs={{0,1},{1,0},{2,3},{3,2},{4,5},{5,4},{6,7},{7,6},{8,9},{9,8},{10,11... | collective-permute-start | bytes 2359304 | tf_op jit(solution)/shard_map/ppermute | solution.py:310
  109.3 20.7 %copy-start.20 = (bf16[128,1536]{1,0:T(8,128)(2,1)S(1)}, bf16[128,1536]{1,0:T(8,128)(2,1)}, u32[]{:S(2)}) copy-start(bf16[128,1536]{1,0:T(8,128)(2,1)} %copy-done.19) | copy-start | bytes 1179652
  109.3 6.2 %collective-permute-start.16 = (bf16[128,768]{1,0:T(8,128)(2,1)S(1)}, bf16[128,768]{1,0:T(8,128)(2,1)S(1)}, u32[]{:S(2)}, u32[]{:S(2)}) collective-permute-start(bf16[128,768]{1,0:T(8,128)(2,1)S(1)} %get-tuple-element.79), channel_id=1, source_target_pairs={{0,4},{4,0},{8,12},{12,8},{1,5},{5,1},{9,13},{13,9},{2,6},{6,2},{1... | collective-permute-start | bytes 589832 | tf_op jit(solution)/shard_map/ppermute | solution.py:306
  110.6 7.1 %collective-permute-start.17 = (bf16[128,768]{1,0:T(8,128)(2,1)S(1)}, bf16[128,768]{1,0:T(8,128)(2,1)S(1)}, u32[]{:S(2)}, u32[]{:S(2)}) collective-permute-start(bf16[128,768]{1,0:T(8,128)(2,1)S(1)} %get-tuple-element.80), channel_id=1, source_target_pairs={{0,8},{4,12},{8,0},{12,4},{1,9},{5,13},{9,1},{13,5},{2,10},{6,14},... | collective-permute-start | bytes 589832 | tf_op jit(solution)/shard_map/ppermute | solution.py:306
  111.8 9.8 %collective-permute-start.18 = (bf16[128,768]{1,0:T(8,128)(2,1)S(1)}, bf16[128,768]{1,0:T(8,128)(2,1)S(1)}, u32[]{:S(2)}, u32[]{:S(2)}) collective-permute-start(bf16[128,768]{1,0:T(8,128)(2,1)S(1)} %get-tuple-element.81), channel_id=1, source_target_pairs={{0,12},{4,8},{8,4},{12,0},{1,13},{5,9},{9,5},{13,1},{2,14},{6,10},... | collective-permute-start | bytes 589832 | tf_op jit(solution)/shard_map/ppermute | solution.py:306
  112.7 21.3 %copy-start.10 = (bf16[1536,768]{1,0:T(8,128)(2,1)S(1)}, bf16[1536,768]{1,0:T(8,128)(2,1)}, u32[]{:S(2)}) copy-start(bf16[1536,768]{1,0:T(8,128)(2,1)} %gate_ref.1) | copy-start | bytes 7077892
  112.8 11.1 %collective-permute-start.12 = (bf16[128,768]{1,0:T(8,128)(2,1)S(1)}, bf16[128,768]{1,0:T(8,128)(2,1)S(1)}, u32[]{:S(2)}, u32[]{:S(2)}) collective-permute-start(bf16[128,768]{1,0:T(8,128)(2,1)S(1)} %get-tuple-element.71), channel_id=1, source_target_pairs={{0,4},{4,0},{8,12},{12,8},{1,5},{5,1},{9,13},{13,9},{2,6},{6,2},{1... | collective-permute-start | bytes 589832 | tf_op jit(solution)/shard_map/ppermute | solution.py:306
  113.4 11.4 %collective-permute-start.13 = (bf16[128,768]{1,0:T(8,128)(2,1)S(1)}, bf16[128,768]{1,0:T(8,128)(2,1)S(1)}, u32[]{:S(2)}, u32[]{:S(2)}) collective-permute-start(bf16[128,768]{1,0:T(8,128)(2,1)S(1)} %get-tuple-element.72), channel_id=1, source_target_pairs={{0,8},{4,12},{8,0},{12,4},{1,9},{5,13},{9,1},{13,5},{2,10},{6,14},... | collective-permute-start | bytes 589832 | tf_op jit(solution)/shard_map/ppermute | solution.py:306
  115.5 14.5 %collective-permute-start.14 = (bf16[128,768]{1,0:T(8,128)(2,1)S(1)}, bf16[128,768]{1,0:T(8,128)(2,1)S(1)}, u32[]{:S(2)}, u32[]{:S(2)}) collective-permute-start(bf16[128,768]{1,0:T(8,128)(2,1)S(1)} %get-tuple-element.73), channel_id=1, source_target_pairs={{0,12},{4,8},{8,4},{12,0},{1,13},{5,9},{9,5},{13,1},{2,14},{6,10},... | collective-permute-start | bytes 589832 | tf_op jit(solution)/shard_map/ppermute | solution.py:306
  130.0 4.0 %copy-start.9 = (bf16[1536,768]{1,0:T(8,128)(2,1)S(1)}, bf16[1536,768]{1,0:T(8,128)(2,1)}, u32[]{:S(2)}) copy-start(bf16[1536,768]{1,0:T(8,128)(2,1)} %value_ref.1) | copy-start | bytes 7077892
  134.0 2.5 %copy-start.7 = (bf16[256,1536]{1,0:T(8,128)(2,1)}, bf16[256,1536]{1,0:T(8,128)(2,1)S(1)}, u32[]{:S(2)}) copy-start(bf16[256,1536]{1,0:T(8,128)(2,1)S(1)} %all_gather.10.mid_ref) | copy-start | bytes 2359300
  134.0 9.6 %copy-start.2 = (s32[8,280,128]{2,1,0:T(8,128)S(1)}, s32[8,280,128]{2,1,0:T(8,128)}, u32[]{:S(2)}) copy-start(s32[8,280,128]{2,1,0:T(8,128)} %copy-done.1) | copy-start | bytes 3440644
  136.5 0.7 copy-start.11
  137.3 12.7 %collective-permute-start.19 = (bf16[16,768]{1,0:T(8,128)(2,1)}, bf16[16,768]{1,0:T(8,128)(2,1)S(1)}, u32[]{:S(2)}, u32[]{:S(2)}) collective-permute-start(bf16[16,768]{1,0:T(8,128)(2,1)} %get-tuple-element.87), channel_id=1, source_target_pairs={{0,2},{2,4},{4,6},{6,8},{8,10},{10,12},{12,14},{14,16},{16,18},{18... | collective-permute-start | bytes 73736 | tf_op jit(solution)/shard_map/ppermute | solution.py:281
  140.4 9.6 %collective-permute-start.20 = (bf16[16,768]{1,0:T(8,128)(2,1)}, bf16[16,768]{1,0:T(8,128)(2,1)}, u32[]{:S(2)}, u32[]{:S(2)}) collective-permute-start(bf16[16,768]{1,0:T(8,128)(2,1)} %get-tuple-element.88), channel_id=1, source_target_pairs={{2,0},{4,2},{6,4},{8,6},{10,8},{12,10},{14,12},{16,14},{18,16},{20... | collective-permute-start | bytes 73736 | tf_op jit(solution)/shard_map/ppermute | solution.py:282
  143.7 1.0 copy-start.12
  144.7 0.9 copy-start.17
  145.6 4.4 %copy-start.18 = (f32[32,768]{1,0:T(8,128)S(1)}, f32[32,768]{1,0:T(8,128)}, u32[]{:S(2)}) copy-start(f32[32,768]{1,0:T(8,128)} %taps_ref.3) | copy-start | bytes 294916
  149.9 4.6 %copy-start.8 = (bf16[256,1536]{1,0:T(8,128)(2,1)S(1)}, bf16[256,1536]{1,0:T(8,128)(2,1)}, u32[]{:S(2)}) copy-start(bf16[256,1536]{1,0:T(8,128)(2,1)} %copy-done.7) | copy-start | bytes 2359300

commit v4 on v3

--- a/solution.py
+++ b/solution.py
@@ -111,9 +111,10 @@
 
 
 def part_kernel(both_ref, first_ref, second_ref):
-    half = first_ref.shape[0]
-    first_ref[...] = both_ref[:half]
-    second_ref[...] = both_ref[half:]
+    half, shard, _ = first_ref.shape
+    skip = both_ref.shape[1] - shard
+    first_ref[...] = both_ref[:half, skip:, :]
+    second_ref[...] = both_ref[half:, skip:, :]
 
 
 def norm_kernel(start_ref, whole_ref, gain_ref, mine_ref, out_ref):
@@ -130,19 +131,20 @@
         out_ref[i * rows : (i + 1) * rows] = piece[...]
 
 
-def interleave(full_ref, base, block, own_refs, other_refs, me_l, skip=0):
+def interleave(full_ref, base, block, own_refs, other_refs, me_l, last=False):
     for refs, turn in ((own_refs, me_l), (other_refs, 1 - me_l)):
         blocks = [(ref, j) for ref in refs for j in range(ref.shape[0])]
         for i, (ref, j) in enumerate(blocks):
             at = pl.multiple_of(base + (2 * i + turn) * block, block)
+            skip = ref.shape[1] - block if last else 0
             full_ref[pl.ds(at, block), :] = ref[j, skip : skip + block, :]
 
 
-def hidden_kernel(me_ref, x_ref, b_ref, bx_ref, h_ref, w_ref):
+def hidden_kernel(me_ref, x_ref, both_ref, both_x_ref, z_ref, zx_ref, h_ref, w_ref):
     me_l, me_a = me_ref[0], me_ref[2]
-    part, block = w_ref.shape[0] // 2, b_ref.shape[1] // 2
-    interleave(w_ref, me_a * part, block, [b_ref], [bx_ref], me_l)
-    interleave(w_ref, (1 - me_a) * part, block, [b_ref], [bx_ref], me_l, block)
+    part, block = w_ref.shape[0] // 2, z_ref.shape[1]
+    interleave(w_ref, me_a * part, block, [both_ref], [both_x_ref], me_l)
+    interleave(w_ref, (1 - me_a) * part, block, [z_ref], [zx_ref], me_l)
     step = 256
     for at in range(0, x_ref.shape[0], step):
         pre = jnp.dot(x_ref[at : at + step, :], w_ref[...], preferred_element_type=jnp.float32)
@@ -151,7 +153,8 @@
 
 def sums_kernel(n_own, me_ref, own_ref, oth_ref, *refs):
     *blocks, kept_ref, sent_ref, w_ref = refs
-    interleave(w_ref, 0, blocks[0].shape[1], blocks[:n_own], blocks[n_own:], me_ref[0])
+    block = w_ref.shape[0] // 8
+    interleave(w_ref, 0, block, blocks[:n_own], blocks[n_own:], me_ref[0], True)
     step = 256
     for h_ref, out_ref in ((oth_ref, sent_ref), (own_ref, kept_ref)):
         for at in range(0, h_ref.shape[0], step):
@@ -327,8 +330,8 @@
 
     block, pair = (4, shard, units), (2, shard, units)
     in_far = swap(w_in, "ah")
-    (out_cut,) = kernel_call(cut_kernel, [(block, bf16)], [w_out.T])
-    out_o = recut(out_cut)
+    (both,) = kernel_call(cut_kernel, [((4, 2 * shard, units), bf16)], [w_in, w_out.T])
+    both = recut(both)
     whole = lax.all_gather(tokens, "hid", axis=1, tiled=True)
     mine, normed = kernel_call(
         norm_kernel,
@@ -337,18 +340,19 @@
         scalars=1,
     )
     frames1 = partner(normed, 1)
-    in_far, out_o, normed, frames1, early = tie((in_far, out_o, normed, frames1, early))
-    (in_both,) = kernel_call(cut_kernel, [((4, 2 * shard, units), bf16)], [w_in, in_far])
-    in_b = recut(in_both)
-    out_1, out_2 = kernel_call(part_kernel, [(pair, bf16)] * 2, [out_o])
+    in_far, both, normed, frames1, early = tie((in_far, both, normed, frames1, early))
+    both_x = swap(both, "al")
+    (in_z,) = kernel_call(cut_kernel, [(block, bf16)], [in_far])
+    in_z = recut(in_z)
+    out_1, out_2 = kernel_call(part_kernel, [(pair, bf16)] * 2, [both])
     out_z1 = swap(out_1, "ah")
-    out_x = swap(out_o, "al")
-    in_b, out_z1, out_2, out_o, out_x, normed = tie((in_b, out_z1, out_2, out_o, out_x, normed))
-    in_bx = swap(in_b, "al")
+    frames3 = partner(normed, 3)
+    both_x, in_z = tie((both_x, in_z))
+    out_z1, out_2, normed, frames3 = tie((out_z1, out_2, normed, frames3))
+    in_zx = swap(in_z, "al")
     out_z2 = swap(out_2, "ah")
     frames2 = partner(normed, 2)
-    frames3 = partner(normed, 3)
-    out_z1, out_z2, in_bx, frames2, frames3 = tie((out_z1, out_z2, in_bx, frames2, frames3))
+    in_zx, out_z1, out_z2, frames2 = tie((in_zx, out_z1, out_z2, frames2))
     out_zx1 = swap(out_z1, "al")
     out_zx2 = swap(out_z2, "al")
     (x_own,) = kernel_call(
@@ -360,7 +364,7 @@
         return kernel_call(
             hidden_kernel,
             [((4 * half, units), bf16)],
-            [me, x, in_b, in_bx],
+            [me, x, both, both_x, in_z, in_zx],
             scratch=[pltpu.VMEM((wide, units), bf16)],
             scalars=1,
         )[0]
@@ -384,7 +388,7 @@
         )
         return [total[0]] + [partner(v, k + 1) for k, v in enumerate(total[1:])]
 
-    near, out_zx1, out_zx2 = tie((products([out_o], [out_x]), out_zx1, out_zx2))
+    near, out_zx1, out_zx2 = tie((products([both], [both_x]), out_zx1, out_zx2))
     far = products([out_z1, out_z2], [out_zx1, out_zx2])
     (mid_rows,) = kernel_call(
         mid_kernel, [((half, wide), bf16)], [me, mine, *scatter(*near), *scatter(*far)], scalars=1

time: 158 us -> 153 us (0.968)
  waiting for transfers between devices: 67.8 us -> 62.9 us
  Pallas kernels: 24.9 us -> 27.7 us
  starting transfers between devices: 38.8 us -> 37.1 us
    ppermute x10, waiting for transfers between devices: 46.2 us -> 28.8 us  [swap(): return lax.ppermute(values, axis, SWAP)]
    ppermute x9, waiting for transfers between devices: 21.2 us -> 30.3 us  [partner(): return lax.ppermute(values, GROUP, [(i, i ^ step) for i in range(4)])]
    ppermute x9, starting transfers between devices: 10.4 us -> 6.71 us  [partner(): return lax.ppermute(values, GROUP, [(i, i ^ step) for i in range(4)])]
    all_to_all x2, waiting for transfers between devices: 0.38 us -> 3.88 us  [recut(): return lax.all_to_all(parts, GROUP, 0, 0)]
    pallas_call x16, Pallas kernels: 24.9 us -> 27.7 us  [kernel_call(): pl.pallas_call(body, out_shape=[jax.ShapeDtypeStruct(shape, dtype) for sh...]
    unnamed x52 -> x42, local copies, waits for them, and re-layouts: 10.8 us -> 9.94 us
  transfers between devices with their start and end apart: 23 -> 23, of which waited for: 14 -> 14; matrix products, arithmetic and copies ran while one was open for 1% -> 1% of each run, Pallas kernels for 9% -> 12%
where the time goes in v4:
time: 153 us; the launch traced here: 152 us
  waiting for transfers between devices  62.9 us (41%)
  starting transfers between devices  37.1 us (24%)
  Pallas kernels  27.7 us (18%)
  local copies, waits for them, and re-layouts  12 us (8%)
  blocking collectives  10.2 us (7%)
  matrix products  1.53 us (1%)
    ppermute x9, waiting for transfers between devices, partner(): return lax.ppermute(values, GROUP, [(i, i ^ step) for i in range(4)])  30.3 us
    ppermute x10, waiting for transfers between devices, swap(): return lax.ppermute(values, axis, SWAP)  28.8 us
    pallas_call x16, Pallas kernels, kernel_call(): pl.pallas_call(body, out_shape=[jax.ShapeDtypeStruct(shape, dtype) for sh...  27.7 us
    ppermute x10, starting transfers between devices, swap(): return lax.ppermute(values, axis, SWAP)  15.5 us
    unnamed x42, local copies, waits for them, and re-layouts  9.94 us
    all_to_all x2, starting transfers between devices, recut(): return lax.all_to_all(parts, GROUP, 0, 0)  8.56 us
    ppermute x9, starting transfers between devices, partner(): return lax.ppermute(values, GROUP, [(i, i ^ step) for i in range(4)])  6.71 us
    ppermute x1, starting transfers between devices, grouped_conv_module(): bottom = lax.ppermute(head, axis, [(i + 1, i) for i in range(count - 1)])  4.2 us
  transfers between devices with their start and end apart: 23, of which 14 were waited for; matrix products, arithmetic and copies ran while one was open for 1% of the time, Pallas kernels for 12%

profile of v4, /device:TPU:5, one launch (start us, length us, event | category | flops | bytes accessed | tf_op | source)
XLA Modules:
  0.0 151.8 jit_solution(9957209842166548701)
XLA Ops:
  0.0 1.2 copy-done.12
  1.2 1.1 copy-done.13
  2.4 1.0 copy-done.3
  3.4 3.9 %all-to-all-start = ((bf16[4,192,768]{2,1,0:T(8,128)(2,1)}), bf16[4,192,768]{2,1,0:T(8,128)(2,1)S(1)}, u32[]{:S(2)}, u32[]{:S(2)}) async-start(bf16[4,192,768]{2,1,0:T(8,128)(2,1)} %copy-done.3), calls=%async_computation | async-start | bytes 2359296 | tf_op jit(solution)/shard_map/all_to_all | solution.py:317
  7.3 2.3 %collective-permute-start = (bf16[96,3072]{1,0:T(8,128)(2,1)}, bf16[96,3072]{1,0:T(8,128)(2,1)}, u32[]{:S(2)}, u32[]{:S(2)}) collective-permute-start(bf16[96,3072]{1,0:T(8,128)(2,1)} %refs_0_.1), channel_id=1, source_target_pairs={{0,16},{16,0},{1,17},{17,1},{2,18},{18,2},{3,19},{19,3},{4,20},{20... | collective-permute-start | bytes 1769480 | tf_op jit(solution)/shard_map/ppermute | solution.py:313
  9.6 3.7 %all_gather.9.whole_ref = bf16[256,1536]{1,0:T(8,128)(2,1)S(1)} all-gather(bf16[256,768]{1,0:T(8,128)(2,1)} %param.12), channel_id=1, replica_groups=mesh['ah'=2,'bh'=2,'bl'=2,'al'=2,'hid'=2] {'hid'}, dimensions={1}, use_global_device_ids=true | all-gather | bytes 1179648 | tf_op jit(solution)/shard_map/all_gather | solution.py:335
  13.3 1.1 shard_map.118
  14.4 0.7 copy-done.16
  15.2 0.7 broadcast_in_dim.21.gain_ref
  15.9 0.7 broadcast_in_dim.22.scale_ref
  16.6 0.7 broadcast_in_dim.23.shift_ref
  17.2 0.7 copy-done.18
  17.9 2.4 %shard_map.120.utter_ref = s32[8,280,128]{2,1,0:T(8,128)S(1)} custom-call(s32[1]{0:T(128)} %bitcast.5.first_ref, s32[64]{0:T(128)S(1)} %copy-done.18), custom_call_target="tpu_custom_call" | custom-call | tf_op jit(solution)/shard_map/pallas_call | solution.py:83
  20.3 1.0 copy-done.1
  21.3 9.8 %collective-permute-done.1.refs_1_ = bf16[128,1536]{1,0:T(8,128)(2,1)} collective-permute-done((bf16[128,1536]{1,0:T(8,128)(2,1)}, bf16[128,1536]{1,0:T(8,128)(2,1)}, u32[]{:S(2)}, u32[]{:S(2)}) %collective-permute-start.1) | collective-permute-done | bytes 393248 | tf_op jit(solution)/shard_map/ppermute | solution.py:309
  31.1 0.9 collective-permute-done.refs_0_
  32.0 2.0 %all-to-all-done.both_ref.refs_0_ = bf16[4,192,768]{2,1,0:T(8,128)(2,1)S(1)} async-done(((bf16[4,192,768]{2,1,0:T(8,128)(2,1)}), bf16[4,192,768]{2,1,0:T(8,128)(2,1)S(1)}, u32[]{:S(2)}, u32[]{:S(2)}) %all-to-all-start) | async-done | bytes 1179680 | tf_op jit(solution)/shard_map/all_to_all | solution.py:317
  34.0 1.2 collective-permute-start.4
  35.2 1.1 shard_map.122
  36.3 0.8 copy-done.8
  37.1 4.7 %all-to-all-start.1 = ((bf16[4,96,768]{2,1,0:T(8,128)(2,1)}), bf16[4,96,768]{2,1,0:T(8,128)(2,1)}, u32[]{:S(2)}, u32[]{:S(2)}) async-start(bf16[4,96,768]{2,1,0:T(8,128)(2,1)} %copy-done.8), calls=%async_computation.1 | async-start | bytes 1179648 | tf_op jit(solution)/shard_map/all_to_all | solution.py:317
  41.8 1.8 %collective-permute-start.3 = (bf16[128,1536]{1,0:T(8,128)(2,1)}, bf16[128,1536]{1,0:T(8,128)(2,1)}, u32[]{:S(2)}, u32[]{:S(2)}) collective-permute-start(bf16[128,1536]{1,0:T(8,128)(2,1)} %get-tuple-element.52.refs_0_), channel_id=1, source_target_pairs={{0,12},{4,8},{8,4},{12,0},{1,13},{5,9},{9,5},{13,1},{2,14},{6,10},... | collective-permute-start | bytes 1179656 | tf_op jit(solution)/shard_map/ppermute | solution.py:309
  43.6 0.8 shard_map.121
  44.3 0.7 copy-done.19
  45.1 2.1 %collective-permute-start.2 = (bf16[2,96,768]{2,1,0:T(8,128)(2,1)}, bf16[2,96,768]{2,1,0:T(8,128)(2,1)}, u32[]{:S(2)}, u32[]{:S(2)}) collective-permute-start(bf16[2,96,768]{2,1,0:T(8,128)(2,1)} %get-tuple-element.49), channel_id=1, source_target_pairs={{0,16},{16,0},{1,17},{17,1},{2,18},{18,2},{3,19},{19,3},{4,20},{20... | collective-permute-start | bytes 884744 | tf_op jit(solution)/shard_map/ppermute | solution.py:313
  47.1 1.9 %all-to-all-done.1.z_ref = bf16[4,96,768]{2,1,0:T(8,128)(2,1)} async-done(((bf16[4,96,768]{2,1,0:T(8,128)(2,1)}), bf16[4,96,768]{2,1,0:T(8,128)(2,1)}, u32[]{:S(2)}, u32[]{:S(2)}) %all-to-all-start.1) | async-done | bytes 589856 | tf_op jit(solution)/shard_map/all_to_all | solution.py:317
  49.0 10.9 %collective-permute-done.4.both_x_ref.refs_1_ = bf16[4,192,768]{2,1,0:T(8,128)(2,1)} collective-permute-done((bf16[4,192,768]{2,1,0:T(8,128)(2,1)S(1)}, bf16[4,192,768]{2,1,0:T(8,128)(2,1)}, u32[]{:S(2)}, u32[]{:S(2)}) %collective-permute-start.4) | collective-permute-done | bytes 1179680 | tf_op jit(solution)/shard_map/ppermute | solution.py:313
  59.9 1.2 collective-permute-start.5
  61.1 2.6 %collective-permute-done.3.refs_3_ = bf16[128,1536]{1,0:T(8,128)(2,1)} collective-permute-done((bf16[128,1536]{1,0:T(8,128)(2,1)}, bf16[128,1536]{1,0:T(8,128)(2,1)}, u32[]{:S(2)}, u32[]{:S(2)}) %collective-permute-start.3) | collective-permute-done | bytes 393248 | tf_op jit(solution)/shard_map/ppermute | solution.py:309
  63.7 1.9 %collective-permute-start.7 = (bf16[128,1536]{1,0:T(8,128)(2,1)}, bf16[128,1536]{1,0:T(8,128)(2,1)S(1)}, u32[]{:S(2)}, u32[]{:S(2)}) collective-permute-start(bf16[128,1536]{1,0:T(8,128)(2,1)} %get-tuple-element.52.refs_0_), channel_id=1, source_target_pairs={{0,8},{4,12},{8,0},{12,4},{1,9},{5,13},{9,1},{13,5},{2,10},{6,14},... | collective-permute-start | bytes 1179656 | tf_op jit(solution)/shard_map/ppermute | solution.py:309
  65.6 10.7 %collective-permute-done.6.refs_1_ = bf16[2,96,768]{2,1,0:T(8,128)(2,1)S(1)} collective-permute-done((bf16[2,96,768]{2,1,0:T(8,128)(2,1)}, bf16[2,96,768]{2,1,0:T(8,128)(2,1)S(1)}, u32[]{:S(2)}, u32[]{:S(2)}) %collective-permute-start.6) | collective-permute-done | bytes 294944 | tf_op jit(solution)/shard_map/ppermute | solution.py:313
  76.3 1.4 collective-permute-done.7.refs_2_
  77.7 1.3 shard_map.123.x_ref
  79.1 6.2 %collective-permute-start.8 = (bf16[512,1536]{1,0:T(8,128)(2,1)S(1)}, bf16[512,1536]{1,0:T(8,128)(2,1)S(1)}, u32[]{:S(2)}, u32[]{:S(2)}) collective-permute-start(bf16[512,1536]{1,0:T(8,128)(2,1)S(1)} %shard_map.123.x_ref), channel_id=1, source_target_pairs={{0,1},{1,0},{2,3},{3,2},{4,5},{5,4},{6,7},{7,6},{8,9},{9,8},{10,11... | collective-permute-start | bytes 4718600 | tf_op jit(solution)/shard_map/ppermute | solution.py:313
  85.3 0.3 collective-permute-start.10
  85.6 1.2 collective-permute-start.9
  86.9 3.1 %shard_map.124.own_ref = bf16[512,768]{1,0:T(8,128)(2,1)S(1)} custom-call(s32[3]{0:T(128)S(1)} %pad_add_fusion.me_ref, bf16[512,1536]{1,0:T(8,128)(2,1)S(1)} %shard_map.123.x_ref, bf16[4,192,768]{2,1,0:T(8,128)(2,1)S(1)} %all-to-all-done.both_ref.refs_0_, bf16[4,192,768]{2,1,0:T(8,128)(2,1)} %collective-permute-done.4.both_x_ref.refs_1_, ...), custom_call_target="tpu_custom_call" | custom-call | tf_op jit(solution)/shard_map/pallas_call | solution.py:83
  90.0 3.1 %shard_map.125.oth_ref = bf16[512,768]{1,0:T(8,128)(2,1)S(1)} custom-call(s32[3]{0:T(128)S(1)} %pad_add_fusion.me_ref, bf16[512,1536]{1,0:T(8,128)(2,1)S(1)} %collective-permute-done.8.x_ref, bf16[4,192,768]{2,1,0:T(8,128)(2,1)S(1)} %all-to-all-done.both_ref.refs_0_, bf16[4,192,768]{2,1,0:T(8,128)(2,1)} %collective-permute-done.4.both_x_ref.refs_1_, ...), custom_call_target="tpu_custom_call" | custom-call | tf_op jit(solution)/shard_map/pallas_call | solution.py:83
  93.0 2.8 %shard_map.126 = (f32[512,768]{1,0:T(8,128)S(1)}, bf16[512,768]{1,0:T(8,128)(2,1)S(1)}) custom-call(s32[3]{0:T(128)S(1)} %pad_add_fusion.me_ref, bf16[512,768]{1,0:T(8,128)(2,1)S(1)} %shard_map.124.own_ref, bf16[512,768]{1,0:T(8,128)(2,1)S(1)} %shard_map.125.oth_ref, bf16[4,192,768]{2,1,0:T(8,128)(2,1)S(1)} %all-to-all-done.both_ref.refs_0_, ...), custom_call_target="tpu_custom_call" | custom-call | tf_op jit(solution)/shard_map/pallas_call | solution.py:83
  95.8 4.4 %collective-permute-done.9.refs_2_ = bf16[2,96,768]{2,1,0:T(8,128)(2,1)S(1)} collective-permute-done((bf16[2,96,768]{2,1,0:T(8,128)(2,1)}, bf16[2,96,768]{2,1,0:T(8,128)(2,1)S(1)}, u32[]{:S(2)}, u32[]{:S(2)}) %collective-permute-start.9) | collective-permute-done | bytes 294944 | tf_op jit(solution)/shard_map/ppermute | solution.py:313
  100.2 2.5 %shard_map.128 = (f32[512,768]{1,0:T(8,128)S(1)}, bf16[512,768]{1,0:T(8,128)(2,1)S(1)}) custom-call(s32[3]{0:T(128)S(1)} %pad_add_fusion.me_ref, bf16[512,768]{1,0:T(8,128)(2,1)S(1)} %shard_map.124.own_ref, bf16[512,768]{1,0:T(8,128)(2,1)S(1)} %shard_map.125.oth_ref, bf16[2,96,768]{2,1,0:T(8,128)(2,1)} %collective-permute-done.2.refs_0_, ...), custom_call_target="tpu_custom_call" | custom-call | tf_op jit(solution)/shard_map/pallas_call | solution.py:83
  102.7 0.9 collective-permute-start.15
  103.7 1.8 %collective-permute-done.15.came_ref = bf16[512,768]{1,0:T(8,128)(2,1)S(1)} collective-permute-done((bf16[512,768]{1,0:T(8,128)(2,1)S(1)}, bf16[512,768]{1,0:T(8,128)(2,1)S(1)}, u32[]{:S(2)}, u32[]{:S(2)}) %collective-permute-start.15) | collective-permute-done | bytes 786464 | tf_op jit(solution)/shard_map/ppermute | solution.py:313
  105.6 0.1 shard_map.129
  105.9 2.6 %collective-permute-start.18 = (bf16[128,768]{1,0:T(8,128)(2,1)S(1)}, bf16[128,768]{1,0:T(8,128)(2,1)S(1)}, u32[]{:S(2)}, u32[]{:S(2)}) collective-permute-start(bf16[128,768]{1,0:T(8,128)(2,1)S(1)} %get-tuple-element.79), channel_id=1, source_target_pairs={{0,12},{4,8},{8,4},{12,0},{1,13},{5,9},{9,5},{13,1},{2,14},{6,10},... | collective-permute-start | bytes 589832 | tf_op jit(solution)/shard_map/ppermute | solution.py:309
  108.4 0.1 shard_map.127
  108.5 0.1 collective-permute-start.12
  108.7 0.2 collective-permute-start.13
  108.9 3.0 %collective-permute-done.16.refs_5_ = bf16[128,768]{1,0:T(8,128)(2,1)S(1)} collective-permute-done((bf16[128,768]{1,0:T(8,128)(2,1)S(1)}, bf16[128,768]{1,0:T(8,128)(2,1)S(1)}, u32[]{:S(2)}, u32[]{:S(2)}) %collective-permute-start.16) | collective-permute-done | bytes 196640 | tf_op jit(solution)/shard_map/ppermute | solution.py:309
  111.9 5.1 %collective-permute-done.18.refs_7_ = bf16[128,768]{1,0:T(8,128)(2,1)S(1)} collective-permute-done((bf16[128,768]{1,0:T(8,128)(2,1)S(1)}, bf16[128,768]{1,0:T(8,128)(2,1)S(1)}, u32[]{:S(2)}, u32[]{:S(2)}) %collective-permute-start.18) | collective-permute-done | bytes 196640 | tf_op jit(solution)/shard_map/ppermute | solution.py:309
  117.0 3.3 %collective-permute-done.12.refs_1_ = bf16[128,768]{1,0:T(8,128)(2,1)S(1)} collective-permute-done((bf16[128,768]{1,0:T(8,128)(2,1)S(1)}, bf16[128,768]{1,0:T(8,128)(2,1)S(1)}, u32[]{:S(2)}, u32[]{:S(2)}) %collective-permute-start.12) | collective-permute-done | bytes 196640 | tf_op jit(solution)/shard_map/ppermute | solution.py:309
  120.3 5.1 %collective-permute-done.14.refs_3_ = bf16[128,768]{1,0:T(8,128)(2,1)S(1)} collective-permute-done((bf16[128,768]{1,0:T(8,128)(2,1)S(1)}, bf16[128,768]{1,0:T(8,128)(2,1)S(1)}, u32[]{:S(2)}, u32[]{:S(2)}) %collective-permute-start.14) | collective-permute-done | bytes 196640 | tf_op jit(solution)/shard_map/ppermute | solution.py:309
  125.4 0.8 shard_map.130
  126.2 3.5 %all_gather.10.mid_ref = bf16[256,1536]{1,0:T(8,128)(2,1)S(1)} all-gather(bf16[128,1536]{1,0:T(8,128)(2,1)S(1)} %shard_map.130), channel_id=1, replica_groups=mesh['ah'=2,'bh'=2,'bl'=2,'al'=2,'hid'=2] {'hid'}, dimensions={0}, use_global_device_ids=true | all-gather | bytes 1179648 | tf_op jit(solution)/shard_map/all_gather | solution.py:396
  129.8 2.5 %shard_map.131 = (bf16[256,768]{1,0:T(8,128)(2,1)S(1)}, bf16[16,768]{1,0:T(8,128)(2,1)}, bf16[16,768]{1,0:T(8,128)(2,1)}) custom-call(bf16[256,1536]{1,0:T(8,128)(2,1)S(1)} %all_gather.10.mid_ref, f32[1,1536]{1,0:T(1,128)S(1)} %broadcast_in_dim.21.gain_ref, bf16[1536,768]{1,0:T(8,128)(2,1)S(1)} %copy-done.6, bf16[1536,768]{1,0:T(8,128)(2,1)S(1)} %copy-done.7), custom_call_target="tpu_custom_call" | custom-call | flops 1207959552 | bytes 4718592 | tf_op jit(solution)/shard_map/pallas_call | solution.py:83
  132.3 0.7 copy-done.9
  133.0 2.1 %collective-permute-start.19 = (bf16[16,768]{1,0:T(8,128)(2,1)}, bf16[16,768]{1,0:T(8,128)(2,1)S(1)}, u32[]{:S(2)}, u32[]{:S(2)}) collective-permute-start(bf16[16,768]{1,0:T(8,128)(2,1)} %get-tuple-element.85), channel_id=1, source_target_pairs={{0,2},{2,4},{4,6},{6,8},{8,10},{10,12},{12,14},{14,16},{16,18},{18... | collective-permute-start | bytes 73736 | tf_op jit(solution)/shard_map/ppermute | solution.py:284
  135.2 4.2 %collective-permute-start.20 = (bf16[16,768]{1,0:T(8,128)(2,1)}, bf16[16,768]{1,0:T(8,128)(2,1)}, u32[]{:S(2)}, u32[]{:S(2)}) collective-permute-start(bf16[16,768]{1,0:T(8,128)(2,1)} %get-tuple-element.86), channel_id=1, source_target_pairs={{2,0},{4,2},{6,4},{8,6},{10,8},{12,10},{14,12},{16,14},{18,16},{20... | collective-permute-start | bytes 73736 | tf_op jit(solution)/shard_map/ppermute | solution.py:285
  139.4 1.0 copy-done.10
  140.4 0.9 copy-done.14
  141.3 4.4 %shard_map.132.act_ref = bf16[256,768]{1,0:T(8,128)(2,1)S(1)} custom-call(bf16[256,768]{1,0:T(8,128)(2,1)S(1)} %copy-done.10, s32[8,280,128]{2,1,0:T(8,128)S(1)} %copy-done.2, f32[32,768]{1,0:T(8,128)S(1)} %copy-done.14, f32[1,768]{1,0:T(1,128)S(1)} %broadcast_in_dim.22.scale_ref, f32[1,768]{1,0:T(1,128)S(1)} %broadcast_in_dim.23.shift_ref), custom_call_target="tpu_custom_call" | custom-call | flops 6291456 | bytes 3145728 | tf_op jit(solution)/shard_map/pallas_call | solution.py:83
  145.7 1.6 %shard_map.133 = bf16[256,768]{1,0:T(8,128)(2,1)S(1)} custom-call(bf16[256,768]{1,0:T(8,128)(2,1)S(1)} %shard_map.132.act_ref, bf16[16,768]{1,0:T(8,128)(2,1)S(1)} %collective-permute-done.19.top_ref, bf16[256,768]{1,0:T(8,128)(2,1)S(1)} %copy-done.11, bf16[16,768]{1,0:T(8,128)(2,1)} %collective-permute-done.20.bottom_ref, s32[8,280,128]{2,1,0:T(8,128)S(1)} %copy-done.2, ...), custom_call_target="tpu_custom_call" | custom-call | flops 393216 | bytes 786432 | tf_op jit(solution)/shard_map/pallas_call | solution.py:83
  147.3 2.9 %all_gather.11 = bf16[256,1536]{1,0:T(8,128)(2,1)S(1)} all-gather(bf16[256,768]{1,0:T(8,128)(2,1)S(1)} %shard_map.133), channel_id=1, replica_groups=mesh['ah'=2,'bh'=2,'bl'=2,'al'=2,'hid'=2] {'hid'}, dimensions={1}, use_global_device_ids=true | all-gather | bytes 1179648 | tf_op jit(solution)/shard_map/all_gather | solution.py:303
  150.3 1.5 %add_convert_fusion = bf16[256,768]{1,0:T(8,128)(2,1)} fusion(bf16[256,1536]{1,0:T(8,128)(2,1)S(1)} %copy-done.5, s32[]{:T(128)S(6)} %select_n.3, bf16[256,1536]{1,0:T(8,128)(2,1)S(1)} %all_gather.11, bf16[1536,768]{1,0:T(8,128)(2,1)S(1)} %copy-done), kind=kOutput, calls=%fused_computation | convolution fusion | flops 604569600 | bytes 3932164 | tf_op jit(solution)/shard_map/dot_general | solution.py:304
  (49 shorter events, 0.5 us)
Async XLA Ops:
  0.0 150.3 %copy-start = (bf16[1536,768]{1,0:T(8,128)(2,1)S(1)}, bf16[1536,768]{1,0:T(8,128)(2,1)}, u32[]{:S(2)}) copy-start(bf16[1536,768]{1,0:T(8,128)(2,1)} %param.22) | copy-start | bytes 7077892
  0.0 1.2 copy-start.12
  1.2 1.1 copy-start.13
  2.4 1.1 copy-start.3
  3.4 6.2 %copy-start.20 = (f32[1536]{0:T(1024)S(1)}, f32[1536]{0:T(1024)}, u32[]{:S(2)}) copy-start(f32[1536]{0:T(1024)} %param.13) | copy-start | bytes 18436
  3.4 30.6 %all-to-all-start = ((bf16[4,192,768]{2,1,0:T(8,128)(2,1)}), bf16[4,192,768]{2,1,0:T(8,128)(2,1)S(1)}, u32[]{:S(2)}, u32[]{:S(2)}) async-start(bf16[4,192,768]{2,1,0:T(8,128)(2,1)} %copy-done.3), calls=%async_computation | async-start | bytes 2359296 | tf_op jit(solution)/shard_map/all_to_all | solution.py:317
  7.3 24.7 %collective-permute-start = (bf16[96,3072]{1,0:T(8,128)(2,1)}, bf16[96,3072]{1,0:T(8,128)(2,1)}, u32[]{:S(2)}, u32[]{:S(2)}) collective-permute-start(bf16[96,3072]{1,0:T(8,128)(2,1)} %refs_0_.1), channel_id=1, source_target_pairs={{0,16},{16,0},{1,17},{17,1},{2,18},{18,2},{3,19},{19,3},{4,20},{20... | collective-permute-start | bytes 1769480 | tf_op jit(solution)/shard_map/ppermute | solution.py:313
  14.4 0.7 copy-start.16
  15.2 15.9 %collective-permute-start.1 = (bf16[128,1536]{1,0:T(8,128)(2,1)}, bf16[128,1536]{1,0:T(8,128)(2,1)}, u32[]{:S(2)}, u32[]{:S(2)}) collective-permute-start(bf16[128,1536]{1,0:T(8,128)(2,1)} %get-tuple-element.52.refs_0_), channel_id=1, source_target_pairs={{0,4},{4,0},{8,12},{12,8},{1,5},{5,1},{9,13},{13,9},{2,6},{6,2},{1... | collective-permute-start | bytes 1179656 | tf_op jit(solution)/shard_map/ppermute | solution.py:309
  17.2 0.7 copy-start.18
  20.3 1.0 copy-start.1
  34.0 25.9 %collective-permute-start.4 = (bf16[4,192,768]{2,1,0:T(8,128)(2,1)S(1)}, bf16[4,192,768]{2,1,0:T(8,128)(2,1)}, u32[]{:S(2)}, u32[]{:S(2)}) collective-permute-start(bf16[4,192,768]{2,1,0:T(8,128)(2,1)S(1)} %all-to-all-done.both_ref.refs_0_), channel_id=1, source_target_pairs={{0,2},{2,0},{1,3},{3,1},{4,6},{6,4},{5,7},{7,5},{8,10},{10,8},{9,1... | collective-permute-start | bytes 3538952 | tf_op jit(solution)/shard_map/ppermute | solution.py:313
  36.3 0.8 copy-start.8
  37.1 11.9 %all-to-all-start.1 = ((bf16[4,96,768]{2,1,0:T(8,128)(2,1)}), bf16[4,96,768]{2,1,0:T(8,128)(2,1)}, u32[]{:S(2)}, u32[]{:S(2)}) async-start(bf16[4,96,768]{2,1,0:T(8,128)(2,1)} %copy-done.8), calls=%async_computation.1 | async-start | bytes 1179648 | tf_op jit(solution)/shard_map/all_to_all | solution.py:317
  41.8 21.9 %collective-permute-start.3 = (bf16[128,1536]{1,0:T(8,128)(2,1)}, bf16[128,1536]{1,0:T(8,128)(2,1)}, u32[]{:S(2)}, u32[]{:S(2)}) collective-permute-start(bf16[128,1536]{1,0:T(8,128)(2,1)} %get-tuple-element.52.refs_0_), channel_id=1, source_target_pairs={{0,12},{4,8},{8,4},{12,0},{1,13},{5,9},{9,5},{13,1},{2,14},{6,10},... | collective-permute-start | bytes 1179656 | tf_op jit(solution)/shard_map/ppermute | solution.py:309
  44.3 0.7 copy-start.19
  45.1 16.0 %collective-permute-start.2 = (bf16[2,96,768]{2,1,0:T(8,128)(2,1)}, bf16[2,96,768]{2,1,0:T(8,128)(2,1)}, u32[]{:S(2)}, u32[]{:S(2)}) collective-permute-start(bf16[2,96,768]{2,1,0:T(8,128)(2,1)} %get-tuple-element.49), channel_id=1, source_target_pairs={{0,16},{16,0},{1,17},{17,1},{2,18},{18,2},{3,19},{19,3},{4,20},{20... | collective-permute-start | bytes 884744 | tf_op jit(solution)/shard_map/ppermute | solution.py:313
  59.9 17.9 %collective-permute-start.5 = (bf16[4,96,768]{2,1,0:T(8,128)(2,1)}, bf16[4,96,768]{2,1,0:T(8,128)(2,1)S(1)}, u32[]{:S(2)}, u32[]{:S(2)}) collective-permute-start(bf16[4,96,768]{2,1,0:T(8,128)(2,1)} %all-to-all-done.1.z_ref), channel_id=1, source_target_pairs={{0,2},{2,0},{1,3},{3,1},{4,6},{6,4},{5,7},{7,5},{8,10},{10,8},{9,1... | collective-permute-start | bytes 1769480 | tf_op jit(solution)/shard_map/ppermute | solution.py:313
  63.7 14.0 %collective-permute-start.7 = (bf16[128,1536]{1,0:T(8,128)(2,1)}, bf16[128,1536]{1,0:T(8,128)(2,1)S(1)}, u32[]{:S(2)}, u32[]{:S(2)}) collective-permute-start(bf16[128,1536]{1,0:T(8,128)(2,1)} %get-tuple-element.52.refs_0_), channel_id=1, source_target_pairs={{0,8},{4,12},{8,0},{12,4},{1,9},{5,13},{9,1},{13,5},{2,10},{6,14},... | collective-permute-start | bytes 1179656 | tf_op jit(solution)/shard_map/ppermute | solution.py:309
  65.6 10.7 %collective-permute-start.6 = (bf16[2,96,768]{2,1,0:T(8,128)(2,1)}, bf16[2,96,768]{2,1,0:T(8,128)(2,1)S(1)}, u32[]{:S(2)}, u32[]{:S(2)}) collective-permute-start(bf16[2,96,768]{2,1,0:T(8,128)(2,1)} %copy-done.19), channel_id=1, source_target_pairs={{0,16},{16,0},{1,17},{17,1},{2,18},{18,2},{3,19},{19,3},{4,20},{20... | collective-permute-start | bytes 884744 | tf_op jit(solution)/shard_map/ppermute | solution.py:313
  79.1 10.9 %collective-permute-start.8 = (bf16[512,1536]{1,0:T(8,128)(2,1)S(1)}, bf16[512,1536]{1,0:T(8,128)(2,1)S(1)}, u32[]{:S(2)}, u32[]{:S(2)}) collective-permute-start(bf16[512,1536]{1,0:T(8,128)(2,1)S(1)} %shard_map.123.x_ref), channel_id=1, source_target_pairs={{0,1},{1,0},{2,3},{3,2},{4,5},{5,4},{6,7},{7,6},{8,9},{9,8},{10,11... | collective-permute-start | bytes 4718600 | tf_op jit(solution)/shard_map/ppermute | solution.py:313
  85.3 10.5 %collective-permute-start.10 = (bf16[2,96,768]{2,1,0:T(8,128)(2,1)S(1)}, bf16[2,96,768]{2,1,0:T(8,128)(2,1)S(1)}, u32[]{:S(2)}, u32[]{:S(2)}) collective-permute-start(bf16[2,96,768]{2,1,0:T(8,128)(2,1)S(1)} %collective-permute-done.6.refs_1_), channel_id=1, source_target_pairs={{0,2},{2,0},{1,3},{3,1},{4,6},{6,4},{5,7},{7,5},{8,10},{10,8},{9,1... | collective-permute-start | bytes 884744 | tf_op jit(solution)/shard_map/ppermute | solution.py:313
  85.6 14.6 %collective-permute-start.9 = (bf16[2,96,768]{2,1,0:T(8,128)(2,1)}, bf16[2,96,768]{2,1,0:T(8,128)(2,1)S(1)}, u32[]{:S(2)}, u32[]{:S(2)}) collective-permute-start(bf16[2,96,768]{2,1,0:T(8,128)(2,1)} %collective-permute-done.2.refs_0_), channel_id=1, source_target_pairs={{0,2},{2,0},{1,3},{3,1},{4,6},{6,4},{5,7},{7,5},{8,10},{10,8},{9,1... | collective-permute-start | bytes 884744 | tf_op jit(solution)/shard_map/ppermute | solution.py:313
  102.7 2.8 %collective-permute-start.15 = (bf16[512,768]{1,0:T(8,128)(2,1)S(1)}, bf16[512,768]{1,0:T(8,128)(2,1)S(1)}, u32[]{:S(2)}, u32[]{:S(2)}) collective-permute-start(bf16[512,768]{1,0:T(8,128)(2,1)S(1)} %get-tuple-element.75), channel_id=1, source_target_pairs={{0,1},{1,0},{2,3},{3,2},{4,5},{5,4},{6,7},{7,6},{8,9},{9,8},{10,11... | collective-permute-start | bytes 2359304 | tf_op jit(solution)/shard_map/ppermute | solution.py:313
  103.6 4.8 %collective-permute-start.11 = (bf16[512,768]{1,0:T(8,128)(2,1)S(1)}, bf16[512,768]{1,0:T(8,128)(2,1)S(1)}, u32[]{:S(2)}, u32[]{:S(2)}) collective-permute-start(bf16[512,768]{1,0:T(8,128)(2,1)S(1)} %get-tuple-element.67), channel_id=1, source_target_pairs={{0,1},{1,0},{2,3},{3,2},{4,5},{5,4},{6,7},{7,6},{8,9},{9,8},{10,11... | collective-permute-start | bytes 2359304 | tf_op jit(solution)/shard_map/ppermute | solution.py:313
  105.7 19.7 %copy-start.17 = (bf16[128,1536]{1,0:T(8,128)(2,1)S(1)}, bf16[128,1536]{1,0:T(8,128)(2,1)}, u32[]{:S(2)}) copy-start(bf16[128,1536]{1,0:T(8,128)(2,1)} %copy-done.16) | copy-start | bytes 1179652
  105.7 6.2 %collective-permute-start.16 = (bf16[128,768]{1,0:T(8,128)(2,1)S(1)}, bf16[128,768]{1,0:T(8,128)(2,1)S(1)}, u32[]{:S(2)}, u32[]{:S(2)}) collective-permute-start(bf16[128,768]{1,0:T(8,128)(2,1)S(1)} %get-tuple-element.77), channel_id=1, source_target_pairs={{0,4},{4,0},{8,12},{12,8},{1,5},{5,1},{9,13},{13,9},{2,6},{6,2},{1... | collective-permute-start | bytes 589832 | tf_op jit(solution)/shard_map/ppermute | solution.py:309
  105.8 6.1 %collective-permute-start.17 = (bf16[128,768]{1,0:T(8,128)(2,1)S(1)}, bf16[128,768]{1,0:T(8,128)(2,1)S(1)}, u32[]{:S(2)}, u32[]{:S(2)}) collective-permute-start(bf16[128,768]{1,0:T(8,128)(2,1)S(1)} %get-tuple-element.78), channel_id=1, source_target_pairs={{0,8},{4,12},{8,0},{12,4},{1,9},{5,13},{9,1},{13,5},{2,10},{6,14},... | collective-permute-start | bytes 589832 | tf_op jit(solution)/shard_map/ppermute | solution.py:309
  105.9 11.1 %collective-permute-start.18 = (bf16[128,768]{1,0:T(8,128)(2,1)S(1)}, bf16[128,768]{1,0:T(8,128)(2,1)S(1)}, u32[]{:S(2)}, u32[]{:S(2)}) collective-permute-start(bf16[128,768]{1,0:T(8,128)(2,1)S(1)} %get-tuple-element.79), channel_id=1, source_target_pairs={{0,12},{4,8},{8,4},{12,0},{1,13},{5,9},{9,5},{13,1},{2,14},{6,10},... | collective-permute-start | bytes 589832 | tf_op jit(solution)/shard_map/ppermute | solution.py:309
  108.4 21.3 %copy-start.7 = (bf16[1536,768]{1,0:T(8,128)(2,1)S(1)}, bf16[1536,768]{1,0:T(8,128)(2,1)}, u32[]{:S(2)}) copy-start(bf16[1536,768]{1,0:T(8,128)(2,1)} %gate_ref.1) | copy-start | bytes 7077892
  108.5 11.8 %collective-permute-start.12 = (bf16[128,768]{1,0:T(8,128)(2,1)S(1)}, bf16[128,768]{1,0:T(8,128)(2,1)S(1)}, u32[]{:S(2)}, u32[]{:S(2)}) collective-permute-start(bf16[128,768]{1,0:T(8,128)(2,1)S(1)} %get-tuple-element.69), channel_id=1, source_target_pairs={{0,4},{4,0},{8,12},{12,8},{1,5},{5,1},{9,13},{13,9},{2,6},{6,2},{1... | collective-permute-start | bytes 589832 | tf_op jit(solution)/shard_map/ppermute | solution.py:309
  108.7 11.6 %collective-permute-start.13 = (bf16[128,768]{1,0:T(8,128)(2,1)S(1)}, bf16[128,768]{1,0:T(8,128)(2,1)S(1)}, u32[]{:S(2)}, u32[]{:S(2)}) collective-permute-start(bf16[128,768]{1,0:T(8,128)(2,1)S(1)} %get-tuple-element.70), channel_id=1, source_target_pairs={{0,8},{4,12},{8,0},{12,4},{1,9},{5,13},{9,1},{13,5},{2,10},{6,14},... | collective-permute-start | bytes 589832 | tf_op jit(solution)/shard_map/ppermute | solution.py:309
  111.9 13.5 %collective-permute-start.14 = (bf16[128,768]{1,0:T(8,128)(2,1)S(1)}, bf16[128,768]{1,0:T(8,128)(2,1)S(1)}, u32[]{:S(2)}, u32[]{:S(2)}) collective-permute-start(bf16[128,768]{1,0:T(8,128)(2,1)S(1)} %get-tuple-element.71), channel_id=1, source_target_pairs={{0,12},{4,8},{8,4},{12,0},{1,13},{5,9},{9,5},{13,1},{2,14},{6,10},... | collective-permute-start | bytes 589832 | tf_op jit(solution)/shard_map/ppermute | solution.py:309
  125.4 4.3 %copy-start.6 = (bf16[1536,768]{1,0:T(8,128)(2,1)S(1)}, bf16[1536,768]{1,0:T(8,128)(2,1)}, u32[]{:S(2)}) copy-start(bf16[1536,768]{1,0:T(8,128)(2,1)} %value_ref.1) | copy-start | bytes 7077892
  129.7 2.5 %copy-start.4 = (bf16[256,1536]{1,0:T(8,128)(2,1)}, bf16[256,1536]{1,0:T(8,128)(2,1)S(1)}, u32[]{:S(2)}) copy-start(bf16[256,1536]{1,0:T(8,128)(2,1)S(1)} %all_gather.10.mid_ref) | copy-start | bytes 2359300
  129.7 9.6 %copy-start.2 = (s32[8,280,128]{2,1,0:T(8,128)S(1)}, s32[8,280,128]{2,1,0:T(8,128)}, u32[]{:S(2)}) copy-start(s32[8,280,128]{2,1,0:T(8,128)} %copy-done.1) | copy-start | bytes 3440644
  132.3 0.7 copy-start.9
  133.0 12.7 %collective-permute-start.19 = (bf16[16,768]{1,0:T(8,128)(2,1)}, bf16[16,768]{1,0:T(8,128)(2,1)S(1)}, u32[]{:S(2)}, u32[]{:S(2)}) collective-permute-start(bf16[16,768]{1,0:T(8,128)(2,1)} %get-tuple-element.85), channel_id=1, source_target_pairs={{0,2},{2,4},{4,6},{6,8},{8,10},{10,12},{12,14},{14,16},{16,18},{18... | collective-permute-start | bytes 73736 | tf_op jit(solution)/shard_map/ppermute | solution.py:284
  135.2 10.5 %collective-permute-start.20 = (bf16[16,768]{1,0:T(8,128)(2,1)}, bf16[16,768]{1,0:T(8,128)(2,1)}, u32[]{:S(2)}, u32[]{:S(2)}) collective-permute-start(bf16[16,768]{1,0:T(8,128)(2,1)} %get-tuple-element.86), channel_id=1, source_target_pairs={{2,0},{4,2},{6,4},{8,6},{10,8},{12,10},{14,12},{16,14},{18,16},{20... | collective-permute-start | bytes 73736 | tf_op jit(solution)/shard_map/ppermute | solution.py:285
  139.4 1.0 copy-start.10
  140.4 0.9 copy-start.14
  141.3 4.4 %copy-start.11 = (bf16[256,768]{1,0:T(8,128)(2,1)S(1)}, bf16[256,768]{1,0:T(8,128)(2,1)}, u32[]{:S(2)}) copy-start(bf16[256,768]{1,0:T(8,128)(2,1)} %copy-done.9) | copy-start | bytes 1179652
  141.3 4.4 %copy-start.15 = (f32[32,768]{1,0:T(8,128)S(1)}, f32[32,768]{1,0:T(8,128)}, u32[]{:S(2)}) copy-start(f32[32,768]{1,0:T(8,128)} %taps_ref.3) | copy-start | bytes 294916
  145.7 4.6 %copy-start.5 = (bf16[256,1536]{1,0:T(8,128)(2,1)S(1)}, bf16[256,1536]{1,0:T(8,128)(2,1)}, u32[]{:S(2)}) copy-start(bf16[256,1536]{1,0:T(8,128)(2,1)} %copy-done.4) | copy-start | bytes 2359300

commit v5 on v4

--- a/solution.py
+++ b/solution.py
@@ -117,18 +117,23 @@
     second_ref[...] = both_ref[half:, skip:, :]
 
 
-def norm_kernel(start_ref, whole_ref, gain_ref, mine_ref, out_ref):
-    rows = mine_ref.shape[0]
-    mine = whole_ref[pl.ds(pl.multiple_of(start_ref[0], rows), rows), :]
-    mine_ref[...] = mine
-    out_ref[...] = norm_rows(f32(mine), gain_ref[...]).astype(jnp.bfloat16)
+def norm_kernel(me_ref, whole_ref, gain_ref, near_ref, far_ref, out_ref, upper_ref, lower_ref):
+    rows, width = near_ref.shape
+    at = pl.ds(pl.multiple_of(me_ref[1] * rows, rows), rows)
+    for place, ref in ((me_ref[2], near_ref), (1 - me_ref[2], far_ref)):
+        ref[...] = whole_ref[at, pl.ds(pl.multiple_of(place * width, width), width)]
+    normed = norm_rows(f32(whole_ref[at, :]), gain_ref[...]).astype(jnp.bfloat16)
+    out_ref[...] = normed
+    upper_ref[...] = normed[: rows // 2]
+    lower_ref[...] = normed[rows // 2 :]
 
 
 def join_kernel(*refs):
     *pieces, out_ref = refs
-    rows = pieces[0].shape[0]
-    for i, piece in enumerate(pieces):
-        out_ref[i * rows : (i + 1) * rows] = piece[...]
+    at = 0
+    for piece in pieces:
+        out_ref[at : at + piece.shape[0]] = piece[...]
+        at += piece.shape[0]
 
 
 def interleave(full_ref, base, block, own_refs, other_refs, me_l, last=False):
@@ -173,15 +178,12 @@
         out_ref[...] = (kept_ref[at, :] + f32(came_ref[at, :])).astype(out_ref.dtype)
 
 
-def mid_kernel(me_ref, mine_ref, *refs):
-    *sums, out_ref = refs
-    for place, part in ((me_ref[2], sums[:4]), (1 - me_ref[2], sums[4:])):
-        total = part[0][...]
-        for other in part[1:]:
-            total = total + f32(other[...])
-        width = part[0].shape[1]
-        at = pl.ds(pl.multiple_of(place * width, width), width)
-        out_ref[:, at] = (f32(mine_ref[:, at]) + 0.5 * total).astype(jnp.bfloat16)
+def mid_kernel(mine_ref, first_ref, *refs):
+    *others, out_ref = refs
+    total = first_ref[...]
+    for other in others:
+        total = total + f32(other[...])
+    out_ref[...] = (f32(mine_ref[...]) + 0.5 * total).astype(jnp.bfloat16)
 
 
 HALO = 16
@@ -201,7 +203,17 @@
         out_ref[r] = base_ref[1 + r : 1 + r + out_ref.shape[1], :]
 
 
-def glu_kernel(mid_ref, gain_ref, value_ref, gate_ref, glu_ref, head_ref, tail_ref):
+def glu_kernel(
+    me_ref, near_ref, near_oth_ref, far_ref, far_oth_ref, gain_ref, value_ref, gate_ref,
+    glu_ref, head_ref, tail_ref, own_ref, mid_ref
+):
+    rows, width = near_ref.shape
+    me_c, me_a = me_ref[1], me_ref[2]
+    for core, near, far in ((me_c, near_ref, far_ref), (1 - me_c, near_oth_ref, far_oth_ref)):
+        at = pl.ds(pl.multiple_of(core * rows, rows), rows)
+        for place, ref in ((me_a, near), (1 - me_a, far)):
+            mid_ref[at, pl.ds(pl.multiple_of(place * width, width), width)] = ref[...]
+    own_ref[...] = mid_ref[:, pl.ds(pl.multiple_of(me_c * width, width), width)]
     normed = norm_rows(f32(mid_ref[...]), gain_ref[...]).astype(jnp.bfloat16)
     value = jnp.dot(normed, value_ref[...], preferred_element_type=jnp.float32)
     gate = jnp.dot(normed, gate_ref[...], preferred_element_type=jnp.float32)
@@ -269,14 +281,17 @@
     )[0]
 
 
-def grouped_conv_module(mid_own, mid_full, axis, early, w_value, w_gate, depth_kernel, w_proj):
-    rows, width = mid_own.shape
+def grouped_conv_module(mid, me, axis, early, w_value, w_gate, depth_kernel, w_proj):
+    half, width = mid[0].shape
+    rows = 2 * half
     utter, conv_gain, bn_scale, bn_shift = early
     bf16 = jnp.bfloat16
-    glu, head, tail = kernel_call(
+    glu, head, tail, mid_own = kernel_call(
         glu_kernel,
-        [((rows, width), bf16)] + [((HALO, width), bf16)] * 2,
-        [mid_full, conv_gain, w_value, w_gate],
+        [((rows, width), bf16)] + [((HALO, width), bf16)] * 2 + [((rows, width), bf16)],
+        [me, *mid, conv_gain, w_value, w_gate],
+        scratch=[pltpu.VMEM((rows, 2 * width), bf16)],
+        scalars=1,
         flops=4 * rows * w_value.size,
         moved=4 * w_value.size,
     )
@@ -333,30 +348,32 @@
     (both,) = kernel_call(cut_kernel, [((4, 2 * shard, units), bf16)], [w_in, w_out.T])
     both = recut(both)
     whole = lax.all_gather(tokens, "hid", axis=1, tiled=True)
-    mine, normed = kernel_call(
+    *mine, normed, upper, lower = kernel_call(
         norm_kernel,
-        [((half, wide), bf16)] * 2,
-        [(me_c * half)[None], whole, ffn_gain[None, :]],
+        [((half, width), bf16)] * 2 + [((half, wide), bf16)] + [((half // 2, wide), bf16)] * 2,
+        [me, whole, ffn_gain[None, :]],
         scalars=1,
     )
     frames1 = partner(normed, 1)
-    in_far, both, normed, frames1, early = tie((in_far, both, normed, frames1, early))
+    in_far, both, normed, upper, lower, frames1, early = tie(
+        (in_far, both, normed, upper, lower, frames1, early)
+    )
     both_x = swap(both, "al")
     (in_z,) = kernel_call(cut_kernel, [(block, bf16)], [in_far])
     in_z = recut(in_z)
     out_1, out_2 = kernel_call(part_kernel, [(pair, bf16)] * 2, [both])
     out_z1 = swap(out_1, "ah")
     frames3 = partner(normed, 3)
-    both_x, in_z = tie((both_x, in_z))
-    out_z1, out_2, normed, frames3 = tie((out_z1, out_2, normed, frames3))
+    both_x, in_z, out_z1, out_2 = tie((both_x, in_z, out_z1, out_2))
     in_zx = swap(in_z, "al")
     out_z2 = swap(out_2, "ah")
-    frames2 = partner(normed, 2)
+    normed, upper, lower, frames3 = tie((normed, upper, lower, frames3))
+    frames2 = [partner(upper, 2), partner(lower, 2)]
     in_zx, out_z1, out_z2, frames2 = tie((in_zx, out_z1, out_z2, frames2))
     out_zx1 = swap(out_z1, "al")
     out_zx2 = swap(out_z2, "al")
     (x_own,) = kernel_call(
-        join_kernel, [((4 * half, wide), bf16)], [normed, frames1, frames2, frames3]
+        join_kernel, [((4 * half, wide), bf16)], [normed, frames1, *frames2, frames3]
     )
     x_oth = swap(x_own, "hid")
 
@@ -390,12 +407,14 @@
 
     near, out_zx1, out_zx2 = tie((products([both], [both_x]), out_zx1, out_zx2))
     far = products([out_z1, out_z2], [out_zx1, out_zx2])
-    (mid_rows,) = kernel_call(
-        mid_kernel, [((half, wide), bf16)], [me, mine, *scatter(*near), *scatter(*far)], scalars=1
-    )
-    mid_full = lax.all_gather(mid_rows, "hid", axis=0, tiled=True)
-    mid_own = lax.dynamic_slice_in_dim(mid_full, me_c * width, width, 1)
-    return mid_own, mid_full, early
+    mine_near, mine_far = mine
+
+    def mid(rows, parts):
+        (own,) = kernel_call(mid_kernel, [((half, width), bf16)], [rows, *parts])
+        return own, swap(own, "hid")
+
+    near, parts = tie((mid(mine_near, scatter(*near)), scatter(*far)))
+    return near + mid(mine_far, parts), me, early
 
 
 def solution(mesh):
@@ -412,10 +431,8 @@
             w_value, w_gate, depth_kernel, bn_scale, bn_shift, w_proj, lengths = rest
             utter = utterances(tokens.shape[0], tok, lengths, depth_kernel.shape[0])
             early = utter, conv_gain[None, :], bn_scale[None, :], bn_shift[None, :]
-            mid_own, mid_full, early = grouped_ffn(tokens, ffn_gain, w_in, w_out, early)
-            return grouped_conv_module(
-                mid_own, mid_full, tok, early, w_value, w_gate, depth_kernel, w_proj
-            )
+            mid, me, early = grouped_ffn(tokens, ffn_gain, w_in, w_out, early)
+            return grouped_conv_module(mid, me, tok, early, w_value, w_gate, depth_kernel, w_proj)
         mid_own, mid_full = gathered_ffn(tokens, ffn_gain, w_in, w_out)
         return conv_module(mid_own, mid_full, tok, conv_gain, *rest)
 

time: 153 us -> 144 us (0.941)
  waiting for transfers between devices: 62.9 us -> 55.2 us
  blocking collectives: 10.2 us -> 6.64 us
  starting transfers between devices: 37.1 us -> 40.6 us
    ppermute x10 -> x12, waiting for transfers between devices: 28.8 us -> 15.9 us  [swap(): return lax.ppermute(values, axis, SWAP)]
    ppermute x9 -> x10, waiting for transfers between devices: 30.3 us -> 35.2 us  [partner(): return lax.ppermute(values, GROUP, [(i, i ^ step) for i in range(4)])]
    ppermute x10 -> x12, starting transfers between devices: 15.5 us -> 19.7 us  [swap(): return lax.ppermute(values, axis, SWAP)]
    all_gather x1 -> x0, blocking collectives: 3.52 us -> none  [grouped_ffn(): mid_full = lax.all_gather(mid_rows, 'hid', axis=0, tiled=True)]
    pallas_call x16 -> x17, Pallas kernels: 27.7 us -> 26.2 us  [kernel_call(): pl.pallas_call(body, out_shape=[jax.ShapeDtypeStruct(shape, dtype) for sh...]
    unnamed x42 -> x38, local copies, waits for them, and re-layouts: 9.94 us -> 8.65 us
    ppermute x9 -> x10, starting transfers between devices: 6.71 us -> 6.46 us  [partner(): return lax.ppermute(values, GROUP, [(i, i ^ step) for i in range(4)])]
  transfers between devices with their start and end apart: 23 -> 26, of which waited for: 14 -> 15; matrix products, arithmetic and copies ran while one was open for 1% -> 2% of each run, Pallas kernels for 12% -> 15%
where the time goes in v5:
time: 144 us; the launch traced here: 142 us
  waiting for transfers between devices  55.2 us (38%)
  starting transfers between devices  40.6 us (28%)
  Pallas kernels  26.2 us (18%)
  local copies, waits for them, and re-layouts  12 us (8%)
  blocking collectives  6.64 us (5%)
  matrix products  1.53 us (1%)
    ppermute x10, waiting for transfers between devices, partner(): return lax.ppermute(values, GROUP, [(i, i ^ step) for i in range(4)])  35.2 us
    pallas_call x17, Pallas kernels, kernel_call(): pl.pallas_call(body, out_shape=[jax.ShapeDtypeStruct(shape, dtype) for sh...  26.2 us
    ppermute x12, starting transfers between devices, swap(): return lax.ppermute(values, axis, SWAP)  19.7 us
    ppermute x12, waiting for transfers between devices, swap(): return lax.ppermute(values, axis, SWAP)  15.9 us
    unnamed x38, local copies, waits for them, and re-layouts  8.65 us
    all_to_all x2, starting transfers between devices, recut(): return lax.all_to_all(parts, GROUP, 0, 0)  8.1 us
    ppermute x10, starting transfers between devices, partner(): return lax.ppermute(values, GROUP, [(i, i ^ step) for i in range(4)])  6.46 us
    ppermute x1, starting transfers between devices, grouped_conv_module(): bottom = lax.ppermute(head, axis, [(i + 1, i) for i in range(count - 1)])  4.16 us
  transfers between devices with their start and end apart: 26, of which 15 were waited for; matrix products, arithmetic and copies ran while one was open for 2% of the time, Pallas kernels for 15%

profile of v5, /device:TPU:5, one launch (start us, length us, event | category | flops | bytes accessed | tf_op | source)
XLA Modules:
  0.0 142.5 jit_solution(1445889998399794232)
XLA Ops:
  0.0 1.2 copy-done.7
  1.2 1.1 copy-done.8
  2.4 1.1 copy-done.3
  3.4 3.7 %all-to-all-start = ((bf16[4,192,768]{2,1,0:T(8,128)(2,1)}), bf16[4,192,768]{2,1,0:T(8,128)(2,1)S(1)}, u32[]{:S(2)}, u32[]{:S(2)}) async-start(bf16[4,192,768]{2,1,0:T(8,128)(2,1)} %copy-done.3), calls=%async_computation | async-start | bytes 2359296 | tf_op jit(solution)/shard_map/all_to_all | solution.py:332
  7.2 2.3 %collective-permute-start = (bf16[96,3072]{1,0:T(8,128)(2,1)}, bf16[96,3072]{1,0:T(8,128)(2,1)}, u32[]{:S(2)}, u32[]{:S(2)}) collective-permute-start(bf16[96,3072]{1,0:T(8,128)(2,1)} %refs_0_.1), channel_id=1, source_target_pairs={{0,16},{16,0},{1,17},{17,1},{2,18},{18,2},{3,19},{19,3},{4,20},{20... | collective-permute-start | bytes 1769480 | tf_op jit(solution)/shard_map/ppermute | solution.py:328
  9.5 0.7 broadcast_in_dim.15.gain_ref
  10.3 3.7 %all_gather.6.whole_ref = bf16[256,1536]{1,0:T(8,128)(2,1)S(1)} all-gather(bf16[256,768]{1,0:T(8,128)(2,1)} %param.12), channel_id=1, replica_groups=mesh['ah'=2,'bh'=2,'bl'=2,'al'=2,'hid'=2] {'hid'}, dimensions={1}, use_global_device_ids=true | all-gather | bytes 1179648 | tf_op jit(solution)/shard_map/all_gather | solution.py:350
  14.0 1.6 %shard_map.118 = (bf16[128,768]{1,0:T(8,128)(2,1)S(1)}, bf16[128,768]{1,0:T(8,128)(2,1)S(1)}, bf16[128,1536]{1,0:T(8,128)(2,1)}, bf16[64,1536]{1,0:T(8,128)(2,1)S(1)}, bf16[64,1536]{1,0:T(8,128)(2,1)S(1)}) custom-call(s32[3]{0:T(128)S(1)} %pad_add_fusion.me_ref, bf16[256,1536]{1,0:T(8,128)(2,1)S(1)} %all_gather.6.whole_ref, ...), custom_call_target="tpu_custom_call" | custom-call | tf_op jit(solution)/shard_map/pallas_call | solution.py:83
  15.6 0.7 copy-done.10
  16.3 0.7 copy-done.12
  17.0 0.7 copy-done.17
  17.6 0.7 copy-done.18
  18.3 1.3 broadcast_in_dim.17.gain_ref
  19.6 0.7 broadcast_in_dim.18.scale_ref
  20.3 0.7 broadcast_in_dim.19.shift_ref
  21.0 2.4 %shard_map.120.utter_ref = s32[8,280,128]{2,1,0:T(8,128)S(1)} custom-call(s32[1]{0:T(128)} %bitcast.4.first_ref, s32[64]{0:T(128)S(1)} %copy-done.15), custom_call_target="tpu_custom_call" | custom-call | tf_op jit(solution)/shard_map/pallas_call | solution.py:83
  23.4 1.0 copy-done.1
  24.4 9.8 %collective-permute-done.1.refs_1_ = bf16[128,1536]{1,0:T(8,128)(2,1)} collective-permute-done((bf16[128,1536]{1,0:T(8,128)(2,1)}, bf16[128,1536]{1,0:T(8,128)(2,1)}, u32[]{:S(2)}, u32[]{:S(2)}) %collective-permute-start.1) | collective-permute-done | bytes 393248 | tf_op jit(solution)/shard_map/ppermute | solution.py:324
  34.2 1.2 collective-permute-start.3
  35.4 1.1 shard_map.121
  36.5 0.8 copy-done.6
  37.3 4.4 %all-to-all-start.1 = ((bf16[4,96,768]{2,1,0:T(8,128)(2,1)}), bf16[4,96,768]{2,1,0:T(8,128)(2,1)}, u32[]{:S(2)}, u32[]{:S(2)}) async-start(bf16[4,96,768]{2,1,0:T(8,128)(2,1)} %copy-done.6), calls=%async_computation.1 | async-start | bytes 1179648 | tf_op jit(solution)/shard_map/all_to_all | solution.py:332
  41.8 0.7 copy-done.16
  42.5 2.1 %collective-permute-start.4 = (bf16[2,96,768]{2,1,0:T(8,128)(2,1)S(1)}, bf16[2,96,768]{2,1,0:T(8,128)(2,1)}, u32[]{:S(2)}, u32[]{:S(2)}) collective-permute-start(bf16[2,96,768]{2,1,0:T(8,128)(2,1)S(1)} %get-tuple-element.72), channel_id=1, source_target_pairs={{0,16},{16,0},{1,17},{17,1},{2,18},{18,2},{3,19},{19,3},{4,20},{20... | collective-permute-start | bytes 884744 | tf_op jit(solution)/shard_map/ppermute | solution.py:328
  44.6 1.7 %collective-permute-start.2 = (bf16[128,1536]{1,0:T(8,128)(2,1)}, bf16[128,1536]{1,0:T(8,128)(2,1)}, u32[]{:S(2)}, u32[]{:S(2)}) collective-permute-start(bf16[128,1536]{1,0:T(8,128)(2,1)} %get-tuple-element.68.refs_0_), channel_id=1, source_target_pairs={{0,12},{4,8},{8,4},{12,0},{1,13},{5,9},{9,5},{13,1},{2,14},{6,10},... | collective-permute-start | bytes 1179656 | tf_op jit(solution)/shard_map/ppermute | solution.py:324
  46.3 5.9 %collective-permute-done.4.refs_0_ = bf16[2,96,768]{2,1,0:T(8,128)(2,1)} collective-permute-done((bf16[2,96,768]{2,1,0:T(8,128)(2,1)S(1)}, bf16[2,96,768]{2,1,0:T(8,128)(2,1)}, u32[]{:S(2)}, u32[]{:S(2)}) %collective-permute-start.4) | collective-permute-done | bytes 294944 | tf_op jit(solution)/shard_map/ppermute | solution.py:328
  52.2 4.1 %all-to-all-done.1.z_ref = bf16[4,96,768]{2,1,0:T(8,128)(2,1)} async-done(((bf16[4,96,768]{2,1,0:T(8,128)(2,1)}), bf16[4,96,768]{2,1,0:T(8,128)(2,1)}, u32[]{:S(2)}, u32[]{:S(2)}) %all-to-all-start.1) | async-done | bytes 589856 | tf_op jit(solution)/shard_map/all_to_all | solution.py:332
  56.2 4.2 %collective-permute-done.3.both_x_ref.refs_1_ = bf16[4,192,768]{2,1,0:T(8,128)(2,1)} collective-permute-done((bf16[4,192,768]{2,1,0:T(8,128)(2,1)S(1)}, bf16[4,192,768]{2,1,0:T(8,128)(2,1)}, u32[]{:S(2)}, u32[]{:S(2)}) %collective-permute-start.3) | collective-permute-done | bytes 1179680 | tf_op jit(solution)/shard_map/ppermute | solution.py:328
  60.5 1.2 collective-permute-start.5
  61.6 0.2 collective-permute-start.6
  61.9 3.0 %collective-permute-done.2.refs_4_ = bf16[128,1536]{1,0:T(8,128)(2,1)} collective-permute-done((bf16[128,1536]{1,0:T(8,128)(2,1)}, bf16[128,1536]{1,0:T(8,128)(2,1)}, u32[]{:S(2)}, u32[]{:S(2)}) %collective-permute-start.2) | collective-permute-done | bytes 393248 | tf_op jit(solution)/shard_map/ppermute | solution.py:324
  64.9 1.4 %collective-permute-start.8 = (bf16[64,1536]{1,0:T(8,128)(2,1)}, bf16[64,1536]{1,0:T(8,128)(2,1)S(1)}, u32[]{:S(2)}, u32[]{:S(2)}) collective-permute-start(bf16[64,1536]{1,0:T(8,128)(2,1)} %copy-done.17), channel_id=1, source_target_pairs={{0,8},{4,12},{8,0},{12,4},{1,9},{5,13},{9,1},{13,5},{2,10},{6,14},... | collective-permute-start | bytes 589832 | tf_op jit(solution)/shard_map/ppermute | solution.py:324
  66.3 5.1 %collective-permute-done.7.refs_2_ = bf16[64,1536]{1,0:T(8,128)(2,1)S(1)} collective-permute-done((bf16[64,1536]{1,0:T(8,128)(2,1)}, bf16[64,1536]{1,0:T(8,128)(2,1)S(1)}, u32[]{:S(2)}, u32[]{:S(2)}) %collective-permute-start.7) | collective-permute-done | bytes 196640 | tf_op jit(solution)/shard_map/ppermute | solution.py:324
  71.5 4.2 %collective-permute-done.8.refs_3_ = bf16[64,1536]{1,0:T(8,128)(2,1)S(1)} collective-permute-done((bf16[64,1536]{1,0:T(8,128)(2,1)}, bf16[64,1536]{1,0:T(8,128)(2,1)S(1)}, u32[]{:S(2)}, u32[]{:S(2)}) %collective-permute-start.8) | collective-permute-done | bytes 196640 | tf_op jit(solution)/shard_map/ppermute | solution.py:324
  75.7 1.3 shard_map.123.x_ref
  77.0 5.6 %collective-permute-start.9 = (bf16[512,1536]{1,0:T(8,128)(2,1)S(1)}, bf16[512,1536]{1,0:T(8,128)(2,1)S(1)}, u32[]{:S(2)}, u32[]{:S(2)}) collective-permute-start(bf16[512,1536]{1,0:T(8,128)(2,1)S(1)} %shard_map.123.x_ref), channel_id=1, source_target_pairs={{0,1},{1,0},{2,3},{3,2},{4,5},{5,4},{6,7},{7,6},{8,9},{9,8},{10,11... | collective-permute-start | bytes 4718600 | tf_op jit(solution)/shard_map/ppermute | solution.py:328
  82.6 0.3 collective-permute-start.10
  82.9 1.2 collective-permute-start.11
  84.1 3.1 %shard_map.124.own_ref = bf16[512,768]{1,0:T(8,128)(2,1)S(1)} custom-call(s32[3]{0:T(128)S(1)} %pad_add_fusion.me_ref, bf16[512,1536]{1,0:T(8,128)(2,1)S(1)} %shard_map.123.x_ref, bf16[4,192,768]{2,1,0:T(8,128)(2,1)S(1)} %all-to-all-done.both_ref.refs_0_, bf16[4,192,768]{2,1,0:T(8,128)(2,1)} %collective-permute-done.3.both_x_ref.refs_1_, ...), custom_call_target="tpu_custom_call" | custom-call | tf_op jit(solution)/shard_map/pallas_call | solution.py:83
  87.2 3.1 %shard_map.125.oth_ref = bf16[512,768]{1,0:T(8,128)(2,1)S(1)} custom-call(s32[3]{0:T(128)S(1)} %pad_add_fusion.me_ref, bf16[512,1536]{1,0:T(8,128)(2,1)S(1)} %collective-permute-done.9.x_ref, bf16[4,192,768]{2,1,0:T(8,128)(2,1)S(1)} %all-to-all-done.both_ref.refs_0_, bf16[4,192,768]{2,1,0:T(8,128)(2,1)} %collective-permute-done.3.both_x_ref.refs_1_, ...), custom_call_target="tpu_custom_call" | custom-call | tf_op jit(solution)/shard_map/pallas_call | solution.py:83
  90.2 2.8 %shard_map.126 = (f32[512,768]{1,0:T(8,128)S(1)}, bf16[512,768]{1,0:T(8,128)(2,1)S(1)}) custom-call(s32[3]{0:T(128)S(1)} %pad_add_fusion.me_ref, bf16[512,768]{1,0:T(8,128)(2,1)S(1)} %shard_map.124.own_ref, bf16[512,768]{1,0:T(8,128)(2,1)S(1)} %shard_map.125.oth_ref, bf16[4,192,768]{2,1,0:T(8,128)(2,1)S(1)} %all-to-all-done.both_ref.refs_0_, ...), custom_call_target="tpu_custom_call" | custom-call | tf_op jit(solution)/shard_map/pallas_call | solution.py:83
  93.0 4.7 %collective-permute-done.11.refs_3_ = bf16[2,96,768]{2,1,0:T(8,128)(2,1)S(1)} collective-permute-done((bf16[2,96,768]{2,1,0:T(8,128)(2,1)S(1)}, bf16[2,96,768]{2,1,0:T(8,128)(2,1)S(1)}, u32[]{:S(2)}, u32[]{:S(2)}) %collective-permute-start.11) | collective-permute-done | bytes 294944 | tf_op jit(solution)/shard_map/ppermute | solution.py:328
  97.7 0.8 collective-permute-start.12
  98.6 2.5 %shard_map.129 = (f32[512,768]{1,0:T(8,128)S(1)}, bf16[512,768]{1,0:T(8,128)(2,1)S(1)}) custom-call(s32[3]{0:T(128)S(1)} %pad_add_fusion.me_ref, bf16[512,768]{1,0:T(8,128)(2,1)S(1)} %shard_map.124.own_ref, bf16[512,768]{1,0:T(8,128)(2,1)S(1)} %shard_map.125.oth_ref, bf16[2,96,768]{2,1,0:T(8,128)(2,1)} %collective-permute-done.4.refs_0_, ...), custom_call_target="tpu_custom_call" | custom-call | tf_op jit(solution)/shard_map/pallas_call | solution.py:83
  101.1 0.1 shard_map.127
  101.3 0.6 collective-permute-start.13
  101.9 2.1 %collective-permute-start.15 = (bf16[128,768]{1,0:T(8,128)(2,1)S(1)}, bf16[128,768]{1,0:T(8,128)(2,1)S(1)}, u32[]{:S(2)}, u32[]{:S(2)}) collective-permute-start(bf16[128,768]{1,0:T(8,128)(2,1)S(1)} %get-tuple-element.93), channel_id=1, source_target_pairs={{0,12},{4,8},{8,4},{12,0},{1,13},{5,9},{9,5},{13,1},{2,14},{6,10},... | collective-permute-start | bytes 589832 | tf_op jit(solution)/shard_map/ppermute | solution.py:324
  104.2 0.6 collective-permute-start.18
  104.7 2.6 %collective-permute-done.13.refs_0_ = bf16[128,768]{1,0:T(8,128)(2,1)S(1)} collective-permute-done((bf16[128,768]{1,0:T(8,128)(2,1)S(1)}, bf16[128,768]{1,0:T(8,128)(2,1)S(1)}, u32[]{:S(2)}, u32[]{:S(2)}) %collective-permute-start.13) | collective-permute-done | bytes 196640 | tf_op jit(solution)/shard_map/ppermute | solution.py:324
  107.3 0.2 collective-permute-done.14.refs_1_
  107.5 4.9 %collective-permute-done.15.refs_2_ = bf16[128,768]{1,0:T(8,128)(2,1)S(1)} collective-permute-done((bf16[128,768]{1,0:T(8,128)(2,1)S(1)}, bf16[128,768]{1,0:T(8,128)(2,1)S(1)}, u32[]{:S(2)}, u32[]{:S(2)}) %collective-permute-start.15) | collective-permute-done | bytes 196640 | tf_op jit(solution)/shard_map/ppermute | solution.py:324
  112.6 3.0 %collective-permute-start.16 = (bf16[128,768]{1,0:T(8,128)(2,1)S(1)}, bf16[128,768]{1,0:T(8,128)(2,1)S(1)}, u32[]{:S(2)}, u32[]{:S(2)}) collective-permute-start(bf16[128,768]{1,0:T(8,128)(2,1)S(1)} %shard_map.128.near_ref), channel_id=1, source_target_pairs={{0,1},{1,0},{2,3},{3,2},{4,5},{5,4},{6,7},{7,6},{8,9},{9,8},{10,11... | collective-permute-start | bytes 589832 | tf_op jit(solution)/shard_map/ppermute | solution.py:328
  115.6 0.2 collective-permute-done.18.refs_0_
  115.8 0.2 collective-permute-done.19.refs_1_
  116.0 4.9 %collective-permute-done.20.refs_2_ = bf16[128,768]{1,0:T(8,128)(2,1)S(1)} collective-permute-done((bf16[128,768]{1,0:T(8,128)(2,1)S(1)}, bf16[128,768]{1,0:T(8,128)(2,1)S(1)}, u32[]{:S(2)}, u32[]{:S(2)}) %collective-permute-start.20) | collective-permute-done | bytes 196640 | tf_op jit(solution)/shard_map/ppermute | solution.py:324
  121.0 1.7 %collective-permute-start.21 = (bf16[128,768]{1,0:T(8,128)(2,1)S(1)}, bf16[128,768]{1,0:T(8,128)(2,1)S(1)}, u32[]{:S(2)}, u32[]{:S(2)}) collective-permute-start(bf16[128,768]{1,0:T(8,128)(2,1)S(1)} %shard_map.131.far_ref), channel_id=1, source_target_pairs={{0,1},{1,0},{2,3},{3,2},{4,5},{5,4},{6,7},{7,6},{8,9},{9,8},{10,11... | collective-permute-start | bytes 589832 | tf_op jit(solution)/shard_map/ppermute | solution.py:328
  122.8 1.1 collective-permute-done.21.far_oth_ref
  123.8 2.5 %shard_map.132 = (bf16[256,768]{1,0:T(8,128)(2,1)S(1)}, bf16[16,768]{1,0:T(8,128)(2,1)S(1)}, bf16[16,768]{1,0:T(8,128)(2,1)S(1)}, bf16[256,768]{1,0:T(8,128)(2,1)S(1)}) custom-call(s32[3]{0:T(128)S(1)} %pad_add_fusion.me_ref, bf16[128,768]{1,0:T(8,128)(2,1)S(1)} %shard_map.128.near_ref, bf16[128,768]{1,0:T(8,128)(2,1)S(1)} %collective-permute-done.16.near_oth_ref, ...), custom_call_target="tpu_custom_call" | custom-call | flops 1207959552 | bytes 4718592 | tf_op jit(solution)/shard_map/pallas_call | solution.py:83
  126.3 2.2 %collective-permute-start.22 = (bf16[16,768]{1,0:T(8,128)(2,1)S(1)}, bf16[16,768]{1,0:T(8,128)(2,1)S(1)}, u32[]{:S(2)}, u32[]{:S(2)}) collective-permute-start(bf16[16,768]{1,0:T(8,128)(2,1)S(1)} %get-tuple-element.115), channel_id=1, source_target_pairs={{0,2},{2,4},{4,6},{6,8},{8,10},{10,12},{12,14},{14,16},{16,18},{18... | collective-permute-start | bytes 73736 | tf_op jit(solution)/shard_map/ppermute | solution.py:299
  128.5 4.2 %collective-permute-start.23 = (bf16[16,768]{1,0:T(8,128)(2,1)S(1)}, bf16[16,768]{1,0:T(8,128)(2,1)S(1)}, u32[]{:S(2)}, u32[]{:S(2)}) collective-permute-start(bf16[16,768]{1,0:T(8,128)(2,1)S(1)} %get-tuple-element.116), channel_id=1, source_target_pairs={{2,0},{4,2},{6,4},{8,6},{10,8},{12,10},{14,12},{16,14},{18,16},{20... | collective-permute-start | bytes 73736 | tf_op jit(solution)/shard_map/ppermute | solution.py:300
  132.7 4.4 %shard_map.133.act_ref = bf16[256,768]{1,0:T(8,128)(2,1)S(1)} custom-call(bf16[256,768]{1,0:T(8,128)(2,1)S(1)} %get-tuple-element.111.glu_ref, s32[8,280,128]{2,1,0:T(8,128)S(1)} %copy-done.2, f32[32,768]{1,0:T(8,128)S(1)} %copy-done.9, f32[1,768]{1,0:T(1,128)S(1)} %broadcast_in_dim.18.scale_ref, f32[1,768]{1,0:T(1,128)S(1)} %broadcast_in_dim.19.shift_ref), custom_call_target="tpu_custom_call" | custom-call | flops 6291456 | bytes 3145728 | tf_op jit(solution)/shard_map/pallas_call | solution.py:83
  137.2 0.8 shard_map.134
  138.0 2.9 %all_gather.7 = bf16[256,1536]{1,0:T(8,128)(2,1)S(1)} all-gather(bf16[256,768]{1,0:T(8,128)(2,1)S(1)} %shard_map.134), channel_id=1, replica_groups=mesh['ah'=2,'bh'=2,'bl'=2,'al'=2,'hid'=2] {'hid'}, dimensions={1}, use_global_device_ids=true | all-gather | bytes 1179648 | tf_op jit(solution)/shard_map/all_gather | solution.py:318
  140.9 1.5 %add_convert_fusion = bf16[256,768]{1,0:T(8,128)(2,1)} fusion(bf16[256,768]{1,0:T(8,128)(2,1)S(1)} %get-tuple-element.110, bf16[256,1536]{1,0:T(8,128)(2,1)S(1)} %all_gather.7, bf16[1536,768]{1,0:T(8,128)(2,1)S(1)} %copy-done), kind=kOutput, calls=%fused_computation | convolution fusion | flops 604569600 | bytes 3932160 | tf_op jit(solution)/shard_map/dot_general | solution.py:319
  (51 shorter events, 0.8 us)
Async XLA Ops:
  0.0 140.9 %copy-start = (bf16[1536,768]{1,0:T(8,128)(2,1)S(1)}, bf16[1536,768]{1,0:T(8,128)(2,1)}, u32[]{:S(2)}) copy-start(bf16[1536,768]{1,0:T(8,128)(2,1)} %param.22) | copy-start | bytes 7077892
  0.0 1.2 copy-start.7
  1.2 1.1 copy-start.8
  2.4 1.1 copy-start.3
  3.4 30.8 %all-to-all-start = ((bf16[4,192,768]{2,1,0:T(8,128)(2,1)}), bf16[4,192,768]{2,1,0:T(8,128)(2,1)S(1)}, u32[]{:S(2)}, u32[]{:S(2)}) async-start(bf16[4,192,768]{2,1,0:T(8,128)(2,1)} %copy-done.3), calls=%async_computation | async-start | bytes 2359296 | tf_op jit(solution)/shard_map/all_to_all | solution.py:332
  7.2 13.8 %copy-start.15 = (s32[64]{0:T(128)S(1)}, s32[64]{0:T(128)}, u32[]{:S(2)}) copy-start(s32[64]{0:T(128)} %lengths_ref.1) | copy-start | bytes 772
  7.2 27.0 %collective-permute-start = (bf16[96,3072]{1,0:T(8,128)(2,1)}, bf16[96,3072]{1,0:T(8,128)(2,1)}, u32[]{:S(2)}, u32[]{:S(2)}) collective-permute-start(bf16[96,3072]{1,0:T(8,128)(2,1)} %refs_0_.1), channel_id=1, source_target_pairs={{0,16},{16,0},{1,17},{17,1},{2,18},{18,2},{3,19},{19,3},{4,20},{20... | collective-permute-start | bytes 1769480 | tf_op jit(solution)/shard_map/ppermute | solution.py:328
  15.6 0.7 copy-start.10
  16.3 0.7 copy-start.12
  16.9 0.7 copy-start.17
  17.6 0.7 copy-start.18
  18.3 15.9 %collective-permute-start.1 = (bf16[128,1536]{1,0:T(8,128)(2,1)}, bf16[128,1536]{1,0:T(8,128)(2,1)}, u32[]{:S(2)}, u32[]{:S(2)}) collective-permute-start(bf16[128,1536]{1,0:T(8,128)(2,1)} %get-tuple-element.68.refs_0_), channel_id=1, source_target_pairs={{0,4},{4,0},{8,12},{12,8},{1,5},{5,1},{9,13},{13,9},{2,6},{6,2},{1... | collective-permute-start | bytes 1179656 | tf_op jit(solution)/shard_map/ppermute | solution.py:324
  23.4 1.0 copy-start.1
  34.2 26.2 %collective-permute-start.3 = (bf16[4,192,768]{2,1,0:T(8,128)(2,1)S(1)}, bf16[4,192,768]{2,1,0:T(8,128)(2,1)}, u32[]{:S(2)}, u32[]{:S(2)}) collective-permute-start(bf16[4,192,768]{2,1,0:T(8,128)(2,1)S(1)} %all-to-all-done.both_ref.refs_0_), channel_id=1, source_target_pairs={{0,2},{2,0},{1,3},{3,1},{4,6},{6,4},{5,7},{7,5},{8,10},{10,8},{9,1... | collective-permute-start | bytes 3538952 | tf_op jit(solution)/shard_map/ppermute | solution.py:328
  36.5 0.8 copy-start.6
  37.3 18.9 %all-to-all-start.1 = ((bf16[4,96,768]{2,1,0:T(8,128)(2,1)}), bf16[4,96,768]{2,1,0:T(8,128)(2,1)}, u32[]{:S(2)}, u32[]{:S(2)}) async-start(bf16[4,96,768]{2,1,0:T(8,128)(2,1)} %copy-done.6), calls=%async_computation.1 | async-start | bytes 1179648 | tf_op jit(solution)/shard_map/all_to_all | solution.py:332
  41.7 0.7 copy-start.16
  42.5 9.7 %collective-permute-start.4 = (bf16[2,96,768]{2,1,0:T(8,128)(2,1)S(1)}, bf16[2,96,768]{2,1,0:T(8,128)(2,1)}, u32[]{:S(2)}, u32[]{:S(2)}) collective-permute-start(bf16[2,96,768]{2,1,0:T(8,128)(2,1)S(1)} %get-tuple-element.72), channel_id=1, source_target_pairs={{0,16},{16,0},{1,17},{17,1},{2,18},{18,2},{3,19},{19,3},{4,20},{20... | collective-permute-start | bytes 884744 | tf_op jit(solution)/shard_map/ppermute | solution.py:328
  44.6 20.3 %collective-permute-start.2 = (bf16[128,1536]{1,0:T(8,128)(2,1)}, bf16[128,1536]{1,0:T(8,128)(2,1)}, u32[]{:S(2)}, u32[]{:S(2)}) collective-permute-start(bf16[128,1536]{1,0:T(8,128)(2,1)} %get-tuple-element.68.refs_0_), channel_id=1, source_target_pairs={{0,12},{4,8},{8,4},{12,0},{1,13},{5,9},{9,5},{13,1},{2,14},{6,10},... | collective-permute-start | bytes 1179656 | tf_op jit(solution)/shard_map/ppermute | solution.py:324
  60.5 15.2 %collective-permute-start.5 = (bf16[4,96,768]{2,1,0:T(8,128)(2,1)}, bf16[4,96,768]{2,1,0:T(8,128)(2,1)S(1)}, u32[]{:S(2)}, u32[]{:S(2)}) collective-permute-start(bf16[4,96,768]{2,1,0:T(8,128)(2,1)} %all-to-all-done.1.z_ref), channel_id=1, source_target_pairs={{0,2},{2,0},{1,3},{3,1},{4,6},{6,4},{5,7},{7,5},{8,10},{10,8},{9,1... | collective-permute-start | bytes 1769480 | tf_op jit(solution)/shard_map/ppermute | solution.py:328
  61.6 14.0 %collective-permute-start.6 = (bf16[2,96,768]{2,1,0:T(8,128)(2,1)}, bf16[2,96,768]{2,1,0:T(8,128)(2,1)S(1)}, u32[]{:S(2)}, u32[]{:S(2)}) collective-permute-start(bf16[2,96,768]{2,1,0:T(8,128)(2,1)} %copy-done.16), channel_id=1, source_target_pairs={{0,16},{16,0},{1,17},{17,1},{2,18},{18,2},{3,19},{19,3},{4,20},{20... | collective-permute-start | bytes 884744 | tf_op jit(solution)/shard_map/ppermute | solution.py:328
  64.9 6.6 %collective-permute-start.7 = (bf16[64,1536]{1,0:T(8,128)(2,1)}, bf16[64,1536]{1,0:T(8,128)(2,1)S(1)}, u32[]{:S(2)}, u32[]{:S(2)}) collective-permute-start(bf16[64,1536]{1,0:T(8,128)(2,1)} %copy-done.18), channel_id=1, source_target_pairs={{0,8},{4,12},{8,0},{12,4},{1,9},{5,13},{9,1},{13,5},{2,10},{6,14},... | collective-permute-start | bytes 589832 | tf_op jit(solution)/shard_map/ppermute | solution.py:324
  64.9 10.8 %collective-permute-start.8 = (bf16[64,1536]{1,0:T(8,128)(2,1)}, bf16[64,1536]{1,0:T(8,128)(2,1)S(1)}, u32[]{:S(2)}, u32[]{:S(2)}) collective-permute-start(bf16[64,1536]{1,0:T(8,128)(2,1)} %copy-done.17), channel_id=1, source_target_pairs={{0,8},{4,12},{8,0},{12,4},{1,9},{5,13},{9,1},{13,5},{2,10},{6,14},... | collective-permute-start | bytes 589832 | tf_op jit(solution)/shard_map/ppermute | solution.py:324
  77.0 10.1 %collective-permute-start.9 = (bf16[512,1536]{1,0:T(8,128)(2,1)S(1)}, bf16[512,1536]{1,0:T(8,128)(2,1)S(1)}, u32[]{:S(2)}, u32[]{:S(2)}) collective-permute-start(bf16[512,1536]{1,0:T(8,128)(2,1)S(1)} %shard_map.123.x_ref), channel_id=1, source_target_pairs={{0,1},{1,0},{2,3},{3,2},{4,5},{5,4},{6,7},{7,6},{8,9},{9,8},{10,11... | collective-permute-start | bytes 4718600 | tf_op jit(solution)/shard_map/ppermute | solution.py:328
  82.6 10.4 %collective-permute-start.10 = (bf16[2,96,768]{2,1,0:T(8,128)(2,1)}, bf16[2,96,768]{2,1,0:T(8,128)(2,1)S(1)}, u32[]{:S(2)}, u32[]{:S(2)}) collective-permute-start(bf16[2,96,768]{2,1,0:T(8,128)(2,1)} %collective-permute-done.4.refs_0_), channel_id=1, source_target_pairs={{0,2},{2,0},{1,3},{3,1},{4,6},{6,4},{5,7},{7,5},{8,10},{10,8},{9,1... | collective-permute-start | bytes 884744 | tf_op jit(solution)/shard_map/ppermute | solution.py:328
  82.9 14.8 %collective-permute-start.11 = (bf16[2,96,768]{2,1,0:T(8,128)(2,1)S(1)}, bf16[2,96,768]{2,1,0:T(8,128)(2,1)S(1)}, u32[]{:S(2)}, u32[]{:S(2)}) collective-permute-start(bf16[2,96,768]{2,1,0:T(8,128)(2,1)S(1)} %collective-permute-done.6.refs_1_), channel_id=1, source_target_pairs={{0,2},{2,0},{1,3},{3,1},{4,6},{6,4},{5,7},{7,5},{8,10},{10,8},{9,1... | collective-permute-start | bytes 884744 | tf_op jit(solution)/shard_map/ppermute | solution.py:328
  97.7 3.4 %collective-permute-start.12 = (bf16[512,768]{1,0:T(8,128)(2,1)S(1)}, bf16[512,768]{1,0:T(8,128)(2,1)S(1)}, u32[]{:S(2)}, u32[]{:S(2)}) collective-permute-start(bf16[512,768]{1,0:T(8,128)(2,1)S(1)} %get-tuple-element.89), channel_id=1, source_target_pairs={{0,1},{1,0},{2,3},{3,2},{4,5},{5,4},{6,7},{7,6},{8,9},{9,8},{10,11... | collective-permute-start | bytes 2359304 | tf_op jit(solution)/shard_map/ppermute | solution.py:328
  101.0 3.0 %collective-permute-start.17 = (bf16[512,768]{1,0:T(8,128)(2,1)S(1)}, bf16[512,768]{1,0:T(8,128)(2,1)S(1)}, u32[]{:S(2)}, u32[]{:S(2)}) collective-permute-start(bf16[512,768]{1,0:T(8,128)(2,1)S(1)} %get-tuple-element.97), channel_id=1, source_target_pairs={{0,1},{1,0},{2,3},{3,2},{4,5},{5,4},{6,7},{7,6},{8,9},{9,8},{10,11... | collective-permute-start | bytes 2359304 | tf_op jit(solution)/shard_map/ppermute | solution.py:328
  101.3 11.2 %copy-start.13 = (bf16[128,768]{1,0:T(8,128)(2,1)S(1)}, bf16[128,768]{1,0:T(8,128)(2,1)}, u32[]{:S(2)}) copy-start(bf16[128,768]{1,0:T(8,128)(2,1)} %copy-done.12) | copy-start | bytes 589828
  101.3 6.0 %collective-permute-start.13 = (bf16[128,768]{1,0:T(8,128)(2,1)S(1)}, bf16[128,768]{1,0:T(8,128)(2,1)S(1)}, u32[]{:S(2)}, u32[]{:S(2)}) collective-permute-start(bf16[128,768]{1,0:T(8,128)(2,1)S(1)} %get-tuple-element.91), channel_id=1, source_target_pairs={{0,4},{4,0},{8,12},{12,8},{1,5},{5,1},{9,13},{13,9},{2,6},{6,2},{1... | collective-permute-start | bytes 589832 | tf_op jit(solution)/shard_map/ppermute | solution.py:324
  101.9 5.7 %collective-permute-start.14 = (bf16[128,768]{1,0:T(8,128)(2,1)S(1)}, bf16[128,768]{1,0:T(8,128)(2,1)S(1)}, u32[]{:S(2)}, u32[]{:S(2)}) collective-permute-start(bf16[128,768]{1,0:T(8,128)(2,1)S(1)} %get-tuple-element.92), channel_id=1, source_target_pairs={{0,8},{4,12},{8,0},{12,4},{1,9},{5,13},{9,1},{13,5},{2,10},{6,14},... | collective-permute-start | bytes 589832 | tf_op jit(solution)/shard_map/ppermute | solution.py:324
  101.9 10.6 %collective-permute-start.15 = (bf16[128,768]{1,0:T(8,128)(2,1)S(1)}, bf16[128,768]{1,0:T(8,128)(2,1)S(1)}, u32[]{:S(2)}, u32[]{:S(2)}) collective-permute-start(bf16[128,768]{1,0:T(8,128)(2,1)S(1)} %get-tuple-element.93), channel_id=1, source_target_pairs={{0,12},{4,8},{8,4},{12,0},{1,13},{5,9},{9,5},{13,1},{2,14},{6,10},... | collective-permute-start | bytes 589832 | tf_op jit(solution)/shard_map/ppermute | solution.py:324
  104.0 16.9 %copy-start.11 = (bf16[128,768]{1,0:T(8,128)(2,1)S(1)}, bf16[128,768]{1,0:T(8,128)(2,1)}, u32[]{:S(2)}) copy-start(bf16[128,768]{1,0:T(8,128)(2,1)} %copy-done.10) | copy-start | bytes 589828
  104.0 19.8 %copy-start.5 = (bf16[1536,768]{1,0:T(8,128)(2,1)S(1)}, bf16[1536,768]{1,0:T(8,128)(2,1)}, u32[]{:S(2)}) copy-start(bf16[1536,768]{1,0:T(8,128)(2,1)} %gate_ref.1) | copy-start | bytes 7077892
  104.1 19.7 %copy-start.4 = (bf16[1536,768]{1,0:T(8,128)(2,1)S(1)}, bf16[1536,768]{1,0:T(8,128)(2,1)}, u32[]{:S(2)}) copy-start(bf16[1536,768]{1,0:T(8,128)(2,1)} %value_ref.1) | copy-start | bytes 7077892
  104.2 19.7 %copy-start.14 = (f32[1,1536]{1,0:T(1,128)S(1)}, f32[1,1536]{1,0:T(1,128)}, u32[]{:S(2)}) copy-start(f32[1,1536]{1,0:T(1,128)} %broadcast_in_dim.17.gain_ref) | copy-start | bytes 18436
  104.2 11.6 %collective-permute-start.18 = (bf16[128,768]{1,0:T(8,128)(2,1)S(1)}, bf16[128,768]{1,0:T(8,128)(2,1)S(1)}, u32[]{:S(2)}, u32[]{:S(2)}) collective-permute-start(bf16[128,768]{1,0:T(8,128)(2,1)S(1)} %get-tuple-element.99), channel_id=1, source_target_pairs={{0,4},{4,0},{8,12},{12,8},{1,5},{5,1},{9,13},{13,9},{2,6},{6,2},{1... | collective-permute-start | bytes 589832 | tf_op jit(solution)/shard_map/ppermute | solution.py:324
  104.7 11.3 %collective-permute-start.19 = (bf16[128,768]{1,0:T(8,128)(2,1)S(1)}, bf16[128,768]{1,0:T(8,128)(2,1)S(1)}, u32[]{:S(2)}, u32[]{:S(2)}) collective-permute-start(bf16[128,768]{1,0:T(8,128)(2,1)S(1)} %get-tuple-element.100), channel_id=1, source_target_pairs={{0,8},{4,12},{8,0},{12,4},{1,9},{5,13},{9,1},{13,5},{2,10},{6,14},... | collective-permute-start | bytes 589832 | tf_op jit(solution)/shard_map/ppermute | solution.py:324
  107.3 13.6 %collective-permute-start.20 = (bf16[128,768]{1,0:T(8,128)(2,1)S(1)}, bf16[128,768]{1,0:T(8,128)(2,1)S(1)}, u32[]{:S(2)}, u32[]{:S(2)}) collective-permute-start(bf16[128,768]{1,0:T(8,128)(2,1)S(1)} %get-tuple-element.101), channel_id=1, source_target_pairs={{0,12},{4,8},{8,4},{12,0},{1,13},{5,9},{9,5},{13,1},{2,14},{6,10},... | collective-permute-start | bytes 589832 | tf_op jit(solution)/shard_map/ppermute | solution.py:324
  112.6 8.3 %collective-permute-start.16 = (bf16[128,768]{1,0:T(8,128)(2,1)S(1)}, bf16[128,768]{1,0:T(8,128)(2,1)S(1)}, u32[]{:S(2)}, u32[]{:S(2)}) collective-permute-start(bf16[128,768]{1,0:T(8,128)(2,1)S(1)} %shard_map.128.near_ref), channel_id=1, source_target_pairs={{0,1},{1,0},{2,3},{3,2},{4,5},{5,4},{6,7},{7,6},{8,9},{9,8},{10,11... | collective-permute-start | bytes 589832 | tf_op jit(solution)/shard_map/ppermute | solution.py:328
  121.0 11.7 %copy-start.2 = (s32[8,280,128]{2,1,0:T(8,128)S(1)}, s32[8,280,128]{2,1,0:T(8,128)}, u32[]{:S(2)}) copy-start(s32[8,280,128]{2,1,0:T(8,128)} %copy-done.1) | copy-start | bytes 3440644
  121.0 11.7 %copy-start.9 = (f32[32,768]{1,0:T(8,128)S(1)}, f32[32,768]{1,0:T(8,128)}, u32[]{:S(2)}) copy-start(f32[32,768]{1,0:T(8,128)} %taps_ref.3) | copy-start | bytes 294916
  121.0 2.8 %collective-permute-start.21 = (bf16[128,768]{1,0:T(8,128)(2,1)S(1)}, bf16[128,768]{1,0:T(8,128)(2,1)S(1)}, u32[]{:S(2)}, u32[]{:S(2)}) collective-permute-start(bf16[128,768]{1,0:T(8,128)(2,1)S(1)} %shard_map.131.far_ref), channel_id=1, source_target_pairs={{0,1},{1,0},{2,3},{3,2},{4,5},{5,4},{6,7},{7,6},{8,9},{9,8},{10,11... | collective-permute-start | bytes 589832 | tf_op jit(solution)/shard_map/ppermute | solution.py:328
  126.3 10.8 %collective-permute-start.22 = (bf16[16,768]{1,0:T(8,128)(2,1)S(1)}, bf16[16,768]{1,0:T(8,128)(2,1)S(1)}, u32[]{:S(2)}, u32[]{:S(2)}) collective-permute-start(bf16[16,768]{1,0:T(8,128)(2,1)S(1)} %get-tuple-element.115), channel_id=1, source_target_pairs={{0,2},{2,4},{4,6},{6,8},{8,10},{10,12},{12,14},{14,16},{16,18},{18... | collective-permute-start | bytes 73736 | tf_op jit(solution)/shard_map/ppermute | solution.py:299
  128.5 8.6 %collective-permute-start.23 = (bf16[16,768]{1,0:T(8,128)(2,1)S(1)}, bf16[16,768]{1,0:T(8,128)(2,1)S(1)}, u32[]{:S(2)}, u32[]{:S(2)}) collective-permute-start(bf16[16,768]{1,0:T(8,128)(2,1)S(1)} %get-tuple-element.116), channel_id=1, source_target_pairs={{2,0},{4,2},{6,4},{8,6},{10,8},{12,10},{14,12},{16,14},{18,16},{20... | collective-permute-start | bytes 73736 | tf_op jit(solution)/shard_map/ppermute | solution.py:300

commit v6 on v5

--- a/solution.py
+++ b/solution.py
@@ -74,19 +74,18 @@
 
 
 GROUP = ("bh", "bl")
-VMEM_LIMIT = 40 * 2**20
 VMEM = pl.BlockSpec(memory_space=pltpu.VMEM)
 SMEM = pl.BlockSpec(memory_space=pltpu.SMEM)
 
 
-def kernel_call(body, outs, ins, scratch=(), scalars=0, flops=0, moved=0):
+def kernel_call(body, outs, ins, scratch=(), scalars=0, flops=0, moved=0, limit=40):
     return pl.pallas_call(
         body,
         out_shape=[jax.ShapeDtypeStruct(shape, dtype) for shape, dtype in outs],
         in_specs=[SMEM] * scalars + [VMEM] * (len(ins) - scalars),
         out_specs=[VMEM] * len(outs),
         scratch_shapes=list(scratch),
-        compiler_params=pltpu.CompilerParams(vmem_limit_bytes=VMEM_LIMIT),
+        compiler_params=pltpu.CompilerParams(vmem_limit_bytes=limit * 2**20),
         cost_estimate=pl.CostEstimate(flops=flops, bytes_accessed=moved, transcendentals=0),
     )(*ins)
 
@@ -117,23 +116,18 @@
     second_ref[...] = both_ref[half:, skip:, :]
 
 
-def norm_kernel(me_ref, whole_ref, gain_ref, near_ref, far_ref, out_ref, upper_ref, lower_ref):
+def norm_kernel(me_ref, whole_ref, gain_ref, near_ref, far_ref, out_ref):
     rows, width = near_ref.shape
     at = pl.ds(pl.multiple_of(me_ref[1] * rows, rows), rows)
     for place, ref in ((me_ref[2], near_ref), (1 - me_ref[2], far_ref)):
         ref[...] = whole_ref[at, pl.ds(pl.multiple_of(place * width, width), width)]
-    normed = norm_rows(f32(whole_ref[at, :]), gain_ref[...]).astype(jnp.bfloat16)
-    out_ref[...] = normed
-    upper_ref[...] = normed[: rows // 2]
-    lower_ref[...] = normed[rows // 2 :]
-
-
-def join_kernel(*refs):
-    *pieces, out_ref = refs
-    at = 0
-    for piece in pieces:
-        out_ref[at : at + piece.shape[0]] = piece[...]
-        at += piece.shape[0]
+    out_ref[...] = norm_rows(f32(whole_ref[at, :]), gain_ref[...]).astype(jnp.bfloat16)
+
+
+def part_rows_kernel(ref, first_ref, second_ref):
+    half = first_ref.shape[0]
+    first_ref[...] = ref[:half]
+    second_ref[...] = ref[half:]
 
 
 def interleave(full_ref, base, block, own_refs, other_refs, me_l, last=False):
@@ -145,11 +139,16 @@
             full_ref[pl.ds(at, block), :] = ref[j, skip : skip + block, :]
 
 
-def hidden_kernel(me_ref, x_ref, both_ref, both_x_ref, z_ref, zx_ref, h_ref, w_ref):
+def hidden_kernel(n_x, me_ref, *refs):
+    pieces, (both_ref, both_x_ref, z_ref, zx_ref, h_ref, w_ref, x_ref) = refs[:n_x], refs[n_x:]
     me_l, me_a = me_ref[0], me_ref[2]
     part, block = w_ref.shape[0] // 2, z_ref.shape[1]
     interleave(w_ref, me_a * part, block, [both_ref], [both_x_ref], me_l)
     interleave(w_ref, (1 - me_a) * part, block, [z_ref], [zx_ref], me_l)
+    at = 0
+    for piece in pieces:
+        x_ref[at : at + piece.shape[0], :] = piece[...]
+        at += piece.shape[0]
     step = 256
     for at in range(0, x_ref.shape[0], step):
         pre = jnp.dot(x_ref[at : at + step, :], w_ref[...], preferred_element_type=jnp.float32)
@@ -345,48 +344,47 @@
 
     block, pair = (4, shard, units), (2, shard, units)
     in_far = swap(w_in, "ah")
-    (both,) = kernel_call(cut_kernel, [((4, 2 * shard, units), bf16)], [w_in, w_out.T])
+    (both,) = kernel_call(cut_kernel, [((4, 2 * shard, units), bf16)], [w_in, w_out.T], limit=60)
     both = recut(both)
     whole = lax.all_gather(tokens, "hid", axis=1, tiled=True)
-    *mine, normed, upper, lower = kernel_call(
+    *mine, normed = kernel_call(
         norm_kernel,
-        [((half, width), bf16)] * 2 + [((half, wide), bf16)] + [((half // 2, wide), bf16)] * 2,
+        [((half, width), bf16)] * 2 + [((half, wide), bf16)],
         [me, whole, ffn_gain[None, :]],
         scalars=1,
     )
     frames1 = partner(normed, 1)
-    in_far, both, normed, upper, lower, frames1, early = tie(
-        (in_far, both, normed, upper, lower, frames1, early)
-    )
+    in_far, both, normed, frames1, early = tie((in_far, both, normed, frames1, early))
     both_x = swap(both, "al")
     (in_z,) = kernel_call(cut_kernel, [(block, bf16)], [in_far])
     in_z = recut(in_z)
     out_1, out_2 = kernel_call(part_kernel, [(pair, bf16)] * 2, [both])
     out_z1 = swap(out_1, "ah")
-    frames3 = partner(normed, 3)
-    both_x, in_z, out_z1, out_2 = tie((both_x, in_z, out_z1, out_2))
+    frames2 = partner(normed, 2)
+    normed_oth, frames1_oth = swap(normed, "hid"), swap(frames1, "hid")
+    both_x, in_z, out_z1, out_2, normed_oth, frames1_oth = tie(
+        (both_x, in_z, out_z1, out_2, normed_oth, frames1_oth)
+    )
     in_zx = swap(in_z, "al")
     out_z2 = swap(out_2, "ah")
-    normed, upper, lower, frames3 = tie((normed, upper, lower, frames3))
-    frames2 = [partner(upper, 2), partner(lower, 2)]
-    in_zx, out_z1, out_z2, frames2 = tie((in_zx, out_z1, out_z2, frames2))
+    upper, lower = kernel_call(part_rows_kernel, [((half // 2, wide), bf16)] * 2, [frames2])
+    frames3 = [partner(upper, 1), partner(lower, 1)]
+    in_zx, out_z1, out_z2, frames3 = tie((in_zx, out_z1, out_z2, frames3))
     out_zx1 = swap(out_z1, "al")
     out_zx2 = swap(out_z2, "al")
-    (x_own,) = kernel_call(
-        join_kernel, [((4 * half, wide), bf16)], [normed, frames1, *frames2, frames3]
-    )
-    x_oth = swap(x_own, "hid")
-
-    def units_of(x):
+    own = [normed, frames1, frames2, *frames3]
+    others = [normed_oth, frames1_oth] + [swap(v, "hid") for v in own[2:]]
+
+    def units_of(pieces):
         return kernel_call(
-            hidden_kernel,
+            functools.partial(hidden_kernel, len(pieces)),
             [((4 * half, units), bf16)],
-            [me, x, both, both_x, in_z, in_zx],
-            scratch=[pltpu.VMEM((wide, units), bf16)],
+            [me, *pieces, both, both_x, in_z, in_zx],
+            scratch=[pltpu.VMEM((wide, units), bf16), pltpu.VMEM((4 * half, wide), bf16)],
             scalars=1,
         )[0]
 
-    hidden = [units_of(x_own), units_of(x_oth)]
+    hidden = [units_of(own), units_of(others)]
 
     def products(own, other):
         return kernel_call(

time: 144 us -> 137 us (0.951)
  waiting for transfers between devices: 55.2 us -> 36.5 us
  starting transfers between devices: 40.6 us -> 51.9 us
  local copies, waits for them, and re-layouts: 12 us -> 9.56 us
  Pallas kernels: 26.2 us -> 28.3 us
    ppermute x10, waiting for transfers between devices: 35.2 us -> 22 us  [partner(): return lax.ppermute(values, GROUP, [(i, i ^ step) for i in range(4)])]
    ppermute x12 -> x16, starting transfers between devices: 19.7 us -> 25.8 us  [swap(): return lax.ppermute(values, axis, SWAP)]
    ppermute x10, starting transfers between devices: 6.46 us -> 11.2 us  [partner(): return lax.ppermute(values, GROUP, [(i, i ^ step) for i in range(4)])]
    all_to_all x2, waiting for transfers between devices: 4.07 us -> 1.01 us  [recut(): return lax.all_to_all(parts, GROUP, 0, 0)]
    unnamed x38 -> x40, local copies, waits for them, and re-layouts: 8.65 us -> 6.18 us
    ppermute x12 -> x16, waiting for transfers between devices: 15.9 us -> 13.5 us  [swap(): return lax.ppermute(values, axis, SWAP)]
    pallas_call x17, Pallas kernels: 26.2 us -> 28.3 us  [kernel_call(): pl.pallas_call(body, out_shape=[jax.ShapeDtypeStruct(shape, dtype) for sh...]
  transfers between devices with their start and end apart: 26 -> 30, of which waited for: 15 -> 10; matrix products, arithmetic and copies ran while one was open for 2% -> 3% of each run, Pallas kernels for 15% -> 17%
where the time goes in v6:
time: 137 us; the launch traced here: 135 us
  starting transfers between devices  51.9 us (38%)
  waiting for transfers between devices  36.5 us (27%)
  Pallas kernels  28.3 us (21%)
  local copies, waits for them, and re-layouts  9.56 us (7%)
  blocking collectives  6.64 us (5%)
  matrix products  1.52 us (1%)
    pallas_call x17, Pallas kernels, kernel_call(): pl.pallas_call(body, out_shape=[jax.ShapeDtypeStruct(shape, dtype) for sh...  28.3 us
    ppermute x16, starting transfers between devices, swap(): return lax.ppermute(values, axis, SWAP)  25.8 us
    ppermute x10, waiting for transfers between devices, partner(): return lax.ppermute(values, GROUP, [(i, i ^ step) for i in range(4)])  22 us
    ppermute x16, waiting for transfers between devices, swap(): return lax.ppermute(values, axis, SWAP)  13.5 us
    ppermute x10, starting transfers between devices, partner(): return lax.ppermute(values, GROUP, [(i, i ^ step) for i in range(4)])  11.2 us
    all_to_all x2, starting transfers between devices, recut(): return lax.all_to_all(parts, GROUP, 0, 0)  8.56 us
    unnamed x40, local copies, waits for them, and re-layouts  6.18 us
    all_gather x1, blocking collectives, grouped_ffn(): whole = lax.all_gather(tokens, 'hid', axis=1, tiled=True)  3.71 us
  transfers between devices with their start and end apart: 30, of which 10 were waited for; matrix products, arithmetic and copies ran while one was open for 3% of the time, Pallas kernels for 17%

profile of v6, /device:TPU:5, one launch (start us, length us, event | category | flops | bytes accessed | tf_op | source)
XLA Modules:
  0.0 134.9 jit_solution(3567581436373102079)
XLA Ops:
  0.0 2.5 %shard_map.119 = bf16[4,192,768]{2,1,0:T(8,128)(2,1)} custom-call(bf16[96,3072]{1,0:T(8,128)(2,1)} %refs_0_.1, bf16[96,3072]{1,0:T(8,128)(2,1)} %bitcast.7), custom_call_target="tpu_custom_call" | custom-call | tf_op jit(solution)/shard_map/pallas_call | solution.py:82
  2.5 3.9 %all-to-all-start = ((bf16[4,192,768]{2,1,0:T(8,128)(2,1)}), bf16[4,192,768]{2,1,0:T(8,128)(2,1)S(1)}, u32[]{:S(2)}, u32[]{:S(2)}) async-start(bf16[4,192,768]{2,1,0:T(8,128)(2,1)} %shard_map.119), calls=%async_computation | async-start | bytes 2359296 | tf_op jit(solution)/shard_map/all_to_all | solution.py:331
  6.4 2.3 %collective-permute-start = (bf16[96,3072]{1,0:T(8,128)(2,1)}, bf16[96,3072]{1,0:T(8,128)(2,1)}, u32[]{:S(2)}, u32[]{:S(2)}) collective-permute-start(bf16[96,3072]{1,0:T(8,128)(2,1)} %refs_0_.1), channel_id=1, source_target_pairs={{0,16},{16,0},{1,17},{17,1},{2,18},{18,2},{3,19},{19,3},{4,20},{20... | collective-permute-start | bytes 1769480 | tf_op jit(solution)/shard_map/ppermute | solution.py:327
  8.7 0.7 broadcast_in_dim.15.gain_ref
  9.5 3.7 %all_gather.6.whole_ref = bf16[256,1536]{1,0:T(8,128)(2,1)S(1)} all-gather(bf16[256,768]{1,0:T(8,128)(2,1)} %param.12), channel_id=1, replica_groups=mesh['ah'=2,'bh'=2,'bl'=2,'al'=2,'hid'=2] {'hid'}, dimensions={1}, use_global_device_ids=true | all-gather | bytes 1179648 | tf_op jit(solution)/shard_map/all_gather | solution.py:349
  13.2 1.6 %shard_map.118 = (bf16[128,768]{1,0:T(8,128)(2,1)S(1)}, bf16[128,768]{1,0:T(8,128)(2,1)S(1)}, bf16[128,1536]{1,0:T(8,128)(2,1)}) custom-call(s32[3]{0:T(128)S(1)} %pad_add_fusion.me_ref, bf16[256,1536]{1,0:T(8,128)(2,1)S(1)} %all_gather.6.whole_ref, f32[1,1536]{1,0:T(1,128)S(1)} %broadcast_in_dim.15.gain_ref), custom_call_target="tpu_custom_call" | custom-call | tf_op jit(solution)/shard_map/pallas_call | solution.py:82
  14.8 0.7 copy-done.13
  15.5 0.7 copy-done.15
  16.2 1.3 broadcast_in_dim.17.gain_ref
  17.5 0.7 broadcast_in_dim.18.scale_ref
  18.2 0.7 broadcast_in_dim.19.shift_ref
  18.9 2.4 %shard_map.120.utter_ref = s32[8,280,128]{2,1,0:T(8,128)S(1)} custom-call(s32[1]{0:T(128)} %bitcast.4.first_ref, s32[64]{0:T(128)S(1)} %copy-done.18), custom_call_target="tpu_custom_call" | custom-call | tf_op jit(solution)/shard_map/pallas_call | solution.py:82
  21.3 1.0 copy-done.1
  22.3 9.8 %collective-permute-done.1.refs_1_ = bf16[128,1536]{1,0:T(8,128)(2,1)} collective-permute-done((bf16[128,1536]{1,0:T(8,128)(2,1)}, bf16[128,1536]{1,0:T(8,128)(2,1)}, u32[]{:S(2)}, u32[]{:S(2)}) %collective-permute-start.1) | collective-permute-done | bytes 393248 | tf_op jit(solution)/shard_map/ppermute | solution.py:323
  32.1 1.0 all-to-all-done.both_ref.refs_5_.refs_0_
  33.1 1.2 collective-permute-start.3
  34.3 1.1 shard_map.121
  35.4 0.8 copy-done.5
  36.3 4.7 %all-to-all-start.1 = ((bf16[4,96,768]{2,1,0:T(8,128)(2,1)}), bf16[4,96,768]{2,1,0:T(8,128)(2,1)}, u32[]{:S(2)}, u32[]{:S(2)}) async-start(bf16[4,96,768]{2,1,0:T(8,128)(2,1)} %copy-done.5), calls=%async_computation.1 | async-start | bytes 1179648 | tf_op jit(solution)/shard_map/all_to_all | solution.py:331
  40.9 2.7 %collective-permute-start.5 = (bf16[128,1536]{1,0:T(8,128)(2,1)}, bf16[128,1536]{1,0:T(8,128)(2,1)S(1)}, u32[]{:S(2)}, u32[]{:S(2)}) collective-permute-start(bf16[128,1536]{1,0:T(8,128)(2,1)} %get-tuple-element.59.refs_0_), channel_id=1, source_target_pairs={{0,1},{1,0},{2,3},{3,2},{4,5},{5,4},{6,7},{7,6},{8,9},{9,8},{10,11... | collective-permute-start | bytes 1179656 | tf_op jit(solution)/shard_map/ppermute | solution.py:327
  43.7 0.7 copy-done.19
  44.4 2.4 %collective-permute-start.4 = (bf16[2,96,768]{2,1,0:T(8,128)(2,1)S(1)}, bf16[2,96,768]{2,1,0:T(8,128)(2,1)S(1)}, u32[]{:S(2)}, u32[]{:S(2)}) collective-permute-start(bf16[2,96,768]{2,1,0:T(8,128)(2,1)S(1)} %get-tuple-element.63), channel_id=1, source_target_pairs={{0,16},{16,0},{1,17},{17,1},{2,18},{18,2},{3,19},{19,3},{4,20},{20... | collective-permute-start | bytes 884744 | tf_op jit(solution)/shard_map/ppermute | solution.py:327
  46.8 1.3 collective-permute-start.2
  48.0 10.2 %collective-permute-done.4.refs_0_ = bf16[2,96,768]{2,1,0:T(8,128)(2,1)S(1)} collective-permute-done((bf16[2,96,768]{2,1,0:T(8,128)(2,1)S(1)}, bf16[2,96,768]{2,1,0:T(8,128)(2,1)S(1)}, u32[]{:S(2)}, u32[]{:S(2)}) %collective-permute-start.4) | collective-permute-done | bytes 294944 | tf_op jit(solution)/shard_map/ppermute | solution.py:327
  58.2 0.7 copy-done.11
  58.9 0.8 copy-done.7
  59.7 0.8 copy-done.9
  60.4 0.3 collective-permute-start.7
  60.7 0.4 collective-permute-start.8
  61.1 1.9 %collective-permute-done.2.ref.refs_2_ = bf16[128,1536]{1,0:T(8,128)(2,1)} collective-permute-done((bf16[128,1536]{1,0:T(8,128)(2,1)}, bf16[128,1536]{1,0:T(8,128)(2,1)}, u32[]{:S(2)}, u32[]{:S(2)}) %collective-permute-start.2) | collective-permute-done | bytes 393248 | tf_op jit(solution)/shard_map/ppermute | solution.py:323
  63.0 1.0 shard_map.123
  64.0 0.2 collective-permute-start.9
  64.2 1.4 %collective-permute-start.10 = (bf16[64,1536]{1,0:T(8,128)(2,1)S(1)}, bf16[64,1536]{1,0:T(8,128)(2,1)S(1)}, u32[]{:S(2)}, u32[]{:S(2)}) collective-permute-start(bf16[64,1536]{1,0:T(8,128)(2,1)S(1)} %get-tuple-element.69), channel_id=1, source_target_pairs={{0,4},{4,0},{8,12},{12,8},{1,5},{5,1},{9,13},{13,9},{2,6},{6,2},{1... | collective-permute-start | bytes 589832 | tf_op jit(solution)/shard_map/ppermute | solution.py:323
  65.6 6.3 %collective-permute-start.11 = (bf16[128,1536]{1,0:T(8,128)(2,1)}, bf16[128,1536]{1,0:T(8,128)(2,1)S(1)}, u32[]{:S(2)}, u32[]{:S(2)}) collective-permute-start(bf16[128,1536]{1,0:T(8,128)(2,1)} %collective-permute-done.2.ref.refs_2_), channel_id=1, source_target_pairs={{0,1},{1,0},{2,3},{3,2},{4,5},{5,4},{6,7},{7,6},{8,9},{9,8},{10,11... | collective-permute-start | bytes 1179656 | tf_op jit(solution)/shard_map/ppermute | solution.py:327
  71.9 2.3 %collective-permute-done.8.refs_1_ = bf16[2,96,768]{2,1,0:T(8,128)(2,1)S(1)} collective-permute-done((bf16[2,96,768]{2,1,0:T(8,128)(2,1)}, bf16[2,96,768]{2,1,0:T(8,128)(2,1)S(1)}, u32[]{:S(2)}, u32[]{:S(2)}) %collective-permute-start.8) | collective-permute-done | bytes 294944 | tf_op jit(solution)/shard_map/ppermute | solution.py:327
  74.2 1.1 collective-permute-start.14
  75.3 0.3 collective-permute-start.15
  75.6 4.0 %collective-permute-start.12 = (bf16[64,1536]{1,0:T(8,128)(2,1)S(1)}, bf16[64,1536]{1,0:T(8,128)(2,1)S(1)}, u32[]{:S(2)}, u32[]{:S(2)}) collective-permute-start(bf16[64,1536]{1,0:T(8,128)(2,1)S(1)} %collective-permute-done.9.refs_3_), channel_id=1, source_target_pairs={{0,1},{1,0},{2,3},{3,2},{4,5},{5,4},{6,7},{7,6},{8,9},{9,8},{10,11... | collective-permute-start | bytes 589832 | tf_op jit(solution)/shard_map/ppermute | solution.py:327
  79.7 3.4 %shard_map.124.own_ref = bf16[512,768]{1,0:T(8,128)(2,1)S(1)} custom-call(s32[3]{0:T(128)S(1)} %pad_add_fusion.me_ref, bf16[128,1536]{1,0:T(8,128)(2,1)} %get-tuple-element.59.refs_0_, bf16[128,1536]{1,0:T(8,128)(2,1)} %collective-permute-done.1.refs_1_, bf16[128,1536]{1,0:T(8,128)(2,1)} %collective-permute-done.2.ref.refs_2_, ...), custom_call_target="tpu_custom_call" | custom-call | tf_op jit(solution)/shard_map/pallas_call | solution.py:82
  83.2 3.1 %shard_map.125.oth_ref = bf16[512,768]{1,0:T(8,128)(2,1)S(1)} custom-call(s32[3]{0:T(128)S(1)} %pad_add_fusion.me_ref, bf16[128,1536]{1,0:T(8,128)(2,1)S(1)} %copy-done.8, bf16[128,1536]{1,0:T(8,128)(2,1)S(1)} %copy-done.10, bf16[128,1536]{1,0:T(8,128)(2,1)S(1)} %collective-permute-done.11.refs_2_, bf16[64,1536]{1,0:T(8,128)(2,1)S(1)} %collective-permute-done.12.refs_3_, ...), custom_call_target="tpu_custom_call" | custom-call | tf_op jit(solution)/shard_map/pallas_call | solution.py:82
  86.2 2.8 %shard_map.126 = (f32[512,768]{1,0:T(8,128)S(1)}, bf16[512,768]{1,0:T(8,128)(2,1)S(1)}) custom-call(s32[3]{0:T(128)S(1)} %pad_add_fusion.me_ref, bf16[512,768]{1,0:T(8,128)(2,1)S(1)} %shard_map.124.own_ref, bf16[512,768]{1,0:T(8,128)(2,1)S(1)} %shard_map.125.oth_ref, bf16[4,192,768]{2,1,0:T(8,128)(2,1)S(1)} %all-to-all-done.both_ref.refs_5_.refs_0_, ...), custom_call_target="tpu_custom_call" | custom-call | tf_op jit(solution)/shard_map/pallas_call | solution.py:82
  89.1 1.0 collective-permute-start.16
  90.1 2.0 %shard_map.129 = (f32[512,768]{1,0:T(8,128)S(1)}, bf16[512,768]{1,0:T(8,128)(2,1)S(1)}) custom-call(s32[3]{0:T(128)S(1)} %pad_add_fusion.me_ref, bf16[512,768]{1,0:T(8,128)(2,1)S(1)} %shard_map.124.own_ref, bf16[512,768]{1,0:T(8,128)(2,1)S(1)} %shard_map.125.oth_ref, bf16[2,96,768]{2,1,0:T(8,128)(2,1)S(1)} %copy-done.12, ...), custom_call_target="tpu_custom_call" | custom-call | tf_op jit(solution)/shard_map/pallas_call | solution.py:82
  92.3 0.1 shard_map.127
  92.4 0.2 collective-permute-start.17
  92.6 2.7 %collective-permute-start.18 = (bf16[128,768]{1,0:T(8,128)(2,1)S(1)}, bf16[128,768]{1,0:T(8,128)(2,1)S(1)}, u32[]{:S(2)}, u32[]{:S(2)}) collective-permute-start(bf16[128,768]{1,0:T(8,128)(2,1)S(1)} %get-tuple-element.84), channel_id=1, source_target_pairs={{0,8},{4,12},{8,0},{12,4},{1,9},{5,13},{9,1},{13,5},{2,10},{6,14},... | collective-permute-start | bytes 589832 | tf_op jit(solution)/shard_map/ppermute | solution.py:323
  95.3 1.1 collective-permute-start.19
  96.6 0.4 collective-permute-start.22
  96.9 1.2 collective-permute-start.23
  98.2 0.3 collective-permute-done.17.refs_0_
  98.5 2.7 %collective-permute-start.24 = (bf16[128,768]{1,0:T(8,128)(2,1)S(1)}, bf16[128,768]{1,0:T(8,128)(2,1)S(1)}, u32[]{:S(2)}, u32[]{:S(2)}) collective-permute-start(bf16[128,768]{1,0:T(8,128)(2,1)S(1)} %get-tuple-element.93), channel_id=1, source_target_pairs={{0,12},{4,8},{8,4},{12,0},{1,13},{5,9},{9,5},{13,1},{2,14},{6,10},... | collective-permute-start | bytes 589832 | tf_op jit(solution)/shard_map/ppermute | solution.py:323
  101.2 4.0 %collective-permute-done.19.refs_2_ = bf16[128,768]{1,0:T(8,128)(2,1)S(1)} collective-permute-done((bf16[128,768]{1,0:T(8,128)(2,1)S(1)}, bf16[128,768]{1,0:T(8,128)(2,1)S(1)}, u32[]{:S(2)}, u32[]{:S(2)}) %collective-permute-start.19) | collective-permute-done | bytes 196640 | tf_op jit(solution)/shard_map/ppermute | solution.py:323
  105.3 2.3 %collective-permute-start.20 = (bf16[128,768]{1,0:T(8,128)(2,1)S(1)}, bf16[128,768]{1,0:T(8,128)(2,1)S(1)}, u32[]{:S(2)}, u32[]{:S(2)}) collective-permute-start(bf16[128,768]{1,0:T(8,128)(2,1)S(1)} %shard_map.128.near_ref), channel_id=1, source_target_pairs={{0,1},{1,0},{2,3},{3,2},{4,5},{5,4},{6,7},{7,6},{8,9},{9,8},{10,11... | collective-permute-start | bytes 589832 | tf_op jit(solution)/shard_map/ppermute | solution.py:327
  107.7 1.0 collective-permute-done.23.refs_1_
  108.6 5.0 %collective-permute-done.24.refs_2_ = bf16[128,768]{1,0:T(8,128)(2,1)S(1)} collective-permute-done((bf16[128,768]{1,0:T(8,128)(2,1)S(1)}, bf16[128,768]{1,0:T(8,128)(2,1)S(1)}, u32[]{:S(2)}, u32[]{:S(2)}) %collective-permute-start.24) | collective-permute-done | bytes 196640 | tf_op jit(solution)/shard_map/ppermute | solution.py:323
  113.8 1.4 %collective-permute-start.25 = (bf16[128,768]{1,0:T(8,128)(2,1)S(1)}, bf16[128,768]{1,0:T(8,128)(2,1)S(1)}, u32[]{:S(2)}, u32[]{:S(2)}) collective-permute-start(bf16[128,768]{1,0:T(8,128)(2,1)S(1)} %shard_map.131.far_ref), channel_id=1, source_target_pairs={{0,1},{1,0},{2,3},{3,2},{4,5},{5,4},{6,7},{7,6},{8,9},{9,8},{10,11... | collective-permute-start | bytes 589832 | tf_op jit(solution)/shard_map/ppermute | solution.py:327
  115.2 1.1 collective-permute-done.25.far_oth_ref
  116.2 2.5 %shard_map.132 = (bf16[256,768]{1,0:T(8,128)(2,1)S(1)}, bf16[16,768]{1,0:T(8,128)(2,1)S(1)}, bf16[16,768]{1,0:T(8,128)(2,1)S(1)}, bf16[256,768]{1,0:T(8,128)(2,1)S(1)}) custom-call(s32[3]{0:T(128)S(1)} %pad_add_fusion.me_ref, bf16[128,768]{1,0:T(8,128)(2,1)S(1)} %shard_map.128.near_ref, bf16[128,768]{1,0:T(8,128)(2,1)S(1)} %collective-permute-done.20.near_oth_ref, ...), custom_call_target="tpu_custom_call" | custom-call | flops 1207959552 | bytes 4718592 | tf_op jit(solution)/shard_map/pallas_call | solution.py:82
  118.7 2.9 %collective-permute-start.26 = (bf16[16,768]{1,0:T(8,128)(2,1)S(1)}, bf16[16,768]{1,0:T(8,128)(2,1)S(1)}, u32[]{:S(2)}, u32[]{:S(2)}) collective-permute-start(bf16[16,768]{1,0:T(8,128)(2,1)S(1)} %get-tuple-element.107), channel_id=1, source_target_pairs={{0,2},{2,4},{4,6},{6,8},{8,10},{10,12},{12,14},{14,16},{16,18},{18... | collective-permute-start | bytes 73736 | tf_op jit(solution)/shard_map/ppermute | solution.py:298
  121.6 3.5 %collective-permute-start.27 = (bf16[16,768]{1,0:T(8,128)(2,1)S(1)}, bf16[16,768]{1,0:T(8,128)(2,1)S(1)}, u32[]{:S(2)}, u32[]{:S(2)}) collective-permute-start(bf16[16,768]{1,0:T(8,128)(2,1)S(1)} %get-tuple-element.108), channel_id=1, source_target_pairs={{2,0},{4,2},{6,4},{8,6},{10,8},{12,10},{14,12},{16,14},{18,16},{20... | collective-permute-start | bytes 73736 | tf_op jit(solution)/shard_map/ppermute | solution.py:299
  125.1 4.4 %shard_map.133.act_ref = bf16[256,768]{1,0:T(8,128)(2,1)S(1)} custom-call(bf16[256,768]{1,0:T(8,128)(2,1)S(1)} %get-tuple-element.103.glu_ref, s32[8,280,128]{2,1,0:T(8,128)S(1)} %copy-done.2, f32[32,768]{1,0:T(8,128)S(1)} %copy-done.6, f32[1,768]{1,0:T(1,128)S(1)} %broadcast_in_dim.18.scale_ref, f32[1,768]{1,0:T(1,128)S(1)} %broadcast_in_dim.19.shift_ref), custom_call_target="tpu_custom_call" | custom-call | flops 6291456 | bytes 3145728 | tf_op jit(solution)/shard_map/pallas_call | solution.py:82
  129.6 0.8 shard_map.134
  130.4 2.9 %all_gather.7 = bf16[256,1536]{1,0:T(8,128)(2,1)S(1)} all-gather(bf16[256,768]{1,0:T(8,128)(2,1)S(1)} %shard_map.134), channel_id=1, replica_groups=mesh['ah'=2,'bh'=2,'bl'=2,'al'=2,'hid'=2] {'hid'}, dimensions={1}, use_global_device_ids=true | all-gather | bytes 1179648 | tf_op jit(solution)/shard_map/all_gather | solution.py:317
  133.3 1.5 %add_convert_fusion = bf16[256,768]{1,0:T(8,128)(2,1)} fusion(bf16[256,768]{1,0:T(8,128)(2,1)S(1)} %get-tuple-element.102, bf16[256,1536]{1,0:T(8,128)(2,1)S(1)} %all_gather.7, bf16[1536,768]{1,0:T(8,128)(2,1)S(1)} %copy-done), kind=kOutput, calls=%fused_computation | convolution fusion | flops 604569600 | bytes 3932160 | tf_op jit(solution)/shard_map/dot_general | solution.py:318
  (61 shorter events, 0.7 us)
Async XLA Ops:
  0.0 133.3 %copy-start = (bf16[1536,768]{1,0:T(8,128)(2,1)S(1)}, bf16[1536,768]{1,0:T(8,128)(2,1)}, u32[]{:S(2)}) copy-start(bf16[1536,768]{1,0:T(8,128)(2,1)} %param.22) | copy-start | bytes 7077892
  2.5 16.3 %copy-start.18 = (s32[64]{0:T(128)S(1)}, s32[64]{0:T(128)}, u32[]{:S(2)}) copy-start(s32[64]{0:T(128)} %lengths_ref.1) | copy-start | bytes 772
  2.5 30.6 %all-to-all-start = ((bf16[4,192,768]{2,1,0:T(8,128)(2,1)}), bf16[4,192,768]{2,1,0:T(8,128)(2,1)S(1)}, u32[]{:S(2)}, u32[]{:S(2)}) async-start(bf16[4,192,768]{2,1,0:T(8,128)(2,1)} %shard_map.119), calls=%async_computation | async-start | bytes 2359296 | tf_op jit(solution)/shard_map/all_to_all | solution.py:331
  6.4 25.7 %collective-permute-start = (bf16[96,3072]{1,0:T(8,128)(2,1)}, bf16[96,3072]{1,0:T(8,128)(2,1)}, u32[]{:S(2)}, u32[]{:S(2)}) collective-permute-start(bf16[96,3072]{1,0:T(8,128)(2,1)} %refs_0_.1), channel_id=1, source_target_pairs={{0,16},{16,0},{1,17},{17,1},{2,18},{18,2},{3,19},{19,3},{4,20},{20... | collective-permute-start | bytes 1769480 | tf_op jit(solution)/shard_map/ppermute | solution.py:327
  14.8 0.7 copy-start.13
  15.5 0.7 copy-start.15
  16.2 15.9 %collective-permute-start.1 = (bf16[128,1536]{1,0:T(8,128)(2,1)}, bf16[128,1536]{1,0:T(8,128)(2,1)}, u32[]{:S(2)}, u32[]{:S(2)}) collective-permute-start(bf16[128,1536]{1,0:T(8,128)(2,1)} %get-tuple-element.59.refs_0_), channel_id=1, source_target_pairs={{0,4},{4,0},{8,12},{12,8},{1,5},{5,1},{9,13},{13,9},{2,6},{6,2},{1... | collective-permute-start | bytes 1179656 | tf_op jit(solution)/shard_map/ppermute | solution.py:323
  21.3 1.0 copy-start.1
  33.1 27.3 %collective-permute-start.3 = (bf16[4,192,768]{2,1,0:T(8,128)(2,1)S(1)}, bf16[4,192,768]{2,1,0:T(8,128)(2,1)}, u32[]{:S(2)}, u32[]{:S(2)}) collective-permute-start(bf16[4,192,768]{2,1,0:T(8,128)(2,1)S(1)} %all-to-all-done.both_ref.refs_5_.refs_0_), channel_id=1, source_target_pairs={{0,2},{2,0},{1,3},{3,1},{4,6},{6,4},{5,7},{7,5},{8,10},{10,8},{9,1... | collective-permute-start | bytes 3538952 | tf_op jit(solution)/shard_map/ppermute | solution.py:327
  35.4 0.8 copy-start.5
  36.3 24.2 %all-to-all-start.1 = ((bf16[4,96,768]{2,1,0:T(8,128)(2,1)}), bf16[4,96,768]{2,1,0:T(8,128)(2,1)}, u32[]{:S(2)}, u32[]{:S(2)}) async-start(bf16[4,96,768]{2,1,0:T(8,128)(2,1)} %copy-done.5), calls=%async_computation.1 | async-start | bytes 1179648 | tf_op jit(solution)/shard_map/all_to_all | solution.py:331
  40.9 17.3 %collective-permute-start.5 = (bf16[128,1536]{1,0:T(8,128)(2,1)}, bf16[128,1536]{1,0:T(8,128)(2,1)S(1)}, u32[]{:S(2)}, u32[]{:S(2)}) collective-permute-start(bf16[128,1536]{1,0:T(8,128)(2,1)} %get-tuple-element.59.refs_0_), channel_id=1, source_target_pairs={{0,1},{1,0},{2,3},{3,2},{4,5},{5,4},{6,7},{7,6},{8,9},{9,8},{10,11... | collective-permute-start | bytes 1179656 | tf_op jit(solution)/shard_map/ppermute | solution.py:327
  43.6 16.1 %collective-permute-start.6 = (bf16[128,1536]{1,0:T(8,128)(2,1)}, bf16[128,1536]{1,0:T(8,128)(2,1)S(1)}, u32[]{:S(2)}, u32[]{:S(2)}) collective-permute-start(bf16[128,1536]{1,0:T(8,128)(2,1)} %collective-permute-done.1.refs_1_), channel_id=1, source_target_pairs={{0,1},{1,0},{2,3},{3,2},{4,5},{5,4},{6,7},{7,6},{8,9},{9,8},{10,11... | collective-permute-start | bytes 1179656 | tf_op jit(solution)/shard_map/ppermute | solution.py:327
  43.7 0.7 copy-start.19
  44.4 13.8 %collective-permute-start.4 = (bf16[2,96,768]{2,1,0:T(8,128)(2,1)S(1)}, bf16[2,96,768]{2,1,0:T(8,128)(2,1)S(1)}, u32[]{:S(2)}, u32[]{:S(2)}) collective-permute-start(bf16[2,96,768]{2,1,0:T(8,128)(2,1)S(1)} %get-tuple-element.63), channel_id=1, source_target_pairs={{0,16},{16,0},{1,17},{17,1},{2,18},{18,2},{3,19},{19,3},{4,20},{20... | collective-permute-start | bytes 884744 | tf_op jit(solution)/shard_map/ppermute | solution.py:327
  46.8 16.3 %collective-permute-start.2 = (bf16[128,1536]{1,0:T(8,128)(2,1)}, bf16[128,1536]{1,0:T(8,128)(2,1)}, u32[]{:S(2)}, u32[]{:S(2)}) collective-permute-start(bf16[128,1536]{1,0:T(8,128)(2,1)} %get-tuple-element.59.refs_0_), channel_id=1, source_target_pairs={{0,8},{4,12},{8,0},{12,4},{1,9},{5,13},{9,1},{13,5},{2,10},{6,14},... | collective-permute-start | bytes 1179656 | tf_op jit(solution)/shard_map/ppermute | solution.py:323
  58.2 0.7 copy-start.11
  58.9 0.8 copy-start.7
  59.7 0.8 copy-start.9
  60.4 13.7 %collective-permute-start.7 = (bf16[4,96,768]{2,1,0:T(8,128)(2,1)}, bf16[4,96,768]{2,1,0:T(8,128)(2,1)S(1)}, u32[]{:S(2)}, u32[]{:S(2)}) collective-permute-start(bf16[4,96,768]{2,1,0:T(8,128)(2,1)} %all-to-all-done.1.refs_7_), channel_id=1, source_target_pairs={{0,2},{2,0},{1,3},{3,1},{4,6},{6,4},{5,7},{7,5},{8,10},{10,8},{9,1... | collective-permute-start | bytes 1769480 | tf_op jit(solution)/shard_map/ppermute | solution.py:327
  60.7 13.5 %collective-permute-start.8 = (bf16[2,96,768]{2,1,0:T(8,128)(2,1)}, bf16[2,96,768]{2,1,0:T(8,128)(2,1)S(1)}, u32[]{:S(2)}, u32[]{:S(2)}) collective-permute-start(bf16[2,96,768]{2,1,0:T(8,128)(2,1)} %copy-done.19), channel_id=1, source_target_pairs={{0,16},{16,0},{1,17},{17,1},{2,18},{18,2},{3,19},{19,3},{4,20},{20... | collective-permute-start | bytes 884744 | tf_op jit(solution)/shard_map/ppermute | solution.py:327
  64.0 7.9 %collective-permute-start.9 = (bf16[64,1536]{1,0:T(8,128)(2,1)S(1)}, bf16[64,1536]{1,0:T(8,128)(2,1)S(1)}, u32[]{:S(2)}, u32[]{:S(2)}) collective-permute-start(bf16[64,1536]{1,0:T(8,128)(2,1)S(1)} %get-tuple-element.68), channel_id=1, source_target_pairs={{0,4},{4,0},{8,12},{12,8},{1,5},{5,1},{9,13},{13,9},{2,6},{6,2},{1... | collective-permute-start | bytes 589832 | tf_op jit(solution)/shard_map/ppermute | solution.py:323
  64.2 18.9 %copy-start.8 = (bf16[128,1536]{1,0:T(8,128)(2,1)S(1)}, bf16[128,1536]{1,0:T(8,128)(2,1)}, u32[]{:S(2)}) copy-start(bf16[128,1536]{1,0:T(8,128)(2,1)} %copy-done.7) | copy-start | bytes 1179652
  64.2 18.9 %copy-start.10 = (bf16[128,1536]{1,0:T(8,128)(2,1)S(1)}, bf16[128,1536]{1,0:T(8,128)(2,1)}, u32[]{:S(2)}) copy-start(bf16[128,1536]{1,0:T(8,128)(2,1)} %copy-done.9) | copy-start | bytes 1179652
  64.2 7.7 %collective-permute-start.10 = (bf16[64,1536]{1,0:T(8,128)(2,1)S(1)}, bf16[64,1536]{1,0:T(8,128)(2,1)S(1)}, u32[]{:S(2)}, u32[]{:S(2)}) collective-permute-start(bf16[64,1536]{1,0:T(8,128)(2,1)S(1)} %get-tuple-element.69), channel_id=1, source_target_pairs={{0,4},{4,0},{8,12},{12,8},{1,5},{5,1},{9,13},{13,9},{2,6},{6,2},{1... | collective-permute-start | bytes 589832 | tf_op jit(solution)/shard_map/ppermute | solution.py:323
  65.6 17.5 %collective-permute-start.11 = (bf16[128,1536]{1,0:T(8,128)(2,1)}, bf16[128,1536]{1,0:T(8,128)(2,1)S(1)}, u32[]{:S(2)}, u32[]{:S(2)}) collective-permute-start(bf16[128,1536]{1,0:T(8,128)(2,1)} %collective-permute-done.2.ref.refs_2_), channel_id=1, source_target_pairs={{0,1},{1,0},{2,3},{3,2},{4,5},{5,4},{6,7},{7,6},{8,9},{9,8},{10,11... | collective-permute-start | bytes 1179656 | tf_op jit(solution)/shard_map/ppermute | solution.py:327
  74.2 14.9 %collective-permute-start.14 = (bf16[2,96,768]{2,1,0:T(8,128)(2,1)}, bf16[2,96,768]{2,1,0:T(8,128)(2,1)S(1)}, u32[]{:S(2)}, u32[]{:S(2)}) collective-permute-start(bf16[2,96,768]{2,1,0:T(8,128)(2,1)} %copy-done.11), channel_id=1, source_target_pairs={{0,2},{2,0},{1,3},{3,1},{4,6},{6,4},{5,7},{7,5},{8,10},{10,8},{9,1... | collective-permute-start | bytes 884744 | tf_op jit(solution)/shard_map/ppermute | solution.py:327
  75.3 13.8 %collective-permute-start.15 = (bf16[2,96,768]{2,1,0:T(8,128)(2,1)S(1)}, bf16[2,96,768]{2,1,0:T(8,128)(2,1)S(1)}, u32[]{:S(2)}, u32[]{:S(2)}) collective-permute-start(bf16[2,96,768]{2,1,0:T(8,128)(2,1)S(1)} %collective-permute-done.8.refs_1_), channel_id=1, source_target_pairs={{0,2},{2,0},{1,3},{3,1},{4,6},{6,4},{5,7},{7,5},{8,10},{10,8},{9,1... | collective-permute-start | bytes 884744 | tf_op jit(solution)/shard_map/ppermute | solution.py:327
  75.6 7.5 %collective-permute-start.12 = (bf16[64,1536]{1,0:T(8,128)(2,1)S(1)}, bf16[64,1536]{1,0:T(8,128)(2,1)S(1)}, u32[]{:S(2)}, u32[]{:S(2)}) collective-permute-start(bf16[64,1536]{1,0:T(8,128)(2,1)S(1)} %collective-permute-done.9.refs_3_), channel_id=1, source_target_pairs={{0,1},{1,0},{2,3},{3,2},{4,5},{5,4},{6,7},{7,6},{8,9},{9,8},{10,11... | collective-permute-start | bytes 589832 | tf_op jit(solution)/shard_map/ppermute | solution.py:327
  79.7 3.5 %collective-permute-start.13 = (bf16[64,1536]{1,0:T(8,128)(2,1)S(1)}, bf16[64,1536]{1,0:T(8,128)(2,1)S(1)}, u32[]{:S(2)}, u32[]{:S(2)}) collective-permute-start(bf16[64,1536]{1,0:T(8,128)(2,1)S(1)} %collective-permute-done.10.refs_4_), channel_id=1, source_target_pairs={{0,1},{1,0},{2,3},{3,2},{4,5},{5,4},{6,7},{7,6},{8,9},{9,8},{10,11... | collective-permute-start | bytes 589832 | tf_op jit(solution)/shard_map/ppermute | solution.py:327
  86.2 3.9 %copy-start.12 = (bf16[2,96,768]{2,1,0:T(8,128)(2,1)S(1)}, bf16[2,96,768]{2,1,0:T(8,128)(2,1)}, u32[]{:S(2)}) copy-start(bf16[2,96,768]{2,1,0:T(8,128)(2,1)} %copy-done.11) | copy-start | bytes 884740
  89.1 3.2 %collective-permute-start.16 = (bf16[512,768]{1,0:T(8,128)(2,1)S(1)}, bf16[512,768]{1,0:T(8,128)(2,1)S(1)}, u32[]{:S(2)}, u32[]{:S(2)}) collective-permute-start(bf16[512,768]{1,0:T(8,128)(2,1)S(1)} %get-tuple-element.81), channel_id=1, source_target_pairs={{0,1},{1,0},{2,3},{3,2},{4,5},{5,4},{6,7},{7,6},{8,9},{9,8},{10,11... | collective-permute-start | bytes 2359304 | tf_op jit(solution)/shard_map/ppermute | solution.py:327
  92.2 13.0 %copy-start.16 = (bf16[128,768]{1,0:T(8,128)(2,1)S(1)}, bf16[128,768]{1,0:T(8,128)(2,1)}, u32[]{:S(2)}) copy-start(bf16[128,768]{1,0:T(8,128)(2,1)} %copy-done.15) | copy-start | bytes 589828
  92.2 4.2 %collective-permute-start.21 = (bf16[512,768]{1,0:T(8,128)(2,1)S(1)}, bf16[512,768]{1,0:T(8,128)(2,1)S(1)}, u32[]{:S(2)}, u32[]{:S(2)}) collective-permute-start(bf16[512,768]{1,0:T(8,128)(2,1)S(1)} %get-tuple-element.89), channel_id=1, source_target_pairs={{0,1},{1,0},{2,3},{3,2},{4,5},{5,4},{6,7},{7,6},{8,9},{9,8},{10,11... | collective-permute-start | bytes 2359304 | tf_op jit(solution)/shard_map/ppermute | solution.py:327
  92.4 21.2 %copy-start.14 = (bf16[128,768]{1,0:T(8,128)(2,1)S(1)}, bf16[128,768]{1,0:T(8,128)(2,1)}, u32[]{:S(2)}) copy-start(bf16[128,768]{1,0:T(8,128)(2,1)} %copy-done.13) | copy-start | bytes 589828
  92.4 6.0 %collective-permute-start.17 = (bf16[128,768]{1,0:T(8,128)(2,1)S(1)}, bf16[128,768]{1,0:T(8,128)(2,1)S(1)}, u32[]{:S(2)}, u32[]{:S(2)}) collective-permute-start(bf16[128,768]{1,0:T(8,128)(2,1)S(1)} %get-tuple-element.83), channel_id=1, source_target_pairs={{0,4},{4,0},{8,12},{12,8},{1,5},{5,1},{9,13},{13,9},{2,6},{6,2},{1... | collective-permute-start | bytes 589832 | tf_op jit(solution)/shard_map/ppermute | solution.py:323
  92.6 8.6 %collective-permute-start.18 = (bf16[128,768]{1,0:T(8,128)(2,1)S(1)}, bf16[128,768]{1,0:T(8,128)(2,1)S(1)}, u32[]{:S(2)}, u32[]{:S(2)}) collective-permute-start(bf16[128,768]{1,0:T(8,128)(2,1)S(1)} %get-tuple-element.84), channel_id=1, source_target_pairs={{0,8},{4,12},{8,0},{12,4},{1,9},{5,13},{9,1},{13,5},{2,10},{6,14},... | collective-permute-start | bytes 589832 | tf_op jit(solution)/shard_map/ppermute | solution.py:323
  95.3 9.9 %collective-permute-start.19 = (bf16[128,768]{1,0:T(8,128)(2,1)S(1)}, bf16[128,768]{1,0:T(8,128)(2,1)S(1)}, u32[]{:S(2)}, u32[]{:S(2)}) collective-permute-start(bf16[128,768]{1,0:T(8,128)(2,1)S(1)} %get-tuple-element.85), channel_id=1, source_target_pairs={{0,12},{4,8},{8,4},{12,0},{1,13},{5,9},{9,5},{13,1},{2,14},{6,10},... | collective-permute-start | bytes 589832 | tf_op jit(solution)/shard_map/ppermute | solution.py:323
  96.4 19.8 %copy-start.3 = (bf16[1536,768]{1,0:T(8,128)(2,1)S(1)}, bf16[1536,768]{1,0:T(8,128)(2,1)}, u32[]{:S(2)}) copy-start(bf16[1536,768]{1,0:T(8,128)(2,1)} %value_ref.1) | copy-start | bytes 7077892
  96.4 19.8 %copy-start.4 = (bf16[1536,768]{1,0:T(8,128)(2,1)S(1)}, bf16[1536,768]{1,0:T(8,128)(2,1)}, u32[]{:S(2)}) copy-start(bf16[1536,768]{1,0:T(8,128)(2,1)} %gate_ref.1) | copy-start | bytes 7077892
  96.4 19.8 %copy-start.17 = (f32[1,1536]{1,0:T(1,128)S(1)}, f32[1,1536]{1,0:T(1,128)}, u32[]{:S(2)}) copy-start(f32[1,1536]{1,0:T(1,128)} %broadcast_in_dim.17.gain_ref) | copy-start | bytes 18436
  96.6 11.1 %collective-permute-start.22 = (bf16[128,768]{1,0:T(8,128)(2,1)S(1)}, bf16[128,768]{1,0:T(8,128)(2,1)S(1)}, u32[]{:S(2)}, u32[]{:S(2)}) collective-permute-start(bf16[128,768]{1,0:T(8,128)(2,1)S(1)} %get-tuple-element.91), channel_id=1, source_target_pairs={{0,4},{4,0},{8,12},{12,8},{1,5},{5,1},{9,13},{13,9},{2,6},{6,2},{1... | collective-permute-start | bytes 589832 | tf_op jit(solution)/shard_map/ppermute | solution.py:323
  96.9 11.7 %collective-permute-start.23 = (bf16[128,768]{1,0:T(8,128)(2,1)S(1)}, bf16[128,768]{1,0:T(8,128)(2,1)S(1)}, u32[]{:S(2)}, u32[]{:S(2)}) collective-permute-start(bf16[128,768]{1,0:T(8,128)(2,1)S(1)} %get-tuple-element.92), channel_id=1, source_target_pairs={{0,8},{4,12},{8,0},{12,4},{1,9},{5,13},{9,1},{13,5},{2,10},{6,14},... | collective-permute-start | bytes 589832 | tf_op jit(solution)/shard_map/ppermute | solution.py:323
  98.5 15.1 %collective-permute-start.24 = (bf16[128,768]{1,0:T(8,128)(2,1)S(1)}, bf16[128,768]{1,0:T(8,128)(2,1)S(1)}, u32[]{:S(2)}, u32[]{:S(2)}) collective-permute-start(bf16[128,768]{1,0:T(8,128)(2,1)S(1)} %get-tuple-element.93), channel_id=1, source_target_pairs={{0,12},{4,8},{8,4},{12,0},{1,13},{5,9},{9,5},{13,1},{2,14},{6,10},... | collective-permute-start | bytes 589832 | tf_op jit(solution)/shard_map/ppermute | solution.py:323
  105.3 8.3 %collective-permute-start.20 = (bf16[128,768]{1,0:T(8,128)(2,1)S(1)}, bf16[128,768]{1,0:T(8,128)(2,1)S(1)}, u32[]{:S(2)}, u32[]{:S(2)}) collective-permute-start(bf16[128,768]{1,0:T(8,128)(2,1)S(1)} %shard_map.128.near_ref), channel_id=1, source_target_pairs={{0,1},{1,0},{2,3},{3,2},{4,5},{5,4},{6,7},{7,6},{8,9},{9,8},{10,11... | collective-permute-start | bytes 589832 | tf_op jit(solution)/shard_map/ppermute | solution.py:327
  113.7 11.4 %copy-start.2 = (s32[8,280,128]{2,1,0:T(8,128)S(1)}, s32[8,280,128]{2,1,0:T(8,128)}, u32[]{:S(2)}) copy-start(s32[8,280,128]{2,1,0:T(8,128)} %copy-done.1) | copy-start | bytes 3440644
  113.8 11.4 %copy-start.6 = (f32[32,768]{1,0:T(8,128)S(1)}, f32[32,768]{1,0:T(8,128)}, u32[]{:S(2)}) copy-start(f32[32,768]{1,0:T(8,128)} %taps_ref.3) | copy-start | bytes 294916
  113.8 2.5 %collective-permute-start.25 = (bf16[128,768]{1,0:T(8,128)(2,1)S(1)}, bf16[128,768]{1,0:T(8,128)(2,1)S(1)}, u32[]{:S(2)}, u32[]{:S(2)}) collective-permute-start(bf16[128,768]{1,0:T(8,128)(2,1)S(1)} %shard_map.131.far_ref), channel_id=1, source_target_pairs={{0,1},{1,0},{2,3},{3,2},{4,5},{5,4},{6,7},{7,6},{8,9},{9,8},{10,11... | collective-permute-start | bytes 589832 | tf_op jit(solution)/shard_map/ppermute | solution.py:327
  118.7 10.8 %collective-permute-start.26 = (bf16[16,768]{1,0:T(8,128)(2,1)S(1)}, bf16[16,768]{1,0:T(8,128)(2,1)S(1)}, u32[]{:S(2)}, u32[]{:S(2)}) collective-permute-start(bf16[16,768]{1,0:T(8,128)(2,1)S(1)} %get-tuple-element.107), channel_id=1, source_target_pairs={{0,2},{2,4},{4,6},{6,8},{8,10},{10,12},{12,14},{14,16},{16,18},{18... | collective-permute-start | bytes 73736 | tf_op jit(solution)/shard_map/ppermute | solution.py:298
  121.6 8.0 %collective-permute-start.27 = (bf16[16,768]{1,0:T(8,128)(2,1)S(1)}, bf16[16,768]{1,0:T(8,128)(2,1)S(1)}, u32[]{:S(2)}, u32[]{:S(2)}) collective-permute-start(bf16[16,768]{1,0:T(8,128)(2,1)S(1)} %get-tuple-element.108), channel_id=1, source_target_pairs={{2,0},{4,2},{6,4},{8,6},{10,8},{12,10},{14,12},{16,14},{18,16},{20... | collective-permute-start | bytes 73736 | tf_op jit(solution)/shard_map/ppermute | solution.py:299

commit v7 on v6

--- a/solution.py
+++ b/solution.py
@@ -116,12 +116,14 @@
     second_ref[...] = both_ref[half:, skip:, :]
 
 
-def norm_kernel(me_ref, whole_ref, gain_ref, near_ref, far_ref, out_ref):
+def norm_kernel(me_ref, whole_ref, gain_ref, near_ref, far_ref, out_ref, oth_ref):
     rows, width = near_ref.shape
     at = pl.ds(pl.multiple_of(me_ref[1] * rows, rows), rows)
     for place, ref in ((me_ref[2], near_ref), (1 - me_ref[2], far_ref)):
         ref[...] = whole_ref[at, pl.ds(pl.multiple_of(place * width, width), width)]
+    oth = pl.ds(pl.multiple_of((1 - me_ref[1]) * rows, rows), rows)
     out_ref[...] = norm_rows(f32(whole_ref[at, :]), gain_ref[...]).astype(jnp.bfloat16)
+    oth_ref[...] = norm_rows(f32(whole_ref[oth, :]), gain_ref[...]).astype(jnp.bfloat16)
 
 
 def part_rows_kernel(ref, first_ref, second_ref):
@@ -347,24 +349,24 @@
     (both,) = kernel_call(cut_kernel, [((4, 2 * shard, units), bf16)], [w_in, w_out.T], limit=60)
     both = recut(both)
     whole = lax.all_gather(tokens, "hid", axis=1, tiled=True)
-    *mine, normed = kernel_call(
+    *mine, normed, normed_oth = kernel_call(
         norm_kernel,
-        [((half, width), bf16)] * 2 + [((half, wide), bf16)],
+        [((half, width), bf16)] * 2 + [((half, wide), bf16)] * 2,
         [me, whole, ffn_gain[None, :]],
         scalars=1,
     )
     frames1 = partner(normed, 1)
-    in_far, both, normed, frames1, early = tie((in_far, both, normed, frames1, early))
+    in_far, both, normed, normed_oth, frames1, early = tie(
+        (in_far, both, normed, normed_oth, frames1, early)
+    )
     both_x = swap(both, "al")
     (in_z,) = kernel_call(cut_kernel, [(block, bf16)], [in_far])
     in_z = recut(in_z)
     out_1, out_2 = kernel_call(part_kernel, [(pair, bf16)] * 2, [both])
     out_z1 = swap(out_1, "ah")
     frames2 = partner(normed, 2)
-    normed_oth, frames1_oth = swap(normed, "hid"), swap(frames1, "hid")
-    both_x, in_z, out_z1, out_2, normed_oth, frames1_oth = tie(
-        (both_x, in_z, out_z1, out_2, normed_oth, frames1_oth)
-    )
+    frames1_oth = swap(frames1, "hid")
+    both_x, in_z, out_z1, out_2, frames1_oth = tie((both_x, in_z, out_z1, out_2, frames1_oth))
     in_zx = swap(in_z, "al")
     out_z2 = swap(out_2, "ah")
     upper, lower = kernel_call(part_rows_kernel, [((half // 2, wide), bf16)] * 2, [frames2])

time: 137 us -> 137 us (level)
  waiting for transfers between devices: 36.5 us -> 38.3 us
  starting transfers between devices: 51.9 us -> 50.5 us
    ppermute x16 -> x15, waiting for transfers between devices: 13.5 us -> 15.3 us  [swap(): return lax.ppermute(values, axis, SWAP)]
    ppermute x10, starting transfers between devices: 11.2 us -> 9.62 us  [partner(): return lax.ppermute(values, GROUP, [(i, i ^ step) for i in range(4)])]
    unnamed x40 -> x36, local copies, waits for them, and re-layouts: 6.18 us -> 5.47 us
    ppermute x16 -> x15, starting transfers between devices: 25.8 us -> 26.1 us  [swap(): return lax.ppermute(values, axis, SWAP)]
  transfers between devices with their start and end apart: 30 -> 29, of which waited for: 10 -> 10; matrix products, arithmetic and copies ran while one was open for 3% -> 3% of each run, Pallas kernels for 17% -> 17%
where the time goes in v7:
time: 137 us; the launch traced here: 135 us
  starting transfers between devices  50.5 us (37%)
  waiting for transfers between devices  38.3 us (28%)
  Pallas kernels  28.8 us (21%)
  local copies, waits for them, and re-layouts  8.84 us (6%)
  blocking collectives  6.64 us (5%)
  matrix products  1.52 us (1%)
    pallas_call x17, Pallas kernels, kernel_call(): pl.pallas_call(body, out_shape=[jax.ShapeDtypeStruct(shape, dtype) for sh...  28.8 us
    ppermute x15, starting transfers between devices, swap(): return lax.ppermute(values, axis, SWAP)  26.1 us
    ppermute x10, waiting for transfers between devices, partner(): return lax.ppermute(values, GROUP, [(i, i ^ step) for i in range(4)])  22.8 us
    ppermute x15, waiting for transfers between devices, swap(): return lax.ppermute(values, axis, SWAP)  15.3 us
    ppermute x10, starting transfers between devices, partner(): return lax.ppermute(values, GROUP, [(i, i ^ step) for i in range(4)])  9.62 us
    all_to_all x2, starting transfers between devices, recut(): return lax.all_to_all(parts, GROUP, 0, 0)  8.45 us
    unnamed x36, local copies, waits for them, and re-layouts  5.47 us
    all_gather x1, blocking collectives, grouped_ffn(): whole = lax.all_gather(tokens, 'hid', axis=1, tiled=True)  3.71 us
  transfers between devices with their start and end apart: 29, of which 10 were waited for; matrix products, arithmetic and copies ran while one was open for 3% of the time, Pallas kernels for 17%

profile of v7, /device:TPU:5, one launch (start us, length us, event | category | flops | bytes accessed | tf_op | source)
XLA Modules:
  0.0 135.0 jit_solution(17409471544015523424)
XLA Ops:
  0.0 2.5 %shard_map.119 = bf16[4,192,768]{2,1,0:T(8,128)(2,1)} custom-call(bf16[96,3072]{1,0:T(8,128)(2,1)} %refs_0_.1, bf16[96,3072]{1,0:T(8,128)(2,1)} %bitcast.7), custom_call_target="tpu_custom_call" | custom-call | tf_op jit(solution)/shard_map/pallas_call | solution.py:82
  2.5 3.9 %all-to-all-start = ((bf16[4,192,768]{2,1,0:T(8,128)(2,1)}), bf16[4,192,768]{2,1,0:T(8,128)(2,1)S(1)}, u32[]{:S(2)}, u32[]{:S(2)}) async-start(bf16[4,192,768]{2,1,0:T(8,128)(2,1)} %shard_map.119), calls=%async_computation | async-start | bytes 2359296 | tf_op jit(solution)/shard_map/all_to_all | solution.py:333
  6.4 2.3 %collective-permute-start = (bf16[96,3072]{1,0:T(8,128)(2,1)}, bf16[96,3072]{1,0:T(8,128)(2,1)}, u32[]{:S(2)}, u32[]{:S(2)}) collective-permute-start(bf16[96,3072]{1,0:T(8,128)(2,1)} %refs_0_.1), channel_id=1, source_target_pairs={{0,16},{16,0},{1,17},{17,1},{2,18},{18,2},{3,19},{19,3},{4,20},{20... | collective-permute-start | bytes 1769480 | tf_op jit(solution)/shard_map/ppermute | solution.py:329
  8.7 0.7 broadcast_in_dim.15.gain_ref
  9.5 3.7 %all_gather.6.whole_ref = bf16[256,1536]{1,0:T(8,128)(2,1)S(1)} all-gather(bf16[256,768]{1,0:T(8,128)(2,1)} %param.12), channel_id=1, replica_groups=mesh['ah'=2,'bh'=2,'bl'=2,'al'=2,'hid'=2] {'hid'}, dimensions={1}, use_global_device_ids=true | all-gather | bytes 1179648 | tf_op jit(solution)/shard_map/all_gather | solution.py:351
  13.2 1.8 %shard_map.118 = (bf16[128,768]{1,0:T(8,128)(2,1)S(1)}, bf16[128,768]{1,0:T(8,128)(2,1)S(1)}, bf16[128,1536]{1,0:T(8,128)(2,1)}, bf16[128,1536]{1,0:T(8,128)(2,1)S(1)}) custom-call(s32[3]{0:T(128)S(1)} %pad_add_fusion.me_ref, bf16[256,1536]{1,0:T(8,128)(2,1)S(1)} %all_gather.6.whole_ref, f32[1,1536]{1,0:T(1,128)S(1)} %broadcast_in_dim.15.gain_ref), custom_call_target="tpu_custom_call" | custom-call | tf_op jit(solution)/shard_map/pallas_call | solution.py:82
  15.0 0.8 copy-done.7
  15.7 0.7 copy-done.11
  16.4 0.7 copy-done.13
  17.1 1.3 broadcast_in_dim.17.gain_ref
  18.4 0.7 broadcast_in_dim.18.scale_ref
  19.1 0.7 broadcast_in_dim.19.shift_ref
  19.8 2.4 %shard_map.120.utter_ref = s32[8,280,128]{2,1,0:T(8,128)S(1)} custom-call(s32[1]{0:T(128)} %bitcast.4.first_ref, s32[64]{0:T(128)S(1)} %copy-done.16), custom_call_target="tpu_custom_call" | custom-call | tf_op jit(solution)/shard_map/pallas_call | solution.py:82
  22.2 1.0 copy-done.1
  23.2 9.8 %collective-permute-done.1.refs_1_ = bf16[128,1536]{1,0:T(8,128)(2,1)} collective-permute-done((bf16[128,1536]{1,0:T(8,128)(2,1)}, bf16[128,1536]{1,0:T(8,128)(2,1)}, u32[]{:S(2)}, u32[]{:S(2)}) %collective-permute-start.1) | collective-permute-done | bytes 393248 | tf_op jit(solution)/shard_map/ppermute | solution.py:325
  33.0 0.2 all-to-all-done.both_ref.refs_5_.refs_0_
  33.2 1.2 collective-permute-start.3
  34.5 1.1 shard_map.121
  35.6 0.8 copy-done.5
  36.4 4.6 %all-to-all-start.1 = ((bf16[4,96,768]{2,1,0:T(8,128)(2,1)}), bf16[4,96,768]{2,1,0:T(8,128)(2,1)}, u32[]{:S(2)}, u32[]{:S(2)}) async-start(bf16[4,96,768]{2,1,0:T(8,128)(2,1)} %copy-done.5), calls=%async_computation.1 | async-start | bytes 1179648 | tf_op jit(solution)/shard_map/all_to_all | solution.py:333
  41.0 2.7 %collective-permute-start.5 = (bf16[128,1536]{1,0:T(8,128)(2,1)}, bf16[128,1536]{1,0:T(8,128)(2,1)S(1)}, u32[]{:S(2)}, u32[]{:S(2)}) collective-permute-start(bf16[128,1536]{1,0:T(8,128)(2,1)} %collective-permute-done.1.refs_1_), channel_id=1, source_target_pairs={{0,1},{1,0},{2,3},{3,2},{4,5},{5,4},{6,7},{7,6},{8,9},{9,8},{10,11... | collective-permute-start | bytes 1179656 | tf_op jit(solution)/shard_map/ppermute | solution.py:329
  43.7 0.7 copy-done.17
  44.4 2.4 %collective-permute-start.4 = (bf16[2,96,768]{2,1,0:T(8,128)(2,1)S(1)}, bf16[2,96,768]{2,1,0:T(8,128)(2,1)}, u32[]{:S(2)}, u32[]{:S(2)}) collective-permute-start(bf16[2,96,768]{2,1,0:T(8,128)(2,1)S(1)} %get-tuple-element.65), channel_id=1, source_target_pairs={{0,16},{16,0},{1,17},{17,1},{2,18},{18,2},{3,19},{19,3},{4,20},{20... | collective-permute-start | bytes 884744 | tf_op jit(solution)/shard_map/ppermute | solution.py:329
  46.8 1.2 collective-permute-start.2
  48.0 11.5 %collective-permute-done.4.refs_0_ = bf16[2,96,768]{2,1,0:T(8,128)(2,1)} collective-permute-done((bf16[2,96,768]{2,1,0:T(8,128)(2,1)S(1)}, bf16[2,96,768]{2,1,0:T(8,128)(2,1)}, u32[]{:S(2)}, u32[]{:S(2)}) %collective-permute-start.4) | collective-permute-done | bytes 294944 | tf_op jit(solution)/shard_map/ppermute | solution.py:329
  59.5 0.7 copy-done.9
  60.2 0.3 collective-permute-start.6
  60.5 0.6 collective-permute-start.7
  61.1 1.9 %collective-permute-done.2.ref.refs_2_ = bf16[128,1536]{1,0:T(8,128)(2,1)} collective-permute-done((bf16[128,1536]{1,0:T(8,128)(2,1)}, bf16[128,1536]{1,0:T(8,128)(2,1)}, u32[]{:S(2)}, u32[]{:S(2)}) %collective-permute-start.2) | collective-permute-done | bytes 393248 | tf_op jit(solution)/shard_map/ppermute | solution.py:325
  63.0 1.0 shard_map.123
  64.0 0.2 collective-permute-start.8
  64.2 1.4 %collective-permute-start.9 = (bf16[64,1536]{1,0:T(8,128)(2,1)S(1)}, bf16[64,1536]{1,0:T(8,128)(2,1)S(1)}, u32[]{:S(2)}, u32[]{:S(2)}) collective-permute-start(bf16[64,1536]{1,0:T(8,128)(2,1)S(1)} %get-tuple-element.71), channel_id=1, source_target_pairs={{0,4},{4,0},{8,12},{12,8},{1,5},{5,1},{9,13},{13,9},{2,6},{6,2},{1... | collective-permute-start | bytes 589832 | tf_op jit(solution)/shard_map/ppermute | solution.py:325
  65.6 6.0 %collective-permute-start.10 = (bf16[128,1536]{1,0:T(8,128)(2,1)}, bf16[128,1536]{1,0:T(8,128)(2,1)S(1)}, u32[]{:S(2)}, u32[]{:S(2)}) collective-permute-start(bf16[128,1536]{1,0:T(8,128)(2,1)} %collective-permute-done.2.ref.refs_2_), channel_id=1, source_target_pairs={{0,1},{1,0},{2,3},{3,2},{4,5},{5,4},{6,7},{7,6},{8,9},{9,8},{10,11... | collective-permute-start | bytes 1179656 | tf_op jit(solution)/shard_map/ppermute | solution.py:329
  71.6 2.7 %collective-permute-done.7.refs_1_ = bf16[2,96,768]{2,1,0:T(8,128)(2,1)S(1)} collective-permute-done((bf16[2,96,768]{2,1,0:T(8,128)(2,1)}, bf16[2,96,768]{2,1,0:T(8,128)(2,1)S(1)}, u32[]{:S(2)}, u32[]{:S(2)}) %collective-permute-start.7) | collective-permute-done | bytes 294944 | tf_op jit(solution)/shard_map/ppermute | solution.py:329
  74.3 1.7 %collective-permute-start.13 = (bf16[2,96,768]{2,1,0:T(8,128)(2,1)}, bf16[2,96,768]{2,1,0:T(8,128)(2,1)S(1)}, u32[]{:S(2)}, u32[]{:S(2)}) collective-permute-start(bf16[2,96,768]{2,1,0:T(8,128)(2,1)} %collective-permute-done.4.refs_0_), channel_id=1, source_target_pairs={{0,2},{2,0},{1,3},{3,1},{4,6},{6,4},{5,7},{7,5},{8,10},{10,8},{9,1... | collective-permute-start | bytes 884744 | tf_op jit(solution)/shard_map/ppermute | solution.py:329
  76.0 3.4 %collective-permute-start.11 = (bf16[64,1536]{1,0:T(8,128)(2,1)S(1)}, bf16[64,1536]{1,0:T(8,128)(2,1)S(1)}, u32[]{:S(2)}, u32[]{:S(2)}) collective-permute-start(bf16[64,1536]{1,0:T(8,128)(2,1)S(1)} %collective-permute-done.8.refs_3_), channel_id=1, source_target_pairs={{0,1},{1,0},{2,3},{3,2},{4,5},{5,4},{6,7},{7,6},{8,9},{9,8},{10,11... | collective-permute-start | bytes 589832 | tf_op jit(solution)/shard_map/ppermute | solution.py:329
  79.4 3.4 %shard_map.124.own_ref = bf16[512,768]{1,0:T(8,128)(2,1)S(1)} custom-call(s32[3]{0:T(128)S(1)} %pad_add_fusion.me_ref, bf16[128,1536]{1,0:T(8,128)(2,1)} %get-tuple-element.61.refs_0_, bf16[128,1536]{1,0:T(8,128)(2,1)} %collective-permute-done.1.refs_1_, bf16[128,1536]{1,0:T(8,128)(2,1)} %collective-permute-done.2.ref.refs_2_, ...), custom_call_target="tpu_custom_call" | custom-call | tf_op jit(solution)/shard_map/pallas_call | solution.py:82
  82.9 3.1 %shard_map.125.oth_ref = bf16[512,768]{1,0:T(8,128)(2,1)S(1)} custom-call(s32[3]{0:T(128)S(1)} %pad_add_fusion.me_ref, bf16[128,1536]{1,0:T(8,128)(2,1)S(1)} %copy-done.8, bf16[128,1536]{1,0:T(8,128)(2,1)S(1)} %copy-done.10, bf16[128,1536]{1,0:T(8,128)(2,1)S(1)} %collective-permute-done.10.refs_2_, bf16[64,1536]{1,0:T(8,128)(2,1)S(1)} %collective-permute-done.11.refs_3_, ...), custom_call_target="tpu_custom_call" | custom-call | tf_op jit(solution)/shard_map/pallas_call | solution.py:82
  86.0 2.8 %shard_map.126 = (f32[512,768]{1,0:T(8,128)S(1)}, bf16[512,768]{1,0:T(8,128)(2,1)S(1)}) custom-call(s32[3]{0:T(128)S(1)} %pad_add_fusion.me_ref, bf16[512,768]{1,0:T(8,128)(2,1)S(1)} %shard_map.124.own_ref, bf16[512,768]{1,0:T(8,128)(2,1)S(1)} %shard_map.125.oth_ref, bf16[4,192,768]{2,1,0:T(8,128)(2,1)S(1)} %all-to-all-done.both_ref.refs_5_.refs_0_, ...), custom_call_target="tpu_custom_call" | custom-call | tf_op jit(solution)/shard_map/pallas_call | solution.py:82
  88.8 1.7 %collective-permute-start.15 = (bf16[512,768]{1,0:T(8,128)(2,1)S(1)}, bf16[512,768]{1,0:T(8,128)(2,1)S(1)}, u32[]{:S(2)}, u32[]{:S(2)}) collective-permute-start(bf16[512,768]{1,0:T(8,128)(2,1)S(1)} %get-tuple-element.83), channel_id=1, source_target_pairs={{0,1},{1,0},{2,3},{3,2},{4,5},{5,4},{6,7},{7,6},{8,9},{9,8},{10,11... | collective-permute-start | bytes 2359304 | tf_op jit(solution)/shard_map/ppermute | solution.py:329
  90.5 2.5 %shard_map.129 = (f32[512,768]{1,0:T(8,128)S(1)}, bf16[512,768]{1,0:T(8,128)(2,1)S(1)}) custom-call(s32[3]{0:T(128)S(1)} %pad_add_fusion.me_ref, bf16[512,768]{1,0:T(8,128)(2,1)S(1)} %shard_map.124.own_ref, bf16[512,768]{1,0:T(8,128)(2,1)S(1)} %shard_map.125.oth_ref, bf16[2,96,768]{2,1,0:T(8,128)(2,1)} %collective-permute-done.4.refs_0_, ...), custom_call_target="tpu_custom_call" | custom-call | tf_op jit(solution)/shard_map/pallas_call | solution.py:82
  93.0 0.1 shard_map.127
  93.2 0.6 collective-permute-start.16
  93.8 1.7 %collective-permute-start.17 = (bf16[128,768]{1,0:T(8,128)(2,1)S(1)}, bf16[128,768]{1,0:T(8,128)(2,1)S(1)}, u32[]{:S(2)}, u32[]{:S(2)}) collective-permute-start(bf16[128,768]{1,0:T(8,128)(2,1)S(1)} %get-tuple-element.86), channel_id=1, source_target_pairs={{0,8},{4,12},{8,0},{12,4},{1,9},{5,13},{9,1},{13,5},{2,10},{6,14},... | collective-permute-start | bytes 589832 | tf_op jit(solution)/shard_map/ppermute | solution.py:325
  95.5 1.1 collective-permute-start.18
  96.6 0.1 shard_map.130
  96.7 0.4 collective-permute-start.21
  97.1 1.2 collective-permute-start.22
  98.4 0.9 collective-permute-done.16.refs_0_
  99.2 1.9 %collective-permute-start.23 = (bf16[128,768]{1,0:T(8,128)(2,1)S(1)}, bf16[128,768]{1,0:T(8,128)(2,1)S(1)}, u32[]{:S(2)}, u32[]{:S(2)}) collective-permute-start(bf16[128,768]{1,0:T(8,128)(2,1)S(1)} %get-tuple-element.95), channel_id=1, source_target_pairs={{0,12},{4,8},{8,4},{12,0},{1,13},{5,9},{9,5},{13,1},{2,14},{6,10},... | collective-permute-start | bytes 589832 | tf_op jit(solution)/shard_map/ppermute | solution.py:325
  101.1 4.2 %collective-permute-done.18.refs_2_ = bf16[128,768]{1,0:T(8,128)(2,1)S(1)} collective-permute-done((bf16[128,768]{1,0:T(8,128)(2,1)S(1)}, bf16[128,768]{1,0:T(8,128)(2,1)S(1)}, u32[]{:S(2)}, u32[]{:S(2)}) %collective-permute-start.18) | collective-permute-done | bytes 196640 | tf_op jit(solution)/shard_map/ppermute | solution.py:325
  105.4 0.1 shard_map.128.near_ref
  105.5 2.3 %collective-permute-start.19 = (bf16[128,768]{1,0:T(8,128)(2,1)S(1)}, bf16[128,768]{1,0:T(8,128)(2,1)S(1)}, u32[]{:S(2)}, u32[]{:S(2)}) collective-permute-start(bf16[128,768]{1,0:T(8,128)(2,1)S(1)} %shard_map.128.near_ref), channel_id=1, source_target_pairs={{0,1},{1,0},{2,3},{3,2},{4,5},{5,4},{6,7},{7,6},{8,9},{9,8},{10,11... | collective-permute-start | bytes 589832 | tf_op jit(solution)/shard_map/ppermute | solution.py:329
  107.8 0.5 collective-permute-done.22.refs_1_
  108.4 5.4 %collective-permute-done.23.refs_2_ = bf16[128,768]{1,0:T(8,128)(2,1)S(1)} collective-permute-done((bf16[128,768]{1,0:T(8,128)(2,1)S(1)}, bf16[128,768]{1,0:T(8,128)(2,1)S(1)}, u32[]{:S(2)}, u32[]{:S(2)}) %collective-permute-start.23) | collective-permute-done | bytes 196640 | tf_op jit(solution)/shard_map/ppermute | solution.py:325
  114.0 1.4 %collective-permute-start.24 = (bf16[128,768]{1,0:T(8,128)(2,1)S(1)}, bf16[128,768]{1,0:T(8,128)(2,1)S(1)}, u32[]{:S(2)}, u32[]{:S(2)}) collective-permute-start(bf16[128,768]{1,0:T(8,128)(2,1)S(1)} %shard_map.131.far_ref), channel_id=1, source_target_pairs={{0,1},{1,0},{2,3},{3,2},{4,5},{5,4},{6,7},{7,6},{8,9},{9,8},{10,11... | collective-permute-start | bytes 589832 | tf_op jit(solution)/shard_map/ppermute | solution.py:329
  115.4 1.1 collective-permute-done.24.far_oth_ref
  116.4 2.5 %shard_map.132 = (bf16[256,768]{1,0:T(8,128)(2,1)S(1)}, bf16[16,768]{1,0:T(8,128)(2,1)S(1)}, bf16[16,768]{1,0:T(8,128)(2,1)S(1)}, bf16[256,768]{1,0:T(8,128)(2,1)S(1)}) custom-call(s32[3]{0:T(128)S(1)} %pad_add_fusion.me_ref, bf16[128,768]{1,0:T(8,128)(2,1)S(1)} %shard_map.128.near_ref, bf16[128,768]{1,0:T(8,128)(2,1)S(1)} %collective-permute-done.19.near_oth_ref, ...), custom_call_target="tpu_custom_call" | custom-call | flops 1207959552 | bytes 4718592 | tf_op jit(solution)/shard_map/pallas_call | solution.py:82
  118.9 2.7 %collective-permute-start.25 = (bf16[16,768]{1,0:T(8,128)(2,1)S(1)}, bf16[16,768]{1,0:T(8,128)(2,1)S(1)}, u32[]{:S(2)}, u32[]{:S(2)}) collective-permute-start(bf16[16,768]{1,0:T(8,128)(2,1)S(1)} %get-tuple-element.109), channel_id=1, source_target_pairs={{0,2},{2,4},{4,6},{6,8},{8,10},{10,12},{12,14},{14,16},{16,18},{18... | collective-permute-start | bytes 73736 | tf_op jit(solution)/shard_map/ppermute | solution.py:300
  121.6 3.7 %collective-permute-start.26 = (bf16[16,768]{1,0:T(8,128)(2,1)S(1)}, bf16[16,768]{1,0:T(8,128)(2,1)S(1)}, u32[]{:S(2)}, u32[]{:S(2)}) collective-permute-start(bf16[16,768]{1,0:T(8,128)(2,1)S(1)} %get-tuple-element.110), channel_id=1, source_target_pairs={{2,0},{4,2},{6,4},{8,6},{10,8},{12,10},{14,12},{16,14},{18,16},{20... | collective-permute-start | bytes 73736 | tf_op jit(solution)/shard_map/ppermute | solution.py:301
  125.3 4.4 %shard_map.133.act_ref = bf16[256,768]{1,0:T(8,128)(2,1)S(1)} custom-call(bf16[256,768]{1,0:T(8,128)(2,1)S(1)} %get-tuple-element.105.glu_ref, s32[8,280,128]{2,1,0:T(8,128)S(1)} %copy-done.2, f32[32,768]{1,0:T(8,128)S(1)} %copy-done.6, f32[1,768]{1,0:T(1,128)S(1)} %broadcast_in_dim.18.scale_ref, f32[1,768]{1,0:T(1,128)S(1)} %broadcast_in_dim.19.shift_ref), custom_call_target="tpu_custom_call" | custom-call | flops 6291456 | bytes 3145728 | tf_op jit(solution)/shard_map/pallas_call | solution.py:82
  129.7 0.8 shard_map.134
  130.6 2.9 %all_gather.7 = bf16[256,1536]{1,0:T(8,128)(2,1)S(1)} all-gather(bf16[256,768]{1,0:T(8,128)(2,1)S(1)} %shard_map.134), channel_id=1, replica_groups=mesh['ah'=2,'bh'=2,'bl'=2,'al'=2,'hid'=2] {'hid'}, dimensions={1}, use_global_device_ids=true | all-gather | bytes 1179648 | tf_op jit(solution)/shard_map/all_gather | solution.py:319
  133.5 1.5 %add_convert_fusion = bf16[256,768]{1,0:T(8,128)(2,1)} fusion(bf16[256,768]{1,0:T(8,128)(2,1)S(1)} %get-tuple-element.104, bf16[256,1536]{1,0:T(8,128)(2,1)S(1)} %all_gather.7, bf16[1536,768]{1,0:T(8,128)(2,1)S(1)} %copy-done), kind=kOutput, calls=%fused_computation | convolution fusion | flops 604569600 | bytes 3932160 | tf_op jit(solution)/shard_map/dot_general | solution.py:320
  (55 shorter events, 0.5 us)
Async XLA Ops:
  0.0 133.5 %copy-start = (bf16[1536,768]{1,0:T(8,128)(2,1)S(1)}, bf16[1536,768]{1,0:T(8,128)(2,1)}, u32[]{:S(2)}) copy-start(bf16[1536,768]{1,0:T(8,128)(2,1)} %param.22) | copy-start | bytes 7077892
  2.5 17.2 %copy-start.16 = (s32[64]{0:T(128)S(1)}, s32[64]{0:T(128)}, u32[]{:S(2)}) copy-start(s32[64]{0:T(128)} %lengths_ref.1) | copy-start | bytes 772
  2.5 30.7 %all-to-all-start = ((bf16[4,192,768]{2,1,0:T(8,128)(2,1)}), bf16[4,192,768]{2,1,0:T(8,128)(2,1)S(1)}, u32[]{:S(2)}, u32[]{:S(2)}) async-start(bf16[4,192,768]{2,1,0:T(8,128)(2,1)} %shard_map.119), calls=%async_computation | async-start | bytes 2359296 | tf_op jit(solution)/shard_map/all_to_all | solution.py:333
  6.4 26.6 %collective-permute-start = (bf16[96,3072]{1,0:T(8,128)(2,1)}, bf16[96,3072]{1,0:T(8,128)(2,1)}, u32[]{:S(2)}, u32[]{:S(2)}) collective-permute-start(bf16[96,3072]{1,0:T(8,128)(2,1)} %refs_0_.1), channel_id=1, source_target_pairs={{0,16},{16,0},{1,17},{17,1},{2,18},{18,2},{3,19},{19,3},{4,20},{20... | collective-permute-start | bytes 1769480 | tf_op jit(solution)/shard_map/ppermute | solution.py:329
  15.0 0.8 copy-start.7
  15.7 0.7 copy-start.11
  16.4 0.7 copy-start.13
  17.1 15.9 %collective-permute-start.1 = (bf16[128,1536]{1,0:T(8,128)(2,1)}, bf16[128,1536]{1,0:T(8,128)(2,1)}, u32[]{:S(2)}, u32[]{:S(2)}) collective-permute-start(bf16[128,1536]{1,0:T(8,128)(2,1)} %get-tuple-element.61.refs_0_), channel_id=1, source_target_pairs={{0,4},{4,0},{8,12},{12,8},{1,5},{5,1},{9,13},{13,9},{2,6},{6,2},{1... | collective-permute-start | bytes 1179656 | tf_op jit(solution)/shard_map/ppermute | solution.py:325
  22.2 1.0 copy-start.1
  33.2 27.0 %collective-permute-start.3 = (bf16[4,192,768]{2,1,0:T(8,128)(2,1)S(1)}, bf16[4,192,768]{2,1,0:T(8,128)(2,1)}, u32[]{:S(2)}, u32[]{:S(2)}) collective-permute-start(bf16[4,192,768]{2,1,0:T(8,128)(2,1)S(1)} %all-to-all-done.both_ref.refs_5_.refs_0_), channel_id=1, source_target_pairs={{0,2},{2,0},{1,3},{3,1},{4,6},{6,4},{5,7},{7,5},{8,10},{10,8},{9,1... | collective-permute-start | bytes 3538952 | tf_op jit(solution)/shard_map/ppermute | solution.py:329
  35.6 0.8 copy-start.5
  36.4 23.8 %all-to-all-start.1 = ((bf16[4,96,768]{2,1,0:T(8,128)(2,1)}), bf16[4,96,768]{2,1,0:T(8,128)(2,1)}, u32[]{:S(2)}, u32[]{:S(2)}) async-start(bf16[4,96,768]{2,1,0:T(8,128)(2,1)} %copy-done.5), calls=%async_computation.1 | async-start | bytes 1179648 | tf_op jit(solution)/shard_map/all_to_all | solution.py:333
  41.0 18.5 %collective-permute-start.5 = (bf16[128,1536]{1,0:T(8,128)(2,1)}, bf16[128,1536]{1,0:T(8,128)(2,1)S(1)}, u32[]{:S(2)}, u32[]{:S(2)}) collective-permute-start(bf16[128,1536]{1,0:T(8,128)(2,1)} %collective-permute-done.1.refs_1_), channel_id=1, source_target_pairs={{0,1},{1,0},{2,3},{3,2},{4,5},{5,4},{6,7},{7,6},{8,9},{9,8},{10,11... | collective-permute-start | bytes 1179656 | tf_op jit(solution)/shard_map/ppermute | solution.py:329
  43.7 0.7 copy-start.17
  44.4 15.1 %collective-permute-start.4 = (bf16[2,96,768]{2,1,0:T(8,128)(2,1)S(1)}, bf16[2,96,768]{2,1,0:T(8,128)(2,1)}, u32[]{:S(2)}, u32[]{:S(2)}) collective-permute-start(bf16[2,96,768]{2,1,0:T(8,128)(2,1)S(1)} %get-tuple-element.65), channel_id=1, source_target_pairs={{0,16},{16,0},{1,17},{17,1},{2,18},{18,2},{3,19},{19,3},{4,20},{20... | collective-permute-start | bytes 884744 | tf_op jit(solution)/shard_map/ppermute | solution.py:329
  46.8 16.3 %collective-permute-start.2 = (bf16[128,1536]{1,0:T(8,128)(2,1)}, bf16[128,1536]{1,0:T(8,128)(2,1)}, u32[]{:S(2)}, u32[]{:S(2)}) collective-permute-start(bf16[128,1536]{1,0:T(8,128)(2,1)} %get-tuple-element.61.refs_0_), channel_id=1, source_target_pairs={{0,8},{4,12},{8,0},{12,4},{1,9},{5,13},{9,1},{13,5},{2,10},{6,14},... | collective-permute-start | bytes 1179656 | tf_op jit(solution)/shard_map/ppermute | solution.py:325
  59.5 0.7 copy-start.9
  60.2 14.1 %collective-permute-start.6 = (bf16[4,96,768]{2,1,0:T(8,128)(2,1)}, bf16[4,96,768]{2,1,0:T(8,128)(2,1)S(1)}, u32[]{:S(2)}, u32[]{:S(2)}) collective-permute-start(bf16[4,96,768]{2,1,0:T(8,128)(2,1)} %all-to-all-done.1.refs_7_), channel_id=1, source_target_pairs={{0,2},{2,0},{1,3},{3,1},{4,6},{6,4},{5,7},{7,5},{8,10},{10,8},{9,1... | collective-permute-start | bytes 1769480 | tf_op jit(solution)/shard_map/ppermute | solution.py:329
  60.5 13.8 %collective-permute-start.7 = (bf16[2,96,768]{2,1,0:T(8,128)(2,1)}, bf16[2,96,768]{2,1,0:T(8,128)(2,1)S(1)}, u32[]{:S(2)}, u32[]{:S(2)}) collective-permute-start(bf16[2,96,768]{2,1,0:T(8,128)(2,1)} %copy-done.17), channel_id=1, source_target_pairs={{0,16},{16,0},{1,17},{17,1},{2,18},{18,2},{3,19},{19,3},{4,20},{20... | collective-permute-start | bytes 884744 | tf_op jit(solution)/shard_map/ppermute | solution.py:329
  64.0 7.6 %collective-permute-start.8 = (bf16[64,1536]{1,0:T(8,128)(2,1)S(1)}, bf16[64,1536]{1,0:T(8,128)(2,1)S(1)}, u32[]{:S(2)}, u32[]{:S(2)}) collective-permute-start(bf16[64,1536]{1,0:T(8,128)(2,1)S(1)} %get-tuple-element.70), channel_id=1, source_target_pairs={{0,4},{4,0},{8,12},{12,8},{1,5},{5,1},{9,13},{13,9},{2,6},{6,2},{1... | collective-permute-start | bytes 589832 | tf_op jit(solution)/shard_map/ppermute | solution.py:325
  64.2 18.6 %copy-start.8 = (bf16[128,1536]{1,0:T(8,128)(2,1)S(1)}, bf16[128,1536]{1,0:T(8,128)(2,1)}, u32[]{:S(2)}) copy-start(bf16[128,1536]{1,0:T(8,128)(2,1)} %copy-done.7) | copy-start | bytes 1179652
  64.2 18.6 %copy-start.10 = (bf16[128,1536]{1,0:T(8,128)(2,1)S(1)}, bf16[128,1536]{1,0:T(8,128)(2,1)}, u32[]{:S(2)}) copy-start(bf16[128,1536]{1,0:T(8,128)(2,1)} %copy-done.9) | copy-start | bytes 1179652
  64.2 7.4 %collective-permute-start.9 = (bf16[64,1536]{1,0:T(8,128)(2,1)S(1)}, bf16[64,1536]{1,0:T(8,128)(2,1)S(1)}, u32[]{:S(2)}, u32[]{:S(2)}) collective-permute-start(bf16[64,1536]{1,0:T(8,128)(2,1)S(1)} %get-tuple-element.71), channel_id=1, source_target_pairs={{0,4},{4,0},{8,12},{12,8},{1,5},{5,1},{9,13},{13,9},{2,6},{6,2},{1... | collective-permute-start | bytes 589832 | tf_op jit(solution)/shard_map/ppermute | solution.py:325
  65.6 17.3 %collective-permute-start.10 = (bf16[128,1536]{1,0:T(8,128)(2,1)}, bf16[128,1536]{1,0:T(8,128)(2,1)S(1)}, u32[]{:S(2)}, u32[]{:S(2)}) collective-permute-start(bf16[128,1536]{1,0:T(8,128)(2,1)} %collective-permute-done.2.ref.refs_2_), channel_id=1, source_target_pairs={{0,1},{1,0},{2,3},{3,2},{4,5},{5,4},{6,7},{7,6},{8,9},{9,8},{10,11... | collective-permute-start | bytes 1179656 | tf_op jit(solution)/shard_map/ppermute | solution.py:329
  74.3 14.4 %collective-permute-start.13 = (bf16[2,96,768]{2,1,0:T(8,128)(2,1)}, bf16[2,96,768]{2,1,0:T(8,128)(2,1)S(1)}, u32[]{:S(2)}, u32[]{:S(2)}) collective-permute-start(bf16[2,96,768]{2,1,0:T(8,128)(2,1)} %collective-permute-done.4.refs_0_), channel_id=1, source_target_pairs={{0,2},{2,0},{1,3},{3,1},{4,6},{6,4},{5,7},{7,5},{8,10},{10,8},{9,1... | collective-permute-start | bytes 884744 | tf_op jit(solution)/shard_map/ppermute | solution.py:329
  76.0 12.8 %collective-permute-start.14 = (bf16[2,96,768]{2,1,0:T(8,128)(2,1)S(1)}, bf16[2,96,768]{2,1,0:T(8,128)(2,1)S(1)}, u32[]{:S(2)}, u32[]{:S(2)}) collective-permute-start(bf16[2,96,768]{2,1,0:T(8,128)(2,1)S(1)} %collective-permute-done.7.refs_1_), channel_id=1, source_target_pairs={{0,2},{2,0},{1,3},{3,1},{4,6},{6,4},{5,7},{7,5},{8,10},{10,8},{9,1... | collective-permute-start | bytes 884744 | tf_op jit(solution)/shard_map/ppermute | solution.py:329
  76.0 6.8 %collective-permute-start.11 = (bf16[64,1536]{1,0:T(8,128)(2,1)S(1)}, bf16[64,1536]{1,0:T(8,128)(2,1)S(1)}, u32[]{:S(2)}, u32[]{:S(2)}) collective-permute-start(bf16[64,1536]{1,0:T(8,128)(2,1)S(1)} %collective-permute-done.8.refs_3_), channel_id=1, source_target_pairs={{0,1},{1,0},{2,3},{3,2},{4,5},{5,4},{6,7},{7,6},{8,9},{9,8},{10,11... | collective-permute-start | bytes 589832 | tf_op jit(solution)/shard_map/ppermute | solution.py:329
  79.4 3.5 %collective-permute-start.12 = (bf16[64,1536]{1,0:T(8,128)(2,1)S(1)}, bf16[64,1536]{1,0:T(8,128)(2,1)S(1)}, u32[]{:S(2)}, u32[]{:S(2)}) collective-permute-start(bf16[64,1536]{1,0:T(8,128)(2,1)S(1)} %collective-permute-done.9.refs_4_), channel_id=1, source_target_pairs={{0,1},{1,0},{2,3},{3,2},{4,5},{5,4},{6,7},{7,6},{8,9},{9,8},{10,11... | collective-permute-start | bytes 589832 | tf_op jit(solution)/shard_map/ppermute | solution.py:329
  88.8 4.3 %collective-permute-start.15 = (bf16[512,768]{1,0:T(8,128)(2,1)S(1)}, bf16[512,768]{1,0:T(8,128)(2,1)S(1)}, u32[]{:S(2)}, u32[]{:S(2)}) collective-permute-start(bf16[512,768]{1,0:T(8,128)(2,1)S(1)} %get-tuple-element.83), channel_id=1, source_target_pairs={{0,1},{1,0},{2,3},{3,2},{4,5},{5,4},{6,7},{7,6},{8,9},{9,8},{10,11... | collective-permute-start | bytes 2359304 | tf_op jit(solution)/shard_map/ppermute | solution.py:329
  92.9 12.4 %copy-start.14 = (bf16[128,768]{1,0:T(8,128)(2,1)S(1)}, bf16[128,768]{1,0:T(8,128)(2,1)}, u32[]{:S(2)}) copy-start(bf16[128,768]{1,0:T(8,128)(2,1)} %copy-done.13) | copy-start | bytes 589828
  93.0 3.6 %collective-permute-start.20 = (bf16[512,768]{1,0:T(8,128)(2,1)S(1)}, bf16[512,768]{1,0:T(8,128)(2,1)S(1)}, u32[]{:S(2)}, u32[]{:S(2)}) collective-permute-start(bf16[512,768]{1,0:T(8,128)(2,1)S(1)} %get-tuple-element.91), channel_id=1, source_target_pairs={{0,1},{1,0},{2,3},{3,2},{4,5},{5,4},{6,7},{7,6},{8,9},{9,8},{10,11... | collective-permute-start | bytes 2359304 | tf_op jit(solution)/shard_map/ppermute | solution.py:329
  93.2 20.6 %copy-start.12 = (bf16[128,768]{1,0:T(8,128)(2,1)S(1)}, bf16[128,768]{1,0:T(8,128)(2,1)}, u32[]{:S(2)}) copy-start(bf16[128,768]{1,0:T(8,128)(2,1)} %copy-done.11) | copy-start | bytes 589828
  93.2 6.0 %collective-permute-start.16 = (bf16[128,768]{1,0:T(8,128)(2,1)S(1)}, bf16[128,768]{1,0:T(8,128)(2,1)S(1)}, u32[]{:S(2)}, u32[]{:S(2)}) collective-permute-start(bf16[128,768]{1,0:T(8,128)(2,1)S(1)} %get-tuple-element.85), channel_id=1, source_target_pairs={{0,4},{4,0},{8,12},{12,8},{1,5},{5,1},{9,13},{13,9},{2,6},{6,2},{1... | collective-permute-start | bytes 589832 | tf_op jit(solution)/shard_map/ppermute | solution.py:325
  93.8 7.3 %collective-permute-start.17 = (bf16[128,768]{1,0:T(8,128)(2,1)S(1)}, bf16[128,768]{1,0:T(8,128)(2,1)S(1)}, u32[]{:S(2)}, u32[]{:S(2)}) collective-permute-start(bf16[128,768]{1,0:T(8,128)(2,1)S(1)} %get-tuple-element.86), channel_id=1, source_target_pairs={{0,8},{4,12},{8,0},{12,4},{1,9},{5,13},{9,1},{13,5},{2,10},{6,14},... | collective-permute-start | bytes 589832 | tf_op jit(solution)/shard_map/ppermute | solution.py:325
  95.5 9.9 %collective-permute-start.18 = (bf16[128,768]{1,0:T(8,128)(2,1)S(1)}, bf16[128,768]{1,0:T(8,128)(2,1)S(1)}, u32[]{:S(2)}, u32[]{:S(2)}) collective-permute-start(bf16[128,768]{1,0:T(8,128)(2,1)S(1)} %get-tuple-element.87), channel_id=1, source_target_pairs={{0,12},{4,8},{8,4},{12,0},{1,13},{5,9},{9,5},{13,1},{2,14},{6,10},... | collective-permute-start | bytes 589832 | tf_op jit(solution)/shard_map/ppermute | solution.py:325
  96.6 19.8 %copy-start.3 = (bf16[1536,768]{1,0:T(8,128)(2,1)S(1)}, bf16[1536,768]{1,0:T(8,128)(2,1)}, u32[]{:S(2)}) copy-start(bf16[1536,768]{1,0:T(8,128)(2,1)} %value_ref.1) | copy-start | bytes 7077892
  96.6 19.8 %copy-start.4 = (bf16[1536,768]{1,0:T(8,128)(2,1)S(1)}, bf16[1536,768]{1,0:T(8,128)(2,1)}, u32[]{:S(2)}) copy-start(bf16[1536,768]{1,0:T(8,128)(2,1)} %gate_ref.1) | copy-start | bytes 7077892
  96.6 19.8 %copy-start.15 = (f32[1,1536]{1,0:T(1,128)S(1)}, f32[1,1536]{1,0:T(1,128)}, u32[]{:S(2)}) copy-start(f32[1,1536]{1,0:T(1,128)} %broadcast_in_dim.17.gain_ref) | copy-start | bytes 18436
  96.7 11.1 %collective-permute-start.21 = (bf16[128,768]{1,0:T(8,128)(2,1)S(1)}, bf16[128,768]{1,0:T(8,128)(2,1)S(1)}, u32[]{:S(2)}, u32[]{:S(2)}) collective-permute-start(bf16[128,768]{1,0:T(8,128)(2,1)S(1)} %get-tuple-element.93), channel_id=1, source_target_pairs={{0,4},{4,0},{8,12},{12,8},{1,5},{5,1},{9,13},{13,9},{2,6},{6,2},{1... | collective-permute-start | bytes 589832 | tf_op jit(solution)/shard_map/ppermute | solution.py:325
  97.1 11.3 %collective-permute-start.22 = (bf16[128,768]{1,0:T(8,128)(2,1)S(1)}, bf16[128,768]{1,0:T(8,128)(2,1)S(1)}, u32[]{:S(2)}, u32[]{:S(2)}) collective-permute-start(bf16[128,768]{1,0:T(8,128)(2,1)S(1)} %get-tuple-element.94), channel_id=1, source_target_pairs={{0,8},{4,12},{8,0},{12,4},{1,9},{5,13},{9,1},{13,5},{2,10},{6,14},... | collective-permute-start | bytes 589832 | tf_op jit(solution)/shard_map/ppermute | solution.py:325
  99.2 14.6 %collective-permute-start.23 = (bf16[128,768]{1,0:T(8,128)(2,1)S(1)}, bf16[128,768]{1,0:T(8,128)(2,1)S(1)}, u32[]{:S(2)}, u32[]{:S(2)}) collective-permute-start(bf16[128,768]{1,0:T(8,128)(2,1)S(1)} %get-tuple-element.95), channel_id=1, source_target_pairs={{0,12},{4,8},{8,4},{12,0},{1,13},{5,9},{9,5},{13,1},{2,14},{6,10},... | collective-permute-start | bytes 589832 | tf_op jit(solution)/shard_map/ppermute | solution.py:325
  105.5 8.3 %collective-permute-start.19 = (bf16[128,768]{1,0:T(8,128)(2,1)S(1)}, bf16[128,768]{1,0:T(8,128)(2,1)S(1)}, u32[]{:S(2)}, u32[]{:S(2)}) collective-permute-start(bf16[128,768]{1,0:T(8,128)(2,1)S(1)} %shard_map.128.near_ref), channel_id=1, source_target_pairs={{0,1},{1,0},{2,3},{3,2},{4,5},{5,4},{6,7},{7,6},{8,9},{9,8},{10,11... | collective-permute-start | bytes 589832 | tf_op jit(solution)/shard_map/ppermute | solution.py:329
  113.9 11.4 %copy-start.2 = (s32[8,280,128]{2,1,0:T(8,128)S(1)}, s32[8,280,128]{2,1,0:T(8,128)}, u32[]{:S(2)}) copy-start(s32[8,280,128]{2,1,0:T(8,128)} %copy-done.1) | copy-start | bytes 3440644
  113.9 11.4 %copy-start.6 = (f32[32,768]{1,0:T(8,128)S(1)}, f32[32,768]{1,0:T(8,128)}, u32[]{:S(2)}) copy-start(f32[32,768]{1,0:T(8,128)} %taps_ref.3) | copy-start | bytes 294916
  114.0 2.5 %collective-permute-start.24 = (bf16[128,768]{1,0:T(8,128)(2,1)S(1)}, bf16[128,768]{1,0:T(8,128)(2,1)S(1)}, u32[]{:S(2)}, u32[]{:S(2)}) collective-permute-start(bf16[128,768]{1,0:T(8,128)(2,1)S(1)} %shard_map.131.far_ref), channel_id=1, source_target_pairs={{0,1},{1,0},{2,3},{3,2},{4,5},{5,4},{6,7},{7,6},{8,9},{9,8},{10,11... | collective-permute-start | bytes 589832 | tf_op jit(solution)/shard_map/ppermute | solution.py:329
  118.9 10.8 %collective-permute-start.25 = (bf16[16,768]{1,0:T(8,128)(2,1)S(1)}, bf16[16,768]{1,0:T(8,128)(2,1)S(1)}, u32[]{:S(2)}, u32[]{:S(2)}) collective-permute-start(bf16[16,768]{1,0:T(8,128)(2,1)S(1)} %get-tuple-element.109), channel_id=1, source_target_pairs={{0,2},{2,4},{4,6},{6,8},{8,10},{10,12},{12,14},{14,16},{16,18},{18... | collective-permute-start | bytes 73736 | tf_op jit(solution)/shard_map/ppermute | solution.py:300
  121.6 8.1 %collective-permute-start.26 = (bf16[16,768]{1,0:T(8,128)(2,1)S(1)}, bf16[16,768]{1,0:T(8,128)(2,1)S(1)}, u32[]{:S(2)}, u32[]{:S(2)}) collective-permute-start(bf16[16,768]{1,0:T(8,128)(2,1)S(1)} %get-tuple-element.110), channel_id=1, source_target_pairs={{2,0},{4,2},{6,4},{8,6},{10,8},{12,10},{14,12},{16,14},{18,16},{20... | collective-permute-start | bytes 73736 | tf_op jit(solution)/shard_map/ppermute | solution.py:301

commit v8 on v7

--- a/solution.py
+++ b/solution.py
@@ -253,23 +253,43 @@
 
 def inner_conv_kernel(glu_ref, utter_ref, taps_ref, scale_ref, shift_ref, out_ref, ext_ref):
     ext_ref[...] = f32(glu_ref[...])
+    edge = jnp.zeros((HALO, out_ref.shape[1]), out_ref.dtype)
+    out_ref[:HALO, :] = edge
+    out_ref[out_ref.shape[0] - HALO :, :] = edge
     step = 2 * HALO
     tiles = [(at - HALO, at, at) for at in range(HALO, out_ref.shape[0] - HALO, step)]
     conv_rows(ext_ref, utter_ref, taps_ref, scale_ref, shift_ref, out_ref, tiles, step)
 
 
 def edge_conv_kernel(
-    act_ref, top_ref, glu_ref, bottom_ref, utter_ref, taps_ref, scale_ref, shift_ref, out_ref, ext_ref
+    top_ref, glu_ref, bottom_ref, utter_ref, taps_ref, scale_ref, shift_ref, out_ref, ext_ref
 ):
-    rows = out_ref.shape[0]
+    rows = glu_ref.shape[0]
     last = rows - HALO
-    out_ref[HALO:last, :] = act_ref[HALO:last, :]
     ext_ref[:HALO, :] = f32(top_ref[...])
     ext_ref[HALO : 3 * HALO, :] = f32(glu_ref[: 2 * HALO, :])
     ext_ref[3 * HALO : 5 * HALO, :] = f32(glu_ref[rows - 2 * HALO :, :])
     ext_ref[5 * HALO :, :] = f32(bottom_ref[...])
-    tiles = [(0, 0, 0), (3 * HALO, last, last)]
+    tiles = [(0, 0, 0), (3 * HALO, last, HALO)]
     conv_rows(ext_ref, utter_ref, taps_ref, scale_ref, shift_ref, out_ref, tiles, HALO)
+
+
+def project_kernel(
+    me_ref, inner_ref, inner_oth_ref, edge_ref, edge_oth_ref, mid_ref, w_ref, out_ref, act_ref
+):
+    rows, width = out_ref.shape
+    last = rows - HALO
+    me_c = me_ref[1]
+    for core, inner, edge in (
+        (me_c, inner_ref, edge_ref),
+        (1 - me_c, inner_oth_ref, edge_oth_ref),
+    ):
+        at = pl.ds(pl.multiple_of(core * width, width), width)
+        act_ref[:HALO, at] = edge[:HALO, :]
+        act_ref[HALO:last, at] = inner[HALO:last, :]
+        act_ref[last:, at] = edge[HALO:, :]
+    projected = jnp.dot(act_ref[...], w_ref[...], preferred_element_type=jnp.float32)
+    out_ref[...] = (f32(mid_ref[...]) + projected).astype(out_ref.dtype)
 
 
 def utterances(rows, axis, lengths, taps):
@@ -300,7 +320,7 @@
     top = lax.ppermute(tail, axis, [(i, i + 1) for i in range(count - 1)])
     bottom = lax.ppermute(head, axis, [(i + 1, i) for i in range(count - 1)])
     rest = [utter, depth_kernel, bn_scale, bn_shift]
-    (act,) = kernel_call(
+    (inner,) = kernel_call(
         inner_conv_kernel,
         [((rows, width), bf16)],
         [glu, *rest],
@@ -308,17 +328,25 @@
         flops=rows * depth_kernel.size,
         moved=16 * rows * width,
     )
-    (act,) = kernel_call(
+    inner_oth = swap(inner, "hid")
+    (edge,) = kernel_call(
         edge_conv_kernel,
-        [((rows, width), bf16)],
-        [act, top, glu, bottom, *rest],
+        [((2 * HALO, width), bf16)],
+        [top, glu, bottom, *rest],
         scratch=[pltpu.VMEM((6 * HALO, width), jnp.float32)],
         flops=HALO * depth_kernel.size,
         moved=4 * rows * width,
     )
-    act_full = lax.all_gather(act, "hid", axis=1, tiled=True)
-    projected = jnp.dot(act_full, w_proj, preferred_element_type=jnp.float32)
-    return (mid_own.astype(jnp.float32) + projected).astype(jnp.bfloat16)
+    (out,) = kernel_call(
+        project_kernel,
+        [((rows, width), bf16)],
+        [me, inner, inner_oth, edge, swap(edge, "hid"), mid_own, w_proj],
+        scratch=[pltpu.VMEM((rows, 2 * width), bf16)],
+        scalars=1,
+        flops=4 * rows * width * width,
+        moved=2 * w_proj.size,
+    )
+    return out
 
 
 def partner(values, step):

time: 137 us -> 140 us (1.022)
  waiting for transfers between devices: 38.3 us -> 46.6 us
  blocking collectives: 6.64 us -> 3.5 us
  starting transfers between devices: 50.5 us -> 52.2 us
  matrix products: 1.52 us -> 0 us
  local copies, waits for them, and re-layouts: 8.84 us -> 7.35 us
    ppermute x10, waiting for transfers between devices: 22.8 us -> 26.4 us  [partner(): return lax.ppermute(values, GROUP, [(i, i ^ step) for i in range(4)])]
    all_gather x1 -> x0, blocking collectives: 2.93 us -> none  [grouped_conv_module(): act_full = lax.all_gather(act, 'hid', axis=1, tiled=True)]
    ppermute x15 -> x17, starting transfers between devices: 26.1 us -> 28.7 us  [swap(): return lax.ppermute(values, axis, SWAP)]
    broadcast_in_dim x3, local copies, waits for them, and re-layouts: 2.67 us -> 0.01 us  [local(): early = (utter, conv_gain[None, :], bn_scale[None, :], bn_shift[None, :])]
    ppermute x15 -> x17, waiting for transfers between devices: 15.3 us -> 17.7 us  [swap(): return lax.ppermute(values, axis, SWAP)]
    unnamed x36 -> x48, local copies, waits for them, and re-layouts: 5.47 us -> 7.33 us
    ppermute x10, starting transfers between devices: 9.62 us -> 8 us  [partner(): return lax.ppermute(values, GROUP, [(i, i ^ step) for i in range(4)])]
    ppermute x1, waiting for transfers between devices: 0.01 us -> 1.59 us  [grouped_conv_module(): bottom = lax.ppermute(head, axis, [(i + 1, i) for i in range(count - 1)])]
  transfers between devices with their start and end apart: 29 -> 31, of which waited for: 10 -> 13; matrix products, arithmetic and copies ran while one was open for 3% -> 0% of each run, Pallas kernels for 17% -> 12%
where the time goes in v8:
time: 140 us; the launch traced here: 138 us
  starting transfers between devices  52.2 us (37%)
  waiting for transfers between devices  46.6 us (33%)
  Pallas kernels  27.5 us (20%)
  local copies, waits for them, and re-layouts  7.35 us (5%)
  blocking collectives  3.5 us (2%)
    ppermute x17, starting transfers between devices, swap(): return lax.ppermute(values, axis, SWAP)  28.7 us
    pallas_call x18, Pallas kernels, kernel_call(): pl.pallas_call(body, out_shape=[jax.ShapeDtypeStruct(shape, dtype) for sh...  27.5 us
    ppermute x10, waiting for transfers between devices, partner(): return lax.ppermute(values, GROUP, [(i, i ^ step) for i in range(4)])  26.4 us
    ppermute x17, waiting for transfers between devices, swap(): return lax.ppermute(values, axis, SWAP)  17.7 us
    all_to_all x2, starting transfers between devices, recut(): return lax.all_to_all(parts, GROUP, 0, 0)  9.35 us
    ppermute x10, starting transfers between devices, partner(): return lax.ppermute(values, GROUP, [(i, i ^ step) for i in range(4)])  8 us
    unnamed x48, local copies, waits for them, and re-layouts  7.33 us
    all_gather x1, blocking collectives, grouped_ffn(): whole = lax.all_gather(tokens, 'hid', axis=1, tiled=True)  3.5 us
  transfers between devices with their start and end apart: 31, of which 13 were waited for; matrix products, arithmetic and copies ran while one was open for 0% of the time, Pallas kernels for 12%

profile of v8, /device:TPU:5, one launch (start us, length us, event | category | flops | bytes accessed | tf_op | source)
XLA Modules:
  0.0 137.7 jit_solution(9466152500251425429)
XLA Ops:
  0.0 2.3 %shard_map.119 = bf16[4,192,768]{2,1,0:T(8,128)(2,1)} custom-call(bf16[96,3072]{1,0:T(8,128)(2,1)} %refs_0_.1, bf16[96,3072]{1,0:T(8,128)(2,1)} %bitcast.5), custom_call_target="tpu_custom_call" | custom-call | tf_op jit(solution)/shard_map/pallas_call | solution.py:82
  2.3 3.9 %all-to-all-start = ((bf16[4,192,768]{2,1,0:T(8,128)(2,1)}), bf16[4,192,768]{2,1,0:T(8,128)(2,1)S(1)}, u32[]{:S(2)}, u32[]{:S(2)}) async-start(bf16[4,192,768]{2,1,0:T(8,128)(2,1)} %shard_map.119), calls=%async_computation | async-start | bytes 2359296 | tf_op jit(solution)/shard_map/all_to_all | solution.py:361
  6.2 2.4 %collective-permute-start = (bf16[96,3072]{1,0:T(8,128)(2,1)}, bf16[96,3072]{1,0:T(8,128)(2,1)S(1)}, u32[]{:S(2)}, u32[]{:S(2)}) collective-permute-start(bf16[96,3072]{1,0:T(8,128)(2,1)} %refs_0_.1), channel_id=1, source_target_pairs={{0,16},{16,0},{1,17},{17,1},{2,18},{18,2},{3,19},{19,3},{4,20},{20... | collective-permute-start | bytes 1769480 | tf_op jit(solution)/shard_map/ppermute | solution.py:357
  8.7 3.5 %all_gather.3.whole_ref = bf16[256,1536]{1,0:T(8,128)(2,1)S(1)} all-gather(bf16[256,768]{1,0:T(8,128)(2,1)S(1)} %copy-done.19), channel_id=1, replica_groups=mesh['ah'=2,'bh'=2,'bl'=2,'al'=2,'hid'=2] {'hid'}, dimensions={1}, use_global_device_ids=true | all-gather | bytes 1179648 | tf_op jit(solution)/shard_map/all_gather | solution.py:379
  12.2 1.1 shard_map.118
  13.3 0.8 copy-done.6
  14.1 0.7 copy-done.13
  14.7 0.7 copy-done.15
  15.5 2.4 %shard_map.120.utter_ref = s32[8,280,128]{2,1,0:T(8,128)S(1)} custom-call(s32[1]{0:T(128)} %bitcast.4.first_ref, s32[64]{0:T(128)S(1)} %copy-done.17), custom_call_target="tpu_custom_call" | custom-call | tf_op jit(solution)/shard_map/pallas_call | solution.py:82
  17.9 13.2 %collective-permute-done.1.refs_1_ = bf16[128,1536]{1,0:T(8,128)(2,1)} collective-permute-done((bf16[128,1536]{1,0:T(8,128)(2,1)S(1)}, bf16[128,1536]{1,0:T(8,128)(2,1)}, u32[]{:S(2)}, u32[]{:S(2)}) %collective-permute-start.1) | collective-permute-done | bytes 393248 | tf_op jit(solution)/shard_map/ppermute | solution.py:353
  31.1 0.8 copy-done.4
  31.9 0.9 all-to-all-done.both_ref.refs_5_.refs_0_
  32.8 1.2 collective-permute-start.3
  34.1 1.1 copy-done.5
  35.2 0.8 copy-done.3
  36.0 5.5 %all-to-all-start.1 = ((bf16[4,96,768]{2,1,0:T(8,128)(2,1)}), bf16[4,96,768]{2,1,0:T(8,128)(2,1)}, u32[]{:S(2)}, u32[]{:S(2)}) async-start(bf16[4,96,768]{2,1,0:T(8,128)(2,1)} %copy-done.3), calls=%async_computation.1 | async-start | bytes 1179648 | tf_op jit(solution)/shard_map/all_to_all | solution.py:361
  41.5 2.7 %collective-permute-start.5 = (bf16[128,1536]{1,0:T(8,128)(2,1)}, bf16[128,1536]{1,0:T(8,128)(2,1)S(1)}, u32[]{:S(2)}, u32[]{:S(2)}) collective-permute-start(bf16[128,1536]{1,0:T(8,128)(2,1)} %collective-permute-done.1.refs_1_), channel_id=1, source_target_pairs={{0,1},{1,0},{2,3},{3,2},{4,5},{5,4},{6,7},{7,6},{8,9},{9,8},{10,11... | collective-permute-start | bytes 1179656 | tf_op jit(solution)/shard_map/ppermute | solution.py:357
  44.2 0.7 copy-done.18
  44.9 2.4 %collective-permute-start.4 = (bf16[2,96,768]{2,1,0:T(8,128)(2,1)S(1)}, bf16[2,96,768]{2,1,0:T(8,128)(2,1)}, u32[]{:S(2)}, u32[]{:S(2)}) collective-permute-start(bf16[2,96,768]{2,1,0:T(8,128)(2,1)S(1)} %get-tuple-element.65), channel_id=1, source_target_pairs={{0,16},{16,0},{1,17},{17,1},{2,18},{18,2},{3,19},{19,3},{4,20},{20... | collective-permute-start | bytes 884744 | tf_op jit(solution)/shard_map/ppermute | solution.py:357
  47.4 1.2 collective-permute-start.2
  48.6 11.7 %collective-permute-done.4.refs_0_ = bf16[2,96,768]{2,1,0:T(8,128)(2,1)} collective-permute-done((bf16[2,96,768]{2,1,0:T(8,128)(2,1)S(1)}, bf16[2,96,768]{2,1,0:T(8,128)(2,1)}, u32[]{:S(2)}, u32[]{:S(2)}) %collective-permute-start.4) | collective-permute-done | bytes 294944 | tf_op jit(solution)/shard_map/ppermute | solution.py:357
  60.2 0.7 copy-done.10
  61.0 0.3 collective-permute-start.6
  61.2 0.3 collective-permute-start.7
  61.5 2.1 %collective-permute-done.2.ref.refs_2_ = bf16[128,1536]{1,0:T(8,128)(2,1)} collective-permute-done((bf16[128,1536]{1,0:T(8,128)(2,1)}, bf16[128,1536]{1,0:T(8,128)(2,1)}, u32[]{:S(2)}, u32[]{:S(2)}) %collective-permute-start.2) | collective-permute-done | bytes 393248 | tf_op jit(solution)/shard_map/ppermute | solution.py:353
  63.6 1.1 shard_map.123
  64.8 1.4 %collective-permute-start.9 = (bf16[64,1536]{1,0:T(8,128)(2,1)S(1)}, bf16[64,1536]{1,0:T(8,128)(2,1)S(1)}, u32[]{:S(2)}, u32[]{:S(2)}) collective-permute-start(bf16[64,1536]{1,0:T(8,128)(2,1)S(1)} %get-tuple-element.71), channel_id=1, source_target_pairs={{0,4},{4,0},{8,12},{12,8},{1,5},{5,1},{9,13},{13,9},{2,6},{6,2},{1... | collective-permute-start | bytes 589832 | tf_op jit(solution)/shard_map/ppermute | solution.py:353
  66.2 5.6 %collective-permute-start.10 = (bf16[128,1536]{1,0:T(8,128)(2,1)}, bf16[128,1536]{1,0:T(8,128)(2,1)S(1)}, u32[]{:S(2)}, u32[]{:S(2)}) collective-permute-start(bf16[128,1536]{1,0:T(8,128)(2,1)} %collective-permute-done.2.ref.refs_2_), channel_id=1, source_target_pairs={{0,1},{1,0},{2,3},{3,2},{4,5},{5,4},{6,7},{7,6},{8,9},{9,8},{10,11... | collective-permute-start | bytes 1179656 | tf_op jit(solution)/shard_map/ppermute | solution.py:357
  71.8 4.0 %collective-permute-done.7.refs_1_ = bf16[2,96,768]{2,1,0:T(8,128)(2,1)S(1)} collective-permute-done((bf16[2,96,768]{2,1,0:T(8,128)(2,1)}, bf16[2,96,768]{2,1,0:T(8,128)(2,1)S(1)}, u32[]{:S(2)}, u32[]{:S(2)}) %collective-permute-start.7) | collective-permute-done | bytes 294944 | tf_op jit(solution)/shard_map/ppermute | solution.py:357
  75.8 1.3 collective-permute-start.13
  77.1 0.2 collective-permute-start.14
  77.3 2.9 %collective-permute-start.11 = (bf16[64,1536]{1,0:T(8,128)(2,1)S(1)}, bf16[64,1536]{1,0:T(8,128)(2,1)S(1)}, u32[]{:S(2)}, u32[]{:S(2)}) collective-permute-start(bf16[64,1536]{1,0:T(8,128)(2,1)S(1)} %collective-permute-done.8.refs_3_), channel_id=1, source_target_pairs={{0,1},{1,0},{2,3},{3,2},{4,5},{5,4},{6,7},{7,6},{8,9},{9,8},{10,11... | collective-permute-start | bytes 589832 | tf_op jit(solution)/shard_map/ppermute | solution.py:357
  80.2 1.0 copy-done.9
  81.2 3.0 %shard_map.124.own_ref = bf16[512,768]{1,0:T(8,128)(2,1)S(1)} custom-call(s32[3]{0:T(128)S(1)} %pad_add_fusion.me_ref, bf16[128,1536]{1,0:T(8,128)(2,1)S(1)} %copy-done.9, bf16[128,1536]{1,0:T(8,128)(2,1)} %collective-permute-done.1.refs_1_, bf16[128,1536]{1,0:T(8,128)(2,1)} %collective-permute-done.2.ref.refs_2_, ...), custom_call_target="tpu_custom_call" | custom-call | tf_op jit(solution)/shard_map/pallas_call | solution.py:82
  84.2 2.7 %shard_map.125.oth_ref = bf16[512,768]{1,0:T(8,128)(2,1)S(1)} custom-call(s32[3]{0:T(128)S(1)} %pad_add_fusion.me_ref, bf16[128,1536]{1,0:T(8,128)(2,1)S(1)} %copy-done.7, bf16[128,1536]{1,0:T(8,128)(2,1)S(1)} %copy-done.11, bf16[128,1536]{1,0:T(8,128)(2,1)S(1)} %collective-permute-done.10.refs_2_, bf16[64,1536]{1,0:T(8,128)(2,1)S(1)} %collective-permute-done.11.refs_3_, ...), custom_call_target="tpu_custom_call" | custom-call | tf_op jit(solution)/shard_map/pallas_call | solution.py:82
  86.9 2.1 %shard_map.126 = (f32[512,768]{1,0:T(8,128)S(1)}, bf16[512,768]{1,0:T(8,128)(2,1)S(1)}) custom-call(s32[3]{0:T(128)S(1)} %pad_add_fusion.me_ref, bf16[512,768]{1,0:T(8,128)(2,1)S(1)} %shard_map.124.own_ref, bf16[512,768]{1,0:T(8,128)(2,1)S(1)} %shard_map.125.oth_ref, bf16[4,192,768]{2,1,0:T(8,128)(2,1)S(1)} %all-to-all-done.both_ref.refs_5_.refs_0_, ...), custom_call_target="tpu_custom_call" | custom-call | tf_op jit(solution)/shard_map/pallas_call | solution.py:82
  89.0 2.7 %collective-permute-start.15 = (bf16[512,768]{1,0:T(8,128)(2,1)S(1)}, bf16[512,768]{1,0:T(8,128)(2,1)S(1)}, u32[]{:S(2)}, u32[]{:S(2)}) collective-permute-start(bf16[512,768]{1,0:T(8,128)(2,1)S(1)} %get-tuple-element.83), channel_id=1, source_target_pairs={{0,1},{1,0},{2,3},{3,2},{4,5},{5,4},{6,7},{7,6},{8,9},{9,8},{10,11... | collective-permute-start | bytes 2359304 | tf_op jit(solution)/shard_map/ppermute | solution.py:357
  91.8 2.5 %shard_map.129 = (f32[512,768]{1,0:T(8,128)S(1)}, bf16[512,768]{1,0:T(8,128)(2,1)S(1)}) custom-call(s32[3]{0:T(128)S(1)} %pad_add_fusion.me_ref, bf16[512,768]{1,0:T(8,128)(2,1)S(1)} %shard_map.124.own_ref, bf16[512,768]{1,0:T(8,128)(2,1)S(1)} %shard_map.125.oth_ref, bf16[2,96,768]{2,1,0:T(8,128)(2,1)} %collective-permute-done.4.refs_0_, ...), custom_call_target="tpu_custom_call" | custom-call | tf_op jit(solution)/shard_map/pallas_call | solution.py:82
  94.4 0.1 shard_map.127
  94.6 1.4 %collective-permute-start.17 = (bf16[128,768]{1,0:T(8,128)(2,1)S(1)}, bf16[128,768]{1,0:T(8,128)(2,1)S(1)}, u32[]{:S(2)}, u32[]{:S(2)}) collective-permute-start(bf16[128,768]{1,0:T(8,128)(2,1)S(1)} %get-tuple-element.86), channel_id=1, source_target_pairs={{0,8},{4,12},{8,0},{12,4},{1,9},{5,13},{9,1},{13,5},{2,10},{6,14},... | collective-permute-start | bytes 589832 | tf_op jit(solution)/shard_map/ppermute | solution.py:353
  96.0 1.2 collective-permute-start.18
  97.3 0.1 shard_map.130
  97.4 0.2 collective-permute-start.21
  97.7 1.2 collective-permute-start.22
  98.9 1.7 %collective-permute-done.16.refs_0_ = bf16[128,768]{1,0:T(8,128)(2,1)S(1)} collective-permute-done((bf16[128,768]{1,0:T(8,128)(2,1)S(1)}, bf16[128,768]{1,0:T(8,128)(2,1)S(1)}, u32[]{:S(2)}, u32[]{:S(2)}) %collective-permute-start.16) | collective-permute-done | bytes 196640 | tf_op jit(solution)/shard_map/ppermute | solution.py:353
  100.6 1.1 collective-permute-start.23
  101.7 4.1 %collective-permute-done.18.refs_2_ = bf16[128,768]{1,0:T(8,128)(2,1)S(1)} collective-permute-done((bf16[128,768]{1,0:T(8,128)(2,1)S(1)}, bf16[128,768]{1,0:T(8,128)(2,1)S(1)}, u32[]{:S(2)}, u32[]{:S(2)}) %collective-permute-start.18) | collective-permute-done | bytes 196640 | tf_op jit(solution)/shard_map/ppermute | solution.py:353
  105.7 0.1 shard_map.128.near_ref
  105.8 3.0 %collective-permute-start.19 = (bf16[128,768]{1,0:T(8,128)(2,1)S(1)}, bf16[128,768]{1,0:T(8,128)(2,1)S(1)}, u32[]{:S(2)}, u32[]{:S(2)}) collective-permute-start(bf16[128,768]{1,0:T(8,128)(2,1)S(1)} %shard_map.128.near_ref), channel_id=1, source_target_pairs={{0,1},{1,0},{2,3},{3,2},{4,5},{5,4},{6,7},{7,6},{8,9},{9,8},{10,11... | collective-permute-start | bytes 589832 | tf_op jit(solution)/shard_map/ppermute | solution.py:357
  108.8 0.2 collective-permute-done.21.refs_0_
  109.1 5.0 %collective-permute-done.23.refs_2_ = bf16[128,768]{1,0:T(8,128)(2,1)S(1)} collective-permute-done((bf16[128,768]{1,0:T(8,128)(2,1)S(1)}, bf16[128,768]{1,0:T(8,128)(2,1)S(1)}, u32[]{:S(2)}, u32[]{:S(2)}) %collective-permute-start.23) | collective-permute-done | bytes 196640 | tf_op jit(solution)/shard_map/ppermute | solution.py:353
  114.1 0.1 shard_map.131.far_ref
  114.3 1.7 %collective-permute-start.24 = (bf16[128,768]{1,0:T(8,128)(2,1)S(1)}, bf16[128,768]{1,0:T(8,128)(2,1)S(1)}, u32[]{:S(2)}, u32[]{:S(2)}) collective-permute-start(bf16[128,768]{1,0:T(8,128)(2,1)S(1)} %shard_map.131.far_ref), channel_id=1, source_target_pairs={{0,1},{1,0},{2,3},{3,2},{4,5},{5,4},{6,7},{7,6},{8,9},{9,8},{10,11... | collective-permute-start | bytes 589832 | tf_op jit(solution)/shard_map/ppermute | solution.py:357
  116.0 1.1 collective-permute-done.24.far_oth_ref
  117.1 2.5 %shard_map.132 = (bf16[256,768]{1,0:T(8,128)(2,1)S(1)}, bf16[16,768]{1,0:T(8,128)(2,1)S(1)}, bf16[16,768]{1,0:T(8,128)(2,1)S(1)}, bf16[256,768]{1,0:T(8,128)(2,1)S(1)}) custom-call(s32[3]{0:T(128)S(1)} %pad_add_fusion.me_ref, bf16[128,768]{1,0:T(8,128)(2,1)S(1)} %shard_map.128.near_ref, bf16[128,768]{1,0:T(8,128)(2,1)S(1)} %collective-permute-done.19.near_oth_ref, ...), custom_call_target="tpu_custom_call" | custom-call | flops 1207959552 | bytes 4718592 | tf_op jit(solution)/shard_map/pallas_call | solution.py:82
  119.6 4.4 %shard_map.133.inner_ref = bf16[256,768]{1,0:T(8,128)(2,1)S(1)} custom-call(bf16[256,768]{1,0:T(8,128)(2,1)S(1)} %get-tuple-element.104.glu_ref, s32[8,280,128]{2,1,0:T(8,128)S(1)} %shard_map.120.utter_ref, f32[32,768]{1,0:T(8,128)S(1)} %copy-done.12, f32[1,768]{1,0:T(1,128)S(1)} %broadcast_in_dim.18.scale_ref, f32[1,768]{1,0:T(1,128)S(1)} %broadcast_in_dim.19.shift_ref), custom_call_target="tpu_custom_call" | custom-call | flops 6291456 | bytes 3145728 | tf_op jit(solution)/shard_map/pallas_call | solution.py:82
  124.0 0.4 collective-permute-start.25
  124.5 3.2 %collective-permute-start.26 = (bf16[16,768]{1,0:T(8,128)(2,1)S(1)}, bf16[16,768]{1,0:T(8,128)(2,1)S(1)}, u32[]{:S(2)}, u32[]{:S(2)}) collective-permute-start(bf16[16,768]{1,0:T(8,128)(2,1)S(1)} %get-tuple-element.108), channel_id=1, source_target_pairs={{0,2},{2,4},{4,6},{6,8},{8,10},{10,12},{12,14},{14,16},{16,18},{18... | collective-permute-start | bytes 73736 | tf_op jit(solution)/shard_map/ppermute | solution.py:320
  127.7 3.0 %collective-permute-start.27 = (bf16[16,768]{1,0:T(8,128)(2,1)S(1)}, bf16[16,768]{1,0:T(8,128)(2,1)S(1)}, u32[]{:S(2)}, u32[]{:S(2)}) collective-permute-start(bf16[16,768]{1,0:T(8,128)(2,1)S(1)} %get-tuple-element.109), channel_id=1, source_target_pairs={{2,0},{4,2},{6,4},{8,6},{10,8},{12,10},{14,12},{16,14},{18,16},{20... | collective-permute-start | bytes 73736 | tf_op jit(solution)/shard_map/ppermute | solution.py:321
  130.7 1.6 %collective-permute-done.27.bottom_ref = bf16[16,768]{1,0:T(8,128)(2,1)S(1)} collective-permute-done((bf16[16,768]{1,0:T(8,128)(2,1)S(1)}, bf16[16,768]{1,0:T(8,128)(2,1)S(1)}, u32[]{:S(2)}, u32[]{:S(2)}) %collective-permute-start.27) | collective-permute-done | bytes 24608 | tf_op jit(solution)/shard_map/ppermute | solution.py:321
  132.2 0.8 shard_map.134.edge_ref
  133.1 1.6 %collective-permute-start.28 = (bf16[32,768]{1,0:T(8,128)(2,1)S(1)}, bf16[32,768]{1,0:T(8,128)(2,1)S(1)}, u32[]{:S(2)}, u32[]{:S(2)}) collective-permute-start(bf16[32,768]{1,0:T(8,128)(2,1)S(1)} %shard_map.134.edge_ref), channel_id=1, source_target_pairs={{0,1},{1,0},{2,3},{3,2},{4,5},{5,4},{6,7},{7,6},{8,9},{9,8},{10,11... | collective-permute-start | bytes 147464 | tf_op jit(solution)/shard_map/ppermute | solution.py:357
  134.7 0.9 collective-permute-done.28.edge_oth_ref
  135.6 2.1 %shard_map.135 = bf16[256,768]{1,0:T(8,128)(2,1)} custom-call(s32[3]{0:T(128)S(1)} %pad_add_fusion.me_ref, bf16[256,768]{1,0:T(8,128)(2,1)S(1)} %shard_map.133.inner_ref, bf16[256,768]{1,0:T(8,128)(2,1)S(1)} %collective-permute-done.25.inner_oth_ref, bf16[32,768]{1,0:T(8,128)(2,1)S(1)} %shard_map.134.edge_ref, ...), custom_call_target="tpu_custom_call" | custom-call | flops 603979776 | bytes 2359296 | tf_op jit(solution)/shard_map/pallas_call | solution.py:82
  (70 shorter events, 0.7 us)
Async XLA Ops:
  2.3 6.3 %copy-start.20 = (f32[1536]{0:T(1024)S(1)}, f32[1536]{0:T(1024)}, u32[]{:S(2)}) copy-start(f32[1536]{0:T(1024)} %param.13) | copy-start | bytes 18436
  2.3 6.4 %copy-start.19 = (bf16[256,768]{1,0:T(8,128)(2,1)S(1)}, bf16[256,768]{1,0:T(8,128)(2,1)}, u32[]{:S(2)}) copy-start(bf16[256,768]{1,0:T(8,128)(2,1)} %param.12) | copy-start | bytes 1179652
  2.3 30.5 %all-to-all-start = ((bf16[4,192,768]{2,1,0:T(8,128)(2,1)}), bf16[4,192,768]{2,1,0:T(8,128)(2,1)S(1)}, u32[]{:S(2)}, u32[]{:S(2)}) async-start(bf16[4,192,768]{2,1,0:T(8,128)(2,1)} %shard_map.119), calls=%async_computation | async-start | bytes 2359296 | tf_op jit(solution)/shard_map/all_to_all | solution.py:361
  6.2 9.2 %copy-start.21 = (f32[1536]{0:T(1024)S(1)}, f32[1536]{0:T(1024)}, u32[]{:S(2)}) copy-start(f32[1536]{0:T(1024)} %param.16) | copy-start | bytes 18436
  6.2 9.2 %copy-start.22 = (f32[768]{0:T(1024)S(1)}, f32[768]{0:T(1024)}, u32[]{:S(2)}) copy-start(f32[768]{0:T(1024)} %param.20) | copy-start | bytes 9220
  6.2 9.2 %copy-start.23 = (f32[768]{0:T(1024)S(1)}, f32[768]{0:T(1024)}, u32[]{:S(2)}) copy-start(f32[768]{0:T(1024)} %param.21) | copy-start | bytes 9220
  6.2 9.3 %copy-start.17 = (s32[64]{0:T(128)S(1)}, s32[64]{0:T(128)}, u32[]{:S(2)}) copy-start(s32[64]{0:T(128)} %lengths_ref.1) | copy-start | bytes 772
  6.2 24.9 %collective-permute-start = (bf16[96,3072]{1,0:T(8,128)(2,1)}, bf16[96,3072]{1,0:T(8,128)(2,1)S(1)}, u32[]{:S(2)}, u32[]{:S(2)}) collective-permute-start(bf16[96,3072]{1,0:T(8,128)(2,1)} %refs_0_.1), channel_id=1, source_target_pairs={{0,16},{16,0},{1,17},{17,1},{2,18},{18,2},{3,19},{19,3},{4,20},{20... | collective-permute-start | bytes 1769480 | tf_op jit(solution)/shard_map/ppermute | solution.py:357
  13.3 0.8 copy-start.6
  14.0 0.7 copy-start.13
  14.7 0.7 copy-start.15
  15.4 17.4 %copy-start.8 = (bf16[128,1536]{1,0:T(8,128)(2,1)}, bf16[128,1536]{1,0:T(8,128)(2,1)S(1)}, u32[]{:S(2)}) copy-start(bf16[128,1536]{1,0:T(8,128)(2,1)S(1)} %get-tuple-element.61.refs_0_) | copy-start | bytes 1179652
  15.4 15.7 %collective-permute-start.1 = (bf16[128,1536]{1,0:T(8,128)(2,1)S(1)}, bf16[128,1536]{1,0:T(8,128)(2,1)}, u32[]{:S(2)}, u32[]{:S(2)}) collective-permute-start(bf16[128,1536]{1,0:T(8,128)(2,1)S(1)} %get-tuple-element.61.refs_0_), channel_id=1, source_target_pairs={{0,4},{4,0},{8,12},{12,8},{1,5},{5,1},{9,13},{13,9},{2,6},{6,2},{1... | collective-permute-start | bytes 1179656 | tf_op jit(solution)/shard_map/ppermute | solution.py:353
  31.1 0.8 copy-start.4
  32.8 28.1 %collective-permute-start.3 = (bf16[4,192,768]{2,1,0:T(8,128)(2,1)S(1)}, bf16[4,192,768]{2,1,0:T(8,128)(2,1)S(1)}, u32[]{:S(2)}, u32[]{:S(2)}) collective-permute-start(bf16[4,192,768]{2,1,0:T(8,128)(2,1)S(1)} %all-to-all-done.both_ref.refs_5_.refs_0_), channel_id=1, source_target_pairs={{0,2},{2,0},{1,3},{3,1},{4,6},{6,4},{5,7},{7,5},{8,10},{10,8},{9,1... | collective-permute-start | bytes 3538952 | tf_op jit(solution)/shard_map/ppermute | solution.py:357
  34.1 1.1 copy-start.5
  35.2 0.8 copy-start.3
  36.0 25.0 %all-to-all-start.1 = ((bf16[4,96,768]{2,1,0:T(8,128)(2,1)}), bf16[4,96,768]{2,1,0:T(8,128)(2,1)}, u32[]{:S(2)}, u32[]{:S(2)}) async-start(bf16[4,96,768]{2,1,0:T(8,128)(2,1)} %copy-done.3), calls=%async_computation.1 | async-start | bytes 1179648 | tf_op jit(solution)/shard_map/all_to_all | solution.py:361
  41.5 18.8 %collective-permute-start.5 = (bf16[128,1536]{1,0:T(8,128)(2,1)}, bf16[128,1536]{1,0:T(8,128)(2,1)S(1)}, u32[]{:S(2)}, u32[]{:S(2)}) collective-permute-start(bf16[128,1536]{1,0:T(8,128)(2,1)} %collective-permute-done.1.refs_1_), channel_id=1, source_target_pairs={{0,1},{1,0},{2,3},{3,2},{4,5},{5,4},{6,7},{7,6},{8,9},{9,8},{10,11... | collective-permute-start | bytes 1179656 | tf_op jit(solution)/shard_map/ppermute | solution.py:357
  44.2 0.7 copy-start.18
  44.9 15.3 %collective-permute-start.4 = (bf16[2,96,768]{2,1,0:T(8,128)(2,1)S(1)}, bf16[2,96,768]{2,1,0:T(8,128)(2,1)}, u32[]{:S(2)}, u32[]{:S(2)}) collective-permute-start(bf16[2,96,768]{2,1,0:T(8,128)(2,1)S(1)} %get-tuple-element.65), channel_id=1, source_target_pairs={{0,16},{16,0},{1,17},{17,1},{2,18},{18,2},{3,19},{19,3},{4,20},{20... | collective-permute-start | bytes 884744 | tf_op jit(solution)/shard_map/ppermute | solution.py:357
  47.4 16.3 %collective-permute-start.2 = (bf16[128,1536]{1,0:T(8,128)(2,1)}, bf16[128,1536]{1,0:T(8,128)(2,1)}, u32[]{:S(2)}, u32[]{:S(2)}) collective-permute-start(bf16[128,1536]{1,0:T(8,128)(2,1)} %copy-done.8), channel_id=1, source_target_pairs={{0,8},{4,12},{8,0},{12,4},{1,9},{5,13},{9,1},{13,5},{2,10},{6,14},... | collective-permute-start | bytes 1179656 | tf_op jit(solution)/shard_map/ppermute | solution.py:353
  60.2 0.7 copy-start.10
  61.0 14.8 %collective-permute-start.6 = (bf16[4,96,768]{2,1,0:T(8,128)(2,1)}, bf16[4,96,768]{2,1,0:T(8,128)(2,1)S(1)}, u32[]{:S(2)}, u32[]{:S(2)}) collective-permute-start(bf16[4,96,768]{2,1,0:T(8,128)(2,1)} %all-to-all-done.1.refs_7_), channel_id=1, source_target_pairs={{0,2},{2,0},{1,3},{3,1},{4,6},{6,4},{5,7},{7,5},{8,10},{10,8},{9,1... | collective-permute-start | bytes 1769480 | tf_op jit(solution)/shard_map/ppermute | solution.py:357
  61.2 14.6 %collective-permute-start.7 = (bf16[2,96,768]{2,1,0:T(8,128)(2,1)}, bf16[2,96,768]{2,1,0:T(8,128)(2,1)S(1)}, u32[]{:S(2)}, u32[]{:S(2)}) collective-permute-start(bf16[2,96,768]{2,1,0:T(8,128)(2,1)} %copy-done.18), channel_id=1, source_target_pairs={{0,16},{16,0},{1,17},{17,1},{2,18},{18,2},{3,19},{19,3},{4,20},{20... | collective-permute-start | bytes 884744 | tf_op jit(solution)/shard_map/ppermute | solution.py:357
  63.6 20.6 %copy-start.11 = (bf16[128,1536]{1,0:T(8,128)(2,1)S(1)}, bf16[128,1536]{1,0:T(8,128)(2,1)}, u32[]{:S(2)}) copy-start(bf16[128,1536]{1,0:T(8,128)(2,1)} %copy-done.10) | copy-start | bytes 1179652
  64.7 7.1 %collective-permute-start.8 = (bf16[64,1536]{1,0:T(8,128)(2,1)S(1)}, bf16[64,1536]{1,0:T(8,128)(2,1)S(1)}, u32[]{:S(2)}, u32[]{:S(2)}) collective-permute-start(bf16[64,1536]{1,0:T(8,128)(2,1)S(1)} %get-tuple-element.70), channel_id=1, source_target_pairs={{0,4},{4,0},{8,12},{12,8},{1,5},{5,1},{9,13},{13,9},{2,6},{6,2},{1... | collective-permute-start | bytes 589832 | tf_op jit(solution)/shard_map/ppermute | solution.py:353
  64.8 19.4 %copy-start.7 = (bf16[128,1536]{1,0:T(8,128)(2,1)S(1)}, bf16[128,1536]{1,0:T(8,128)(2,1)}, u32[]{:S(2)}) copy-start(bf16[128,1536]{1,0:T(8,128)(2,1)} %copy-done.6) | copy-start | bytes 1179652
  64.8 7.0 %collective-permute-start.9 = (bf16[64,1536]{1,0:T(8,128)(2,1)S(1)}, bf16[64,1536]{1,0:T(8,128)(2,1)S(1)}, u32[]{:S(2)}, u32[]{:S(2)}) collective-permute-start(bf16[64,1536]{1,0:T(8,128)(2,1)S(1)} %get-tuple-element.71), channel_id=1, source_target_pairs={{0,4},{4,0},{8,12},{12,8},{1,5},{5,1},{9,13},{13,9},{2,6},{6,2},{1... | collective-permute-start | bytes 589832 | tf_op jit(solution)/shard_map/ppermute | solution.py:353
  66.2 17.9 %collective-permute-start.10 = (bf16[128,1536]{1,0:T(8,128)(2,1)}, bf16[128,1536]{1,0:T(8,128)(2,1)S(1)}, u32[]{:S(2)}, u32[]{:S(2)}) collective-permute-start(bf16[128,1536]{1,0:T(8,128)(2,1)} %collective-permute-done.2.ref.refs_2_), channel_id=1, source_target_pairs={{0,1},{1,0},{2,3},{3,2},{4,5},{5,4},{6,7},{7,6},{8,9},{9,8},{10,11... | collective-permute-start | bytes 1179656 | tf_op jit(solution)/shard_map/ppermute | solution.py:357
  75.8 13.2 %collective-permute-start.13 = (bf16[2,96,768]{2,1,0:T(8,128)(2,1)}, bf16[2,96,768]{2,1,0:T(8,128)(2,1)S(1)}, u32[]{:S(2)}, u32[]{:S(2)}) collective-permute-start(bf16[2,96,768]{2,1,0:T(8,128)(2,1)} %collective-permute-done.4.refs_0_), channel_id=1, source_target_pairs={{0,2},{2,0},{1,3},{3,1},{4,6},{6,4},{5,7},{7,5},{8,10},{10,8},{9,1... | collective-permute-start | bytes 884744 | tf_op jit(solution)/shard_map/ppermute | solution.py:357
  77.1 11.9 %collective-permute-start.14 = (bf16[2,96,768]{2,1,0:T(8,128)(2,1)S(1)}, bf16[2,96,768]{2,1,0:T(8,128)(2,1)S(1)}, u32[]{:S(2)}, u32[]{:S(2)}) collective-permute-start(bf16[2,96,768]{2,1,0:T(8,128)(2,1)S(1)} %collective-permute-done.7.refs_1_), channel_id=1, source_target_pairs={{0,2},{2,0},{1,3},{3,1},{4,6},{6,4},{5,7},{7,5},{8,10},{10,8},{9,1... | collective-permute-start | bytes 884744 | tf_op jit(solution)/shard_map/ppermute | solution.py:357
  77.3 6.9 %collective-permute-start.11 = (bf16[64,1536]{1,0:T(8,128)(2,1)S(1)}, bf16[64,1536]{1,0:T(8,128)(2,1)S(1)}, u32[]{:S(2)}, u32[]{:S(2)}) collective-permute-start(bf16[64,1536]{1,0:T(8,128)(2,1)S(1)} %collective-permute-done.8.refs_3_), channel_id=1, source_target_pairs={{0,1},{1,0},{2,3},{3,2},{4,5},{5,4},{6,7},{7,6},{8,9},{9,8},{10,11... | collective-permute-start | bytes 589832 | tf_op jit(solution)/shard_map/ppermute | solution.py:357
  80.2 4.0 %collective-permute-start.12 = (bf16[64,1536]{1,0:T(8,128)(2,1)S(1)}, bf16[64,1536]{1,0:T(8,128)(2,1)S(1)}, u32[]{:S(2)}, u32[]{:S(2)}) collective-permute-start(bf16[64,1536]{1,0:T(8,128)(2,1)S(1)} %collective-permute-done.9.refs_4_), channel_id=1, source_target_pairs={{0,1},{1,0},{2,3},{3,2},{4,5},{5,4},{6,7},{7,6},{8,9},{9,8},{10,11... | collective-permute-start | bytes 589832 | tf_op jit(solution)/shard_map/ppermute | solution.py:357
  80.2 1.0 copy-start.9
  89.0 5.4 %collective-permute-start.15 = (bf16[512,768]{1,0:T(8,128)(2,1)S(1)}, bf16[512,768]{1,0:T(8,128)(2,1)S(1)}, u32[]{:S(2)}, u32[]{:S(2)}) collective-permute-start(bf16[512,768]{1,0:T(8,128)(2,1)S(1)} %get-tuple-element.83), channel_id=1, source_target_pairs={{0,1},{1,0},{2,3},{3,2},{4,5},{5,4},{6,7},{7,6},{8,9},{9,8},{10,11... | collective-permute-start | bytes 2359304 | tf_op jit(solution)/shard_map/ppermute | solution.py:357
  94.3 3.0 %collective-permute-start.20 = (bf16[512,768]{1,0:T(8,128)(2,1)S(1)}, bf16[512,768]{1,0:T(8,128)(2,1)S(1)}, u32[]{:S(2)}, u32[]{:S(2)}) collective-permute-start(bf16[512,768]{1,0:T(8,128)(2,1)S(1)} %get-tuple-element.91), channel_id=1, source_target_pairs={{0,1},{1,0},{2,3},{3,2},{4,5},{5,4},{6,7},{7,6},{8,9},{9,8},{10,11... | collective-permute-start | bytes 2359304 | tf_op jit(solution)/shard_map/ppermute | solution.py:357
  94.5 11.2 %copy-start.16 = (bf16[128,768]{1,0:T(8,128)(2,1)S(1)}, bf16[128,768]{1,0:T(8,128)(2,1)}, u32[]{:S(2)}) copy-start(bf16[128,768]{1,0:T(8,128)(2,1)} %copy-done.15) | copy-start | bytes 589828
  94.5 6.0 %collective-permute-start.16 = (bf16[128,768]{1,0:T(8,128)(2,1)S(1)}, bf16[128,768]{1,0:T(8,128)(2,1)S(1)}, u32[]{:S(2)}, u32[]{:S(2)}) collective-permute-start(bf16[128,768]{1,0:T(8,128)(2,1)S(1)} %get-tuple-element.85), channel_id=1, source_target_pairs={{0,4},{4,0},{8,12},{12,8},{1,5},{5,1},{9,13},{13,9},{2,6},{6,2},{1... | collective-permute-start | bytes 589832 | tf_op jit(solution)/shard_map/ppermute | solution.py:353
  94.6 7.0 %collective-permute-start.17 = (bf16[128,768]{1,0:T(8,128)(2,1)S(1)}, bf16[128,768]{1,0:T(8,128)(2,1)S(1)}, u32[]{:S(2)}, u32[]{:S(2)}) collective-permute-start(bf16[128,768]{1,0:T(8,128)(2,1)S(1)} %get-tuple-element.86), channel_id=1, source_target_pairs={{0,8},{4,12},{8,0},{12,4},{1,9},{5,13},{9,1},{13,5},{2,10},{6,14},... | collective-permute-start | bytes 589832 | tf_op jit(solution)/shard_map/ppermute | solution.py:353
  96.0 9.7 %collective-permute-start.18 = (bf16[128,768]{1,0:T(8,128)(2,1)S(1)}, bf16[128,768]{1,0:T(8,128)(2,1)S(1)}, u32[]{:S(2)}, u32[]{:S(2)}) collective-permute-start(bf16[128,768]{1,0:T(8,128)(2,1)S(1)} %get-tuple-element.87), channel_id=1, source_target_pairs={{0,12},{4,8},{8,4},{12,0},{1,13},{5,9},{9,5},{13,1},{2,14},{6,10},... | collective-permute-start | bytes 589832 | tf_op jit(solution)/shard_map/ppermute | solution.py:353
  97.3 16.9 %copy-start.14 = (bf16[128,768]{1,0:T(8,128)(2,1)S(1)}, bf16[128,768]{1,0:T(8,128)(2,1)}, u32[]{:S(2)}) copy-start(bf16[128,768]{1,0:T(8,128)(2,1)} %copy-done.13) | copy-start | bytes 589828
  97.3 19.8 %copy-start.1 = (bf16[1536,768]{1,0:T(8,128)(2,1)S(1)}, bf16[1536,768]{1,0:T(8,128)(2,1)}, u32[]{:S(2)}) copy-start(bf16[1536,768]{1,0:T(8,128)(2,1)} %gate_ref.1) | copy-start | bytes 7077892
  97.4 19.7 %copy-start = (bf16[1536,768]{1,0:T(8,128)(2,1)S(1)}, bf16[1536,768]{1,0:T(8,128)(2,1)}, u32[]{:S(2)}) copy-start(bf16[1536,768]{1,0:T(8,128)(2,1)} %value_ref.1) | copy-start | bytes 7077892
  97.4 11.6 %collective-permute-start.21 = (bf16[128,768]{1,0:T(8,128)(2,1)S(1)}, bf16[128,768]{1,0:T(8,128)(2,1)S(1)}, u32[]{:S(2)}, u32[]{:S(2)}) collective-permute-start(bf16[128,768]{1,0:T(8,128)(2,1)S(1)} %get-tuple-element.93), channel_id=1, source_target_pairs={{0,4},{4,0},{8,12},{12,8},{1,5},{5,1},{9,13},{13,9},{2,6},{6,2},{1... | collective-permute-start | bytes 589832 | tf_op jit(solution)/shard_map/ppermute | solution.py:353
  97.7 11.5 %collective-permute-start.22 = (bf16[128,768]{1,0:T(8,128)(2,1)S(1)}, bf16[128,768]{1,0:T(8,128)(2,1)S(1)}, u32[]{:S(2)}, u32[]{:S(2)}) collective-permute-start(bf16[128,768]{1,0:T(8,128)(2,1)S(1)} %get-tuple-element.94), channel_id=1, source_target_pairs={{0,8},{4,12},{8,0},{12,4},{1,9},{5,13},{9,1},{13,5},{2,10},{6,14},... | collective-permute-start | bytes 589832 | tf_op jit(solution)/shard_map/ppermute | solution.py:353
  100.6 13.6 %collective-permute-start.23 = (bf16[128,768]{1,0:T(8,128)(2,1)S(1)}, bf16[128,768]{1,0:T(8,128)(2,1)S(1)}, u32[]{:S(2)}, u32[]{:S(2)}) collective-permute-start(bf16[128,768]{1,0:T(8,128)(2,1)S(1)} %get-tuple-element.95), channel_id=1, source_target_pairs={{0,12},{4,8},{8,4},{12,0},{1,13},{5,9},{9,5},{13,1},{2,14},{6,10},... | collective-permute-start | bytes 589832 | tf_op jit(solution)/shard_map/ppermute | solution.py:353
  105.8 8.3 %collective-permute-start.19 = (bf16[128,768]{1,0:T(8,128)(2,1)S(1)}, bf16[128,768]{1,0:T(8,128)(2,1)S(1)}, u32[]{:S(2)}, u32[]{:S(2)}) collective-permute-start(bf16[128,768]{1,0:T(8,128)(2,1)S(1)} %shard_map.128.near_ref), channel_id=1, source_target_pairs={{0,1},{1,0},{2,3},{3,2},{4,5},{5,4},{6,7},{7,6},{8,9},{9,8},{10,11... | collective-permute-start | bytes 589832 | tf_op jit(solution)/shard_map/ppermute | solution.py:357
  114.3 5.3 %copy-start.12 = (f32[32,768]{1,0:T(8,128)S(1)}, f32[32,768]{1,0:T(8,128)}, u32[]{:S(2)}) copy-start(f32[32,768]{1,0:T(8,128)} %taps_ref.3) | copy-start | bytes 294916
  114.3 2.8 %collective-permute-start.24 = (bf16[128,768]{1,0:T(8,128)(2,1)S(1)}, bf16[128,768]{1,0:T(8,128)(2,1)S(1)}, u32[]{:S(2)}, u32[]{:S(2)}) collective-permute-start(bf16[128,768]{1,0:T(8,128)(2,1)S(1)} %shard_map.131.far_ref), channel_id=1, source_target_pairs={{0,1},{1,0},{2,3},{3,2},{4,5},{5,4},{6,7},{7,6},{8,9},{9,8},{10,11... | collective-permute-start | bytes 589832 | tf_op jit(solution)/shard_map/ppermute | solution.py:357
  119.6 16.0 %copy-start.2 = (bf16[1536,768]{1,0:T(8,128)(2,1)S(1)}, bf16[1536,768]{1,0:T(8,128)(2,1)}, u32[]{:S(2)}) copy-start(bf16[1536,768]{1,0:T(8,128)(2,1)} %w_ref.1) | copy-start | bytes 7077892
  124.0 11.6 %collective-permute-start.25 = (bf16[256,768]{1,0:T(8,128)(2,1)S(1)}, bf16[256,768]{1,0:T(8,128)(2,1)S(1)}, u32[]{:S(2)}, u32[]{:S(2)}) collective-permute-start(bf16[256,768]{1,0:T(8,128)(2,1)S(1)} %shard_map.133.inner_ref), channel_id=1, source_target_pairs={{0,1},{1,0},{2,3},{3,2},{4,5},{5,4},{6,7},{7,6},{8,9},{9,8},{10,11... | collective-permute-start | bytes 1179656 | tf_op jit(solution)/shard_map/ppermute | solution.py:357
  124.5 6.2 %collective-permute-start.26 = (bf16[16,768]{1,0:T(8,128)(2,1)S(1)}, bf16[16,768]{1,0:T(8,128)(2,1)S(1)}, u32[]{:S(2)}, u32[]{:S(2)}) collective-permute-start(bf16[16,768]{1,0:T(8,128)(2,1)S(1)} %get-tuple-element.108), channel_id=1, source_target_pairs={{0,2},{2,4},{4,6},{6,8},{8,10},{10,12},{12,14},{14,16},{16,18},{18... | collective-permute-start | bytes 73736 | tf_op jit(solution)/shard_map/ppermute | solution.py:320
  127.7 4.6 %collective-permute-start.27 = (bf16[16,768]{1,0:T(8,128)(2,1)S(1)}, bf16[16,768]{1,0:T(8,128)(2,1)S(1)}, u32[]{:S(2)}, u32[]{:S(2)}) collective-permute-start(bf16[16,768]{1,0:T(8,128)(2,1)S(1)} %get-tuple-element.109), channel_id=1, source_target_pairs={{2,0},{4,2},{6,4},{8,6},{10,8},{12,10},{14,12},{16,14},{18,16},{20... | collective-permute-start | bytes 73736 | tf_op jit(solution)/shard_map/ppermute | solution.py:321
  133.1 2.5 %collective-permute-start.28 = (bf16[32,768]{1,0:T(8,128)(2,1)S(1)}, bf16[32,768]{1,0:T(8,128)(2,1)S(1)}, u32[]{:S(2)}, u32[]{:S(2)}) collective-permute-start(bf16[32,768]{1,0:T(8,128)(2,1)S(1)} %shard_map.134.edge_ref), channel_id=1, source_target_pairs={{0,1},{1,0},{2,3},{3,2},{4,5},{5,4},{6,7},{7,6},{8,9},{9,8},{10,11... | collective-permute-start | bytes 147464 | tf_op jit(solution)/shard_map/ppermute | solution.py:357
